TPU v7x, 32 devices: a whole 2x2x4 slice. The times are simulated.
32 devices in a mesh: wide: 8 (over y, x, core), narrow: 4 (over z).
Axes of the slice: x: 2, y: 2, z: 4, core: 2. Of those that a mesh axis runs over, the one named last changes fastest.
Arguments:
- inputs: bfloat16 [2, 32, 512, 768], P(None, ('wide', 'narrow')), may hold values from -6 to 6
- encoder_out: bfloat16 [2, 32, 512, 768], P(None, ('wide', 'narrow')), may hold values from -6 to 6
- segments: int32 [2, 32, 512], P(None, ('wide', 'narrow')), may hold values from 0 to 3, as said below
- enc_segments: int32 [2, 32, 512], P(None, ('wide', 'narrow')), may hold values from 0 to 3, as said below
- buckets: int32 [512], replicated, may hold values from 0 to 31, as said below
- gains: bfloat16 [3, 768], P(None, ('wide', 'narrow')), may hold values from 0.5 to 1.5
- rel_bias: float32 [32, 12], replicated, may hold values from -4 to 4
- self_q: bfloat16 [768, 768], P(('wide', 'narrow')), may hold values from -0.0546875 to 0.0546875
- self_kv: bfloat16 [2, 768, 768], P(None, ('wide', 'narrow')), may hold values from -0.21875 to 0.21875
- self_out: bfloat16 [768, 768], P(None, ('wide', 'narrow')), may hold values from -1.25 to 1.25
- cross_q: bfloat16 [768, 768], P(('wide', 'narrow')), may hold values from -0.0546875 to 0.0546875
- cross_kv: bfloat16 [2, 768, 768], P(None, ('wide', 'narrow')), may hold values from -0.21875 to 0.21875
- cross_out: bfloat16 [768, 768], P(None, ('wide', 'narrow')), may hold values from -1.25 to 1.25
- ffn_in: bfloat16 [768, 3072], P(('wide', 'narrow')), may hold values from -0.21875 to 0.21875
- ffn_out: bfloat16 [3072, 768], P(None, ('wide', 'narrow')), may hold values from -0.15625 to 0.15625
- out_grad: bfloat16 [2, 32, 512, 768], P(None, ('wide', 'narrow')), may hold values from -6 to 6
Outputs:
- layer_out: bfloat16 [2, 32, 512, 768], P(None, ('wide', 'narrow'))
- input_grad: float32 [2, 32, 512, 768], P(None, ('wide', 'narrow'))
- encoder_grad: float32 [2, 32, 512, 768], P(None, ('wide', 'narrow'))
- gains_grad: float32 [3, 768], P(None, ('wide', 'narrow'))
- rel_bias_grad: float32 [32, 12], replicated
- self_q_grad: float32 [768, 768], P(('wide', 'narrow'))
- self_kv_grad: float32 [2, 768, 768], P(None, ('wide', 'narrow'))
- self_out_grad: float32 [768, 768], P(None, ('wide', 'narrow'))
- cross_q_grad: float32 [768, 768], P(('wide', 'narrow'))
- cross_kv_grad: float32 [2, 768, 768], P(None, ('wide', 'narrow'))
- cross_out_grad: float32 [768, 768], P(None, ('wide', 'narrow'))
- ffn_in_grad: float32 [768, 3072], P(('wide', 'narrow'))
- ffn_out_grad: float32 [3072, 768], P(None, ('wide', 'narrow'))
Inputs may be any that keep to these rules, and one draw needn't show every extreme that they name: `segments`: along each row the ids never fall; the first position has 0 and the last 3; a document may be empty. `enc_segments`: along each row the ids never fall, and every id 0 to 3 appears in every row. buckets[0] is 0, the buckets never fall as the distance grows, and the last is 31.
All inputs are finite; a program needn't handle non-finite values.
Results may differ from a plain program's by a relative error of at most 0.023.
The roundings to bfloat16 on the way count: a program that leaves them out, or rounds other values in their place, can miss the bound.
Values may be sent and summed in bfloat16 or wider, within the bound.
No kernel may reach another device: no remote copies, remote signals or barrier semaphores. Data moves between devices by JAX's collectives and lax.ppermute only.
A program may use at most 320 MiB of HBM per device.

v0:
```python
import jax
import jax.numpy as jnp
from jax import lax
from jax.sharding import PartitionSpec as P

D = 768
H = 12
DH = 64
FF = 3072
HD = 768


EPSILON = 1e-06
NEGATIVE = -1e30
ROOT_HALF = 0.7071067811865476
INV_ROOT_TWO_PI = 0.3989422804014327


def matmul(left_rows, right_rows):
    return jnp.dot(left_rows, right_rows, preferred_element_type=jnp.float32)


def outer_sum(left_rows, right_rows):
    return lax.dot_general(
        left_rows, right_rows, (((0,), (0,)), ((), ())), preferred_element_type=jnp.float32
    )


def back_product(grad_rows, weight):
    return lax.dot_general(
        grad_rows, weight, (((1,), (1,)), ((), ())), preferred_element_type=jnp.float32
    )


def gelu_exact(values):
    return values * 0.5 * (1.0 + lax.erf(values * ROOT_HALF))


def gelu_slope(values):
    return (
        0.5 * (1.0 + lax.erf(values * ROOT_HALF))
        + values * jnp.exp(-0.5 * values * values) * INV_ROOT_TWO_PI
    )


def rms_forward(value_rows, gain_row):
    inverse = lax.rsqrt(jnp.mean(value_rows * value_rows, axis=-1, keepdims=True) + EPSILON)
    unit_rows = value_rows * inverse
    return (unit_rows * gain_row, unit_rows, inverse)


def rms_backward(grad_norm, unit_rows, inverse, gain_row):
    grad_gain = jnp.sum(grad_norm * unit_rows, axis=0)
    grad_unit = grad_norm * gain_row
    grad_value = inverse * (
        grad_unit - unit_rows * jnp.mean(grad_unit * unit_rows, axis=-1, keepdims=True)
    )
    return (grad_value, grad_gain)


def expand_bias(bias_params, buckets):
    length = buckets.shape[0]
    one_hot = (buckets[:, None] == jnp.arange(bias_params.shape[0])[None, :]).astype(jnp.float32)
    per_distance = jnp.dot(
        one_hot, bias_params, precision=lax.Precision.HIGHEST, preferred_element_type=jnp.float32
    )
    positions = jnp.arange(length)
    distance = jnp.clip(positions[:, None] - positions[None, :], 0, length - 1)
    return jnp.take(per_distance.T, distance, axis=1)


def bucket_table(buckets, count):
    length = buckets.shape[0]
    positions = jnp.arange(length)
    distance = jnp.clip(positions[:, None] - positions[None, :], 0, length - 1)
    bucket_at = jnp.take(buckets, distance)
    return (bucket_at[:, :, None] == jnp.arange(count)[None, None, :]).astype(jnp.bfloat16)


def split_heads(rows_in):
    return rows_in.reshape(rows_in.shape[0], H, DH)


def merge_heads(heads_in):
    return heads_in.reshape(heads_in.shape[0], H * DH).astype(jnp.bfloat16)


def attend_forward(queries, key_rows, value_rows, bias_term, allowed):
    scores = (
        jnp.einsum(
            "qhd,khd->hqk",
            split_heads(queries),
            split_heads(key_rows),
            preferred_element_type=jnp.float32,
        )
        + bias_term
    )
    scores = jnp.where(allowed[None], scores, NEGATIVE)
    row_top = jnp.max(scores, axis=-1, keepdims=True)
    exponent = jnp.exp(scores - row_top)
    row_total = jnp.sum(exponent, axis=-1, keepdims=True)
    softmax_rows = (exponent / row_total).astype(jnp.bfloat16)
    mixture = jnp.einsum(
        "hqk,khd->qhd", softmax_rows, split_heads(value_rows), preferred_element_type=jnp.float32
    )
    return (merge_heads(mixture), row_top + jnp.log(row_total))


def attend_backward(grad_mix, queries, key_rows, value_rows, bias_term, allowed, log_total):
    heads_q = split_heads(queries)
    heads_k = split_heads(key_rows)
    heads_v = split_heads(value_rows)
    heads_g = split_heads(grad_mix)
    scores = (
        jnp.einsum("qhd,khd->hqk", heads_q, heads_k, preferred_element_type=jnp.float32) + bias_term
    )
    scores = jnp.where(allowed[None], scores, NEGATIVE)
    softmax_rows = jnp.exp(scores - log_total)
    softmax_low = softmax_rows.astype(jnp.bfloat16)
    grad_values = jnp.einsum(
        "hqk,qhd->khd", softmax_low, heads_g, preferred_element_type=jnp.float32
    )
    grad_soft = jnp.einsum("qhd,khd->hqk", heads_g, heads_v, preferred_element_type=jnp.float32)
    inner_sum = jnp.sum(softmax_rows * grad_soft, axis=-1, keepdims=True)
    grad_scores = (softmax_rows * (grad_soft - inner_sum)).astype(jnp.bfloat16)
    grad_queries = jnp.einsum(
        "hqk,khd->qhd", grad_scores, heads_k, preferred_element_type=jnp.float32
    )
    grad_keys = jnp.einsum("hqk,qhd->khd", grad_scores, heads_q, preferred_element_type=jnp.float32)
    return (
        merge_heads(grad_queries),
        merge_heads(grad_keys),
        merge_heads(grad_values),
        grad_scores,
    )


def body(
    inputs,
    encoder_out,
    segments,
    enc_segments,
    buckets,
    gains,
    rel_bias,
    self_q,
    self_kv,
    self_out,
    cross_q,
    cross_kv,
    cross_out,
    ffn_in,
    ffn_out,
    out_grad,
):
    bias_term = expand_bias(rel_bias, buckets)
    bucket_hot = bucket_table(buckets, rel_bias.shape[0])
    length = inputs.shape[2]
    positions = jnp.arange(length)
    zero_sums = (
        jnp.zeros((3, D), jnp.float32),
        jnp.zeros((D, HD), jnp.float32),
        jnp.zeros((2, D, HD), jnp.float32),
        jnp.zeros((HD, D), jnp.float32),
        jnp.zeros((D, HD), jnp.float32),
        jnp.zeros((2, D, HD), jnp.float32),
        jnp.zeros((HD, D), jnp.float32),
        jnp.zeros((D, FF), jnp.float32),
        jnp.zeros((FF, D), jnp.float32),
    )
    zero_bias = jnp.zeros(rel_bias.shape, jnp.float32)

    def one_micro(running, micro_items):
        grad_sums, bias_sum = running
        row_in, enc_rows, seg_row, enc_seg_row, grad_out = micro_items
        causal = (positions[:, None] >= positions[None, :]) & (seg_row[:, None] == seg_row[None, :])
        cross_mask = seg_row[:, None] == enc_seg_row[None, :]
        fwd_full = (
            lax.all_gather(gains, ("wide", "narrow"), axis=1, tiled=True),
            lax.all_gather(self_q, ("wide", "narrow"), axis=0, tiled=True),
            lax.all_gather(self_kv, ("wide", "narrow"), axis=1, tiled=True),
            lax.all_gather(self_out, ("wide", "narrow"), axis=1, tiled=True),
            lax.all_gather(cross_q, ("wide", "narrow"), axis=0, tiled=True),
            lax.all_gather(cross_kv, ("wide", "narrow"), axis=1, tiled=True),
            lax.all_gather(cross_out, ("wide", "narrow"), axis=1, tiled=True),
            lax.all_gather(ffn_in, ("wide", "narrow"), axis=0, tiled=True),
            lax.all_gather(ffn_out, ("wide", "narrow"), axis=1, tiled=True),
        )
        norm_gains, w_query, w_keyval, w_output, c_query, c_keyval, c_output, w_inner, w_outer = (
            fwd_full
        )
        gain_rows = norm_gains.astype(jnp.float32)
        state_in = row_in.astype(jnp.float32)
        normed_one, unit_one, inverse_one = rms_forward(state_in, gain_rows[0])
        normed_one = normed_one.astype(jnp.bfloat16)
        queries = matmul(normed_one, w_query).astype(jnp.bfloat16)
        key_rows = matmul(normed_one, w_keyval[0]).astype(jnp.bfloat16)
        value_rows = matmul(normed_one, w_keyval[1]).astype(jnp.bfloat16)
        attended, lse_self = attend_forward(queries, key_rows, value_rows, bias_term, causal)
        state_two = state_in + matmul(attended, w_output)
        normed_two, unit_two, inverse_two = rms_forward(state_two, gain_rows[1])
        normed_two = normed_two.astype(jnp.bfloat16)
        cross_queries = matmul(normed_two, c_query).astype(jnp.bfloat16)
        cross_keys = matmul(enc_rows, c_keyval[0]).astype(jnp.bfloat16)
        cross_values = matmul(enc_rows, c_keyval[1]).astype(jnp.bfloat16)
        cross_mixed, lse_cross = attend_forward(
            cross_queries, cross_keys, cross_values, 0.0, cross_mask
        )
        state_three = state_two + matmul(cross_mixed, c_output)
        normed_three, unit_three, inverse_three = rms_forward(state_three, gain_rows[2])
        normed_three = normed_three.astype(jnp.bfloat16)
        inner_pre = matmul(normed_three, w_inner)
        inner_act = gelu_exact(inner_pre).astype(jnp.bfloat16)
        layer_rows = (state_three + matmul(inner_act, w_outer)).astype(jnp.bfloat16)
        back_full = (
            lax.all_gather(gains, ("wide", "narrow"), axis=1, tiled=True),
            lax.all_gather(self_q, ("wide", "narrow"), axis=0, tiled=True),
            lax.all_gather(self_kv, ("wide", "narrow"), axis=1, tiled=True),
            lax.all_gather(self_out, ("wide", "narrow"), axis=1, tiled=True),
            lax.all_gather(cross_q, ("wide", "narrow"), axis=0, tiled=True),
            lax.all_gather(cross_kv, ("wide", "narrow"), axis=1, tiled=True),
            lax.all_gather(cross_out, ("wide", "narrow"), axis=1, tiled=True),
            lax.all_gather(ffn_in, ("wide", "narrow"), axis=0, tiled=True),
            lax.all_gather(ffn_out, ("wide", "narrow"), axis=1, tiled=True),
        )
        norm_gains, w_query, w_keyval, w_output, c_query, c_keyval, c_output, w_inner, w_outer = (
            back_full
        )
        gain_rows = norm_gains.astype(jnp.float32)
        grad_top = grad_out.astype(jnp.float32)
        grad_outer = outer_sum(inner_act, grad_out)
        grad_inner = (back_product(grad_out, w_outer) * gelu_slope(inner_pre)).astype(jnp.bfloat16)
        grad_win = outer_sum(normed_three, grad_inner)
        grad_three, gain_three = rms_backward(
            back_product(grad_inner, w_inner), unit_three, inverse_three, gain_rows[2]
        )
        grad_three = grad_top + grad_three
        three_low = grad_three.astype(jnp.bfloat16)
        grad_cout = outer_sum(cross_mixed, three_low)
        grad_cmix = back_product(three_low, c_output).astype(jnp.bfloat16)
        grad_cq, grad_ck, grad_cv, cross_scores = attend_backward(
            grad_cmix, cross_queries, cross_keys, cross_values, 0.0, cross_mask, lse_cross
        )
        grad_cquery = outer_sum(normed_two, grad_cq)
        grad_ckeyval = jnp.stack([outer_sum(enc_rows, grad_ck), outer_sum(enc_rows, grad_cv)])
        grad_encoded = back_product(grad_ck, c_keyval[0]) + back_product(grad_cv, c_keyval[1])
        grad_two, gain_two = rms_backward(
            back_product(grad_cq, c_query), unit_two, inverse_two, gain_rows[1]
        )
        grad_two = grad_three + grad_two
        two_low = grad_two.astype(jnp.bfloat16)
        grad_wout = outer_sum(attended, two_low)
        grad_mix = back_product(two_low, w_output).astype(jnp.bfloat16)
        grad_q, grad_k, grad_v, self_scores = attend_backward(
            grad_mix, queries, key_rows, value_rows, bias_term, causal, lse_self
        )
        grad_wquery = outer_sum(normed_one, grad_q)
        grad_wkeyval = jnp.stack([outer_sum(normed_one, grad_k), outer_sum(normed_one, grad_v)])
        grad_normed = (
            back_product(grad_q, w_query)
            + back_product(grad_k, w_keyval[0])
            + back_product(grad_v, w_keyval[1])
        )
        grad_first, gain_one = rms_backward(grad_normed, unit_one, inverse_one, gain_rows[0])
        grad_input = grad_two + grad_first
        gain_stack = jnp.stack([gain_one, gain_two, gain_three])
        step_grads = (
            gain_stack,
            grad_wquery,
            grad_wkeyval,
            grad_wout,
            grad_cquery,
            grad_ckeyval,
            grad_cout,
            grad_win,
            grad_outer,
        )
        new_sums = tuple(
            (total_now + term_now for total_now, term_now in zip(grad_sums, step_grads))
        )
        new_bias = bias_sum + jnp.einsum(
            "hij,ijb->bh", self_scores, bucket_hot, preferred_element_type=jnp.float32
        )
        return ((new_sums, new_bias), (layer_rows, grad_input, grad_encoded))

    (grad_sums, bias_sum), (layer_rows, grad_inputs, grad_encoded) = lax.scan(
        one_micro,
        (zero_sums, zero_bias),
        (inputs[:, 0], encoder_out[:, 0], segments[:, 0], enc_segments[:, 0], out_grad[:, 0]),
    )
    sum_gain, sum_wq, sum_wkv, sum_wo, sum_cq, sum_ckv, sum_co, sum_wi, sum_wf = grad_sums
    scattered = (
        lax.psum_scatter(sum_gain, ("wide", "narrow"), scatter_dimension=1, tiled=True),
        lax.psum_scatter(sum_wq, ("wide", "narrow"), scatter_dimension=0, tiled=True),
        lax.psum_scatter(sum_wkv, ("wide", "narrow"), scatter_dimension=1, tiled=True),
        lax.psum_scatter(sum_wo, ("wide", "narrow"), scatter_dimension=1, tiled=True),
        lax.psum_scatter(sum_cq, ("wide", "narrow"), scatter_dimension=0, tiled=True),
        lax.psum_scatter(sum_ckv, ("wide", "narrow"), scatter_dimension=1, tiled=True),
        lax.psum_scatter(sum_co, ("wide", "narrow"), scatter_dimension=1, tiled=True),
        lax.psum_scatter(sum_wi, ("wide", "narrow"), scatter_dimension=0, tiled=True),
        lax.psum_scatter(sum_wf, ("wide", "narrow"), scatter_dimension=1, tiled=True),
    )
    bias_total = lax.psum(bias_sum, ("wide", "narrow"))
    return (
        layer_rows[:, None],
        grad_inputs[:, None],
        grad_encoded[:, None],
        scattered[0],
        bias_total,
        scattered[1],
        scattered[2],
        scattered[3],
        scattered[4],
        scattered[5],
        scattered[6],
        scattered[7],
        scattered[8],
    )


def solution(mesh):
    placed = (
        P(None, ("wide", "narrow"), None, None),
        P(None, ("wide", "narrow"), None, None),
        P(None, ("wide", "narrow"), None),
        P(None, ("wide", "narrow"), None),
        P(),
        P(None, ("wide", "narrow")),
        P(),
        P(("wide", "narrow"), None),
        P(None, ("wide", "narrow"), None),
        P(None, ("wide", "narrow")),
        P(("wide", "narrow"), None),
        P(None, ("wide", "narrow"), None),
        P(None, ("wide", "narrow")),
        P(("wide", "narrow"), None),
        P(None, ("wide", "narrow")),
        P(None, ("wide", "narrow"), None, None),
    )
    return jax.shard_map(
        body,
        mesh=mesh,
        in_specs=placed,
        out_specs=(
            P(None, ("wide", "narrow"), None, None),
            P(None, ("wide", "narrow"), None, None),
            P(None, ("wide", "narrow"), None, None),
            P(None, ("wide", "narrow")),
            P(),
            P(("wide", "narrow"), None),
            P(None, ("wide", "narrow"), None),
            P(None, ("wide", "narrow")),
            P(("wide", "narrow"), None),
            P(None, ("wide", "narrow"), None),
            P(None, ("wide", "narrow")),
            P(("wide", "narrow"), None),
            P(None, ("wide", "narrow")),
        ),
        check_vma=False,
    )
```

profile of v0, /device:TPU:0, one launch (start us, length us, event | category | flops | bytes accessed | tf_op | source)
XLA Modules:
  0.0 4802.5 jit_solution(16890147418028455569)
XLA Ops:
  10.7 1631.4 %gather_fusion.1 = s32[262144]{0:T(1024)S(1)} fusion(s32[512]{0:T(512)S(1)} %copy-done.2, s32[262144]{0:T(1024)S(1)} %broadcast_clamp_fusion), kind=kCustom, calls=%fused_computation.1 | custom fusion | bytes 3145728 | tf_op jit(solution)/shard_map/jit(_take)/gather | solution.py:76
  1642.1 861.0 %gather_fusion = f32[262144,12]{1,0:T(8,128)} fusion(f32[12,512]{0,1:T(8,128)} %copy.128, s32[262144]{0:T(1024)S(1)} %broadcast_clamp_fusion), kind=kCustom, calls=%fused_computation | custom fusion | bytes 26214400 | tf_op jit(solution)/shard_map/jit(_take)/gather | solution.py:69
  2503.1 73.5 %copy.129 = f32[512,512,12]{0,1,2:T(8,128)} copy(f32[512,512,12]{2,1,0:T(8,128)} %bitcast.2) | data formatting | bytes 25165824 | tf_op jit(solution)/shard_map/jit(_take)/gather | solution.py:69
  2589.3 1280.7 %while.35 = (s32[]{:T(128)}, f32[3,768]{1,0:T(4,128)}, f32[768,768]{1,0:T(8,128)}, f32[2,768,768]{2,1,0:T(8,128)}, f32[768,768]{1,0:T(8,128)}, /*index=5*/f32[76...) while((s32[]{:T(128)}, f32[3,768]{1,0:T(4,128)}, ...), condition=%wide.region_16.17_spmd.clone, body=%wide.region_0.16_spmd.clone.sunk | while | flops 34249621504 | bytes 1358595072 | solution.py:286
  2595.5 69.8 %all-gather.3 = bf16[32,24,3]{1,2,0:T(4,128)(2,1)S(1)} all-gather(bf16[1,24,3]{1,2,0:T(4,128)(2,1)S(1)} %bitcast.477), channel_id=1, replica_groups=mesh['wide'=8,'narrow'=4] {'wide','narrow'}, dimensions={0}, use_global_device_ids=true | all-gather | bytes 4752 | tf_op jit(solution)/shard_map/while/body/eval_jaxpr/all_gather | solution.py:179
  2669.2 40.5 all-gather.13.cloned.1.call-done
  2736.5 29.0 all-gather.17.cloned.1.call-done
  2768.0 53.3 %all-gather.21.cloned.1.call-done = bf16[768,768]{1,0:T(8,128)(2,1)} async-done(((bf16[24,768]{1,0:T(8,128)(2,1)}), bf16[768,768]{1,0:T(8,128)(2,1)}) %all-gather.21.cloned.1.call-update) | async-done | bytes 1179664 | tf_op jit(solution)/shard_map/while/body/eval_jaxpr/all_gather | solution.py:183
  2823.7 56.9 %all-gather.19.cloned.1.call-done = bf16[2,768,768]{2,1,0:T(8,128)(2,1)} async-done(((bf16[2,24,768]{2,1,0:T(8,128)(2,1)}), bf16[2,768,768]{2,1,0:T(8,128)(2,1)}) %all-gather.19.cloned.1.call-update) | async-done | bytes 2359312 | tf_op jit(solution)/shard_map/while/body/eval_jaxpr/all_gather | solution.py:184
  2901.6 34.7 all-gather.23.cloned.1.call-done
  2939.3 62.3 %all-gather.25.cloned.1.call-done = bf16[768,3072]{1,0:T(8,128)(2,1)} async-done(((bf16[24,3072]{1,0:T(8,128)(2,1)}), bf16[768,3072]{1,0:T(8,128)(2,1)}) %all-gather.25.cloned.1.call-update) | async-done | bytes 4718608 | tf_op jit(solution)/shard_map/while/body/eval_jaxpr/all_gather | solution.py:186
  3009.6 57.2 %all-gather.27.cloned.1.call-done = bf16[3072,768]{0,1:T(8,128)(2,1)} async-done(((bf16[3072,24]{0,1:T(8,128)(2,1)}), bf16[3072,768]{0,1:T(8,128)(2,1)}) %all-gather.27.cloned.1.call-update) | async-done | bytes 4718608 | tf_op jit(solution)/shard_map/while/body/eval_jaxpr/all_gather | solution.py:224
  3119.1 12.3 multiply_reduce_fusion.19
  3146.3 14.8 copy.169
  3234.5 66.4 %all-gather.3 = bf16[32,24,3]{1,2,0:T(4,128)(2,1)S(1)} all-gather(bf16[1,24,3]{1,2,0:T(4,128)(2,1)S(1)} %bitcast.477), channel_id=1, replica_groups=mesh['wide'=8,'narrow'=4] {'wide','narrow'}, dimensions={0}, use_global_device_ids=true | all-gather | bytes 4752 | tf_op jit(solution)/shard_map/while/body/eval_jaxpr/all_gather | solution.py:179
  3304.7 40.2 all-gather.13.cloned.1.call-done
  3371.7 29.1 all-gather.17.cloned.1.call-done
  3403.3 53.3 %all-gather.21.cloned.1.call-done = bf16[768,768]{1,0:T(8,128)(2,1)} async-done(((bf16[24,768]{1,0:T(8,128)(2,1)}), bf16[768,768]{1,0:T(8,128)(2,1)}) %all-gather.21.cloned.1.call-update) | async-done | bytes 1179664 | tf_op jit(solution)/shard_map/while/body/eval_jaxpr/all_gather | solution.py:183
  3459.0 57.0 %all-gather.19.cloned.1.call-done = bf16[2,768,768]{2,1,0:T(8,128)(2,1)} async-done(((bf16[2,24,768]{2,1,0:T(8,128)(2,1)}), bf16[2,768,768]{2,1,0:T(8,128)(2,1)}) %all-gather.19.cloned.1.call-update) | async-done | bytes 2359312 | tf_op jit(solution)/shard_map/while/body/eval_jaxpr/all_gather | solution.py:184
  3537.0 34.7 all-gather.23.cloned.1.call-done
  3574.7 62.1 %all-gather.25.cloned.1.call-done = bf16[768,3072]{1,0:T(8,128)(2,1)} async-done(((bf16[24,3072]{1,0:T(8,128)(2,1)}), bf16[768,3072]{1,0:T(8,128)(2,1)}) %all-gather.25.cloned.1.call-update) | async-done | bytes 4718608 | tf_op jit(solution)/shard_map/while/body/eval_jaxpr/all_gather | solution.py:186
  3644.8 57.1 %all-gather.27.cloned.1.call-done = bf16[3072,768]{0,1:T(8,128)(2,1)} async-done(((bf16[3072,24]{0,1:T(8,128)(2,1)}), bf16[3072,768]{0,1:T(8,128)(2,1)}) %all-gather.27.cloned.1.call-update) | async-done | bytes 4718608 | tf_op jit(solution)/shard_map/while/body/eval_jaxpr/all_gather | solution.py:224
  3781.4 14.8 copy.169
  3890.4 40.1 all-reduce.1
  3931.1 43.5 reduce-scatter.14.cloned.1.call-done
  3974.6 104.5 %reduce-scatter.20.cloned.1.call-done = f32[768,24]{0,1:T(8,128)} async-done(((f32[768,768]{0,1:T(8,128)}), f32[768,24]{0,1:T(8,128)}) %reduce-scatter.20.cloned.1.call-update) | async-done | bytes 73744 | tf_op jit(solution)/shard_map/reduce_scatter | solution.py:299
  4079.1 103.7 %reduce-scatter.10.cloned.1.call-done = f32[24,768]{1,0:T(8,128)} async-done(((f32[768,768]{1,0:T(8,128)}), f32[24,768]{1,0:T(8,128)}) %reduce-scatter.10.cloned.1.call-update) | async-done | bytes 73744 | tf_op jit(solution)/shard_map/reduce_scatter | solution.py:294
  4182.7 104.7 %reduce-scatter.16.cloned.1.call-done = f32[24,768]{1,0:T(8,128)} async-done(((f32[768,768]{1,0:T(8,128)}), f32[24,768]{1,0:T(8,128)}) %reduce-scatter.16.cloned.1.call-update) | async-done | bytes 73744 | tf_op jit(solution)/shard_map/reduce_scatter | solution.py:297
  4287.5 111.9 %reduce-scatter.12.cloned.1.call-done = f32[2,24,768]{2,1,0:T(8,128)} async-done(((f32[2,768,768]{2,1,0:T(8,128)}), f32[2,24,768]{2,1,0:T(8,128)}) %reduce-scatter.12.cloned.1.call-update) | async-done | bytes 147472 | tf_op jit(solution)/shard_map/reduce_scatter | solution.py:295
  4399.4 112.8 %reduce-scatter.18.cloned.1.call-done = f32[2,24,768]{2,1,0:T(8,128)} async-done(((f32[2,768,768]{2,1,0:T(8,128)}), f32[2,24,768]{2,1,0:T(8,128)}) %reduce-scatter.18.cloned.1.call-update) | async-done | bytes 147472 | tf_op jit(solution)/shard_map/reduce_scatter | solution.py:298
  4512.1 141.1 %reduce-scatter.24.cloned.1.call-done = f32[3072,24]{0,1:T(8,128)} async-done(((f32[3072,768]{0,1:T(8,128)}), f32[3072,24]{0,1:T(8,128)}) %reduce-scatter.24.cloned.1.call-update) | async-done | bytes 294928 | tf_op jit(solution)/shard_map/reduce_scatter | solution.py:301
  4653.2 141.9 %reduce-scatter.22.cloned.1.call-done = f32[24,3072]{1,0:T(8,128)} async-done(((f32[768,3072]{1,0:T(8,128)}), f32[24,3072]{1,0:T(8,128)}) %reduce-scatter.22.cloned.1.call-update) | async-done | bytes 294928 | tf_op jit(solution)/shard_map/reduce_scatter | solution.py:300
  (637 shorter events, 465.5 us)
Async XLA Ops:
  2503.1 73.5 %copy-start.64 = (pred[512,512]{1,0:T(8,128)(4,1)S(1)}, pred[512,512]{1,0:T(8,128)(4,1)}, u32[]{:S(2)}) copy-start(pred[512,512]{1,0:T(8,128)(4,1)} %fusion.104) | copy-start | bytes 786436
  2589.8 75.9 %copy-start.73 = (s32[2,512]{1,0:T(2,128)}, s32[2,512]{1,0:T(2,128)S(1)}, u32[]{:S(2)}) copy-start(s32[2,512]{1,0:T(2,128)S(1)} %get-tuple-element.709) | copy-start | bytes 12292 | tf_op jit(solution)/shard_map/while
  2589.8 79.1 %copy-start.71 = (s32[2,512]{1,0:T(2,128)}, s32[2,512]{1,0:T(2,128)S(1)}, u32[]{:S(2)}) copy-start(s32[2,512]{1,0:T(2,128)S(1)} %get-tuple-element.716) | copy-start | bytes 12292 | tf_op jit(solution)/shard_map/while
  2589.8 77.0 %all-gather.15.cloned.1.call-start = ((), (), s32[]{:S(2)}) async-start(), calls=%async_computation.17 | async-start | bytes 1216512 | tf_op jit(solution)/shard_map/while/body/eval_jaxpr/all_gather | solution.py:180
  2590.6 119.2 %all-gather.13.cloned.1.call-start = ((), (), s32[]{:S(2)}) async-start(), calls=%async_computation.16 | async-start | bytes 2433024 | tf_op jit(solution)/shard_map/while/body/eval_jaxpr/all_gather | solution.py:181
  2591.3 174.3 %all-gather.17.cloned.1.call-start = ((), (), s32[]{:S(2)}) async-start(), calls=%async_computation.18 | async-start | bytes 1216512 | tf_op jit(solution)/shard_map/while/body/eval_jaxpr/all_gather | solution.py:182
  2592.0 229.3 %all-gather.21.cloned.1.call-start = ((), (), s32[]{:S(2)}) async-start(), calls=%async_computation.20 | async-start | bytes 1216512 | tf_op jit(solution)/shard_map/while/body/eval_jaxpr/all_gather | solution.py:183
  2592.6 288.0 %all-gather.19.cloned.1.call-start = ((), (), s32[]{:S(2)}) async-start(), calls=%async_computation.19 | async-start | bytes 2433024 | tf_op jit(solution)/shard_map/while/body/eval_jaxpr/all_gather | solution.py:184
  2593.2 343.1 %all-gather.23.cloned.1.call-start = ((), (), s32[]{:S(2)}) async-start(), calls=%async_computation.21 | async-start | bytes 1216512 | tf_op jit(solution)/shard_map/while/body/eval_jaxpr/all_gather | solution.py:185
  2593.8 407.8 %all-gather.25.cloned.1.call-start = ((), (), s32[]{:S(2)}) async-start(), calls=%async_computation.22 | async-start | bytes 4866048 | tf_op jit(solution)/shard_map/while/body/eval_jaxpr/all_gather | solution.py:186
  2594.5 472.3 %all-gather.27.cloned.1.call-start = ((), (), s32[]{:S(2)}) async-start(), calls=%async_computation.23 | async-start | bytes 4866048 | tf_op jit(solution)/shard_map/while/body/eval_jaxpr/all_gather | solution.py:224
  2768.0 343.5 %copy-start.13 = (f32[512,768]{1,0:T(8,128)}, f32[512,768]{1,0:T(8,128)S(1)}, u32[]{:S(2)}) copy-start(f32[512,768]{1,0:T(8,128)S(1)} %get-tuple-element.602) | copy-start | bytes 4718596 | tf_op jit(solution)/shard_map/while
  3229.1 72.1 %copy-start.73 = (s32[2,512]{1,0:T(2,128)}, s32[2,512]{1,0:T(2,128)S(1)}, u32[]{:S(2)}) copy-start(s32[2,512]{1,0:T(2,128)S(1)} %get-tuple-element.709) | copy-start | bytes 12292 | tf_op jit(solution)/shard_map/while
  3229.1 75.3 %copy-start.71 = (s32[2,512]{1,0:T(2,128)}, s32[2,512]{1,0:T(2,128)S(1)}, u32[]{:S(2)}) copy-start(s32[2,512]{1,0:T(2,128)S(1)} %get-tuple-element.716) | copy-start | bytes 12292 | tf_op jit(solution)/shard_map/while
  3229.1 73.2 %all-gather.15.cloned.1.call-start = ((), (), s32[]{:S(2)}) async-start(), calls=%async_computation.17 | async-start | bytes 1216512 | tf_op jit(solution)/shard_map/while/body/eval_jaxpr/all_gather | solution.py:180
  3229.9 115.1 %all-gather.13.cloned.1.call-start = ((), (), s32[]{:S(2)}) async-start(), calls=%async_computation.16 | async-start | bytes 2433024 | tf_op jit(solution)/shard_map/while/body/eval_jaxpr/all_gather | solution.py:181
  3230.4 170.4 %all-gather.17.cloned.1.call-start = ((), (), s32[]{:S(2)}) async-start(), calls=%async_computation.18 | async-start | bytes 1216512 | tf_op jit(solution)/shard_map/while/body/eval_jaxpr/all_gather | solution.py:182
  3231.2 225.4 %all-gather.21.cloned.1.call-start = ((), (), s32[]{:S(2)}) async-start(), calls=%async_computation.20 | async-start | bytes 1216512 | tf_op jit(solution)/shard_map/while/body/eval_jaxpr/all_gather | solution.py:183
  3231.8 284.2 %all-gather.19.cloned.1.call-start = ((), (), s32[]{:S(2)}) async-start(), calls=%async_computation.19 | async-start | bytes 2433024 | tf_op jit(solution)/shard_map/while/body/eval_jaxpr/all_gather | solution.py:184
  3232.5 339.2 %all-gather.23.cloned.1.call-start = ((), (), s32[]{:S(2)}) async-start(), calls=%async_computation.21 | async-start | bytes 1216512 | tf_op jit(solution)/shard_map/while/body/eval_jaxpr/all_gather | solution.py:185
  3233.1 403.7 %all-gather.25.cloned.1.call-start = ((), (), s32[]{:S(2)}) async-start(), calls=%async_computation.22 | async-start | bytes 4866048 | tf_op jit(solution)/shard_map/while/body/eval_jaxpr/all_gather | solution.py:186
  3233.7 468.2 %all-gather.27.cloned.1.call-start = ((), (), s32[]{:S(2)}) async-start(), calls=%async_computation.23 | async-start | bytes 4866048 | tf_op jit(solution)/shard_map/while/body/eval_jaxpr/all_gather | solution.py:224
  3403.2 343.3 %copy-start.13 = (f32[512,768]{1,0:T(8,128)}, f32[512,768]{1,0:T(8,128)S(1)}, u32[]{:S(2)}) copy-start(f32[512,768]{1,0:T(8,128)S(1)} %get-tuple-element.602) | copy-start | bytes 4718596 | tf_op jit(solution)/shard_map/while
  3870.0 104.6 %reduce-scatter.14.cloned.1.call-start = ((), (), s32[]{:S(2)}) async-start(), calls=%async_computation.10 | async-start | bytes 2433024 | tf_op jit(solution)/shard_map/reduce_scatter | solution.py:296
  3873.2 205.8 %reduce-scatter.20.cloned.1.call-start = ((), (), s32[]{:S(2)}) async-start(), calls=%async_computation.13 | async-start | bytes 2433024 | tf_op jit(solution)/shard_map/reduce_scatter | solution.py:299
  3876.9 305.8 %reduce-scatter.10.cloned.1.call-start = ((), (), s32[]{:S(2)}) async-start(), calls=%async_computation.8 | async-start | bytes 2433024 | tf_op jit(solution)/shard_map/reduce_scatter | solution.py:294
  3877.5 410.0 %reduce-scatter.16.cloned.1.call-start = ((), (), s32[]{:S(2)}) async-start(), calls=%async_computation.11 | async-start | bytes 2433024 | tf_op jit(solution)/shard_map/reduce_scatter | solution.py:297
  3878.2 521.1 %reduce-scatter.12.cloned.1.call-start = ((), (), s32[]{:S(2)}) async-start(), calls=%async_computation.9 | async-start | bytes 4866048 | tf_op jit(solution)/shard_map/reduce_scatter | solution.py:295
  3879.0 633.1 %reduce-scatter.18.cloned.1.call-start = ((), (), s32[]{:S(2)}) async-start(), calls=%async_computation.12 | async-start | bytes 4866048 | tf_op jit(solution)/shard_map/reduce_scatter | solution.py:298
  3879.7 773.5 %reduce-scatter.24.cloned.1.call-start = ((), (), s32[]{:S(2)}) async-start(), calls=%async_computation.15 | async-start | bytes 9732096 | tf_op jit(solution)/shard_map/reduce_scatter | solution.py:301
  3889.6 905.5 %reduce-scatter.22.cloned.1.call-start = ((), (), s32[]{:S(2)}) async-start(), calls=%async_computation.14 | async-start | bytes 9732096 | tf_op jit(solution)/shard_map/reduce_scatter | solution.py:300
  3890.2 904.9 %copy-start.1 = (f32[32,12]{0,1:T(8,128)S(1)}, f32[32,12]{0,1:T(8,128)}, u32[]{:S(2)}) copy-start(f32[32,12]{0,1:T(8,128)} %param.24) | copy-start | bytes 4612
  (189 other events, 1339.1 us)
Sparse Core Ops, SparseCore 0:
  2593.5 56.7 all-gather.14
  2653.4 56.3 all-gather.12
  2712.6 52.9 all-gather.16
  2768.2 53.0 all-gather.20
  2824.2 56.3 all-gather.18
  2883.3 52.9 all-gather.22
  2939.1 62.4 all-gather.24
  3004.4 62.3 all-gather.26
  3232.8 52.9 all-gather.14
  3288.7 56.2 all-gather.12
  3347.8 52.9 all-gather.16
  3403.5 53.0 all-gather.20
  3459.6 56.3 all-gather.18
  3518.6 52.9 all-gather.22
  3574.3 62.4 all-gather.24
  3639.5 62.3 all-gather.26
Sparse Core Ops, SparseCore 1:
  3876.3 98.2 reduce-scatter.13
  3981.2 97.8 reduce-scatter.19
  4084.8 97.9 reduce-scatter.9
  4189.5 97.9 reduce-scatter.15
  4293.6 105.8 reduce-scatter.11
  4406.3 105.7 reduce-scatter.17
  4518.5 134.7 reduce-scatter.23
  4660.6 134.5 reduce-scatter.21
where the time goes:
time: 4810 us; the launch traced here: 4800 us
  local copies, waits for them, and re-layouts  2670 us (56%)
  waiting for transfers between devices  1540 us (32%)
  matrix products  308 us (6%)
  blocking collectives  176 us (4%)
  other arithmetic  84.8 us (2%)
    gather x2, local copies, waits for them, and re-layouts, bucket_table(): bucket_at = jnp.take(buckets, distance)  1630 us
    gather x2, local copies, waits for them, and re-layouts, expand_bias(): return jnp.take(per_distance.T, distance, axis=1)  934 us
    reduce_scatter x1, waiting for transfers between devices, body(): lax.psum_scatter(sum_wi, ('wide', 'narrow'), scatter_dimension=0, tiled=T...  142 us
    reduce_scatter x1, waiting for transfers between devices, body(): lax.psum_scatter(sum_wf, ('wide', 'narrow'), scatter_dimension=1, tiled=T...  141 us
    all_gather x2, blocking collectives, one_micro(): lax.all_gather(gains, ('wide', 'narrow'), axis=1, tiled=True)  136 us
    all_gather x2, waiting for transfers between devices, one_micro(): lax.all_gather(ffn_in, ('wide', 'narrow'), axis=0, tiled=True)  124 us
    all_gather x2, waiting for transfers between devices, one_micro(): lax.all_gather(ffn_out, ('wide', 'narrow'), axis=1, tiled=True)  114 us
    all_gather x2, waiting for transfers between devices, one_micro(): lax.all_gather(cross_kv, ('wide', 'narrow'), axis=1, tiled=True)  114 us
  transfers between devices with their start and end apart: 24, of which 22 were waited for; matrix products, arithmetic and copies ran while one was open for 3% of the time, Pallas kernels for 0%

commit v1 on v0

v1 whole, which is shorter than its diff:
```python
import functools
import jax
import jax.numpy as jnp
from jax import lax
from jax.sharding import PartitionSpec as P
from jax.experimental import pallas as pl
from jax.experimental.pallas import tpu as pltpu

DH = 64
NEGATIVE = -1e30
BF = jnp.bfloat16
F32 = jnp.float32
NN = (((1,), (0,)), ((), ()))
NT = (((1,), (1,)), ((), ()))
TN = (((0,), (0,)), ((), ()))
MB = 1 << 20


def dot(a, b, dims=NN):
    return lax.dot_general(a, b, dims, preferred_element_type=F32)


def segment_columns(query_seg, key_seg):
    ids = jnp.arange(128)
    other = (query_seg[..., None] != ids) & (ids < 4)
    query_cols = jnp.where(other, NEGATIVE, 0.0).astype(BF)
    key_cols = (key_seg[..., None] == ids).astype(BF)
    return query_cols, key_cols


def attn_fwd_kernel(causal, q_ref, k_ref, v_ref, qs_ref, ks_ref, *rest):
    if causal:
        t_ref, o_ref, p_ref, bias = rest
    else:
        o_ref, p_ref = rest
    length = q_ref.shape[0]
    if causal:
        @pl.when(pl.program_id(1) == 0)
        def _():
            for h in range(2):
                for d in range(length // 128):
                    row = jnp.concatenate([t_ref[h, :, pl.ds(128 * (d + 1), 128)], t_ref[h, :, pl.ds(128 * d, 128)]], axis=1)
                    tile = pltpu.roll(jnp.broadcast_to(row, (128, 256)), 0, 1, stride=1, stride_axis=0)
                    bias[h, d] = tile[:, :128]
    lane = lax.broadcasted_iota(jnp.int32, (1, 128), 1)
    q = q_ref[...]
    keys = jnp.concatenate([k_ref[...], ks_ref[...]], axis=1)
    v_t = v_ref[...].T
    parts = []
    for h in range(2):
        mine = (lane // DH) == h
        qa = jnp.concatenate([jnp.where(mine, q, 0).astype(BF), qs_ref[...]], axis=1)
        cols = []
        for c in range(length // 256):
            n = 256 * (c + 1) if causal else length
            s = dot(keys[:n], qa[256 * c: 256 * (c + 1)], NT)
            if causal:
                rows = []
                for kb in range(n // 128):
                    tiles = []
                    for qb in (2 * c, 2 * c + 1):
                        st = s[128 * kb:128 * (kb + 1), 128 * (qb - 2 * c):128 * (qb - 2 * c + 1)]
                        if qb >= kb:
                            tiles.append(st + bias[h, qb - kb])
                        else:
                            tiles.append(jnp.full((128, 128), NEGATIVE, F32))
                    rows.append(jnp.concatenate(tiles, axis=1))
                s = jnp.concatenate(rows, axis=0)
            top = jnp.max(s, axis=0, keepdims=True)
            e = jnp.exp(s - top)
            p = (e * (1.0 / jnp.sum(e, axis=0, keepdims=True))).astype(BF)
            p_ref[h, pl.ds(0, n), pl.ds(256 * c, 256)] = p
            if n < length:
                p_ref[h, pl.ds(n, length - n), pl.ds(256 * c, 256)] = jnp.zeros((length - n, 256), BF)
            cols.append(dot(v_t[DH * h: DH * (h + 1), :n], p))
        parts.append(jnp.concatenate(cols, axis=1))
    o_ref[...] = jnp.concatenate(parts, axis=0).T.astype(BF)


def attn_fwd(q_arr, q_col, k_arr, k_col, v_arr, v_col, q_seg, k_seg, table=None):
    rows, length = q_seg.shape[:2]
    pairs = 6
    causal = table is not None
    block = lambda col: pl.BlockSpec((length, 128), lambda h, b: (b, col + h))
    seg = pl.BlockSpec((None, length, 128), lambda h, b: (b, 0, 0))
    in_specs = [block(q_col), block(k_col), block(v_col), seg, seg]
    args = [q_arr, k_arr, v_arr, q_seg, k_seg]
    scratch = []
    if causal:
        in_specs.append(pl.BlockSpec((2, 1, table.shape[2]), lambda h, b: (h, 0, 0)))
        args.append(table)
        scratch = [pltpu.VMEM((2, length // 128, 128, 128), F32)]
    return pl.pallas_call(
        functools.partial(attn_fwd_kernel, causal),
        grid=(pairs, rows),
        in_specs=in_specs,
        out_specs=[pl.BlockSpec((length, 128), lambda h, b: (b, h)), pl.BlockSpec((None, 2, length, length), lambda h, b: (b, h, 0, 0))],
        out_shape=[jax.ShapeDtypeStruct((rows * length, pairs * 128), BF), jax.ShapeDtypeStruct((rows, 2 * pairs, length, length), BF)],
        scratch_shapes=scratch,
        compiler_params=pltpu.CompilerParams(vmem_limit_bytes=32 * MB),
        name="attn_fwd_self" if causal else "attn_fwd_cross",
    )(*args)


def attn_bwd_kernel(causal, q_ref, k_ref, v_ref, g_ref, o_ref, p_ref, *rest):
    if causal:
        dq_ref, dk_ref, dv_ref, diag_ref, acc = rest
    else:
        dq_ref, dk_ref, dv_ref = rest
    length = q_ref.shape[0]
    lane = lax.broadcasted_iota(jnp.int32, (1, 128), 1)
    q = q_ref[...]
    g = g_ref[...]
    values = jnp.concatenate([v_ref[...], jnp.broadcast_to((lane < 2).astype(BF), (length, 128))], axis=1)
    k_t = k_ref[...].T
    prod = g.astype(F32) * o_ref[...].astype(F32)
    if causal:
        @pl.when(pl.program_id(1) == 0)
        def _():
            acc[...] = jnp.zeros_like(acc)
    dq_parts = []
    dk = [None] * (length // 256)
    dv = [None] * (length // 256)
    add = lambda old, new: new if old is None else old + new
    for h in range(2):
        mine = (lane // DH) == h
        delta = -jnp.sum(jnp.where(mine, prod, 0.0), axis=1, keepdims=True)
        high = delta.astype(BF)
        lowp = (delta - high.astype(F32)).astype(BF)
        extra = jnp.where(lane == 0, high, jnp.where(lane == 1, lowp, jnp.zeros_like(lowp)))
        gm = jnp.where(mine, g, 0).astype(BF)
        qm = jnp.where(mine, q, 0).astype(BF)
        ga = jnp.concatenate([gm, extra], axis=1)
        cols = []
        for c in range(length // 256):
            n = 256 * (c + 1) if causal else length
            qsl = slice(256 * c, 256 * (c + 1))
            p = p_ref[h, pl.ds(0, n), pl.ds(256 * c, 256)]
            dp = dot(values[:n], ga[qsl], NT)
            ds = (p.astype(F32) * dp).astype(BF)
            if causal:
                for kb in range(n // 128):
                    for qb in (2 * c, 2 * c + 1):
                        if qb >= kb:
                            acc[h, qb - kb] += ds[128 * kb:128 * (kb + 1), 128 * (qb - 2 * c):128 * (qb - 2 * c + 1)].astype(F32)
            cols.append(dot(k_t[DH * h: DH * (h + 1), :n], ds))
            dkn = dot(ds, qm[qsl])
            dvn = dot(p, gm[qsl])
            for kc in range(n // 256):
                ksl = slice(256 * kc, 256 * (kc + 1))
                dk[kc] = add(dk[kc], dkn[ksl])
                dv[kc] = add(dv[kc], dvn[ksl])
        dq_parts.append(jnp.concatenate(cols, axis=1))
    dq_ref[...] = jnp.concatenate(dq_parts, axis=0).T.astype(BF)
    dk_ref[...] = jnp.concatenate(dk, axis=0).astype(BF)
    dv_ref[...] = jnp.concatenate(dv, axis=0).astype(BF)
    if causal:
        @pl.when(pl.program_id(1) == pl.num_programs(1) - 1)
        def _():
            flip = (lax.broadcasted_iota(jnp.int32, (128, 128), 0) + lax.broadcasted_iota(jnp.int32, (128, 128), 1) == 127).astype(F32)
            for h in range(2):
                for d in range(length // 128):
                    upside = jnp.dot(flip, acc[h, d], precision=lax.Precision.HIGHEST, preferred_element_type=F32)
                    wide = jnp.concatenate([upside, jnp.zeros((128, 128), F32)], axis=1)
                    turned = pltpu.roll(wide, 0, 1, stride=1, stride_axis=0)
                    diag_ref[h, pl.ds(d, 1), :] = jnp.sum(turned, axis=0, keepdims=True)


def attn_bwd(q_arr, q_col, k_arr, k_col, v_arr, v_col, grad, out, probs, causal):
    rows, heads, length = probs.shape[:3]
    pairs = heads // 2
    block = lambda col: pl.BlockSpec((length, 128), lambda h, b: (b, col + h))
    flat = jax.ShapeDtypeStruct((rows * length, pairs * 128), BF)
    out_specs = [block(0)] * 3
    out_shape = [flat] * 3
    scratch = []
    if causal:
        out_specs.append(pl.BlockSpec((2, length // 128, 256), lambda h, b: (h, 0, 0)))
        out_shape.append(jax.ShapeDtypeStruct((heads, length // 128, 256), F32))
        scratch = [pltpu.VMEM((2, length // 128, 128, 128), F32)]
    return pl.pallas_call(
        functools.partial(attn_bwd_kernel, causal),
        grid=(pairs, rows),
        in_specs=[block(q_col), block(k_col), block(v_col), block(0), block(0), pl.BlockSpec((None, 2, length, length), lambda h, b: (b, h, 0, 0))],
        out_specs=out_specs,
        out_shape=out_shape,
        scratch_shapes=scratch,
        compiler_params=pltpu.CompilerParams(vmem_limit_bytes=40 * MB),
        name="attn_bwd_self" if causal else "attn_bwd_cross",
    )(q_arr, k_arr, v_arr, grad, out, probs)


def score_table(rel_bias, buckets):
    hot = buckets[:, None] == jnp.arange(rel_bias.shape[0])[None, :]
    at = jnp.sum(jnp.where(hot[:, :, None], rel_bias[None], 0.0), axis=1)
    return jnp.concatenate([jnp.full((rel_bias.shape[1], 128), NEGATIVE, F32), at.T], axis=1)[:, None]


def bucket_sums(diag, buckets, count):
    heads, blocks, _ = diag.shape
    own = diag[:, :, 127:255]
    before = jnp.pad(diag[:, 1:, :127], ((0, 0), (0, 1), (1, 0)))
    at = (own + before).reshape(heads, blocks * 128)
    hot = buckets[:, None] == jnp.arange(count)[None, :]
    return jnp.sum(jnp.where(hot[:, :, None], at.T[:, None, :], 0.0), axis=0)


EPSILON = 1e-06
ROOT_HALF = 0.7071067811865476
INV_ROOT_TWO_PI = 0.3989422804014327
WIDE, NARROW = "wide", "narrow"


def rms_forward(value_rows, gain_row):
    inverse = lax.rsqrt(jnp.mean(value_rows * value_rows, axis=-1, keepdims=True) + EPSILON)
    unit_rows = value_rows * inverse
    return (unit_rows * gain_row, unit_rows, inverse)


def rms_backward(grad_norm, unit_rows, inverse, gain_row):
    grad_gain = jnp.sum(grad_norm * unit_rows, axis=0)
    grad_unit = grad_norm * gain_row
    grad_value = inverse * (
        grad_unit - unit_rows * jnp.mean(grad_unit * unit_rows, axis=-1, keepdims=True)
    )
    return (grad_value, grad_gain)


def flipped(size, bit):
    return [(i, i ^ bit) for i in range(size)]


def bits_of(size):
    return [1 << i for i in range(size.bit_length() - 1)]


def wide_order(size, turn):
    low, rest = bits_of(size)[:1], bits_of(size)[1:]
    turn = turn % len(rest)
    return rest[turn:] + rest[:turn] + low


def gather_rows(block, sizes, turn):
    wide, narrow = sizes
    at = lax.axis_index(NARROW)
    for bit in bits_of(narrow):
        other = lax.ppermute(block, NARROW, flipped(narrow, bit))
        upper = (at & bit) != 0
        block = jnp.concatenate([jnp.where(upper, other, block), jnp.where(upper, block, other)], axis=0)
    pieces, offsets = [block], [0]
    for bit in wide_order(wide, turn):
        pieces = pieces + [lax.ppermute(piece, WIDE, flipped(wide, bit)) for piece in pieces]
        offsets = offsets + [offset ^ bit for offset in offsets]
    me = lax.axis_index(WIDE)
    rows = block.shape[0]
    whole = jnp.zeros((wide * rows, block.shape[1]), block.dtype)
    for piece, offset in zip(pieces, offsets):
        whole = lax.dynamic_update_slice(whole, piece, ((me ^ offset) * rows, 0))
    return whole


def scatter_rows(total, sizes, turn):
    wide, narrow = sizes
    columns = total.shape[1]
    me, at = lax.axis_index(WIDE), lax.axis_index(NARROW)

    def halve(value, axis_name, size, place, bit, parts):
        value = value.reshape(parts, 2, -1, columns)
        mine = (place // bit) % 2
        keep = lax.dynamic_slice_in_dim(value, mine, 1, 1)
        send = lax.dynamic_slice_in_dim(value, 1 - mine, 1, 1)
        received = lax.ppermute(send, axis_name, flipped(size, bit))
        return keep.astype(F32) + received.astype(F32)

    order = wide_order(wide, turn)[::-1]
    value = total
    left = list(bits_of(wide))
    for bit in order:
        parts = 1 << sum(b > bit for b in left)
        value = halve(value, WIDE, wide, me, bit, parts).astype(BF)
        left.remove(bit)
    for bit in bits_of(narrow)[::-1]:
        value = halve(value, NARROW, narrow, at, bit, 1)
        if bit != 1:
            value = value.astype(BF)
    return value.reshape(-1, columns).astype(F32)


def body(sizes, inputs, encoder_out, segments, enc_segments, buckets, gains, rel_bias, self_q, self_kv, self_out, cross_q, cross_kv, cross_out, ffn_in, ffn_out, out_grad):
    micro, per, length, width = inputs.shape
    rows = micro * per
    hidden = ffn_in.shape[1] // 2
    flat = lambda v: v.reshape(rows * length, width)
    state_in, enc_rows, grad_out = flat(inputs), flat(encoder_out), flat(out_grad)
    seg, enc_seg = segments.reshape(rows, length), enc_segments.reshape(rows, length)
    self_seg = segment_columns(seg, seg)
    cross_seg = segment_columns(seg, enc_seg)
    table = score_table(rel_bias, buckets)

    gain_cols = jnp.pad(gains.T, ((0, 0), (0, 125)))
    slab_self = gather_rows(jnp.concatenate([self_q, self_kv[0], self_kv[1], self_out.T, gain_cols], axis=1), sizes, 0)
    slab_cross = gather_rows(jnp.concatenate([cross_q, cross_kv[0], cross_kv[1], cross_out.T], axis=1), sizes, 1)
    outer_t = ffn_out.T
    slab_ffn = [
        gather_rows(jnp.concatenate([ffn_in[:, hidden * i: hidden * (i + 1)], outer_t[:, hidden * i: hidden * (i + 1)]], axis=1), sizes, i)
        for i in range(2)
    ]
    w_qkv, w_out = slab_self[:, : 3 * width], slab_self[:, 3 * width: 4 * width]
    gain_rows = slab_self[:, 4 * width: 4 * width + 3].T.astype(F32)
    c_query, c_keyval, c_out = slab_cross[:, :width], slab_cross[:, width: 3 * width], slab_cross[:, 3 * width:]

    state_in = state_in.astype(F32)
    normed_one, unit_one, inverse_one = rms_forward(state_in, gain_rows[0])
    normed_one = normed_one.astype(BF)
    qkv = dot(normed_one, w_qkv).astype(BF)
    attended, self_p = attn_fwd(qkv, 0, qkv, 6, qkv, 12, *self_seg, table)
    state_two = state_in + dot(attended, w_out, NT)
    normed_two, unit_two, inverse_two = rms_forward(state_two, gain_rows[1])
    normed_two = normed_two.astype(BF)
    cross_queries = dot(normed_two, c_query).astype(BF)
    cross_keyval = dot(enc_rows, c_keyval).astype(BF)
    mixed, cross_p = attn_fwd(cross_queries, 0, cross_keyval, 0, cross_keyval, 6, *cross_seg)
    state_three = state_two + dot(mixed, c_out, NT)
    normed_three, unit_three, inverse_three = rms_forward(state_three, gain_rows[2])
    normed_three = normed_three.astype(BF)
    layer = state_three
    grad_normed = 0.0
    ffn_grads = []
    for i in range(2):
        w_in, w_back = slab_ffn[i][:, :hidden], slab_ffn[i][:, hidden:]
        pre = dot(normed_three, w_in)
        phi = 0.5 * (1.0 + lax.erf(pre * ROOT_HALF))
        act = (pre * phi).astype(BF)
        layer = layer + dot(act, w_back, NT)
        slope = phi + pre * jnp.exp(-0.5 * pre * pre) * INV_ROOT_TWO_PI
        grad_pre = (dot(grad_out, w_back) * slope).astype(BF)
        grad_normed = grad_normed + dot(grad_pre, w_in, NT)
        pair = jnp.concatenate([dot(normed_three, grad_pre, TN), dot(grad_out, act, TN)], axis=1).astype(BF)
        ffn_grads.append(scatter_rows(pair, sizes, i))
    grad_three, gain_three = rms_backward(grad_normed, unit_three, inverse_three, gain_rows[2])
    grad_three = grad_out.astype(F32) + grad_three
    three_low = grad_three.astype(BF)
    grad_mixed = dot(three_low, c_out).astype(BF)
    grad_cq, grad_ck, grad_cv = attn_bwd(cross_queries, 0, cross_keyval, 0, cross_keyval, 6, grad_mixed, mixed, cross_p, False)
    grad_ckv = jnp.concatenate([grad_ck, grad_cv], axis=1)
    cross_grads = jnp.concatenate([dot(normed_two, grad_cq, TN), dot(enc_rows, grad_ckv, TN), dot(three_low, mixed, TN)], axis=1).astype(BF)
    cross_sum = scatter_rows(cross_grads, sizes, 0)
    grad_encoded = dot(grad_ckv, c_keyval, NT)
    grad_two, gain_two = rms_backward(dot(grad_cq, c_query, NT), unit_two, inverse_two, gain_rows[1])
    grad_two = grad_three + grad_two
    two_low = grad_two.astype(BF)
    grad_att = dot(two_low, w_out).astype(BF)
    grad_q, grad_k, grad_v, diag = attn_bwd(qkv, 0, qkv, 6, qkv, 12, grad_att, attended, self_p, True)
    grad_qkv = jnp.concatenate([grad_q, grad_k, grad_v], axis=1)
    grad_first, gain_one = rms_backward(dot(grad_qkv, w_qkv, NT), unit_one, inverse_one, gain_rows[0])
    grad_input = grad_two + grad_first
    gain_grads = jnp.pad(jnp.stack([gain_one, gain_two, gain_three], axis=1), ((0, 0), (0, 125)))
    self_grads = jnp.concatenate([dot(normed_one, grad_qkv, TN), dot(two_low, attended, TN), gain_grads], axis=1).astype(BF)
    self_sum = scatter_rows(self_grads, sizes, 1)
    bias_sum = lax.psum(bucket_sums(diag, buckets, rel_bias.shape[0]), (WIDE, NARROW))
    part = lambda v, i: v[:, width * i: width * (i + 1)]
    shaped = lambda v: v.reshape(micro, per, length, width)
    return (
        shaped(layer.astype(BF)),
        shaped(grad_input),
        shaped(grad_encoded),
        self_sum[:, 4 * width: 4 * width + 3].T,
        bias_sum,
        part(self_sum, 0),
        jnp.stack([part(self_sum, 1), part(self_sum, 2)]),
        part(self_sum, 3).T,
        part(cross_sum, 0),
        jnp.stack([part(cross_sum, 1), part(cross_sum, 2)]),
        part(cross_sum, 3).T,
        jnp.concatenate([g[:, :hidden] for g in ffn_grads], axis=1),
        jnp.concatenate([g[:, hidden:] for g in ffn_grads], axis=1).T,
    )


def solution(mesh):
    axes = (WIDE, NARROW)
    batch4, batch3 = P(None, axes, None, None), P(None, axes, None)
    first, second, middle = P(axes, None), P(None, axes), P(None, axes, None)
    sizes = (mesh.shape[WIDE], mesh.shape[NARROW])
    weights = (first, middle, second, first, middle, second, first, second)
    return jax.shard_map(
        functools.partial(body, sizes),
        mesh=mesh,
        in_specs=(batch4, batch4, batch3, batch3, P(), second, P()) + weights + (batch4,),
        out_specs=(batch4, batch4, batch4, second, P()) + weights,
        check_vma=False,
    )
```

time: 4810 us -> 716 us (0.15)
  local copies, waits for them, and re-layouts: 2670 us -> 176 us
  waiting for transfers between devices: 1540 us -> 168 us
  matrix products: 308 us -> 113 us
  blocking collectives: 176 us -> 37.8 us
  Pallas kernels: 0 us -> 105 us
  starting transfers between devices: 0.99 us -> 58.9 us
    gather x4 -> x0, local copies, waits for them, and re-layouts: 2570 us -> none  [the longest x2 1630 us: bucket_table(): bucket_at = jnp.take(buckets, distance)]
    reduce_scatter x8 -> x0, waiting for transfers between devices: 864 us -> none  [the longest x1 142 us: body(): lax.psum_scatter(sum_wi, ('wide', 'narrow'), scatter_dimension=0, tiled=T...]
    all_gather x16 -> x0, waiting for transfers between devices: 667 us -> none  [the longest x2 124 us: one_micro(): lax.all_gather(ffn_in, ('wide', 'narrow'), axis=0, tiled=True)]
    dot_general x87 -> x27, matrix products: 308 us -> 113 us  [dot(): return lax.dot_general(a, b, dims, preferred_element_type=F32)]
    ppermute x0 -> x56, waiting for transfers between devices: none -> 168 us  [the longest x20 103 us: halve(): received = lax.ppermute(send, axis_name, flipped(size, bit))]
    all_gather x2 -> x0, blocking collectives: 136 us -> none  [one_micro(): lax.all_gather(gains, ('wide', 'narrow'), axis=1, tiled=True)]
    dynamic_update_slice x0 -> x29, local copies, waits for them, and re-layouts: none -> 115 us  [gather_rows(): whole = lax.dynamic_update_slice(whole, piece, ((me ^ offset) * rows, 0))]
    pallas_call x0 -> x4, Pallas kernels: none -> 105 us  [the longest x2 57.5 us: attn_bwd(): pl.pallas_call(functools.partial(attn_bwd_kernel, causal), grid=(pairs, r...]
  transfers between devices with their start and end apart: 24 -> 56, of which waited for: 22 -> 19; matrix products, arithmetic and copies ran while one was open for 3% -> 29% of each run, Pallas kernels for 0% -> 4%
where the time goes in v1:
time: 716 us; the launch traced here: 707 us
  local copies, waits for them, and re-layouts  176 us (25%)
  waiting for transfers between devices  168 us (23%)
  matrix products  113 us (16%)
  Pallas kernels  105 us (15%)
  starting transfers between devices  58.9 us (8%)
  other arithmetic  45.2 us (6%)
  blocking collectives  37.8 us (5%)
    dynamic_update_slice x29, local copies, waits for them, and re-layouts, gather_rows(): whole = lax.dynamic_update_slice(whole, piece, ((me ^ offset) * rows, 0))  115 us
    dot_general x27, matrix products, dot(): return lax.dot_general(a, b, dims, preferred_element_type=F32)  113 us
    ppermute x20, waiting for transfers between devices, halve(): received = lax.ppermute(send, axis_name, flipped(size, bit))  103 us
    pallas_call x2, Pallas kernels, attn_bwd(): pl.pallas_call(functools.partial(attn_bwd_kernel, causal), grid=(pairs, r...  57.5 us
    pallas_call x2, Pallas kernels, attn_fwd(): pl.pallas_call(functools.partial(attn_fwd_kernel, causal), grid=(pairs, r...  47.4 us
    psum x1, blocking collectives, body(): lax.psum(bucket_sums(diag, buckets, rel_bias.shape[0]), (WIDE, NARROW))  37.8 us
    ppermute x8, waiting for transfers between devices, gather_rows(): other = lax.ppermute(block, NARROW, flipped(narrow, bit))  34.4 us
    ppermute x28, waiting for transfers between devices, gather_rows(): lax.ppermute(piece, WIDE, flipped(wide, bit))  31 us
  transfers between devices with their start and end apart: 56, of which 19 were waited for; matrix products, arithmetic and copies ran while one was open for 29% of the time, Pallas kernels for 4%

profile of v1, /device:TPU:0, one launch (start us, length us, event | category | flops | bytes accessed | tf_op | source)
XLA Modules:
  0.0 706.9 jit_solution(15683714938112568058)
XLA Ops:
  35.6 26.4 %collective-permute-done.19 = bf16[48,3072]{1,0:T(8,128)(2,1)S(1)} collective-permute-done((bf16[48,3072]{1,0:T(8,128)(2,1)S(1)}, bf16[48,3072]{1,0:T(8,128)(2,1)S(1)}, u32[]{:S(2)}, u32[]{:S(2)}) %collective-permute-start.19) | collective-permute-done | bytes 294944 | tf_op jit(solution)/shard_map/ppermute | solution.py:247
  66.7 8.0 %collective-permute-done.10 = bf16[48,3072]{1,0:T(8,128)(2,1)S(1)} collective-permute-done((bf16[48,3072]{1,0:T(8,128)(2,1)S(1)}, bf16[48,3072]{1,0:T(8,128)(2,1)S(1)}, u32[]{:S(2)}, u32[]{:S(2)}) %collective-permute-start.10) | collective-permute-done | bytes 294944 | tf_op jit(solution)/shard_map/ppermute | solution.py:247
  89.5 9.5 %dynamic_update_slice.96 = bf16[768,3200]{0,1:T(8,128)(2,1)} dynamic-update-slice(bf16[768,3200]{0,1:T(8,128)(2,1)} %broadcast_in_dim.43, bf16[96,3200]{0,1:T(8,128)(2,1)} %copy.61, s32[]{:T(128)S(6)} %select_n.287, s32[]{:T(128)} %constant.178.clone.1) | dynamic-update-slice | bytes 1228804 | tf_op jit(solution)/shard_map/dynamic_update_slice | solution.py:258
  126.7 10.7 %dynamic_update_slice.97 = bf16[768,3200]{0,1:T(8,128)(2,1)} dynamic-update-slice(bf16[768,3200]{0,1:T(8,128)(2,1)} %dynamic_update_slice.96, bf16[96,3200]{0,1:T(8,128)(2,1)} %copy.62, s32[]{:T(128)S(6)} %select_n.288, s32[]{:T(128)} %constant.178.clone.1) | dynamic-update-slice | bytes 1228804 | tf_op jit(solution)/shard_map/dynamic_update_slice | solution.py:258
  140.2 9.3 %dynamic_update_slice.98 = bf16[768,3200]{0,1:T(8,128)(2,1)} dynamic-update-slice(bf16[768,3200]{0,1:T(8,128)(2,1)} %dynamic_update_slice.97, bf16[96,3200]{0,1:T(8,128)(2,1)} %copy.63, s32[]{:T(128)S(6)} %select_n.289, s32[]{:T(128)} %constant.178.clone.1) | dynamic-update-slice | bytes 1228804 | tf_op jit(solution)/shard_map/dynamic_update_slice | solution.py:258
  168.2 12.2 %collective-permute-done.31 = bf16[96,3072]{1,0:T(8,128)(2,1)} collective-permute-done((bf16[96,3072]{1,0:T(8,128)(2,1)S(1)}, bf16[96,3072]{1,0:T(8,128)(2,1)}, u32[]{:S(2)}, u32[]{:S(2)}) %collective-permute-start.31) | collective-permute-done | bytes 589856 | tf_op jit(solution)/shard_map/ppermute | solution.py:252
  187.0 11.8 %collective-permute-done.4 = bf16[96,3200]{1,0:T(8,128)(2,1)} collective-permute-done((bf16[96,3200]{1,0:T(8,128)(2,1)}, bf16[96,3200]{1,0:T(8,128)(2,1)}, u32[]{:S(2)}, u32[]{:S(2)}) %collective-permute-start.4) | collective-permute-done | bytes 614432 | tf_op jit(solution)/shard_map/ppermute | solution.py:252
  201.1 10.7 %dynamic_update_slice.99 = bf16[768,3200]{0,1:T(8,128)(2,1)} dynamic-update-slice(bf16[768,3200]{0,1:T(8,128)(2,1)} %dynamic_update_slice.98, bf16[96,3200]{0,1:T(8,128)(2,1)} %copy.64, s32[]{:T(128)S(6)} %select_n.290, s32[]{:T(128)} %constant.178.clone.1) | dynamic-update-slice | bytes 1228804 | tf_op jit(solution)/shard_map/dynamic_update_slice | solution.py:258
  211.8 10.7 %dynamic_update_slice.100 = bf16[768,3200]{0,1:T(8,128)(2,1)} dynamic-update-slice(bf16[768,3200]{0,1:T(8,128)(2,1)} %dynamic_update_slice.99, bf16[96,3200]{0,1:T(8,128)(2,1)} %copy.65, s32[]{:T(128)S(6)} %select_n.291, s32[]{:T(128)} %constant.178.clone.1) | dynamic-update-slice | bytes 1228804 | tf_op jit(solution)/shard_map/dynamic_update_slice | solution.py:258
  224.8 10.7 %dynamic_update_slice.101 = bf16[768,3200]{0,1:T(8,128)(2,1)} dynamic-update-slice(bf16[768,3200]{0,1:T(8,128)(2,1)} %dynamic_update_slice.100, bf16[96,3200]{0,1:T(8,128)(2,1)} %copy.66, s32[]{:T(128)S(6)} %select_n.292, s32[]{:T(128)} %constant.178.clone.1) | dynamic-update-slice | bytes 1228804 | tf_op jit(solution)/shard_map/dynamic_update_slice | solution.py:258
  237.8 10.7 %dynamic_update_slice.102 = bf16[768,3200]{0,1:T(8,128)(2,1)} dynamic-update-slice(bf16[768,3200]{0,1:T(8,128)(2,1)} %dynamic_update_slice.101, bf16[96,3200]{0,1:T(8,128)(2,1)} %copy.67, s32[]{:T(128)S(6)} %select_n.293, s32[]{:T(128)} %constant.178.clone.1) | dynamic-update-slice | bytes 1228804 | tf_op jit(solution)/shard_map/dynamic_update_slice | solution.py:258
  254.3 5.6 fusion.13.k_ref.v_ref
  262.2 10.0 %dynamic_update_slice.103 = bf16[768,3200]{0,1:T(8,128)(2,1)} dynamic-update-slice(bf16[768,3200]{0,1:T(8,128)(2,1)} %dynamic_update_slice.102, bf16[96,3200]{0,1:T(8,128)(2,1)} %copy.68, s32[]{:T(128)S(6)} %select_n.294, s32[]{:T(128)} %constant.178.clone.1) | dynamic-update-slice | bytes 1228804 | tf_op jit(solution)/shard_map/dynamic_update_slice | solution.py:258
  273.4 6.7 convolution_convert_fusion.q_ref.k_ref.v_ref
  280.2 23.0 %attn_fwd_self.1 = (bf16[1024,768]{1,0:T(8,128)(2,1)S(1)}, bf16[2,12,512,512]{3,2,1,0:T(8,128)(2,1)S(1)}) custom-call(bf16[1024,2304]{1,0:T(8,128)(2,1)S(1)} %convolution_convert_fusion.q_ref.k_ref.v_ref, bf16[1024,2304]{1,0:T(8,128)(2,1)S(1)} %convolution_convert_fusion.q_ref.k_ref.v_ref, bf16[1024,2304]{1,0:T(8,128)(2,1)S(1)} %convolution_convert_fusion.q_ref.k_ref.v_ref, ...), custom_call_target="tpu_custom_call" | custom-call | tf_op jit(solution)/shard_map/attn_fwd_self/pallas_call | solution.py:93
  311.7 24.4 %attn_fwd_cross.1 = (bf16[1024,768]{1,0:T(8,128)(2,1)S(1)}, bf16[2,12,512,512]{3,2,1,0:T(8,128)(2,1)S(1)}) custom-call(bf16[1024,768]{1,0:T(8,128)(2,1)S(1)} %convolution_convert_fusion.10.q_ref, bf16[1024,1536]{1,0:T(8,128)(2,1)S(1)} %copy-done.2, bf16[1024,1536]{1,0:T(8,128)(2,1)S(1)} %copy-done.2, bf16[2,512,128]{2,1,0:T(8,128)(2,1)S(1)} %select_convert_fusion.qs_ref, ...), custom_call_target="tpu_custom_call" | custom-call | tf_op jit(solution)/shard_map/attn_fwd_cross/pallas_call | solution.py:93
  349.0 5.2 fusion.11
  361.0 6.0 multiply_convert_fusion.1
  375.2 6.7 fusion.5
  395.1 26.2 %attn_bwd_cross.1 = (bf16[1024,768]{1,0:T(8,128)(2,1)S(1)}, bf16[1024,768]{1,0:T(8,128)(2,1)S(1)}, bf16[1024,768]{1,0:T(8,128)(2,1)S(1)}) custom-call(bf16[1024,768]{1,0:T(8,128)(2,1)S(1)} %convolution_convert_fusion.10.q_ref, bf16[1024,1536]{1,0:T(8,128)(2,1)S(1)} %copy-done.2, bf16[1024,1536]{1,0:T(8,128)(2,1)S(1)} %copy-done.2, ...), custom_call_target="tpu_custom_call" | custom-call | tf_op jit(solution)/shard_map/attn_bwd_cross/pallas_call | solution.py:181
  436.8 5.2 convolution_convert_fusion.3
  453.0 31.3 %attn_bwd_self.1 = (bf16[1024,768]{1,0:T(8,128)(2,1)S(1)}, bf16[1024,768]{1,0:T(8,128)(2,1)S(1)}, bf16[1024,768]{1,0:T(8,128)(2,1)S(1)}, f32[12,4,256]{2,1,0:T(4,128)S(1)}) custom-call(bf16[1024,2304]{1,0:T(8,128)(2,1)S(1)} %bitcast.163, bf16[1024,2304]{1,0:T(8,128)(2,1)S(1)} %bitcast.163, bf16[1024,2304]{1,0:T(8,128)(2,1)S(1)} %bitcast.163, ...), custom_call_target="tpu_custom_call" | custom-call | tf_op jit(solution)/shard_map/attn_bwd_self/pallas_call | solution.py:181
  485.8 5.7 fusion.23
  491.4 5.3 convolution_convert_fusion.1
  524.1 37.8 %psum.7 = f32[32,12]{0,1:T(8,128)} all-reduce(f32[32,12]{0,1:T(8,128)S(1)} %select_reduce_fusion), channel_id=1, replica_groups=mesh['wide'=8,'narrow'=4] {'wide','narrow'}, use_global_device_ids=true, to_apply=%region_11.12 | all-reduce | flops 384 | bytes 3072 | tf_op jit(solution)/shard_map/psum | solution.py:360
  579.5 15.1 %collective-permute-done.52 = bf16[2,1,96,3072]{3,2,1,0:T(8,128)(2,1)S(1)} collective-permute-done((bf16[2,1,96,3072]{3,2,1,0:T(8,128)(2,1)S(1)}, bf16[2,1,96,3072]{3,2,1,0:T(8,128)(2,1)S(1)}, u32[]{:S(2)}, u32[]{:S(2)}) %collective-permute-start.52) | collective-permute-done | bytes 1179680 | tf_op jit(solution)/shard_map/ppermute | solution.py:272
  601.6 23.0 %collective-permute-done.42 = bf16[1,1,192,3072]{3,2,1,0:T(8,128)(2,1)S(1)} collective-permute-done((bf16[1,1,192,3072]{3,2,1,0:T(8,128)(2,1)S(1)}, bf16[1,1,192,3072]{3,2,1,0:T(8,128)(2,1)S(1)}, u32[]{:S(2)}, u32[]{:S(2)}) %collective-permute-start.42) | collective-permute-done | bytes 1179680 | tf_op jit(solution)/shard_map/ppermute | solution.py:272
  628.1 9.2 %collective-permute-done.53 = bf16[1,1,96,3072]{3,2,1,0:T(8,128)(2,1)S(1)} collective-permute-done((bf16[1,1,96,3072]{3,2,1,0:T(8,128)(2,1)S(1)}, bf16[1,1,96,3072]{3,2,1,0:T(8,128)(2,1)S(1)}, u32[]{:S(2)}, u32[]{:S(2)}) %collective-permute-start.53) | collective-permute-done | bytes 589856 | tf_op jit(solution)/shard_map/ppermute | solution.py:272
  651.4 18.8 %collective-permute-done.54 = bf16[1,1,48,3072]{3,2,1,0:T(8,128)(2,1)S(1)} collective-permute-done((bf16[1,1,48,3072]{3,2,1,0:T(8,128)(2,1)S(1)}, bf16[1,1,48,3072]{3,2,1,0:T(8,128)(2,1)S(1)}, u32[]{:S(2)}, u32[]{:S(2)}) %collective-permute-start.54) | collective-permute-done | bytes 294944 | tf_op jit(solution)/shard_map/ppermute | solution.py:272
  670.4 6.2 collective-permute-done.49
  676.8 6.1 collective-permute-done.44
  683.2 8.1 %collective-permute-done.55 = bf16[1,1,24,3072]{3,2,1,0:T(8,128)(2,1)S(1)} collective-permute-done((bf16[1,1,24,3072]{3,2,1,0:T(8,128)(2,1)S(1)}, bf16[1,1,24,3072]{3,2,1,0:T(8,128)(2,1)S(1)}, u32[]{:S(2)}, u32[]{:S(2)}) %collective-permute-start.55) | collective-permute-done | bytes 147488 | tf_op jit(solution)/shard_map/ppermute | solution.py:272
  (422 shorter events, 287.8 us)
Async XLA Ops:
  26.4 35.6 %collective-permute-start.19 = (bf16[48,3072]{1,0:T(8,128)(2,1)S(1)}, bf16[48,3072]{1,0:T(8,128)(2,1)S(1)}, u32[]{:S(2)}, u32[]{:S(2)}) collective-permute-start(bf16[48,3072]{1,0:T(8,128)(2,1)S(1)} %pad_maximum_fusion.8), channel_id=1, source_target_pairs={{0,2},{1,3},{2,0},{3,1},{4,6},{5,7},{6,4},{7,5},{8,10},{9,11},{10,... | collective-permute-start | bytes 884744 | tf_op jit(solution)/shard_map/ppermute | solution.py:247
  30.4 47.4 %collective-permute-start.28 = (bf16[48,3072]{1,0:T(8,128)(2,1)S(1)}, bf16[48,3072]{1,0:T(8,128)(2,1)S(1)}, u32[]{:S(2)}, u32[]{:S(2)}) collective-permute-start(bf16[48,3072]{1,0:T(8,128)(2,1)S(1)} %pad_maximum_fusion.9), channel_id=1, source_target_pairs={{0,2},{1,3},{2,0},{3,1},{4,6},{5,7},{6,4},{7,5},{8,10},{9,11},{10,... | collective-permute-start | bytes 884744 | tf_op jit(solution)/shard_map/ppermute | solution.py:247
  31.5 43.1 %collective-permute-start.10 = (bf16[48,3072]{1,0:T(8,128)(2,1)S(1)}, bf16[48,3072]{1,0:T(8,128)(2,1)S(1)}, u32[]{:S(2)}, u32[]{:S(2)}) collective-permute-start(bf16[48,3072]{1,0:T(8,128)(2,1)S(1)} %pad_maximum_fusion.7), channel_id=1, source_target_pairs={{0,2},{1,3},{2,0},{3,1},{4,6},{5,7},{6,4},{7,5},{8,10},{9,11},{10,... | collective-permute-start | bytes 884744 | tf_op jit(solution)/shard_map/ppermute | solution.py:247
  35.5 45.4 %collective-permute-start.1 = (bf16[48,3200]{1,0:T(8,128)(2,1)S(1)}, bf16[48,3200]{1,0:T(8,128)(2,1)S(1)}, u32[]{:S(2)}, u32[]{:S(2)}) collective-permute-start(bf16[48,3200]{1,0:T(8,128)(2,1)S(1)} %pad_maximum_fusion.6), channel_id=1, source_target_pairs={{0,2},{1,3},{2,0},{3,1},{4,6},{5,7},{6,4},{7,5},{8,10},{9,11},{10,... | collective-permute-start | bytes 921608 | tf_op jit(solution)/shard_map/ppermute | solution.py:247
  63.7 37.7 %collective-permute-start.21 = (bf16[96,3072]{1,0:T(8,128)(2,1)}, bf16[96,3072]{1,0:T(8,128)(2,1)}, u32[]{:S(2)}, u32[]{:S(2)}) collective-permute-start(bf16[96,3072]{1,0:T(8,128)(2,1)} %get-tuple-element.89), channel_id=1, source_target_pairs={{0,16},{4,20},{8,24},{12,28},{16,0},{20,4},{24,8},{28,12},{1,17},{... | collective-permute-start | bytes 1769480 | tf_op jit(solution)/shard_map/ppermute | solution.py:252
  65.2 33.7 %collective-permute-start.20 = (bf16[96,3072]{1,0:T(8,128)(2,1)}, bf16[96,3072]{1,0:T(8,128)(2,1)}, u32[]{:S(2)}, u32[]{:S(2)}) collective-permute-start(bf16[96,3072]{1,0:T(8,128)(2,1)} %get-tuple-element.89), channel_id=1, source_target_pairs={{0,8},{4,12},{8,0},{12,4},{16,24},{20,28},{24,16},{28,20},{1,9},{5... | collective-permute-start | bytes 1769480 | tf_op jit(solution)/shard_map/ppermute | solution.py:252
  76.3 30.5 %collective-permute-start.12 = (bf16[96,3072]{1,0:T(8,128)(2,1)}, bf16[96,3072]{1,0:T(8,128)(2,1)}, u32[]{:S(2)}, u32[]{:S(2)}) collective-permute-start(bf16[96,3072]{1,0:T(8,128)(2,1)} %get-tuple-element.93), channel_id=1, source_target_pairs={{0,8},{4,12},{8,0},{12,4},{16,24},{20,28},{24,16},{28,20},{1,9},{5... | collective-permute-start | bytes 1769480 | tf_op jit(solution)/shard_map/ppermute | solution.py:252
  83.2 33.7 %collective-permute-start.30 = (bf16[96,3072]{1,0:T(8,128)(2,1)}, bf16[96,3072]{1,0:T(8,128)(2,1)}, u32[]{:S(2)}, u32[]{:S(2)}) collective-permute-start(bf16[96,3072]{1,0:T(8,128)(2,1)} %get-tuple-element.85), channel_id=1, source_target_pairs={{0,8},{4,12},{8,0},{12,4},{16,24},{20,28},{24,16},{28,20},{1,9},{5... | collective-permute-start | bytes 1769480 | tf_op jit(solution)/shard_map/ppermute | solution.py:252
  101.4 48.1 %collective-permute-start.5 = (bf16[96,3200]{1,0:T(8,128)(2,1)}, bf16[96,3200]{1,0:T(8,128)(2,1)}, u32[]{:S(2)}, u32[]{:S(2)}) collective-permute-start(bf16[96,3200]{1,0:T(8,128)(2,1)} %pad_maximum_fusion.2), channel_id=1, source_target_pairs={{0,4},{4,0},{8,12},{12,8},{16,20},{20,16},{24,28},{28,24},{1,5},{5... | collective-permute-start | bytes 1843208 | tf_op jit(solution)/shard_map/ppermute | solution.py:252
  103.3 34.1 %collective-permute-start.3 = (bf16[96,3200]{1,0:T(8,128)(2,1)}, bf16[96,3200]{1,0:T(8,128)(2,1)}, u32[]{:S(2)}, u32[]{:S(2)}) collective-permute-start(bf16[96,3200]{1,0:T(8,128)(2,1)} %pad_maximum_fusion.2), channel_id=1, source_target_pairs={{0,16},{4,20},{8,24},{12,28},{16,0},{20,4},{24,8},{28,12},{1,17},{... | collective-permute-start | bytes 1843208 | tf_op jit(solution)/shard_map/ppermute | solution.py:252
  115.5 37.7 %collective-permute-start.22 = (bf16[96,3072]{1,0:T(8,128)(2,1)}, bf16[96,3072]{1,0:T(8,128)(2,1)}, u32[]{:S(2)}, u32[]{:S(2)}) collective-permute-start(bf16[96,3072]{1,0:T(8,128)(2,1)} %collective-permute-done.20), channel_id=1, source_target_pairs={{0,16},{4,20},{8,24},{12,28},{16,0},{20,4},{24,8},{28,12},{1,17},{... | collective-permute-start | bytes 1769480 | tf_op jit(solution)/shard_map/ppermute | solution.py:252
  116.8 38.3 %collective-permute-start.13 = (bf16[96,3072]{1,0:T(8,128)(2,1)}, bf16[96,3072]{1,0:T(8,128)(2,1)}, u32[]{:S(2)}, u32[]{:S(2)}) collective-permute-start(bf16[96,3072]{1,0:T(8,128)(2,1)} %collective-permute-done.11), channel_id=1, source_target_pairs={{0,8},{4,12},{8,0},{12,4},{16,24},{20,28},{24,16},{28,20},{1,9},{5... | collective-permute-start | bytes 1769480 | tf_op jit(solution)/shard_map/ppermute | solution.py:252
  124.4 33.1 %collective-permute-start.23 = (bf16[96,3072]{1,0:T(8,128)(2,1)}, bf16[96,3072]{1,0:T(8,128)(2,1)}, u32[]{:S(2)}, u32[]{:S(2)}) collective-permute-start(bf16[96,3072]{1,0:T(8,128)(2,1)} %get-tuple-element.89), channel_id=1, source_target_pairs={{0,4},{4,0},{8,12},{12,8},{16,20},{20,16},{24,28},{28,24},{1,5},{5... | collective-permute-start | bytes 1769480 | tf_op jit(solution)/shard_map/ppermute | solution.py:252
  149.5 32.8 %collective-permute-start.32 = (bf16[96,3072]{1,0:T(8,128)(2,1)}, bf16[96,3072]{1,0:T(8,128)(2,1)}, u32[]{:S(2)}, u32[]{:S(2)}) collective-permute-start(bf16[96,3072]{1,0:T(8,128)(2,1)} %get-tuple-element.85), channel_id=1, source_target_pairs={{0,4},{4,0},{8,12},{12,8},{16,20},{20,16},{24,28},{28,24},{1,5},{5... | collective-permute-start | bytes 1769480 | tf_op jit(solution)/shard_map/ppermute | solution.py:252
  167.1 68.4 %collective-permute-start.7 = (bf16[96,3200]{1,0:T(8,128)(2,1)}, bf16[96,3200]{1,0:T(8,128)(2,1)}, u32[]{:S(2)}, u32[]{:S(2)}) collective-permute-start(bf16[96,3200]{1,0:T(8,128)(2,1)} %collective-permute-done.3), channel_id=1, source_target_pairs={{0,4},{4,0},{8,12},{12,8},{16,20},{20,16},{24,28},{28,24},{1,5},{5... | collective-permute-start | bytes 1843208 | tf_op jit(solution)/shard_map/ppermute | solution.py:252
  180.3 42.2 %collective-permute-start.6 = (bf16[96,3200]{1,0:T(8,128)(2,1)}, bf16[96,3200]{1,0:T(8,128)(2,1)}, u32[]{:S(2)}, u32[]{:S(2)}) collective-permute-start(bf16[96,3200]{1,0:T(8,128)(2,1)} %collective-permute-done.2), channel_id=1, source_target_pairs={{0,4},{4,0},{8,12},{12,8},{16,20},{20,16},{24,28},{28,24},{1,5},{5... | collective-permute-start | bytes 1843208 | tf_op jit(solution)/shard_map/ppermute | solution.py:252
  184.8 63.8 %collective-permute-start.26 = (bf16[96,3072]{1,0:T(8,128)(2,1)}, bf16[96,3072]{1,0:T(8,128)(2,1)}, u32[]{:S(2)}, u32[]{:S(2)}) collective-permute-start(bf16[96,3072]{1,0:T(8,128)(2,1)} %collective-permute-done.22), channel_id=1, source_target_pairs={{0,4},{4,0},{8,12},{12,8},{16,20},{20,16},{24,28},{28,24},{1,5},{5... | collective-permute-start | bytes 1769480 | tf_op jit(solution)/shard_map/ppermute | solution.py:252
  185.9 64.6 %collective-permute-start.17 = (bf16[96,3072]{1,0:T(8,128)(2,1)}, bf16[96,3072]{1,0:T(8,128)(2,1)}, u32[]{:S(2)}, u32[]{:S(2)}) collective-permute-start(bf16[96,3072]{1,0:T(8,128)(2,1)} %collective-permute-done.13), channel_id=1, source_target_pairs={{0,4},{4,0},{8,12},{12,8},{16,20},{20,16},{24,28},{28,24},{1,5},{5... | collective-permute-start | bytes 1769480 | tf_op jit(solution)/shard_map/ppermute | solution.py:252
  198.8 53.5 %collective-permute-start.35 = (bf16[96,3072]{1,0:T(8,128)(2,1)}, bf16[96,3072]{1,0:T(8,128)(2,1)}, u32[]{:S(2)}, u32[]{:S(2)}) collective-permute-start(bf16[96,3072]{1,0:T(8,128)(2,1)} %collective-permute-done.31), channel_id=1, source_target_pairs={{0,4},{4,0},{8,12},{12,8},{16,20},{20,16},{24,28},{28,24},{1,5},{5... | collective-permute-start | bytes 1769480 | tf_op jit(solution)/shard_map/ppermute | solution.py:252
  444.2 117.8 %collective-permute-start.51 = (bf16[4,1,96,3072]{3,2,1,0:T(8,128)(2,1)}, bf16[4,1,96,3072]{3,2,1,0:T(8,128)(2,1)}, u32[]{:S(2)}, u32[]{:S(2)}) collective-permute-start(bf16[4,1,96,3072]{3,2,1,0:T(8,128)(2,1)} %fusion.28), channel_id=1, source_target_pairs={{0,4},{4,0},{8,12},{12,8},{16,20},{20,16},{24,28},{28,24},{1,5},{5... | collective-permute-start | bytes 7077896 | tf_op jit(solution)/shard_map/ppermute | solution.py:272
  451.8 115.9 %collective-permute-start.46 = (bf16[4,1,96,3072]{3,2,1,0:T(8,128)(2,1)}, bf16[4,1,96,3072]{3,2,1,0:T(8,128)(2,1)}, u32[]{:S(2)}, u32[]{:S(2)}) collective-permute-start(bf16[4,1,96,3072]{3,2,1,0:T(8,128)(2,1)} %fusion.30), channel_id=1, source_target_pairs={{0,4},{4,0},{8,12},{12,8},{16,20},{20,16},{24,28},{28,24},{1,5},{5... | collective-permute-start | bytes 7077896 | tf_op jit(solution)/shard_map/ppermute | solution.py:272
  504.3 71.1 %collective-permute-start.36 = (bf16[4,1,96,3200]{3,2,1,0:T(8,128)(2,1)}, bf16[4,1,96,3200]{3,2,1,0:T(8,128)(2,1)}, u32[]{:S(2)}, u32[]{:S(2)}) collective-permute-start(bf16[4,1,96,3200]{3,2,1,0:T(8,128)(2,1)} %constant_dynamic-slice_fusion.17), channel_id=1, source_target_pairs={{0,4},{4,0},{8,12},{12,8},{16,20},{20,16},{24,28},{28,24},{1,5},{5... | collective-permute-start | bytes 7372808 | tf_op jit(solution)/shard_map/ppermute | solution.py:272
  519.4 53.1 %collective-permute-start.41 = (bf16[4,1,96,3072]{3,2,1,0:T(8,128)(2,1)}, bf16[4,1,96,3072]{3,2,1,0:T(8,128)(2,1)}, u32[]{:S(2)}, u32[]{:S(2)}) collective-permute-start(bf16[4,1,96,3072]{3,2,1,0:T(8,128)(2,1)} %constant_dynamic-slice_fusion.12), channel_id=1, source_target_pairs={{0,4},{4,0},{8,12},{12,8},{16,20},{20,16},{24,28},{28,24},{1,5},{5... | collective-permute-start | bytes 7077896 | tf_op jit(solution)/shard_map/ppermute | solution.py:272
  565.4 29.2 %collective-permute-start.52 = (bf16[2,1,96,3072]{3,2,1,0:T(8,128)(2,1)S(1)}, bf16[2,1,96,3072]{3,2,1,0:T(8,128)(2,1)S(1)}, u32[]{:S(2)}, u32[]{:S(2)}) collective-permute-start(bf16[2,1,96,3072]{3,2,1,0:T(8,128)(2,1)S(1)} %constant_dynamic-slice_fusion.3), channel_id=1, source_target_pairs={{0,8},{4,12},{8,0},{12,4},{16,24},{20,28},{24,16},{28,20},{1,9},{5... | collective-permute-start | bytes 3538952 | tf_op jit(solution)/shard_map/ppermute | solution.py:272
  575.2 49.5 %collective-permute-start.42 = (bf16[1,1,192,3072]{3,2,1,0:T(8,128)(2,1)S(1)}, bf16[1,1,192,3072]{3,2,1,0:T(8,128)(2,1)S(1)}, u32[]{:S(2)}, u32[]{:S(2)}) collective-permute-start(bf16[1,1,192,3072]{3,2,1,0:T(8,128)(2,1)S(1)} %constant_dynamic-slice_fusion.11), channel_id=1, source_target_pairs={{0,16},{4,20},{8,24},{12,28},{16,0},{20,4},{24,8},{28,12},{1,17},{... | collective-permute-start | bytes 3538952 | tf_op jit(solution)/shard_map/ppermute | solution.py:272
  577.9 49.0 %collective-permute-start.37 = (bf16[2,1,96,3200]{3,2,1,0:T(8,128)(2,1)S(1)}, bf16[2,1,96,3200]{3,2,1,0:T(8,128)(2,1)S(1)}, u32[]{:S(2)}, u32[]{:S(2)}) collective-permute-start(bf16[2,1,96,3200]{3,2,1,0:T(8,128)(2,1)S(1)} %constant_dynamic-slice_fusion.16), channel_id=1, source_target_pairs={{0,8},{4,12},{8,0},{12,4},{16,24},{20,28},{24,16},{28,20},{1,9},{5... | collective-permute-start | bytes 3686408 | tf_op jit(solution)/shard_map/ppermute | solution.py:272
  595.1 42.2 %collective-permute-start.53 = (bf16[1,1,96,3072]{3,2,1,0:T(8,128)(2,1)S(1)}, bf16[1,1,96,3072]{3,2,1,0:T(8,128)(2,1)S(1)}, u32[]{:S(2)}, u32[]{:S(2)}) collective-permute-start(bf16[1,1,96,3072]{3,2,1,0:T(8,128)(2,1)S(1)} %constant_dynamic-slice_fusion.2), channel_id=1, source_target_pairs={{0,16},{4,20},{8,24},{12,28},{16,0},{20,4},{24,8},{28,12},{1,17},{... | collective-permute-start | bytes 1769480 | tf_op jit(solution)/shard_map/ppermute | solution.py:272
  599.9 40.7 %collective-permute-start.48 = (bf16[1,1,96,3072]{3,2,1,0:T(8,128)(2,1)S(1)}, bf16[1,1,96,3072]{3,2,1,0:T(8,128)(2,1)S(1)}, u32[]{:S(2)}, u32[]{:S(2)}) collective-permute-start(bf16[1,1,96,3072]{3,2,1,0:T(8,128)(2,1)S(1)} %constant_dynamic-slice_fusion.6), channel_id=1, source_target_pairs={{0,8},{4,12},{8,0},{12,4},{16,24},{20,28},{24,16},{28,20},{1,9},{5... | collective-permute-start | bytes 1769480 | tf_op jit(solution)/shard_map/ppermute | solution.py:272
  637.5 32.7 %collective-permute-start.54 = (bf16[1,1,48,3072]{3,2,1,0:T(8,128)(2,1)S(1)}, bf16[1,1,48,3072]{3,2,1,0:T(8,128)(2,1)S(1)}, u32[]{:S(2)}, u32[]{:S(2)}) collective-permute-start(bf16[1,1,48,3072]{3,2,1,0:T(8,128)(2,1)S(1)} %constant_dynamic-slice_fusion.1), channel_id=1, source_target_pairs={{0,2},{1,3},{2,0},{3,1},{4,6},{5,7},{6,4},{7,5},{8,10},{9,11},{10,... | collective-permute-start | bytes 884744 | tf_op jit(solution)/shard_map/ppermute | solution.py:272
  640.7 35.9 %collective-permute-start.49 = (bf16[1,1,48,3072]{3,2,1,0:T(8,128)(2,1)S(1)}, bf16[1,1,48,3072]{3,2,1,0:T(8,128)(2,1)S(1)}, u32[]{:S(2)}, u32[]{:S(2)}) collective-permute-start(bf16[1,1,48,3072]{3,2,1,0:T(8,128)(2,1)S(1)} %constant_dynamic-slice_fusion.5), channel_id=1, source_target_pairs={{0,2},{1,3},{2,0},{3,1},{4,6},{5,7},{6,4},{7,5},{8,10},{9,11},{10,... | collective-permute-start | bytes 884744 | tf_op jit(solution)/shard_map/ppermute | solution.py:272
  644.4 38.5 %collective-permute-start.44 = (bf16[1,1,48,3072]{3,2,1,0:T(8,128)(2,1)S(1)}, bf16[1,1,48,3072]{3,2,1,0:T(8,128)(2,1)S(1)}, u32[]{:S(2)}, u32[]{:S(2)}) collective-permute-start(bf16[1,1,48,3072]{3,2,1,0:T(8,128)(2,1)S(1)} %constant_dynamic-slice_fusion.9), channel_id=1, source_target_pairs={{0,2},{1,3},{2,0},{3,1},{4,6},{5,7},{6,4},{7,5},{8,10},{9,11},{10,... | collective-permute-start | bytes 884744 | tf_op jit(solution)/shard_map/ppermute | solution.py:272
  648.4 49.9 %collective-permute-start.39 = (bf16[1,1,48,3200]{3,2,1,0:T(8,128)(2,1)S(1)}, bf16[1,1,48,3200]{3,2,1,0:T(8,128)(2,1)S(1)}, u32[]{:S(2)}, u32[]{:S(2)}) collective-permute-start(bf16[1,1,48,3200]{3,2,1,0:T(8,128)(2,1)S(1)} %constant_dynamic-slice_fusion.14), channel_id=1, source_target_pairs={{0,2},{1,3},{2,0},{3,1},{4,6},{5,7},{6,4},{7,5},{8,10},{9,11},{10,... | collective-permute-start | bytes 921608 | tf_op jit(solution)/shard_map/ppermute | solution.py:272
  (94 other events, 1205.0 us)

commit v2 on v1

v2 whole, which is shorter than its diff:
```python
import functools
import jax
import jax.numpy as jnp
from jax import lax
from jax.sharding import PartitionSpec as P
from jax.experimental import pallas as pl
from jax.experimental.pallas import tpu as pltpu

DH = 64
NEGATIVE = -1e30
BF = jnp.bfloat16
F32 = jnp.float32
NN = (((1,), (0,)), ((), ()))
NT = (((1,), (1,)), ((), ()))
TN = (((0,), (0,)), ((), ()))
MB = 1 << 20


def dot(a, b, dims=NN):
    return lax.dot_general(a, b, dims, preferred_element_type=F32)


def segment_columns(query_seg, key_seg):
    ids = jnp.arange(128)
    other = (query_seg[..., None] != ids) & (ids < 4)
    query_cols = jnp.where(other, NEGATIVE, 0.0).astype(BF)
    key_cols = (key_seg[..., None] == ids).astype(BF)
    return query_cols, key_cols


def attn_fwd_kernel(causal, q_ref, k_ref, v_ref, qs_ref, ks_ref, *rest):
    if causal:
        t_ref, o_ref, p_ref, bias = rest
    else:
        o_ref, p_ref = rest
    length = q_ref.shape[0]
    if causal:
        @pl.when(pl.program_id(1) == 0)
        def _():
            for h in range(2):
                for d in range(length // 128):
                    row = jnp.concatenate([t_ref[h, :, pl.ds(128 * (d + 1), 128)], t_ref[h, :, pl.ds(128 * d, 128)]], axis=1)
                    tile = pltpu.roll(jnp.broadcast_to(row, (128, 256)), 0, 1, stride=1, stride_axis=0)
                    bias[h, d] = tile[:, :128]
    lane = lax.broadcasted_iota(jnp.int32, (1, 128), 1)
    q = q_ref[...]
    keys = jnp.concatenate([k_ref[...], ks_ref[...]], axis=1)
    v_t = v_ref[...].T
    parts = []
    for h in range(2):
        mine = (lane // DH) == h
        qa = jnp.concatenate([jnp.where(mine, q, 0).astype(BF), qs_ref[...]], axis=1)
        cols = []
        for c in range(length // 256):
            n = 256 * (c + 1) if causal else length
            s = dot(keys[:n], qa[256 * c: 256 * (c + 1)], NT)
            if causal:
                rows = []
                for kb in range(n // 128):
                    tiles = []
                    for qb in (2 * c, 2 * c + 1):
                        st = s[128 * kb:128 * (kb + 1), 128 * (qb - 2 * c):128 * (qb - 2 * c + 1)]
                        if qb >= kb:
                            tiles.append(st + bias[h, qb - kb])
                        else:
                            tiles.append(jnp.full((128, 128), NEGATIVE, F32))
                    rows.append(jnp.concatenate(tiles, axis=1))
                s = jnp.concatenate(rows, axis=0)
            top = jnp.max(s, axis=0, keepdims=True)
            e = jnp.exp(s - top)
            p = (e * (1.0 / jnp.sum(e, axis=0, keepdims=True))).astype(BF)
            p_ref[h, pl.ds(0, n), pl.ds(256 * c, 256)] = p
            if n < length:
                p_ref[h, pl.ds(n, length - n), pl.ds(256 * c, 256)] = jnp.zeros((length - n, 256), BF)
            cols.append(dot(v_t[DH * h: DH * (h + 1), :n], p))
        parts.append(jnp.concatenate(cols, axis=1))
    o_ref[...] = jnp.concatenate(parts, axis=0).T.astype(BF)


def attn_fwd(span, q_arr, q_col, k_arr, k_col, v_arr, v_col, q_seg, k_seg, table=None):
    rows, length = q_seg.shape[:2]
    begin, pairs = span
    causal = table is not None
    block = lambda col: pl.BlockSpec((length, 128), lambda h, b: (b, begin + col + h))
    seg = pl.BlockSpec((None, length, 128), lambda h, b: (b, 0, 0))
    in_specs = [block(q_col), block(k_col), block(v_col), seg, seg]
    args = [q_arr, k_arr, v_arr, q_seg, k_seg]
    scratch = []
    if causal:
        in_specs.append(pl.BlockSpec((2, 1, table.shape[2]), lambda h, b: (begin + h, 0, 0)))
        args.append(table)
        scratch = [pltpu.VMEM((2, length // 128, 128, 128), F32)]
    return pl.pallas_call(
        functools.partial(attn_fwd_kernel, causal),
        grid=(pairs, rows),
        in_specs=in_specs,
        out_specs=[pl.BlockSpec((length, 128), lambda h, b: (b, h)), pl.BlockSpec((None, 2, length, length), lambda h, b: (b, h, 0, 0))],
        out_shape=[jax.ShapeDtypeStruct((rows * length, pairs * 128), BF), jax.ShapeDtypeStruct((rows, 2 * pairs, length, length), BF)],
        scratch_shapes=scratch,
        compiler_params=pltpu.CompilerParams(vmem_limit_bytes=32 * MB),
        cost_estimate=pl.CostEstimate(flops=16 * rows * pairs * length * length * 256, bytes_accessed=4 * rows * pairs * length * length, transcendentals=0),
        name="attn_fwd_self" if causal else "attn_fwd_cross",
    )(*args)


def attn_bwd_kernel(causal, q_ref, k_ref, v_ref, g_ref, o_ref, p_ref, *rest):
    if causal:
        dq_ref, dk_ref, dv_ref, diag_ref, acc = rest
    else:
        dq_ref, dk_ref, dv_ref = rest
    length = q_ref.shape[0]
    lane = lax.broadcasted_iota(jnp.int32, (1, 128), 1)
    q = q_ref[...]
    g = g_ref[...]
    values = jnp.concatenate([v_ref[...], jnp.broadcast_to((lane < 2).astype(BF), (length, 128))], axis=1)
    k_t = k_ref[...].T
    prod = g.astype(F32) * o_ref[...].astype(F32)
    if causal:
        @pl.when(pl.program_id(1) == 0)
        def _():
            acc[...] = jnp.zeros_like(acc)
    dq_parts = []
    dk = [None] * (length // 256)
    dv = [None] * (length // 256)
    add = lambda old, new: new if old is None else old + new
    for h in range(2):
        mine = (lane // DH) == h
        delta = -jnp.sum(jnp.where(mine, prod, 0.0), axis=1, keepdims=True)
        high = delta.astype(BF)
        lowp = (delta - high.astype(F32)).astype(BF)
        extra = jnp.where(lane == 0, high, jnp.where(lane == 1, lowp, jnp.zeros_like(lowp)))
        gm = jnp.where(mine, g, 0).astype(BF)
        qm = jnp.where(mine, q, 0).astype(BF)
        ga = jnp.concatenate([gm, extra], axis=1)
        cols = []
        for c in range(length // 256):
            n = 256 * (c + 1) if causal else length
            qsl = slice(256 * c, 256 * (c + 1))
            p = p_ref[h, pl.ds(0, n), pl.ds(256 * c, 256)]
            dp = dot(values[:n], ga[qsl], NT)
            ds = (p.astype(F32) * dp).astype(BF)
            if causal:
                for kb in range(n // 128):
                    for qb in (2 * c, 2 * c + 1):
                        if qb >= kb:
                            acc[h, qb - kb] += ds[128 * kb:128 * (kb + 1), 128 * (qb - 2 * c):128 * (qb - 2 * c + 1)].astype(F32)
            cols.append(dot(k_t[DH * h: DH * (h + 1), :n], ds))
            dkn = dot(ds, qm[qsl])
            dvn = dot(p, gm[qsl])
            for kc in range(n // 256):
                ksl = slice(256 * kc, 256 * (kc + 1))
                dk[kc] = add(dk[kc], dkn[ksl])
                dv[kc] = add(dv[kc], dvn[ksl])
        dq_parts.append(jnp.concatenate(cols, axis=1))
    dq_ref[...] = jnp.concatenate(dq_parts, axis=0).T.astype(BF)
    dk_ref[...] = jnp.concatenate(dk, axis=0).astype(BF)
    dv_ref[...] = jnp.concatenate(dv, axis=0).astype(BF)
    if causal:
        @pl.when(pl.program_id(1) == pl.num_programs(1) - 1)
        def _():
            flip = (lax.broadcasted_iota(jnp.int32, (128, 128), 0) + lax.broadcasted_iota(jnp.int32, (128, 128), 1) == 127).astype(F32)
            for h in range(2):
                for d in range(length // 128):
                    upside = jnp.dot(flip, acc[h, d], precision=lax.Precision.HIGHEST, preferred_element_type=F32)
                    wide = jnp.concatenate([upside, jnp.zeros((128, 128), F32)], axis=1)
                    turned = pltpu.roll(wide, 0, 1, stride=1, stride_axis=0)
                    diag_ref[h, pl.ds(d, 1), :] = jnp.sum(turned, axis=0, keepdims=True)


def attn_bwd(span, q_arr, q_col, k_arr, k_col, v_arr, v_col, grad, out, probs, causal):
    rows, heads, length = probs.shape[:3]
    begin, pairs = span
    block = lambda col: pl.BlockSpec((length, 128), lambda h, b: (b, begin + col + h))
    own = pl.BlockSpec((length, 128), lambda h, b: (b, h))
    flat = jax.ShapeDtypeStruct((rows * length, pairs * 128), BF)
    out_specs = [own] * 3
    out_shape = [flat] * 3
    scratch = []
    if causal:
        out_specs.append(pl.BlockSpec((2, length // 128, 256), lambda h, b: (h, 0, 0)))
        out_shape.append(jax.ShapeDtypeStruct((heads, length // 128, 256), F32))
        scratch = [pltpu.VMEM((2, length // 128, 128, 128), F32)]
    return pl.pallas_call(
        functools.partial(attn_bwd_kernel, causal),
        grid=(pairs, rows),
        in_specs=[block(q_col), block(k_col), block(v_col), block(0), own, pl.BlockSpec((None, 2, length, length), lambda h, b: (b, h, 0, 0))],
        out_specs=out_specs,
        out_shape=out_shape,
        scratch_shapes=scratch,
        compiler_params=pltpu.CompilerParams(vmem_limit_bytes=40 * MB),
        cost_estimate=pl.CostEstimate(flops=16 * rows * pairs * length * length * 256, bytes_accessed=4 * rows * pairs * length * length, transcendentals=0),
        name="attn_bwd_self" if causal else "attn_bwd_cross",
    )(q_arr, k_arr, v_arr, grad, out, probs)


def score_table(rel_bias, buckets):
    hot = buckets[:, None] == jnp.arange(rel_bias.shape[0])[None, :]
    at = jnp.sum(jnp.where(hot[:, :, None], rel_bias[None], 0.0), axis=1)
    return jnp.concatenate([jnp.full((rel_bias.shape[1], 128), NEGATIVE, F32), at.T], axis=1)[:, None]


def bucket_sums(diag, buckets, count):
    heads, blocks, _ = diag.shape
    own = diag[:, :, 127:255]
    before = jnp.pad(diag[:, 1:, :127], ((0, 0), (0, 1), (1, 0)))
    at = (own + before).reshape(heads, blocks * 128)
    hot = buckets[:, None] == jnp.arange(count)[None, :]
    return jnp.sum(jnp.where(hot[:, :, None], at.T[:, None, :], 0.0), axis=0)


EPSILON = 1e-06
ROOT_HALF = 0.7071067811865476
INV_ROOT_TWO_PI = 0.3989422804014327
WIDE, NARROW = "wide", "narrow"
VMEM_LIMIT = 56 * MB


def flipped(size, bit):
    return [(i, i ^ bit) for i in range(size)]


def bits_of(size):
    return [1 << i for i in range(size.bit_length() - 1)]


def merge(blocks, at):
    count = len(blocks)
    slots = []
    for j in range(count):
        slot = blocks[j]
        for k in range(count):
            if k != 0:
                slot = jnp.where((at ^ k) == 0, blocks[j ^ k], slot)
        slots.append(slot)
    return jnp.concatenate(slots, axis=0)


def low_bits(wide, rows):
    low = []
    for bit in bits_of(wide):
        if (rows * bit) % 16 == 0:
            break
        low.append(bit)
    return low


def cross_bits(wide, rows, turn):
    bits = [b for b in bits_of(wide) if b not in low_bits(wide, rows)]
    first, rest = bits[:1], bits[1:]
    turn = turn % max(len(rest), 1)
    return rest[turn:] + rest[:turn] + first


class Gather:
    def __init__(self, sizes, blocks):
        self.wide, self.narrow = sizes
        self.groups = [[b] for b in blocks]
        self.flight = None
        rows = blocks[0].shape[0] * self.narrow
        self.low = low_bits(self.wide, rows)
        self.orders = [cross_bits(self.wide, rows, i) for i in range(len(blocks))]
        self.plan = ["narrow"] + [("low", b) for b in self.low] + list(range(len(self.orders[0])))

    def go(self):
        step = self.plan[0]
        if step == "narrow":
            self.flight = [[lax.ppermute(g[0], NARROW, flipped(self.narrow, k)) for k in range(1, self.narrow)] for g in self.groups]
        elif isinstance(step, tuple):
            self.flight = [[lax.ppermute(g[0], WIDE, flipped(self.wide, step[1]))] for g in self.groups]
        else:
            self.flight = [[lax.ppermute(p, WIDE, flipped(self.wide, self.orders[i][step])) for p in g] for i, g in enumerate(self.groups)]

    def land(self):
        step = self.plan.pop(0)
        if step == "narrow":
            at = lax.axis_index(NARROW)
            self.groups = [[merge(g + f, at)] for g, f in zip(self.groups, self.flight)]
        elif isinstance(step, tuple):
            at = (lax.axis_index(WIDE) // step[1]) % 2
            self.groups = [[merge(g + f, at)] for g, f in zip(self.groups, self.flight)]
        else:
            self.groups = [g + f for g, f in zip(self.groups, self.flight)]
        self.flight = None

    def state(self, landing):
        return (self.groups, self.flight if landing else None)

    def put(self, state, landing):
        self.groups = state[0]
        if landing:
            self.flight = state[1]

    def whole(self):
        skip = 1 << len(self.low)
        offsets = []
        for order in self.orders:
            found = [0]
            for bit in order:
                found = found + [f ^ (bit // skip) for f in found]
            offsets.append(found)
        place = (lax.axis_index(WIDE) // skip).astype(jnp.int32).reshape(1)
        return assemble(self.groups, offsets, place)


def assemble_kernel(offsets, columns, me_ref, *refs):
    pieces, out = refs[:-1], refs[-1]
    for g in range(len(columns)):
        for i, offset in enumerate(offsets[g]):
            piece = pieces[g * len(offsets[g]) + i]
            rows, width = piece.shape
            start = pl.multiple_of((me_ref[0] ^ offset) * rows, 16)
            out[pl.ds(start, rows), columns[g]: columns[g] + width] = piece[...]


def assemble(groups, offsets, place):
    widths = [g[0].shape[1] for g in groups]
    columns = [sum(widths[:i]) for i in range(len(groups))]
    flat = [p for g in groups for p in g]
    rows = groups[0][0].shape[0] * len(groups[0])
    return pl.pallas_call(
        functools.partial(assemble_kernel, offsets, columns),
        in_specs=[pl.BlockSpec(memory_space=pltpu.SMEM)] + [pl.BlockSpec(memory_space=pltpu.VMEM)] * len(flat),
        out_specs=pl.BlockSpec(memory_space=pltpu.VMEM),
        out_shape=jax.ShapeDtypeStruct((rows, sum(widths)), BF),
        compiler_params=pltpu.CompilerParams(vmem_limit_bytes=24 * MB),
        cost_estimate=pl.CostEstimate(flops=0, bytes_accessed=4 * rows * sum(widths), transcendentals=0),
        name="assemble",
    )(place, *flat)


class Scatter:
    def __init__(self, sizes, keep, send, first, turn):
        self.wide, self.narrow = sizes
        self.keep, self.sends = keep, [send]
        self.columns, self.lead = keep.shape[-1], keep.shape[0]
        self.left = [b for b in bits_of(self.wide) if b != first]
        high, low = [b for b in self.left if b > first], [b for b in self.left if b < first]
        turn = turn % max(len(high), 1)
        self.plan = [first] + high[turn:] + high[:turn] + low[::-1] + ["narrow"]
        self.flight = None

    def go(self):
        step = self.plan[0]
        if step == "narrow":
            self.flight = [lax.ppermute(s, NARROW, flipped(self.narrow, k + 1)) for k, s in enumerate(self.sends)]
        else:
            self.flight = [lax.ppermute(self.sends[0], WIDE, flipped(self.wide, step))]

    def land(self):
        self.plan.pop(0)
        value = self.keep.astype(F32)
        for received in self.flight:
            value = value + received.astype(F32)
        self.flight = None
        if not self.plan:
            self.keep, self.sends = value.reshape(self.lead, -1, self.columns), []
            return
        value = value.astype(BF)
        step = self.plan[0]
        if step == "narrow":
            value = value.reshape(self.lead, self.narrow, -1, self.columns)
            at = lax.axis_index(NARROW)
            pick = lambda k: lax.dynamic_slice_in_dim(value, at ^ k, 1, 1)[:, 0]
            self.keep, self.sends = pick(0), [pick(k) for k in range(1, self.narrow)]
        else:
            parts = self.lead << sum(b > step for b in self.left)
            self.left.remove(step)
            value = value.reshape(parts, 2, -1, self.columns)
            mine = (lax.axis_index(WIDE) // step) % 2
            pick = lambda k: lax.dynamic_slice_in_dim(value, k, 1, 1)[:, 0]
            self.keep, self.sends = pick(mine), [pick(1 - mine)]

    def state(self, landing):
        return (self.keep, self.sends, self.flight if landing else None)

    def put(self, state, landing):
        self.keep, self.sends = state[0], state[1]
        if landing:
            self.flight = state[2]


class Total:
    def __init__(self, sizes, value):
        self.value = value
        self.flight = None
        self.plan = [(name, size, bit) for name, size in zip((WIDE, NARROW), sizes) for bit in bits_of(size)]

    def go(self):
        name, size, bit = self.plan[0]
        self.flight = lax.ppermute(self.value, name, flipped(size, bit))

    def land(self):
        self.plan.pop(0)
        self.value, self.flight = self.value + self.flight, None

    def state(self, landing):
        return (self.value, self.flight if landing else None)

    def put(self, state, landing):
        self.value = state[0]
        if landing:
            self.flight = state[1]


class Rounds:
    def __init__(self):
        self.live = {}
        self.moving = []

    def __getitem__(self, name):
        return self.live[name]

    def run(self, work=None, go=(), land=()):
        for mover in go:
            mover.go()
            if mover not in self.moving:
                self.moving.append(mover)
        if work is not None:
            self.live.update(work())
        landing = [m for m in self.moving if m in land]
        known = [m for m in self.moving if m.flight is None or m in landing]
        live, states = lax.optimization_barrier((self.live, [m.state(m in landing) for m in known]))
        self.live = live
        for mover, state in zip(known, states):
            mover.put(state, mover in landing)
        for mover in landing:
            mover.land()

    def step(self, work=None, movers=()):
        movers = [m for m in movers if m.plan]
        self.run(work, movers, movers)


def store_halves(me, first_rows, result, keep_ref, send_ref, at):
    low = result.astype(BF)
    for part in range(result.shape[0] // (2 * first_rows)):
        even = low[2 * part * first_rows: (2 * part + 1) * first_rows]
        odd = low[(2 * part + 1) * first_rows: (2 * part + 2) * first_rows]
        index = at(part)
        keep_ref[index] = jnp.where(me == 0, even, odd)
        send_ref[index] = jnp.where(me == 0, odd, even)


def unit_of(value):
    inverse = lax.rsqrt(jnp.mean(value * value, axis=-1, keepdims=True) + EPSILON)
    return value * inverse, inverse


def norm_back(grad_norm, value, gain):
    unit, inverse = unit_of(value)
    grad_gain = jnp.sum(grad_norm * unit, axis=0, keepdims=True)
    grad_unit = grad_norm * gain
    return inverse * (grad_unit - unit * jnp.mean(grad_unit * unit, axis=-1, keepdims=True)), grad_gain


def call(kernel, name, grid, ins, outs, flops, scratch=(), limit=VMEM_LIMIT):
    spec = lambda block, index: pl.BlockSpec(block, index) if index is not None else pl.BlockSpec(memory_space=block)
    size = lambda shape, kind: jnp.dtype(kind).itemsize * functools.reduce(lambda a, b: a * b, shape, 1)
    moved = sum(size(a.shape, a.dtype) for a, _, _ in ins) + sum(size(o[0], o[1]) for o in outs)
    return pl.pallas_call(
        kernel,
        grid=grid,
        in_specs=[spec(b, i) for _, b, i in ins],
        out_specs=[spec(b, i) for _, _, b, i in outs],
        out_shape=[jax.ShapeDtypeStruct(s, d) for s, d, _, _ in outs],
        scratch_shapes=list(scratch),
        compiler_params=pltpu.CompilerParams(vmem_limit_bytes=limit),
        cost_estimate=pl.CostEstimate(flops=flops, bytes_accessed=moved, transcendentals=0),
        name=name,
    )(*[a for a, _, _ in ins])


ROWS = 256
row_map = lambda i: (i, 0)
col_map = lambda i: (0, i)
whole = lambda i: (0, 0)
at_col = lambda c: (lambda i: (0, c))


def proj_self_kernel(x_ref, gain_ref, w_ref, nt_ref, qkv_ref):
    unit, _ = unit_of(x_ref[...].astype(F32))
    n = (unit * gain_ref[0:1, :]).astype(BF)
    nt_ref[...] = n.T
    qkv_ref[...] = dot(n, w_ref[...]).astype(BF)


def spans_dot(refs, w, dims):
    total, at = None, 0
    for ref in refs:
        columns = ref.shape[1]
        term = dot(ref[...], w[:, at: at + columns], dims)
        total = term if total is None else total + term
        at += columns
    return total


def mid_kernel(x_ref, e_ref, gain_ref, wo_ref, wc_ref, *refs):
    o_refs, (x2_ref, nt_ref, qc_ref, kv_ref, et_ref) = refs[:-5], refs[-5:]
    width = x_ref.shape[1]
    e = e_ref[...]
    et_ref[...] = e.T
    kv_ref[...] = dot(e, wc_ref[:, width: 3 * width]).astype(BF)
    x2 = x_ref[...].astype(F32) + spans_dot(o_refs, wo_ref, NT)
    x2_ref[...] = x2
    unit, _ = unit_of(x2)
    n = (unit * gain_ref[1:2, :]).astype(BF)
    nt_ref[...] = n.T
    qc_ref[...] = dot(n, wc_ref[:, :width]).astype(BF)


def third_kernel(x2_ref, g_ref, gain_ref, wo_ref, *refs):
    o_refs, (x3_ref, n_ref, nt_ref, gt_ref) = refs[:-4], refs[-4:]
    x3 = x2_ref[...] + spans_dot(o_refs, wo_ref, NT)
    x3_ref[...] = x3
    unit, _ = unit_of(x3)
    n = (unit * gain_ref[2:3, :]).astype(BF)
    n_ref[...] = n
    nt_ref[...] = n.T
    gt_ref[...] = g_ref[...].T


def ffn_kernel(first_rows, me_ref, n_ref, nt_ref, g_ref, gt_ref, win_ref, wout_ref, y_ref, dn_ref, keep_in_ref, send_in_ref, keep_out_ref, send_out_ref):
    step = pl.program_id(0)
    w_in, w_out = win_ref[...], wout_ref[...]
    tokens = n_ref.shape[0]

    @pl.when(step == 0)
    def _():
        y_ref[...] = jnp.zeros_like(y_ref)
        dn_ref[...] = jnp.zeros_like(dn_ref)

    acts, grads = [], []
    for r in range(tokens // ROWS):
        rows = pl.ds(ROWS * r, ROWS)
        a = dot(n_ref[rows, :], w_in)
        back = dot(g_ref[rows, :], w_out)
        phi = 0.5 * (1.0 + lax.erf(a * ROOT_HALF))
        act = (a * phi).astype(BF)
        slope = phi + a * jnp.exp(-0.5 * a * a) * INV_ROOT_TWO_PI
        da = (back * slope).astype(BF)
        y_ref[rows, :] += dot(act, w_out, NT)
        dn_ref[rows, :] += dot(da, w_in, NT)
        acts.append(act)
        grads.append(da)
    act = jnp.concatenate(acts, axis=0)
    da = jnp.concatenate(grads, axis=0)
    me = me_ref[0]
    store_halves(me, first_rows, dot(nt_ref[...], da), keep_in_ref, send_in_ref, lambda p: (0, p))
    store_halves(me, first_rows, dot(gt_ref[...], act), keep_out_ref, send_out_ref, lambda p: (0, p))


def top_kernel(ya_ref, yb_ref, da_ref, db_ref, x3_ref, g_ref, gain_ref, wo_ref, out_ref, dx_ref, lowt_ref, doc_ref, gg_ref):
    x3 = x3_ref[...]
    out_ref[...] = (x3 + (ya_ref[...] + yb_ref[...])).astype(BF)
    grad, grad_gain = norm_back(da_ref[...] + db_ref[...], x3, gain_ref[2:3, :])
    dx = g_ref[...].astype(F32) + grad
    dx_ref[...] = dx
    low = dx.astype(BF)
    lowt_ref[...] = low.T
    doc_ref[...] = dot(low, wo_ref[...]).astype(BF)

    @pl.when(pl.program_id(0) == 0)
    def _():
        gg_ref[...] = jnp.zeros_like(gg_ref)

    gg_ref[0:1, :] += grad_gain


def second_kernel(x2_ref, dx3_ref, gain_ref, wq_ref, wo_ref, *refs):
    dq_refs, (dx_ref, lowt_ref, do_ref, gg_ref) = refs[:-4], refs[-4:]
    grad, grad_gain = norm_back(spans_dot(dq_refs, wq_ref, NT), x2_ref[...], gain_ref[1:2, :])
    dx = dx3_ref[...] + grad
    dx_ref[...] = dx
    low = dx.astype(BF)
    lowt_ref[...] = low.T
    do_ref[...] = dot(low, wo_ref[...]).astype(BF)

    @pl.when(pl.program_id(0) == 0)
    def _():
        gg_ref[...] = jnp.zeros_like(gg_ref)

    gg_ref[0:1, :] += grad_gain


def last_kernel(x_ref, dx2_ref, gain_ref, wq_ref, wk_ref, wv_ref, ck_ref, cv_ref, *refs):
    d_refs, (dx_ref, de_ref, gg_ref) = refs[:-3], refs[-3:]
    n = len(d_refs) // 5
    dq, dk, dv, dkc, dvc = (d_refs[n * i: n * (i + 1)] for i in range(5))
    dn = spans_dot(dq, wq_ref, NT) + spans_dot(dk, wk_ref, NT) + spans_dot(dv, wv_ref, NT)
    grad, grad_gain = norm_back(dn, x_ref[...].astype(F32), gain_ref[0:1, :])
    dx_ref[...] = dx2_ref[...] + grad
    de_ref[...] = spans_dot(dkc, ck_ref, NT) + spans_dot(dvc, cv_ref, NT)

    @pl.when(pl.program_id(0) == 0)
    def _():
        gg_ref[...] = jnp.zeros_like(gg_ref)

    gg_ref[0:1, :] += grad_gain


def grads_kernel(first_rows, lefts, count, me_ref, *refs):
    n_left = max(lefts) + 1
    left_refs, right_refs = refs[:n_left], refs[n_left: n_left + count]
    keep_ref, send_ref, left_buf, right_buf, sems = refs[n_left + count:]
    width = right_buf.shape[2]
    tile = 384 if width % 256 else 256
    widths = [width] * count

    def copies(p):
        found = [pltpu.make_async_copy(right_refs[p], right_buf.at[p % 2], sems.at[p % 2])]
        if p == 0 or lefts[p] != lefts[p - 1]:
            found.append(pltpu.make_async_copy(left_refs[lefts[p]], left_buf.at[lefts[p] % 2], sems.at[2 + lefts[p] % 2]))
        return found

    for copy in copies(0):
        copy.start()
    for p in range(count):
        if p + 1 < count:
            for copy in copies(p + 1):
                copy.start()
        for copy in copies(p):
            copy.wait()

        base = sum(widths[:p])

        def column(j, carry, p=p, base=base):
            col = pl.multiple_of(j * tile, tile)
            result = dot(left_buf[lefts[p] % 2], right_buf[p % 2, :, pl.ds(col, tile)])
            out = pl.multiple_of(base + j * tile, 128)
            store_halves(me_ref[0], first_rows, result, keep_ref, send_ref, lambda part: (0, part, slice(None), pl.ds(out, tile)))
            return carry

        lax.fori_loop(0, widths[p] // tile, column, 0)


def weight_grads(name, lefts_arrays, lefts, rights, half, first_rows):
    width = lefts_arrays[0].shape[0]
    tokens = rights[0].shape[0]
    columns = rights[0].shape[1]
    count = len(rights)
    shape = (1, width // (2 * first_rows), first_rows, count * columns)
    flops = 2 * width * tokens * columns * count
    return pl.pallas_call(
        functools.partial(grads_kernel, first_rows, lefts, count),
        in_specs=[pl.BlockSpec(memory_space=pltpu.SMEM)] + [pl.BlockSpec(memory_space=pl.ANY)] * (len(lefts_arrays) + count),
        out_specs=[pl.BlockSpec(memory_space=pltpu.VMEM)] * 2,
        out_shape=[jax.ShapeDtypeStruct(shape, BF)] * 2,
        scratch_shapes=[pltpu.VMEM((2, width, tokens), BF), pltpu.VMEM((2, tokens, columns), BF), pltpu.SemaphoreType.DMA((4,))],
        compiler_params=pltpu.CompilerParams(vmem_limit_bytes=VMEM_LIMIT),
        cost_estimate=pl.CostEstimate(flops=flops, bytes_accessed=2 * tokens * columns * count * 2, transcendentals=0),
        name=name,
    )(half, *lefts_arrays, *rights)


SPANS = ((0, 3), (3, 3))


def body(sizes, inputs, encoder_out, segments, enc_segments, buckets, gains, rel_bias, self_q, self_kv, self_out, cross_q, cross_kv, cross_out, ffn_in, ffn_out, out_grad):
    wide, narrow = sizes
    micro, per, length, width = inputs.shape
    rows = micro * per
    tokens = rows * length
    hidden = ffn_in.shape[1] // 2
    flat = lambda v: v.reshape(tokens, width)
    x, enc, grad_out = flat(inputs), flat(encoder_out), flat(out_grad)
    seg, enc_seg = segments.reshape(rows, length), enc_segments.reshape(rows, length)
    me = lax.axis_index(WIDE)

    outer_t = ffn_out.T
    gain_cols = jnp.pad(gains.T, ((0, 0), (0, 125)))
    g_self, g_cross, g_ffn0, g_ffn1 = [Gather(sizes, shard) for shard in (
        [jnp.concatenate([self_q, self_kv[0]], axis=1), jnp.concatenate([self_kv[1], self_out.T, gain_cols], axis=1)],
        [jnp.concatenate([cross_q, cross_kv[0]], axis=1), jnp.concatenate([cross_kv[1], cross_out.T], axis=1)],
        [ffn_in[:, :hidden], outer_t[:, :hidden]],
        [ffn_in[:, hidden:], outer_t[:, hidden:]],
    )]
    block_rows = self_q.shape[0] * narrow
    first = 1 << len(low_bits(wide, block_rows))
    first_rows = block_rows * first
    half = ((me // first) % 2).astype(jnp.int32).reshape(1)
    parts = width // (2 * first_rows)

    steps = (tokens // ROWS,)
    wide_f32 = lambda: ((tokens, width), F32, (ROWS, width), row_map)
    wide_low = lambda n=1: ((tokens, n * width), BF, (ROWS, n * width), row_map)
    turned = lambda: ((width, tokens), BF, (width, ROWS), col_map)
    gain_out = lambda: ((8, width), F32, (8, width), whole)
    rows_in = lambda v: (v, (ROWS, v.shape[1]), row_map)
    entire = lambda v: (v, v.shape, whole)
    piece = lambda slab, c: (slab, (width, width), at_col(c))
    unit = 2 * tokens * width * width

    r = Rounds()
    movers = [g_self, g_cross, g_ffn0, g_ffn1]
    r.moving = list(movers)
    r.live = {"x": x, "enc": enc, "g": grad_out}

    def prepare():
        return {"self_seg": segment_columns(seg, seg), "cross_seg": segment_columns(seg, enc_seg), "table": score_table(rel_bias, buckets)}

    def take_self():
        slab = g_self.whole()
        return {"slab_self": slab, "gain": slab[:, 4 * width: 4 * width + 3].T.astype(F32)}

    def proj():
        n1t, qkv = call(proj_self_kernel, "proj_self", steps, [rows_in(r["x"]), entire(r["gain"]), (r["slab_self"], (width, 3 * width), whole)], [turned(), wide_low(3)], 3 * unit)
        return {"n1t": n1t, "qkv": qkv}

    def fwd_self(i):
        o, p = attn_fwd(SPANS[i], r["qkv"], 0, r["qkv"], 6, r["qkv"], 12, *r["self_seg"], r["table"])
        return {f"o{i}": o, f"p{i}": p}

    def both(name):
        return [r[f"{name}{i}"] for i in range(len(SPANS))]

    def mid():
        out = call(mid_kernel, "mid", steps,
                   [rows_in(r["x"]), rows_in(r["enc"]), entire(r["gain"]), piece(r["slab_self"], 3), (r["slab_cross"], (width, 3 * width), whole)] + [rows_in(o) for o in both("o")],
                   [wide_f32(), turned(), wide_low(), wide_low(2), turned()], 4 * unit)
        return dict(zip(("x2", "n2t", "qc", "kvc", "et"), out))

    def fwd_cross(i):
        o, p = attn_fwd(SPANS[i], r["qc"], 0, r["kvc"], 0, r["kvc"], 6, *r["cross_seg"])
        return {f"oc{i}": o, f"pc{i}": p}

    def third():
        out = call(third_kernel, "third", steps,
                   [rows_in(r["x2"]), rows_in(r["g"]), entire(r["gain"]), piece(r["slab_cross"], 3)] + [rows_in(o) for o in both("oc")],
                   [wide_f32(), wide_low(), turned(), turned()], unit)
        return dict(zip(("x3", "n3", "n3t", "gt"), out))

    tile = 512
    tiles = hidden // tile
    halves = ((1, parts, first_rows, hidden), BF, (1, parts, first_rows, tile), lambda j: (0, 0, 0, j))
    acc_out = ((tokens, width), F32, (tokens, width), whole)

    def ffn(i):
        slab = r[f"slab_ffn{i}"]
        y, dn, *split = call(
            functools.partial(ffn_kernel, first_rows), "ffn", (tiles,),
            [(half, pltpu.SMEM, None), entire(r["n3"]), entire(r["n3t"]), entire(r["g"]), entire(r["gt"]),
             (slab, (width, tile), lambda j: (0, j)), (slab, (width, tile), lambda j: (0, tiles + j))],
            [acc_out, acc_out] + [halves] * 4, 12 * tokens * width * hidden)
        return {f"y{i}": y, f"dn{i}": dn, f"split{i}": split}

    def top():
        out = call(top_kernel, "top", steps,
                   [rows_in(r["y0"]), rows_in(r["y1"]), rows_in(r["dn0"]), rows_in(r["dn1"]), rows_in(r["x3"]), rows_in(r["g"]), entire(r["gain"]), piece(r["slab_cross"], 3)],
                   [wide_low(), wide_f32(), turned(), wide_low(), gain_out()], unit)
        return dict(zip(("layer", "dx3", "three_t", "doc", "gain3"), out))

    def bwd_cross(i):
        out = attn_bwd(SPANS[i], r["qc"], 0, r["kvc"], 0, r["kvc"], 6, r["doc"], r[f"oc{i}"], r[f"pc{i}"], False)
        return dict(zip((f"dqc{i}", f"dkc{i}", f"dvc{i}"), out))

    def second():
        out = call(second_kernel, "second", steps,
                   [rows_in(r["x2"]), rows_in(r["dx3"]), entire(r["gain"]), piece(r["slab_cross"], 0), piece(r["slab_self"], 3)] + [rows_in(d) for d in both("dqc")],
                   [wide_f32(), turned(), wide_low(), gain_out()], 2 * unit)
        return dict(zip(("dx2", "two_t", "do", "gain2"), out))

    def grads_cross():
        rights = both("dqc") + both("dkc") + both("dvc")
        n = len(SPANS)
        return {"cut_cross": weight_grads("grads_cross", [r["n2t"], r["et"]], (0,) * n + (1,) * (2 * n), rights, half, first_rows)}

    def grads_out():
        n = len(SPANS)
        return {"cut_out": weight_grads("grads_out", [r["three_t"], r["two_t"]], (0,) * n + (1,) * n, both("oc") + both("o"), half, first_rows)}

    def bwd_self(i):
        out = attn_bwd(SPANS[i], r["qkv"], 0, r["qkv"], 6, r["qkv"], 12, r["do"], r[f"o{i}"], r[f"p{i}"], True)
        return dict(zip((f"dq{i}", f"dk{i}", f"dv{i}", f"diag{i}"), out))

    def grads_self(i):
        return {f"cut_self{i}": weight_grads("grads_self", [r["n1t"]], (0, 0, 0), [r[f"dq{i}"], r[f"dk{i}"], r[f"dv{i}"]], half, first_rows)}

    def last():
        out = call(last_kernel, "last", steps,
                   [rows_in(r["x"]), rows_in(r["dx2"]), entire(r["gain"])] + [piece(r["slab_self"], c) for c in range(3)] + [piece(r["slab_cross"], c) for c in (1, 2)]
                   + [rows_in(d) for name in ("dq", "dk", "dv", "dkc", "dvc") for d in both(name)],
                   [wide_f32(), wide_f32(), gain_out()], 5 * unit)
        return dict(zip(("dx1", "de", "gain1"), out))

    def cut(pair, turn):
        return Scatter(sizes, pair[0], pair[1], first, turn)

    r.step(prepare, [g_self])
    r.step(None, [g_self, g_cross])
    r.step(None, [g_self, g_cross])
    while g_self.plan:
        r.step(None, [g_self])
    r.step(take_self, [])
    r.step(proj, [g_cross, g_ffn0])
    r.step(lambda: fwd_self(0), [g_cross, g_ffn0])
    r.step(lambda: fwd_self(1), [g_cross, g_ffn0, g_ffn1])
    while g_cross.plan:
        r.step(None, [g_cross])
    r.step(lambda: {"slab_cross": g_cross.whole()}, [])
    r.step(mid, [g_ffn0, g_ffn1])
    r.step(lambda: fwd_cross(0), [g_ffn0, g_ffn1])
    r.step(lambda: fwd_cross(1), [g_ffn0, g_ffn1])
    r.step(third, [g_ffn0, g_ffn1])
    while g_ffn0.plan or g_ffn1.plan:
        r.step(None, [g_ffn0, g_ffn1])
    r.step(lambda: {"slab_ffn0": g_ffn0.whole(), "slab_ffn1": g_ffn1.whole()}, [])
    r.moving = []
    r.step(lambda: ffn(0), [])
    split = r.live.pop("split0")
    f0 = [cut(split[2 * i: 2 * i + 2], i) for i in range(2)]
    r.step(lambda: ffn(1), f0)
    split = r.live.pop("split1")
    f1 = [cut(split[2 * i: 2 * i + 2], i) for i in range(2)]
    r.step(top, f0 + f1)
    r.step(lambda: bwd_cross(0), f0 + f1)
    r.step(lambda: bwd_cross(1), f0 + f1)
    r.step(second, f0 + f1)
    r.step(grads_cross, f1)
    sc = cut(r.live.pop("cut_cross"), 0)
    r.step(grads_out, [sc])
    so = cut(r.live.pop("cut_out"), 1)
    r.step(lambda: bwd_self(0), f1 + [sc, so])
    r.step(lambda: grads_self(0), f1 + [sc, so])
    s0 = cut(r.live.pop("cut_self0"), 1)
    r.step(lambda: bwd_self(1), f1 + [sc, so, s0])
    r.step(lambda: grads_self(1), f1 + [sc, so, s0])
    s1 = cut(r.live.pop("cut_self1"), 0)
    r.step(last, [sc, so, s0, s1])

    def small():
        diag = jnp.concatenate(both("diag"), axis=0)
        bias_rows = bucket_sums(diag, buckets, rel_bias.shape[0])
        return {"small": jnp.concatenate([r["gain1"][0], r["gain2"][0], r["gain3"][0], bias_rows.reshape(-1)]).reshape(-1, 128)}

    r.step(small, [sc, so, s0, s1])
    total = Total(sizes, r.live.pop("small"))
    movers = f0 + f1 + [sc, so, s0, s1, total]
    while any(m.plan for m in movers):
        r.step(None, movers)

    summed = total.value.reshape(-1)
    shard = me * narrow + lax.axis_index(NARROW)
    own = width // (wide * narrow)
    gain_sum = lax.dynamic_slice_in_dim(summed[: 3 * width].reshape(3, width), shard * own, own, 1)
    bias_sum = summed[3 * width:].reshape(rel_bias.shape)

    def columns(sums, index, count):
        found = []
        for s in sums:
            n = s.keep.shape[-1] // count
            found.append(s.keep[0, :, n * index: n * (index + 1)])
        return jnp.concatenate(found, axis=1) if len(found) > 1 else found[0]

    shaped = lambda v: v.reshape(micro, per, length, width)
    selfs = [s0, s1]
    return (
        shaped(r["layer"]),
        shaped(r["dx1"]),
        shaped(r["de"]),
        gain_sum,
        bias_sum,
        columns(selfs, 0, 3),
        jnp.stack([columns(selfs, 1, 3), columns(selfs, 2, 3)]),
        columns([so], 1, 2).T,
        columns([sc], 0, 3),
        jnp.stack([columns([sc], 1, 3), columns([sc], 2, 3)]),
        columns([so], 0, 2).T,
        jnp.concatenate([f0[0].keep[0], f1[0].keep[0]], axis=1),
        jnp.concatenate([f0[1].keep[0], f1[1].keep[0]], axis=1).T,
    )


def solution(mesh):
    axes = (WIDE, NARROW)
    batch4, batch3 = P(None, axes, None, None), P(None, axes, None)
    first, second, middle = P(axes, None), P(None, axes), P(None, axes, None)
    sizes = (mesh.shape[WIDE], mesh.shape[NARROW])
    weights = (first, middle, second, first, middle, second, first, second)
    return jax.shard_map(
        functools.partial(body, sizes),
        mesh=mesh,
        in_specs=(batch4, batch4, batch3, batch3, P(), second, P()) + weights + (batch4,),
        out_specs=(batch4, batch4, batch4, second, P()) + weights,
        check_vma=False,
    )
```

time: 716 us -> 574 us (0.80)
  Pallas kernels: 105 us -> 248 us
  matrix products: 113 us -> 0 us
  local copies, waits for them, and re-layouts: 176 us -> 63.8 us
  starting transfers between devices: 58.9 us -> 127 us
  waiting for transfers between devices: 168 us -> 108 us
  blocking collectives: 37.8 us -> 0 us
  other arithmetic: 45.2 us -> 18.3 us
    pallas_call x0 -> x16, Pallas kernels: none -> 141 us  [the longest x8 107 us: call(): pl.pallas_call(kernel, grid=grid, in_specs=[spec(b, i) for _, b, i in ins...]
    dynamic_update_slice x29 -> x0, local copies, waits for them, and re-layouts: 115 us -> none  [gather_rows(): whole = lax.dynamic_update_slice(whole, piece, ((me ^ offset) * rows, 0))]
    dot_general x27 -> x0, matrix products: 113 us -> none  [dot(): return lax.dot_general(a, b, dims, preferred_element_type=F32)]
    ppermute x56 -> x133, starting transfers between devices: 58.9 us -> 127 us  [the longest x24 39.2 us: go(): lax.ppermute(g[0], NARROW, flipped(self.narrow, k))]
    ppermute x56 -> x133, waiting for transfers between devices: 168 us -> 108 us  [the longest x24 43.9 us: go(): self.flight = [lax.ppermute(self.sends[0], WIDE, flipped(self.wide, step))]]
    psum x1 -> x0, blocking collectives: 37.8 us -> none  [body(): lax.psum(bucket_sums(diag, buckets, rel_bias.shape[0]), (WIDE, NARROW))]
    unnamed x155 -> x210, local copies, waits for them, and re-layouts: 27.2 us -> 51.2 us
    ppermute x7 -> x0, local copies, waits for them, and re-layouts: 15.9 us -> none  [gather_rows(): lax.ppermute(piece, WIDE, flipped(wide, bit))]
  transfers between devices with their start and end apart: 56 -> 133, of which waited for: 19 -> 37; matrix products, arithmetic and copies ran while one was open for 29% -> 3% of each run, Pallas kernels for 4% -> 36%
where the time goes in v2:
time: 574 us; the launch traced here: 568 us
  Pallas kernels  248 us (43%)
  starting transfers between devices  127 us (22%)
  waiting for transfers between devices  108 us (19%)
  local copies, waits for them, and re-layouts  63.8 us (11%)
  other arithmetic  18.3 us (3%)
    pallas_call x8, Pallas kernels, call(): pl.pallas_call(kernel, grid=grid, in_specs=[spec(b, i) for _, b, i in ins...  107 us
    pallas_call x4, Pallas kernels, attn_bwd(): pl.pallas_call(functools.partial(attn_bwd_kernel, causal), grid=(pairs, r...  59.7 us
    unnamed x210, local copies, waits for them, and re-layouts  51.2 us
    pallas_call x4, Pallas kernels, attn_fwd(): pl.pallas_call(functools.partial(attn_fwd_kernel, causal), grid=(pairs, r...  47.4 us
    ppermute x24, waiting for transfers between devices, go(): self.flight = [lax.ppermute(self.sends[0], WIDE, flipped(self.wide, step))]  43.9 us
    ppermute x24, starting transfers between devices, go(): lax.ppermute(g[0], NARROW, flipped(self.narrow, k))  39.2 us
    ppermute x24, starting transfers between devices, go(): lax.ppermute(s, NARROW, flipped(self.narrow, k + 1))  35.7 us
    ppermute x56, starting transfers between devices, go(): lax.ppermute(p, WIDE, flipped(self.wide, self.orders[i][step]))  29.4 us
  transfers between devices with their start and end apart: 133, of which 37 were waited for; matrix products, arithmetic and copies ran while one was open for 3% of the time, Pallas kernels for 36%

profile of v2, /device:TPU:0, one launch (start us, length us, event | category | flops | bytes accessed | tf_op | source)
XLA Modules:
  0.0 568.0 jit_solution(13841536644242383289)
XLA Ops:
  2.3 5.0 collective-permute-start.2
  9.5 3.8 collective-permute-start.5
  48.2 4.5 collective-permute-done.19.refs_9_
  53.2 7.0 %collective-permute-done.18.refs_1_ = bf16[96,1536]{1,0:T(8,128)(2,1)S(1)} collective-permute-done((bf16[96,1536]{1,0:T(8,128)(2,1)S(1)}, bf16[96,1536]{1,0:T(8,128)(2,1)S(1)}, u32[]{:S(2)}, u32[]{:S(2)}) %collective-permute-start.18) | collective-permute-done | bytes 294944 | tf_op jit(solution)/shard_map/ppermute | solution.py:271
  92.6 8.2 %proj_self.1 = (bf16[768,1024]{1,0:T(8,128)(2,1)}, bf16[1024,2304]{1,0:T(8,128)(2,1)}) custom-call(bf16[1024,768]{1,0:T(8,128)(2,1)} %bitcast.225, f32[3,768]{1,0:T(4,128)} %bitcast.239, bf16[768,3200]{1,0:T(8,128)(2,1)} %copy-done.1), custom_call_target="tpu_custom_call" | custom-call | flops 3623878656 | bytes 12788736 | tf_op jit(solution)/shard_map/proj_self/pallas_call | solution.py:460
  105.8 4.6 collective-permute-done.47.refs_9_
  115.2 11.4 %attn_fwd_self.2 = (bf16[1024,384]{1,0:T(8,128)(2,1)S(1)}, bf16[2,6,512,512]{3,2,1,0:T(8,128)(2,1)S(1)}) custom-call(bf16[1024,2304]{1,0:T(8,128)(2,1)S(1)} %copy-done.63, bf16[1024,2304]{1,0:T(8,128)(2,1)S(1)} %copy-done.63, bf16[1024,2304]{1,0:T(8,128)(2,1)S(1)} %copy-done.63, bf16[2,512,128]{2,1,0:T(8,128)(2,1)S(1)} %select_convert_fusion.qs_ref, ...), custom_call_target="tpu_custom_call" | custom-call | flops 6442450944 | bytes 6291456 | tf_op jit(solution)/shard_map/attn_fwd_self/pallas_call | solution.py:93
  140.6 3.6 collective-permute-done.53
  150.0 11.4 %attn_fwd_self.3 = (bf16[1024,384]{1,0:T(8,128)(2,1)S(1)}, bf16[2,6,512,512]{3,2,1,0:T(8,128)(2,1)S(1)}) custom-call(bf16[1024,2304]{1,0:T(8,128)(2,1)S(1)} %copy-done.63, bf16[1024,2304]{1,0:T(8,128)(2,1)S(1)} %copy-done.63, bf16[1024,2304]{1,0:T(8,128)(2,1)S(1)} %copy-done.63, bf16[2,512,128]{2,1,0:T(8,128)(2,1)S(1)} %copy-done.51, ...), custom_call_target="tpu_custom_call" | custom-call | flops 6442450944 | bytes 6291456 | tf_op jit(solution)/shard_map/attn_fwd_self/pallas_call | solution.py:93
  168.7 5.9 %collective-permute-done.67.refs_9_ = bf16[96,1536]{1,0:T(8,128)(2,1)} collective-permute-done((bf16[96,1536]{1,0:T(8,128)(2,1)S(1)}, bf16[96,1536]{1,0:T(8,128)(2,1)}, u32[]{:S(2)}, u32[]{:S(2)}) %collective-permute-start.67) | collective-permute-done | bytes 294944 | tf_op jit(solution)/shard_map/ppermute | solution.py:271
  176.5 12.1 %mid.1 = (f32[1024,768]{1,0:T(8,128)}, bf16[768,1024]{1,0:T(8,128)(2,1)}, bf16[1024,768]{1,0:T(8,128)(2,1)}, bf16[1024,1536]{1,0:T(8,128)(2,1)}, bf16[768,1024]{1,0:T(8,128)(2,1)}) custom-call(bf16[1024,768]{1,0:T(8,128)(2,1)} %bitcast.226, bf16[1024,768]{1,0:T(8,128)(2,1)} %bitcast.258, f32[3,768]{1,0:T(4,128)} %bitcast.240, bf16[768,3200]{1,0:T(8,128)(2,1)} %copy-done.1, ...), custom_call_target="tpu_custom_call" | custom-call | flops 4831838208 | bytes 25371648 | tf_op jit(solution)/shard_map/mid/pallas_call | solution.py:460
  199.0 12.2 %attn_fwd_cross.2 = (bf16[1024,384]{1,0:T(8,128)(2,1)S(1)}, bf16[2,6,512,512]{3,2,1,0:T(8,128)(2,1)S(1)}) custom-call(bf16[1024,768]{1,0:T(8,128)(2,1)S(1)} %copy-done.71, bf16[1024,1536]{1,0:T(8,128)(2,1)S(1)} %copy-done.68, bf16[1024,1536]{1,0:T(8,128)(2,1)S(1)} %copy-done.68, bf16[2,512,128]{2,1,0:T(8,128)(2,1)S(1)} %copy-done.52, ...), custom_call_target="tpu_custom_call" | custom-call | flops 6442450944 | bytes 6291456 | tf_op jit(solution)/shard_map/attn_fwd_cross/pallas_call | solution.py:93
  224.7 12.4 %attn_fwd_cross.3 = (bf16[1024,384]{1,0:T(8,128)(2,1)S(1)}, bf16[2,6,512,512]{3,2,1,0:T(8,128)(2,1)S(1)}) custom-call(bf16[1024,768]{1,0:T(8,128)(2,1)S(1)} %copy-done.72, bf16[1024,1536]{1,0:T(8,128)(2,1)S(1)} %copy-done.69, bf16[1024,1536]{1,0:T(8,128)(2,1)S(1)} %copy-done.69, bf16[2,512,128]{2,1,0:T(8,128)(2,1)S(1)} %copy-done.53, ...), custom_call_target="tpu_custom_call" | custom-call | flops 6442450944 | bytes 6291456 | tf_op jit(solution)/shard_map/attn_fwd_cross/pallas_call | solution.py:93
  240.6 8.3 %third.1 = (f32[1024,768]{1,0:T(8,128)}, bf16[1024,768]{1,0:T(8,128)(2,1)}, bf16[768,1024]{1,0:T(8,128)(2,1)}, bf16[768,1024]{1,0:T(8,128)(2,1)}) custom-call(f32[1024,768]{1,0:T(8,128)} %get-tuple-element.1853.x2_ref, bf16[1024,768]{1,0:T(8,128)(2,1)} %bitcast.209, f32[3,768]{1,0:T(4,128)} %bitcast.241, bf16[768,3072]{1,0:T(8,128)(2,1)} %copy-done, ...), custom_call_target="tpu_custom_call" | custom-call | flops 1207959552 | bytes 18883584 | tf_op jit(solution)/shard_map/third/pallas_call | solution.py:460
  255.7 20.9 %ffn.2 = (f32[1024,768]{1,0:T(8,128)}, f32[1024,768]{1,0:T(8,128)}, bf16[1,4,96,1536]{3,2,1,0:T(8,128)(2,1)}, bf16[1,4,96,1536]{3,2,1,0:T(8,128)(2,1)}, bf16[1,4...) custom-call(s32[1]{0:T(128)} %bitcast.me_ref, bf16[1024,768]{1,0:T(8,128)(2,1)} %get-tuple-element.1654.n_ref, ...), custom_call_target="tpu_custom_call" | custom-call | flops 14495514624 | bytes 26738692 | tf_op jit(solution)/shard_map/ffn/pallas_call | solution.py:460
  277.1 21.3 %ffn.3 = (f32[1024,768]{1,0:T(8,128)}, f32[1024,768]{1,0:T(8,128)}, bf16[1,4,96,1536]{3,2,1,0:T(8,128)(2,1)}, bf16[1,4,96,1536]{3,2,1,0:T(8,128)(2,1)}, bf16[1,4...) custom-call(s32[1]{0:T(128)} %bitcast.me_ref, bf16[1024,768]{1,0:T(8,128)(2,1)} %get-tuple-element.1654.n_ref, ...), custom_call_target="tpu_custom_call" | custom-call | flops 14495514624 | bytes 26738692 | tf_op jit(solution)/shard_map/ffn/pallas_call | solution.py:460
  303.6 11.0 %top.1 = (bf16[1024,768]{1,0:T(8,128)(2,1)}, f32[1024,768]{1,0:T(8,128)}, bf16[768,1024]{1,0:T(8,128)(2,1)}, bf16[1024,768]{1,0:T(8,128)(2,1)}, f32[8,768]{1,0:T(8,128)}) custom-call(f32[1024,768]{1,0:T(8,128)} %get-tuple-element.1699.ya_ref, f32[1024,768]{1,0:T(8,128)} %get-tuple-element.1700.yb_ref, f32[1024,768]{1,0:T(8,128)} %get-tuple-element.1697.da_ref, ...), custom_call_target="tpu_custom_call" | custom-call | flops 1207959552 | bytes 29918208 | tf_op jit(solution)/shard_map/top/pallas_call | solution.py:460
  327.1 13.5 %attn_bwd_cross.2 = (bf16[1024,384]{1,0:T(8,128)(2,1)S(1)}, bf16[1024,384]{1,0:T(8,128)(2,1)S(1)}, bf16[1024,384]{1,0:T(8,128)(2,1)S(1)}) custom-call(bf16[1024,768]{1,0:T(8,128)(2,1)S(1)} %copy-done.73, bf16[1024,1536]{1,0:T(8,128)(2,1)S(1)} %copy-done.70, bf16[1024,1536]{1,0:T(8,128)(2,1)S(1)} %copy-done.70, bf16[1024,768]{1,0:T(8,128)(2,1)S(1)} %copy-done.59, ...), custom_call_target="tpu_custom_call" | custom-call | flops 6442450944 | bytes 6291456 | tf_op jit(solution)/shard_map/attn_bwd_cross/pallas_call | solution.py:183
  357.3 13.7 %attn_bwd_cross.3 = (bf16[1024,384]{1,0:T(8,128)(2,1)S(1)}, bf16[1024,384]{1,0:T(8,128)(2,1)S(1)}, bf16[1024,384]{1,0:T(8,128)(2,1)S(1)}) custom-call(bf16[1024,768]{1,0:T(8,128)(2,1)S(1)} %copy-done.73, bf16[1024,1536]{1,0:T(8,128)(2,1)S(1)} %copy-done.70, bf16[1024,1536]{1,0:T(8,128)(2,1)S(1)} %copy-done.70, bf16[1024,768]{1,0:T(8,128)(2,1)S(1)} %copy-done.59, ...), custom_call_target="tpu_custom_call" | custom-call | flops 6442450944 | bytes 6291456 | tf_op jit(solution)/shard_map/attn_bwd_cross/pallas_call | solution.py:183
  381.0 10.0 %second.1 = (f32[1024,768]{1,0:T(8,128)}, bf16[768,1024]{1,0:T(8,128)(2,1)}, bf16[1024,768]{1,0:T(8,128)(2,1)}, f32[8,768]{1,0:T(8,128)}) custom-call(f32[1024,768]{1,0:T(8,128)} %get-tuple-element.1853.x2_ref, f32[1024,768]{1,0:T(8,128)} %get-tuple-element.1854.dx3_ref, f32[3,768]{1,0:T(4,128)} %bitcast.243, bf16[768,3072]{1,0:T(8,128)(2,1)} %copy-done, ...), custom_call_target="tpu_custom_call" | custom-call | flops 2415919104 | bytes 23823360 | tf_op jit(solution)/shard_map/second/pallas_call | solution.py:460
  392.5 9.9 %grads_cross.1 = (bf16[1,4,96,2304]{3,2,1,0:T(8,128)(2,1)}, bf16[1,4,96,2304]{3,2,1,0:T(8,128)(2,1)}) custom-call(s32[1]{0:T(128)} %bitcast.me_ref, bf16[768,1024]{1,0:T(8,128)(2,1)} %get-tuple-element.1892.refs_0_, bf16[768,1024]{1,0:T(8,128)(2,1)} %get-tuple-element.1893.refs_1_, bf16[1024,384]{1,0:T(8,128)(2,1)} %copy-done.4, ...), custom_call_target="tpu_custom_call" | custom-call | flops 3623878656 | bytes 9437184 | tf_op jit(solution)/shard_map/grads_cross/pallas_call | solution.py:643
  402.5 7.5 %grads_out.1 = (bf16[1,4,96,1536]{3,2,1,0:T(8,128)(2,1)}, bf16[1,4,96,1536]{3,2,1,0:T(8,128)(2,1)}) custom-call(s32[1]{0:T(128)} %bitcast.me_ref, bf16[768,1024]{1,0:T(8,128)(2,1)} %get-tuple-element.1931.refs_0_, bf16[768,1024]{1,0:T(8,128)(2,1)} %get-tuple-element.1932.refs_1_, bf16[1024,384]{1,0:T(8,128)(2,1)} %copy-done.6, bf16[1024,384]{1,0:T(8,128)(2,1)} %copy-done.8, ...), custom_call_target="tpu_custom_call" | custom-call | flops 2415919104 | bytes 6291456 | tf_op jit(solution)/shard_map/grads_out/pallas_call | solution.py:643
  413.9 16.4 %attn_bwd_self.2 = (bf16[1024,384]{1,0:T(8,128)(2,1)S(1)}, bf16[1024,384]{1,0:T(8,128)(2,1)S(1)}, bf16[1024,384]{1,0:T(8,128)(2,1)S(1)}, f32[6,4,256]{2,1,0:T(4,128)S(1)}) custom-call(bf16[1024,2304]{1,0:T(8,128)(2,1)S(1)} %bitcast.207, bf16[1024,2304]{1,0:T(8,128)(2,1)S(1)} %bitcast.207, bf16[1024,2304]{1,0:T(8,128)(2,1)S(1)} %bitcast.207, ...), custom_call_target="tpu_custom_call" | custom-call | flops 6442450944 | bytes 6291456 | tf_op jit(solution)/shard_map/attn_bwd_self/pallas_call | solution.py:183
  430.3 3.9 collective-permute-done.105
  438.5 5.8 %grads_self.2 = (bf16[1,4,96,1152]{3,2,1,0:T(8,128)(2,1)}, bf16[1,4,96,1152]{3,2,1,0:T(8,128)(2,1)}) custom-call(s32[1]{0:T(128)} %bitcast.me_ref, bf16[768,1024]{1,0:T(8,128)(2,1)} %get-tuple-element.2059.refs_0_, bf16[1024,384]{1,0:T(8,128)(2,1)} %copy-done.14, bf16[1024,384]{1,0:T(8,128)(2,1)} %copy-done.15, bf16[1024,384]{1,0:T(8,128)(2,1)} %copy-done.16), custom_call_target="tpu_custom_call" | custom-call | flops 1811939328 | bytes 4718592 | tf_op jit(solution)/shard_map/grads_self/pallas_call | solution.py:643
  444.4 15.4 %collective-permute-done.107 = bf16[1,96,2304]{2,1,0:T(8,128)(2,1)} collective-permute-done((bf16[1,96,2304]{2,1,0:T(8,128)(2,1)}, bf16[1,96,2304]{2,1,0:T(8,128)(2,1)}, u32[]{:S(2)}, u32[]{:S(2)}) %collective-permute-start.107) | collective-permute-done | bytes 442400 | tf_op jit(solution)/shard_map/ppermute | solution.py:347
  466.5 16.2 %attn_bwd_self.3 = (bf16[1024,384]{1,0:T(8,128)(2,1)S(1)}, bf16[1024,384]{1,0:T(8,128)(2,1)S(1)}, bf16[1024,384]{1,0:T(8,128)(2,1)S(1)}, f32[6,4,256]{2,1,0:T(4,128)S(1)}) custom-call(bf16[1024,2304]{1,0:T(8,128)(2,1)S(1)} %bitcast.207, bf16[1024,2304]{1,0:T(8,128)(2,1)S(1)} %bitcast.207, bf16[1024,2304]{1,0:T(8,128)(2,1)S(1)} %bitcast.207, ...), custom_call_target="tpu_custom_call" | custom-call | flops 6442450944 | bytes 6291456 | tf_op jit(solution)/shard_map/attn_bwd_self/pallas_call | solution.py:183
  489.3 5.8 %grads_self.3 = (bf16[1,4,96,1152]{3,2,1,0:T(8,128)(2,1)}, bf16[1,4,96,1152]{3,2,1,0:T(8,128)(2,1)}) custom-call(s32[1]{0:T(128)} %bitcast.me_ref, bf16[768,1024]{1,0:T(8,128)(2,1)} %get-tuple-element.2059.refs_0_, bf16[1024,384]{1,0:T(8,128)(2,1)} %copy-done.17, bf16[1024,384]{1,0:T(8,128)(2,1)} %copy-done.18, bf16[1024,384]{1,0:T(8,128)(2,1)} %copy-done.19), custom_call_target="tpu_custom_call" | custom-call | flops 1811939328 | bytes 4718592 | tf_op jit(solution)/shard_map/grads_self/pallas_call | solution.py:643
  495.2 4.0 collective-permute-done.117
  500.7 15.0 %last.1 = (f32[1024,768]{1,0:T(8,128)}, f32[1024,768]{1,0:T(8,128)}, f32[8,768]{1,0:T(8,128)}) custom-call(bf16[1024,768]{1,0:T(8,128)(2,1)} %bitcast.227, f32[1024,768]{1,0:T(8,128)} %get-tuple-element.2095.dx2_ref, f32[3,768]{1,0:T(4,128)} %bitcast.244, bf16[768,3200]{1,0:T(8,128)(2,1)} %copy-done.1, bf16[768,3200]{1,0:T(8,128)(2,1)} %copy-done.1, ...), custom_call_target="tpu_custom_call" | custom-call | flops 6039797760 | bytes 43090944 | tf_op jit(solution)/shard_map/last/pallas_call | solution.py:460
  525.0 8.0 %collective-permute-done.123 = bf16[2,96,1152]{2,1,0:T(8,128)(2,1)S(1)} collective-permute-done((bf16[2,96,1152]{2,1,0:T(8,128)(2,1)S(1)}, bf16[2,96,1152]{2,1,0:T(8,128)(2,1)S(1)}, u32[]{:S(2)}, u32[]{:S(2)}) %collective-permute-start.123) | collective-permute-done | bytes 442400 | tf_op jit(solution)/shard_map/ppermute | solution.py:347
  534.8 6.3 %collective-permute-done.124 = bf16[1,96,1152]{2,1,0:T(8,128)(2,1)S(1)} collective-permute-done((bf16[1,96,1152]{2,1,0:T(8,128)(2,1)S(1)}, bf16[1,96,1152]{2,1,0:T(8,128)(2,1)S(1)}, u32[]{:S(2)}, u32[]{:S(2)}) %collective-permute-start.124) | collective-permute-done | bytes 221216 | tf_op jit(solution)/shard_map/ppermute | solution.py:347
  (585 shorter events, 250.1 us)
Async XLA Ops:
  23.2 20.1 %collective-permute-start.7 = (bf16[96,1664]{1,0:T(8,128)(2,1)S(1)}, bf16[96,1664]{1,0:T(8,128)(2,1)S(1)}, u32[]{:S(2)}, u32[]{:S(2)}) collective-permute-start(bf16[96,1664]{1,0:T(8,128)(2,1)S(1)} %pad_maximum_fusion.refs_8_), channel_id=1, source_target_pairs={{0,16},{4,20},{8,24},{12,28},{16,0},{20,4},{24,8},{28,12},{1,17},{... | collective-permute-start | bytes 958472 | tf_op jit(solution)/shard_map/ppermute | solution.py:271
  24.8 18.5 %collective-permute-start.6 = (bf16[96,1536]{1,0:T(8,128)(2,1)S(1)}, bf16[96,1536]{1,0:T(8,128)(2,1)S(1)}, u32[]{:S(2)}, u32[]{:S(2)}) collective-permute-start(bf16[96,1536]{1,0:T(8,128)(2,1)S(1)} %pad_maximum_fusion.1.refs_0_), channel_id=1, source_target_pairs={{0,8},{4,12},{8,0},{12,4},{16,24},{20,28},{24,16},{28,20},{1,9},{5... | collective-permute-start | bytes 884744 | tf_op jit(solution)/shard_map/ppermute | solution.py:271
  110.4 19.7 %collective-permute-start.41 = (bf16[96,1536]{1,0:T(8,128)(2,1)S(1)}, bf16[96,1536]{1,0:T(8,128)(2,1)S(1)}, u32[]{:S(2)}, u32[]{:S(2)}) collective-permute-start(bf16[96,1536]{1,0:T(8,128)(2,1)S(1)} %collective-permute-done.29.refs_3_), channel_id=1, source_target_pairs={{0,4},{4,0},{8,12},{12,8},{16,20},{20,16},{24,28},{28,24},{1,5},{5... | collective-permute-start | bytes 884744 | tf_op jit(solution)/shard_map/ppermute | solution.py:271
  111.8 18.3 %collective-permute-start.42 = (bf16[96,1536]{1,0:T(8,128)(2,1)S(1)}, bf16[96,1536]{1,0:T(8,128)(2,1)S(1)}, u32[]{:S(2)}, u32[]{:S(2)}) collective-permute-start(bf16[96,1536]{1,0:T(8,128)(2,1)S(1)} %pad_maximum_fusion.3.refs_8_), channel_id=1, source_target_pairs={{0,4},{4,0},{8,12},{12,8},{16,20},{20,16},{24,28},{28,24},{1,5},{5... | collective-permute-start | bytes 884744 | tf_op jit(solution)/shard_map/ppermute | solution.py:271
  111.8 18.3 %collective-permute-start.43 = (bf16[96,1536]{1,0:T(8,128)(2,1)}, bf16[96,1536]{1,0:T(8,128)(2,1)S(1)}, u32[]{:S(2)}, u32[]{:S(2)}) collective-permute-start(bf16[96,1536]{1,0:T(8,128)(2,1)} %collective-permute-done.19.refs_9_), channel_id=1, source_target_pairs={{0,4},{4,0},{8,12},{12,8},{16,20},{20,16},{24,28},{28,24},{1,5},{5... | collective-permute-start | bytes 884744 | tf_op jit(solution)/shard_map/ppermute | solution.py:271
  112.3 17.8 %collective-permute-start.44 = (bf16[96,1536]{1,0:T(8,128)(2,1)S(1)}, bf16[96,1536]{1,0:T(8,128)(2,1)S(1)}, u32[]{:S(2)}, u32[]{:S(2)}) collective-permute-start(bf16[96,1536]{1,0:T(8,128)(2,1)S(1)} %collective-permute-done.30.refs_10_), channel_id=1, source_target_pairs={{0,4},{4,0},{8,12},{12,8},{16,20},{20,16},{24,28},{28,24},{1,5},{5... | collective-permute-start | bytes 884744 | tf_op jit(solution)/shard_map/ppermute | solution.py:271
  139.2 22.2 %collective-permute-start.55 = (bf16[24,1536]{1,0:T(8,128)(2,1)S(1)}, bf16[24,1536]{1,0:T(8,128)(2,1)S(1)}, u32[]{:S(2)}, u32[]{:S(2)}) collective-permute-start(bf16[24,1536]{1,0:T(8,128)(2,1)S(1)} %copy-done.88), channel_id=1, source_target_pairs={{0,1},{1,0},{2,3},{3,2},{4,5},{5,4},{6,7},{7,6},{8,9},{9,8},{10,11... | collective-permute-start | bytes 221192 | tf_op jit(solution)/shard_map/ppermute | solution.py:267
  191.6 23.1 %collective-permute-start.71 = (bf16[96,1536]{1,0:T(8,128)(2,1)}, bf16[96,1536]{1,0:T(8,128)(2,1)}, u32[]{:S(2)}, u32[]{:S(2)}) collective-permute-start(bf16[96,1536]{1,0:T(8,128)(2,1)} %collective-permute-done.67.refs_9_), channel_id=1, source_target_pairs={{0,8},{4,12},{8,0},{12,4},{16,24},{20,28},{24,16},{28,20},{1,9},{5... | collective-permute-start | bytes 884744 | tf_op jit(solution)/shard_map/ppermute | solution.py:271
  192.4 22.3 %collective-permute-start.70 = (bf16[96,1536]{1,0:T(8,128)(2,1)S(1)}, bf16[96,1536]{1,0:T(8,128)(2,1)}, u32[]{:S(2)}, u32[]{:S(2)}) collective-permute-start(bf16[96,1536]{1,0:T(8,128)(2,1)S(1)} %pad_maximum_fusion.7.refs_8_), channel_id=1, source_target_pairs={{0,8},{4,12},{8,0},{12,4},{16,24},{20,28},{24,16},{28,20},{1,9},{5... | collective-permute-start | bytes 884744 | tf_op jit(solution)/shard_map/ppermute | solution.py:271
  193.7 21.1 %collective-permute-start.69 = (bf16[96,1536]{1,0:T(8,128)(2,1)S(1)}, bf16[96,1536]{1,0:T(8,128)(2,1)S(1)}, u32[]{:S(2)}, u32[]{:S(2)}) collective-permute-start(bf16[96,1536]{1,0:T(8,128)(2,1)S(1)} %collective-permute-done.66.refs_1_), channel_id=1, source_target_pairs={{0,16},{4,20},{8,24},{12,28},{16,0},{20,4},{24,8},{28,12},{1,17},{... | collective-permute-start | bytes 884744 | tf_op jit(solution)/shard_map/ppermute | solution.py:271
  195.1 19.6 %collective-permute-start.68 = (bf16[96,1536]{1,0:T(8,128)(2,1)S(1)}, bf16[96,1536]{1,0:T(8,128)(2,1)S(1)}, u32[]{:S(2)}, u32[]{:S(2)}) collective-permute-start(bf16[96,1536]{1,0:T(8,128)(2,1)S(1)} %pad_maximum_fusion.6.refs_0_), channel_id=1, source_target_pairs={{0,16},{4,20},{8,24},{12,28},{16,0},{20,4},{24,8},{28,12},{1,17},{... | collective-permute-start | bytes 884744 | tf_op jit(solution)/shard_map/ppermute | solution.py:271
  216.7 23.9 %collective-permute-start.76 = (bf16[96,1536]{1,0:T(8,128)(2,1)S(1)}, bf16[96,1536]{1,0:T(8,128)(2,1)S(1)}, u32[]{:S(2)}, u32[]{:S(2)}) collective-permute-start(bf16[96,1536]{1,0:T(8,128)(2,1)S(1)} %pad_maximum_fusion.7.refs_8_), channel_id=1, source_target_pairs={{0,4},{4,0},{8,12},{12,8},{16,20},{20,16},{24,28},{28,24},{1,5},{5... | collective-permute-start | bytes 884744 | tf_op jit(solution)/shard_map/ppermute | solution.py:271
  217.2 23.4 %collective-permute-start.72 = (bf16[96,1536]{1,0:T(8,128)(2,1)S(1)}, bf16[96,1536]{1,0:T(8,128)(2,1)S(1)}, u32[]{:S(2)}, u32[]{:S(2)}) collective-permute-start(bf16[96,1536]{1,0:T(8,128)(2,1)S(1)} %pad_maximum_fusion.6.refs_0_), channel_id=1, source_target_pairs={{0,4},{4,0},{8,12},{12,8},{16,20},{20,16},{24,28},{28,24},{1,5},{5... | collective-permute-start | bytes 884744 | tf_op jit(solution)/shard_map/ppermute | solution.py:271
  218.1 22.5 %collective-permute-start.73 = (bf16[96,1536]{1,0:T(8,128)(2,1)S(1)}, bf16[96,1536]{1,0:T(8,128)(2,1)S(1)}, u32[]{:S(2)}, u32[]{:S(2)}) collective-permute-start(bf16[96,1536]{1,0:T(8,128)(2,1)S(1)} %collective-permute-done.66.refs_1_), channel_id=1, source_target_pairs={{0,4},{4,0},{8,12},{12,8},{16,20},{20,16},{24,28},{28,24},{1,5},{5... | collective-permute-start | bytes 884744 | tf_op jit(solution)/shard_map/ppermute | solution.py:271
  218.5 22.1 %collective-permute-start.74 = (bf16[96,1536]{1,0:T(8,128)(2,1)}, bf16[96,1536]{1,0:T(8,128)(2,1)S(1)}, u32[]{:S(2)}, u32[]{:S(2)}) collective-permute-start(bf16[96,1536]{1,0:T(8,128)(2,1)} %copy-done.38), channel_id=1, source_target_pairs={{0,4},{4,0},{8,12},{12,8},{16,20},{20,16},{24,28},{28,24},{1,5},{5... | collective-permute-start | bytes 884744 | tf_op jit(solution)/shard_map/ppermute | solution.py:271
  219.3 21.2 %collective-permute-start.75 = (bf16[96,1536]{1,0:T(8,128)(2,1)}, bf16[96,1536]{1,0:T(8,128)(2,1)S(1)}, u32[]{:S(2)}, u32[]{:S(2)}) collective-permute-start(bf16[96,1536]{1,0:T(8,128)(2,1)} %copy-done.36), channel_id=1, source_target_pairs={{0,4},{4,0},{8,12},{12,8},{16,20},{20,16},{24,28},{28,24},{1,5},{5... | collective-permute-start | bytes 884744 | tf_op jit(solution)/shard_map/ppermute | solution.py:271
  276.6 21.8 %collective-permute-start.81 = (bf16[1,4,96,1536]{3,2,1,0:T(8,128)(2,1)}, bf16[1,4,96,1536]{3,2,1,0:T(8,128)(2,1)S(1)}, u32[]{:S(2)}, u32[]{:S(2)}) collective-permute-start(bf16[1,4,96,1536]{3,2,1,0:T(8,128)(2,1)} %get-tuple-element.1694), channel_id=1, source_target_pairs={{0,4},{4,0},{8,12},{12,8},{16,20},{20,16},{24,28},{28,24},{1,5},{5... | collective-permute-start | bytes 3538952 | tf_op jit(solution)/shard_map/ppermute | solution.py:347
  277.0 21.4 %collective-permute-start.80 = (bf16[1,4,96,1536]{3,2,1,0:T(8,128)(2,1)}, bf16[1,4,96,1536]{3,2,1,0:T(8,128)(2,1)S(1)}, u32[]{:S(2)}, u32[]{:S(2)}) collective-permute-start(bf16[1,4,96,1536]{3,2,1,0:T(8,128)(2,1)} %get-tuple-element.1692), channel_id=1, source_target_pairs={{0,4},{4,0},{8,12},{12,8},{16,20},{20,16},{24,28},{28,24},{1,5},{5... | collective-permute-start | bytes 3538952 | tf_op jit(solution)/shard_map/ppermute | solution.py:347
  320.1 20.5 %collective-permute-start.87 = (bf16[1,96,1536]{2,1,0:T(8,128)(2,1)S(1)}, bf16[1,96,1536]{2,1,0:T(8,128)(2,1)S(1)}, u32[]{:S(2)}, u32[]{:S(2)}) collective-permute-start(bf16[1,96,1536]{2,1,0:T(8,128)(2,1)S(1)} %get-tuple-element.2296), channel_id=1, source_target_pairs={{0,8},{4,12},{8,0},{12,4},{16,24},{20,28},{24,16},{28,20},{1,9},{5... | collective-permute-start | bytes 884744 | tf_op jit(solution)/shard_map/ppermute | solution.py:347
  322.4 18.3 %collective-permute-start.86 = (bf16[1,96,1536]{2,1,0:T(8,128)(2,1)S(1)}, bf16[1,96,1536]{2,1,0:T(8,128)(2,1)S(1)}, u32[]{:S(2)}, u32[]{:S(2)}) collective-permute-start(bf16[1,96,1536]{2,1,0:T(8,128)(2,1)S(1)} %get-tuple-element.2298), channel_id=1, source_target_pairs={{0,16},{4,20},{8,24},{12,28},{16,0},{20,4},{24,8},{28,12},{1,17},{... | collective-permute-start | bytes 884744 | tf_op jit(solution)/shard_map/ppermute | solution.py:347
  323.0 20.0 %collective-permute-start.89 = (bf16[1,192,1536]{2,1,0:T(8,128)(2,1)S(1)}, bf16[1,192,1536]{2,1,0:T(8,128)(2,1)S(1)}, u32[]{:S(2)}, u32[]{:S(2)}) collective-permute-start(bf16[1,192,1536]{2,1,0:T(8,128)(2,1)S(1)} %get-tuple-element.2276), channel_id=1, source_target_pairs={{0,16},{4,20},{8,24},{12,28},{16,0},{20,4},{24,8},{28,12},{1,17},{... | collective-permute-start | bytes 1769480 | tf_op jit(solution)/shard_map/ppermute | solution.py:347
  324.9 18.1 %collective-permute-start.88 = (bf16[2,96,1536]{2,1,0:T(8,128)(2,1)S(1)}, bf16[2,96,1536]{2,1,0:T(8,128)(2,1)S(1)}, u32[]{:S(2)}, u32[]{:S(2)}) collective-permute-start(bf16[2,96,1536]{2,1,0:T(8,128)(2,1)S(1)} %get-tuple-element.2278), channel_id=1, source_target_pairs={{0,8},{4,12},{8,0},{12,4},{16,24},{20,28},{24,16},{28,20},{1,9},{5... | collective-permute-start | bytes 1769480 | tf_op jit(solution)/shard_map/ppermute | solution.py:347
  347.9 23.2 %collective-permute-start.92 = (bf16[1,24,1536]{2,1,0:T(8,128)(2,1)S(1)}, bf16[1,24,1536]{2,1,0:T(8,128)(2,1)S(1)}, u32[]{:S(2)}, u32[]{:S(2)}) collective-permute-start(bf16[1,24,1536]{2,1,0:T(8,128)(2,1)S(1)} %get-tuple-element.2328), channel_id=1, source_target_pairs={{0,3},{1,2},{2,1},{3,0},{4,7},{5,6},{6,5},{7,4},{8,11},{9,10},{10,... | collective-permute-start | bytes 221192 | tf_op jit(solution)/shard_map/ppermute | solution.py:345
  350.4 20.6 %collective-permute-start.91 = (bf16[1,24,1536]{2,1,0:T(8,128)(2,1)S(1)}, bf16[1,24,1536]{2,1,0:T(8,128)(2,1)S(1)}, u32[]{:S(2)}, u32[]{:S(2)}) collective-permute-start(bf16[1,24,1536]{2,1,0:T(8,128)(2,1)S(1)} %get-tuple-element.2329), channel_id=1, source_target_pairs={{0,2},{1,3},{2,0},{3,1},{4,6},{5,7},{6,4},{7,5},{8,10},{9,11},{10,... | collective-permute-start | bytes 221192 | tf_op jit(solution)/shard_map/ppermute | solution.py:345
  350.6 20.4 %collective-permute-start.90 = (bf16[1,24,1536]{2,1,0:T(8,128)(2,1)S(1)}, bf16[1,24,1536]{2,1,0:T(8,128)(2,1)S(1)}, u32[]{:S(2)}, u32[]{:S(2)}) collective-permute-start(bf16[1,24,1536]{2,1,0:T(8,128)(2,1)S(1)} %get-tuple-element.2330), channel_id=1, source_target_pairs={{0,1},{1,0},{2,3},{3,2},{4,5},{5,4},{6,7},{7,6},{8,9},{9,8},{10,11... | collective-permute-start | bytes 221192 | tf_op jit(solution)/shard_map/ppermute | solution.py:345
  410.0 24.2 %collective-permute-start.106 = (bf16[1,4,96,1536]{3,2,1,0:T(8,128)(2,1)}, bf16[1,4,96,1536]{3,2,1,0:T(8,128)(2,1)S(1)}, u32[]{:S(2)}, u32[]{:S(2)}) collective-permute-start(bf16[1,4,96,1536]{3,2,1,0:T(8,128)(2,1)} %get-tuple-element.1992), channel_id=1, source_target_pairs={{0,4},{4,0},{8,12},{12,8},{16,20},{20,16},{24,28},{28,24},{1,5},{5... | collective-permute-start | bytes 3538952 | tf_op jit(solution)/shard_map/ppermute | solution.py:347
  412.4 21.8 %collective-permute-start.105 = (bf16[2,96,2304]{2,1,0:T(8,128)(2,1)S(1)}, bf16[2,96,2304]{2,1,0:T(8,128)(2,1)S(1)}, u32[]{:S(2)}, u32[]{:S(2)}) collective-permute-start(bf16[2,96,2304]{2,1,0:T(8,128)(2,1)S(1)} %get-tuple-element.2272), channel_id=1, source_target_pairs={{0,8},{4,12},{8,0},{12,4},{16,24},{20,28},{24,16},{28,20},{1,9},{5... | collective-permute-start | bytes 2654216 | tf_op jit(solution)/shard_map/ppermute | solution.py:347
  435.5 24.4 %collective-permute-start.108 = (bf16[1,192,1536]{2,1,0:T(8,128)(2,1)}, bf16[1,192,1536]{2,1,0:T(8,128)(2,1)S(1)}, u32[]{:S(2)}, u32[]{:S(2)}) collective-permute-start(bf16[1,192,1536]{2,1,0:T(8,128)(2,1)} %get-tuple-element.2274), channel_id=1, source_target_pairs={{0,16},{4,20},{8,24},{12,28},{16,0},{20,4},{24,8},{28,12},{1,17},{... | collective-permute-start | bytes 1769480 | tf_op jit(solution)/shard_map/ppermute | solution.py:347
  438.0 21.8 %collective-permute-start.107 = (bf16[1,96,2304]{2,1,0:T(8,128)(2,1)}, bf16[1,96,2304]{2,1,0:T(8,128)(2,1)}, u32[]{:S(2)}, u32[]{:S(2)}) collective-permute-start(bf16[1,96,2304]{2,1,0:T(8,128)(2,1)} %get-tuple-element.2288), channel_id=1, source_target_pairs={{0,16},{4,20},{8,24},{12,28},{16,0},{20,4},{24,8},{28,12},{1,17},{... | collective-permute-start | bytes 1327112 | tf_op jit(solution)/shard_map/ppermute | solution.py:347
  461.0 21.7 %collective-permute-start.111 = (bf16[1,24,2304]{2,1,0:T(8,128)(2,1)S(1)}, bf16[1,24,2304]{2,1,0:T(8,128)(2,1)S(1)}, u32[]{:S(2)}, u32[]{:S(2)}) collective-permute-start(bf16[1,24,2304]{2,1,0:T(8,128)(2,1)S(1)} %get-tuple-element.2304), channel_id=1, source_target_pairs={{0,3},{1,2},{2,1},{3,0},{4,7},{5,6},{6,5},{7,4},{8,11},{9,10},{10,... | collective-permute-start | bytes 331784 | tf_op jit(solution)/shard_map/ppermute | solution.py:345
  463.4 19.4 %collective-permute-start.110 = (bf16[1,24,2304]{2,1,0:T(8,128)(2,1)S(1)}, bf16[1,24,2304]{2,1,0:T(8,128)(2,1)S(1)}, u32[]{:S(2)}, u32[]{:S(2)}) collective-permute-start(bf16[1,24,2304]{2,1,0:T(8,128)(2,1)S(1)} %get-tuple-element.2305), channel_id=1, source_target_pairs={{0,2},{1,3},{2,0},{3,1},{4,6},{5,7},{6,4},{7,5},{8,10},{9,11},{10,... | collective-permute-start | bytes 331784 | tf_op jit(solution)/shard_map/ppermute | solution.py:345
  463.4 19.4 %collective-permute-start.109 = (bf16[1,24,2304]{2,1,0:T(8,128)(2,1)S(1)}, bf16[1,24,2304]{2,1,0:T(8,128)(2,1)S(1)}, u32[]{:S(2)}, u32[]{:S(2)}) collective-permute-start(bf16[1,24,2304]{2,1,0:T(8,128)(2,1)S(1)} %get-tuple-element.2306), channel_id=1, source_target_pairs={{0,1},{1,0},{2,3},{3,2},{4,5},{5,4},{6,7},{7,6},{8,9},{9,8},{10,11... | collective-permute-start | bytes 331784 | tf_op jit(solution)/shard_map/ppermute | solution.py:345
  (202 other events, 1879.9 us)

commit v3 on v2

--- a/solution.py
+++ b/solution.py
@@ -97,7 +97,7 @@
         out_specs=[pl.BlockSpec((length, 128), lambda h, b: (b, h)), pl.BlockSpec((None, 2, length, length), lambda h, b: (b, h, 0, 0))],
         out_shape=[jax.ShapeDtypeStruct((rows * length, pairs * 128), BF), jax.ShapeDtypeStruct((rows, 2 * pairs, length, length), BF)],
         scratch_shapes=scratch,
-        compiler_params=pltpu.CompilerParams(vmem_limit_bytes=32 * MB),
+        compiler_params=pltpu.CompilerParams(vmem_limit_bytes=60 * MB),
         cost_estimate=pl.CostEstimate(flops=16 * rows * pairs * length * length * 256, bytes_accessed=4 * rows * pairs * length * length, transcendentals=0),
         name="attn_fwd_self" if causal else "attn_fwd_cross",
     )(*args)
@@ -187,7 +187,7 @@
         out_specs=out_specs,
         out_shape=out_shape,
         scratch_shapes=scratch,
-        compiler_params=pltpu.CompilerParams(vmem_limit_bytes=40 * MB),
+        compiler_params=pltpu.CompilerParams(vmem_limit_bytes=60 * MB),
         cost_estimate=pl.CostEstimate(flops=16 * rows * pairs * length * length * 256, bytes_accessed=4 * rows * pairs * length * length, transcendentals=0),
         name="attn_bwd_self" if causal else "attn_bwd_cross",
     )(q_arr, k_arr, v_arr, grad, out, probs)
@@ -212,7 +212,7 @@
 ROOT_HALF = 0.7071067811865476
 INV_ROOT_TWO_PI = 0.3989422804014327
 WIDE, NARROW = "wide", "narrow"
-VMEM_LIMIT = 56 * MB
+VMEM_LIMIT = 60 * MB
 
 
 def flipped(size, bit):
@@ -252,13 +252,14 @@
 
 
 class Gather:
-    def __init__(self, sizes, blocks):
+    def __init__(self, sizes, block, cuts):
         self.wide, self.narrow = sizes
-        self.groups = [[b] for b in blocks]
+        self.cuts = cuts
+        self.groups = [[block]]
         self.flight = None
-        rows = blocks[0].shape[0] * self.narrow
+        rows = block.shape[0] * self.narrow
         self.low = low_bits(self.wide, rows)
-        self.orders = [cross_bits(self.wide, rows, i) for i in range(len(blocks))]
+        self.orders = [cross_bits(self.wide, rows, i) for i in range(len(cuts))]
         self.plan = ["narrow"] + [("low", b) for b in self.low] + list(range(len(self.orders[0])))
 
     def go(self):
@@ -272,14 +273,19 @@
 
     def land(self):
         step = self.plan.pop(0)
+        joined = lambda at: [[merge(g + f, at)] for g, f in zip(self.groups, self.flight)]
         if step == "narrow":
-            at = lax.axis_index(NARROW)
-            self.groups = [[merge(g + f, at)] for g, f in zip(self.groups, self.flight)]
+            self.groups = joined(lax.axis_index(NARROW))
         elif isinstance(step, tuple):
-            at = (lax.axis_index(WIDE) // step[1]) % 2
-            self.groups = [[merge(g + f, at)] for g, f in zip(self.groups, self.flight)]
+            self.groups = joined((lax.axis_index(WIDE) // step[1]) % 2)
         else:
             self.groups = [g + f for g, f in zip(self.groups, self.flight)]
+            if step == 0:
+                self.groups = [[jnp.concatenate(g, axis=0)] for g in self.groups]
+        if self.plan and self.plan[0] == 0:
+            block = self.groups[0][0]
+            ends = [sum(self.cuts[:i]) for i in range(len(self.cuts) + 1)]
+            self.groups = [[block[:, ends[i]: ends[i + 1]]] for i in range(len(self.cuts))]
         self.flight = None
 
     def state(self, landing):
@@ -302,27 +308,30 @@
         return assemble(self.groups, offsets, place)
 
 
-def assemble_kernel(offsets, columns, me_ref, *refs):
-    pieces, out = refs[:-1], refs[-1]
+def assemble_kernel(offsets, columns, counts, me_ref, *refs):
+    pieces, out = list(refs[:-1]), refs[-1]
     for g in range(len(columns)):
-        for i, offset in enumerate(offsets[g]):
-            piece = pieces[g * len(offsets[g]) + i]
-            rows, width = piece.shape
-            start = pl.multiple_of((me_ref[0] ^ offset) * rows, 16)
-            out[pl.ds(start, rows), columns[g]: columns[g] + width] = piece[...]
+        found = iter(offsets[g])
+        for _ in range(counts[g]):
+            piece = pieces.pop(0)
+            width = piece.shape[1]
+            rows = out.shape[0] // len(offsets[g])
+            for k in range(piece.shape[0] // rows):
+                start = pl.multiple_of((me_ref[0] ^ next(found)) * rows, 16)
+                out[pl.ds(start, rows), columns[g]: columns[g] + width] = piece[rows * k: rows * (k + 1), :]
 
 
 def assemble(groups, offsets, place):
     widths = [g[0].shape[1] for g in groups]
     columns = [sum(widths[:i]) for i in range(len(groups))]
     flat = [p for g in groups for p in g]
-    rows = groups[0][0].shape[0] * len(groups[0])
+    rows = sum(p.shape[0] for p in groups[0])
     return pl.pallas_call(
-        functools.partial(assemble_kernel, offsets, columns),
+        functools.partial(assemble_kernel, offsets, columns, [len(g) for g in groups]),
         in_specs=[pl.BlockSpec(memory_space=pltpu.SMEM)] + [pl.BlockSpec(memory_space=pltpu.VMEM)] * len(flat),
         out_specs=pl.BlockSpec(memory_space=pltpu.VMEM),
         out_shape=jax.ShapeDtypeStruct((rows, sum(widths)), BF),
-        compiler_params=pltpu.CompilerParams(vmem_limit_bytes=24 * MB),
+        compiler_params=pltpu.CompilerParams(vmem_limit_bytes=VMEM_LIMIT),
         cost_estimate=pl.CostEstimate(flops=0, bytes_accessed=4 * rows * sum(widths), transcendentals=0),
         name="assemble",
     )(place, *flat)
@@ -383,15 +392,29 @@
     def __init__(self, sizes, value):
         self.value = value
         self.flight = None
-        self.plan = [(name, size, bit) for name, size in zip((WIDE, NARROW), sizes) for bit in bits_of(size)]
+        self.narrow = sizes[1]
+        self.plan = [(sizes[0], bit) for bit in bits_of(sizes[0])] + ["narrow"]
 
     def go(self):
-        name, size, bit = self.plan[0]
-        self.flight = lax.ppermute(self.value, name, flipped(size, bit))
+        if self.plan[0] == "narrow":
+            self.flight = [lax.ppermute(self.value, NARROW, flipped(self.narrow, k)) for k in range(1, self.narrow)]
+        else:
+            self.flight = [lax.ppermute(self.value, WIDE, flipped(*self.plan[0]))]
 
     def land(self):
-        self.plan.pop(0)
-        self.value, self.flight = self.value + self.flight, None
+        if self.plan.pop(0) == "narrow":
+            at = lax.axis_index(NARROW)
+            parts = [self.value] + self.flight
+            total = None
+            for j in range(self.narrow):
+                term = parts[0]
+                for k in range(1, self.narrow):
+                    term = jnp.where((at ^ k) == j, parts[k], term)
+                total = term if total is None else total + term
+            self.value = total
+        else:
+            self.value = self.value + self.flight[0]
+        self.flight = None
 
     def state(self, landing):
         return (self.value, self.flight if landing else None)
@@ -519,12 +542,11 @@
     gt_ref[...] = g_ref[...].T
 
 
-def ffn_kernel(first_rows, me_ref, n_ref, nt_ref, g_ref, gt_ref, win_ref, wout_ref, y_ref, dn_ref, keep_in_ref, send_in_ref, keep_out_ref, send_out_ref):
-    step = pl.program_id(0)
+def ffn_kernel(n_ref, nt_ref, g_ref, gt_ref, win_ref, wout_ref, y_ref, dn_ref, dw_ref):
     w_in, w_out = win_ref[...], wout_ref[...]
     tokens = n_ref.shape[0]
 
-    @pl.when(step == 0)
+    @pl.when(pl.program_id(0) == 0)
     def _():
         y_ref[...] = jnp.zeros_like(y_ref)
         dn_ref[...] = jnp.zeros_like(dn_ref)
@@ -542,17 +564,15 @@
         dn_ref[rows, :] += dot(da, w_in, NT)
         acts.append(act)
         grads.append(da)
-    act = jnp.concatenate(acts, axis=0)
-    da = jnp.concatenate(grads, axis=0)
-    me = me_ref[0]
-    store_halves(me, first_rows, dot(nt_ref[...], da), keep_in_ref, send_in_ref, lambda p: (0, p))
-    store_halves(me, first_rows, dot(gt_ref[...], act), keep_out_ref, send_out_ref, lambda p: (0, p))
-
-
-def top_kernel(ya_ref, yb_ref, da_ref, db_ref, x3_ref, g_ref, gain_ref, wo_ref, out_ref, dx_ref, lowt_ref, doc_ref, gg_ref):
+    tile = w_in.shape[1]
+    dw_ref[:, :tile] = dot(nt_ref[...], jnp.concatenate(grads, axis=0)).astype(BF)
+    dw_ref[:, tile:] = dot(gt_ref[...], jnp.concatenate(acts, axis=0)).astype(BF)
+
+
+def top_kernel(y_ref, dn_ref, x3_ref, g_ref, gain_ref, wo_ref, out_ref, dx_ref, lowt_ref, doc_ref, gg_ref):
     x3 = x3_ref[...]
-    out_ref[...] = (x3 + (ya_ref[...] + yb_ref[...])).astype(BF)
-    grad, grad_gain = norm_back(da_ref[...] + db_ref[...], x3, gain_ref[2:3, :])
+    out_ref[...] = (x3 + y_ref[...]).astype(BF)
+    grad, grad_gain = norm_back(dn_ref[...], x3, gain_ref[2:3, :])
     dx = g_ref[...].astype(F32) + grad
     dx_ref[...] = dx
     low = dx.astype(BF)
@@ -582,14 +602,13 @@
     gg_ref[0:1, :] += grad_gain
 
 
-def last_kernel(x_ref, dx2_ref, gain_ref, wq_ref, wk_ref, wv_ref, ck_ref, cv_ref, *refs):
-    d_refs, (dx_ref, de_ref, gg_ref) = refs[:-3], refs[-3:]
-    n = len(d_refs) // 5
-    dq, dk, dv, dkc, dvc = (d_refs[n * i: n * (i + 1)] for i in range(5))
+def last_kernel(x_ref, dx2_ref, gain_ref, wq_ref, wk_ref, wv_ref, *refs):
+    d_refs, (dx_ref, gg_ref) = refs[:-2], refs[-2:]
+    n = len(d_refs) // 3
+    dq, dk, dv = (d_refs[n * i: n * (i + 1)] for i in range(3))
     dn = spans_dot(dq, wq_ref, NT) + spans_dot(dk, wk_ref, NT) + spans_dot(dv, wv_ref, NT)
     grad, grad_gain = norm_back(dn, x_ref[...].astype(F32), gain_ref[0:1, :])
     dx_ref[...] = dx2_ref[...] + grad
-    de_ref[...] = spans_dot(dkc, ck_ref, NT) + spans_dot(dvc, cv_ref, NT)
 
     @pl.when(pl.program_id(0) == 0)
     def _():
@@ -598,13 +617,19 @@
     gg_ref[0:1, :] += grad_gain
 
 
-def grads_kernel(first_rows, lefts, count, me_ref, *refs):
+def encoder_kernel(ck_ref, cv_ref, *refs):
+    n = len(refs) // 2
+    refs[-1][...] = spans_dot(refs[:n], ck_ref, NT) + spans_dot(refs[n: 2 * n], cv_ref, NT)
+
+
+def grads_kernel(first_rows, lefts, groups, me_ref, *refs):
+    count = sum(groups)
     n_left = max(lefts) + 1
     left_refs, right_refs = refs[:n_left], refs[n_left: n_left + count]
-    keep_ref, send_ref, left_buf, right_buf, sems = refs[n_left + count:]
+    outs = refs[n_left + count: n_left + count + 2 * len(groups)]
+    left_buf, right_buf, sems = refs[n_left + count + 2 * len(groups):]
     width = right_buf.shape[2]
     tile = 384 if width % 256 else 256
-    widths = [width] * count
 
     def copies(p):
         found = [pltpu.make_async_copy(right_refs[p], right_buf.at[p % 2], sems.at[p % 2])]
@@ -620,31 +645,27 @@
                 copy.start()
         for copy in copies(p):
             copy.wait()
-
-        base = sum(widths[:p])
-
-        def column(j, carry, p=p, base=base):
-            col = pl.multiple_of(j * tile, tile)
-            result = dot(left_buf[lefts[p] % 2], right_buf[p % 2, :, pl.ds(col, tile)])
-            out = pl.multiple_of(base + j * tile, 128)
-            store_halves(me_ref[0], first_rows, result, keep_ref, send_ref, lambda part: (0, part, slice(None), pl.ds(out, tile)))
-            return carry
-
-        lax.fori_loop(0, widths[p] // tile, column, 0)
-
-
-def weight_grads(name, lefts_arrays, lefts, rights, half, first_rows):
+        group = next(g for g in range(len(groups)) if p < sum(groups[: g + 1]))
+        base = (p - sum(groups[:group])) * width
+        keep_ref, send_ref = outs[2 * group], outs[2 * group + 1]
+        for col in range(0, width, tile):
+            result = dot(left_buf[lefts[p] % 2], right_buf[p % 2, :, col: col + tile])
+            out = slice(base + col, base + col + tile)
+            store_halves(me_ref[0], first_rows, result, keep_ref, send_ref, lambda part: (0, part, slice(None), out))
+
+
+def weight_grads(name, lefts_arrays, lefts, rights, groups, half, first_rows):
     width = lefts_arrays[0].shape[0]
     tokens = rights[0].shape[0]
     columns = rights[0].shape[1]
     count = len(rights)
-    shape = (1, width // (2 * first_rows), first_rows, count * columns)
+    shapes = [(1, width // (2 * first_rows), first_rows, n * columns) for n in groups for _ in range(2)]
     flops = 2 * width * tokens * columns * count
     return pl.pallas_call(
-        functools.partial(grads_kernel, first_rows, lefts, count),
+        functools.partial(grads_kernel, first_rows, lefts, groups),
         in_specs=[pl.BlockSpec(memory_space=pltpu.SMEM)] + [pl.BlockSpec(memory_space=pl.ANY)] * (len(lefts_arrays) + count),
-        out_specs=[pl.BlockSpec(memory_space=pltpu.VMEM)] * 2,
-        out_shape=[jax.ShapeDtypeStruct(shape, BF)] * 2,
+        out_specs=[pl.BlockSpec(memory_space=pltpu.VMEM)] * len(shapes),
+        out_shape=[jax.ShapeDtypeStruct(shape, BF) for shape in shapes],
         scratch_shapes=[pltpu.VMEM((2, width, tokens), BF), pltpu.VMEM((2, tokens, columns), BF), pltpu.SemaphoreType.DMA((4,))],
         compiler_params=pltpu.CompilerParams(vmem_limit_bytes=VMEM_LIMIT),
         cost_estimate=pl.CostEstimate(flops=flops, bytes_accessed=2 * tokens * columns * count * 2, transcendentals=0),
@@ -660,7 +681,7 @@
     micro, per, length, width = inputs.shape
     rows = micro * per
     tokens = rows * length
-    hidden = ffn_in.shape[1] // 2
+    hidden = ffn_in.shape[1]
     flat = lambda v: v.reshape(tokens, width)
     x, enc, grad_out = flat(inputs), flat(encoder_out), flat(out_grad)
     seg, enc_seg = segments.reshape(rows, length), enc_segments.reshape(rows, length)
@@ -668,12 +689,11 @@
 
     outer_t = ffn_out.T
     gain_cols = jnp.pad(gains.T, ((0, 0), (0, 125)))
-    g_self, g_cross, g_ffn0, g_ffn1 = [Gather(sizes, shard) for shard in (
-        [jnp.concatenate([self_q, self_kv[0]], axis=1), jnp.concatenate([self_kv[1], self_out.T, gain_cols], axis=1)],
-        [jnp.concatenate([cross_q, cross_kv[0]], axis=1), jnp.concatenate([cross_kv[1], cross_out.T], axis=1)],
-        [ffn_in[:, :hidden], outer_t[:, :hidden]],
-        [ffn_in[:, hidden:], outer_t[:, hidden:]],
-    )]
+    shard_self = jnp.concatenate([self_q, self_kv[0], self_kv[1], gain_cols], axis=1)
+    shard_cross = jnp.concatenate([cross_q, cross_kv[0], cross_kv[1], cross_out.T, self_out.T], axis=1)
+    g_self = Gather(sizes, shard_self, (9 * 128, 10 * 128))
+    g_cross = Gather(sizes, shard_cross, (15 * 128, 15 * 128))
+    shard_ffn = jnp.concatenate([ffn_in, outer_t], axis=1)
     block_rows = self_q.shape[0] * narrow
     first = 1 << len(low_bits(wide, block_rows))
     first_rows = block_rows * first
@@ -691,7 +711,7 @@
     unit = 2 * tokens * width * width
 
     r = Rounds()
-    movers = [g_self, g_cross, g_ffn0, g_ffn1]
+    movers = [g_self, g_cross]
     r.moving = list(movers)
     r.live = {"x": x, "enc": enc, "g": grad_out}
 
@@ -700,7 +720,7 @@
 
     def take_self():
         slab = g_self.whole()
-        return {"slab_self": slab, "gain": slab[:, 4 * width: 4 * width + 3].T.astype(F32)}
+        return {"slab_self": slab, "gain": slab[:, 3 * width: 3 * width + 3].T.astype(F32)}
 
     def proj():
         n1t, qkv = call(proj_self_kernel, "proj_self", steps, [rows_in(r["x"]), entire(r["gain"]), (r["slab_self"], (width, 3 * width), whole)], [turned(), wide_low(3)], 3 * unit)
@@ -715,7 +735,7 @@
 
     def mid():
         out = call(mid_kernel, "mid", steps,
-                   [rows_in(r["x"]), rows_in(r["enc"]), entire(r["gain"]), piece(r["slab_self"], 3), (r["slab_cross"], (width, 3 * width), whole)] + [rows_in(o) for o in both("o")],
+                   [rows_in(r["x"]), rows_in(r["enc"]), entire(r["gain"]), piece(r["slab_cross"], 4), (r["slab_cross"], (width, 3 * width), whole)] + [rows_in(o) for o in both("o")],
                    [wide_f32(), turned(), wide_low(), wide_low(2), turned()], 4 * unit)
         return dict(zip(("x2", "n2t", "qc", "kvc", "et"), out))
 
@@ -731,21 +751,20 @@
 
     tile = 512
     tiles = hidden // tile
-    halves = ((1, parts, first_rows, hidden), BF, (1, parts, first_rows, tile), lambda j: (0, 0, 0, j))
     acc_out = ((tokens, width), F32, (tokens, width), whole)
 
-    def ffn(i):
-        slab = r[f"slab_ffn{i}"]
-        y, dn, *split = call(
-            functools.partial(ffn_kernel, first_rows), "ffn", (tiles,),
-            [(half, pltpu.SMEM, None), entire(r["n3"]), entire(r["n3t"]), entire(r["g"]), entire(r["gt"]),
+    def ffn():
+        slab = r["slab_ffn"]
+        y, dn, dw = call(
+            ffn_kernel, "ffn", (tiles,),
+            [entire(r["n3"]), entire(r["n3t"]), entire(r["g"]), entire(r["gt"]),
              (slab, (width, tile), lambda j: (0, j)), (slab, (width, tile), lambda j: (0, tiles + j))],
-            [acc_out, acc_out] + [halves] * 4, 12 * tokens * width * hidden)
-        return {f"y{i}": y, f"dn{i}": dn, f"split{i}": split}
+            [acc_out, acc_out, ((width, 2 * hidden), BF, (width, 2 * tile), lambda j: (0, j))], 12 * tokens * width * hidden)
+        return {"y": y, "dn": dn, "dw": dw}
 
     def top():
         out = call(top_kernel, "top", steps,
-                   [rows_in(r["y0"]), rows_in(r["y1"]), rows_in(r["dn0"]), rows_in(r["dn1"]), rows_in(r["x3"]), rows_in(r["g"]), entire(r["gain"]), piece(r["slab_cross"], 3)],
+                   [rows_in(r["y"]), rows_in(r["dn"]), rows_in(r["x3"]), rows_in(r["g"]), entire(r["gain"]), piece(r["slab_cross"], 3)],
                    [wide_low(), wide_f32(), turned(), wide_low(), gain_out()], unit)
         return dict(zip(("layer", "dx3", "three_t", "doc", "gain3"), out))
 
@@ -755,86 +774,88 @@
 
     def second():
         out = call(second_kernel, "second", steps,
-                   [rows_in(r["x2"]), rows_in(r["dx3"]), entire(r["gain"]), piece(r["slab_cross"], 0), piece(r["slab_self"], 3)] + [rows_in(d) for d in both("dqc")],
+                   [rows_in(r["x2"]), rows_in(r["dx3"]), entire(r["gain"]), piece(r["slab_cross"], 0), piece(r["slab_cross"], 4)] + [rows_in(d) for d in both("dqc")],
                    [wide_f32(), turned(), wide_low(), gain_out()], 2 * unit)
         return dict(zip(("dx2", "two_t", "do", "gain2"), out))
 
     def grads_cross():
-        rights = both("dqc") + both("dkc") + both("dvc")
+        rights = both("dqc") + both("dkc") + both("dvc") + both("oc") + both("o")
         n = len(SPANS)
-        return {"cut_cross": weight_grads("grads_cross", [r["n2t"], r["et"]], (0,) * n + (1,) * (2 * n), rights, half, first_rows)}
-
-    def grads_out():
-        n = len(SPANS)
-        return {"cut_out": weight_grads("grads_out", [r["three_t"], r["two_t"]], (0,) * n + (1,) * n, both("oc") + both("o"), half, first_rows)}
+        lefts = [r["n2t"], r["et"], r["three_t"], r["two_t"]]
+        return {"cut_cross": weight_grads("grads_cross", lefts, (0,) * n + (1,) * (2 * n) + (2,) * n + (3,) * n, rights, (3 * n, 2 * n), half, first_rows)}
 
     def bwd_self(i):
         out = attn_bwd(SPANS[i], r["qkv"], 0, r["qkv"], 6, r["qkv"], 12, r["do"], r[f"o{i}"], r[f"p{i}"], True)
         return dict(zip((f"dq{i}", f"dk{i}", f"dv{i}", f"diag{i}"), out))
 
     def grads_self(i):
-        return {f"cut_self{i}": weight_grads("grads_self", [r["n1t"]], (0, 0, 0), [r[f"dq{i}"], r[f"dk{i}"], r[f"dv{i}"]], half, first_rows)}
+        return {f"cut_self{i}": weight_grads("grads_self", [r["n1t"]], (0, 0, 0), [r[f"dq{i}"], r[f"dk{i}"], r[f"dv{i}"]], (3,), half, first_rows)}
 
     def last():
         out = call(last_kernel, "last", steps,
-                   [rows_in(r["x"]), rows_in(r["dx2"]), entire(r["gain"])] + [piece(r["slab_self"], c) for c in range(3)] + [piece(r["slab_cross"], c) for c in (1, 2)]
-                   + [rows_in(d) for name in ("dq", "dk", "dv", "dkc", "dvc") for d in both(name)],
-                   [wide_f32(), wide_f32(), gain_out()], 5 * unit)
-        return dict(zip(("dx1", "de", "gain1"), out))
+                   [rows_in(r["x"]), rows_in(r["dx2"]), entire(r["gain"])] + [piece(r["slab_self"], c) for c in range(3)]
+                   + [rows_in(d) for name in ("dq", "dk", "dv") for d in both(name)],
+                   [wide_f32(), gain_out()], 3 * unit)
+        return dict(zip(("dx1", "gain1"), out))
+
+    def encoder():
+        out = call(encoder_kernel, "encoder_grad", steps,
+                   [piece(r["slab_cross"], c) for c in (1, 2)] + [rows_in(d) for name in ("dkc", "dvc") for d in both(name)],
+                   [wide_f32()], 2 * unit)
+        return {"de": out[0]}
 
     def cut(pair, turn):
         return Scatter(sizes, pair[0], pair[1], first, turn)
 
     r.step(prepare, [g_self])
-    r.step(None, [g_self, g_cross])
     r.step(None, [g_self, g_cross])
     while g_self.plan:
         r.step(None, [g_self])
+    g_self.groups, shard_ffn = lax.optimization_barrier((g_self.groups, shard_ffn))
+    slab_ffn = lax.all_gather(shard_ffn, (WIDE, NARROW), axis=0, tiled=True)
     r.step(take_self, [])
-    r.step(proj, [g_cross, g_ffn0])
-    r.step(lambda: fwd_self(0), [g_cross, g_ffn0])
-    r.step(lambda: fwd_self(1), [g_cross, g_ffn0, g_ffn1])
+    r.step(proj, [g_cross])
+    r.step(lambda: fwd_self(0), [g_cross])
+    r.step(lambda: fwd_self(1), [g_cross])
     while g_cross.plan:
         r.step(None, [g_cross])
     r.step(lambda: {"slab_cross": g_cross.whole()}, [])
-    r.step(mid, [g_ffn0, g_ffn1])
-    r.step(lambda: fwd_cross(0), [g_ffn0, g_ffn1])
-    r.step(lambda: fwd_cross(1), [g_ffn0, g_ffn1])
-    r.step(third, [g_ffn0, g_ffn1])
-    while g_ffn0.plan or g_ffn1.plan:
-        r.step(None, [g_ffn0, g_ffn1])
-    r.step(lambda: {"slab_ffn0": g_ffn0.whole(), "slab_ffn1": g_ffn1.whole()}, [])
+    r.step(mid, [])
+    r.step(lambda: fwd_cross(0), [])
+    r.step(lambda: fwd_cross(1), [])
+    r.step(third, [])
     r.moving = []
-    r.step(lambda: ffn(0), [])
-    split = r.live.pop("split0")
-    f0 = [cut(split[2 * i: 2 * i + 2], i) for i in range(2)]
-    r.step(lambda: ffn(1), f0)
-    split = r.live.pop("split1")
-    f1 = [cut(split[2 * i: 2 * i + 2], i) for i in range(2)]
-    r.step(top, f0 + f1)
-    r.step(lambda: bwd_cross(0), f0 + f1)
-    r.step(lambda: bwd_cross(1), f0 + f1)
-    r.step(second, f0 + f1)
-    r.step(grads_cross, f1)
-    sc = cut(r.live.pop("cut_cross"), 0)
-    r.step(grads_out, [sc])
-    so = cut(r.live.pop("cut_out"), 1)
-    r.step(lambda: bwd_self(0), f1 + [sc, so])
-    r.step(lambda: grads_self(0), f1 + [sc, so])
+    r.live["slab_ffn"] = slab_ffn
+    r.step(None, [])
+    r.step(ffn, [])
+    ffn_sum = lax.psum_scatter(r.live.pop("dw"), (WIDE, NARROW), scatter_dimension=0, tiled=True).astype(F32)
+    ffn_sum = ffn_sum.reshape(-1, tiles, 2, tile)
+    r.step(top, [])
+    r.step(lambda: bwd_cross(0), [])
+    r.step(lambda: bwd_cross(1), [])
+    r.step(second, [])
+    r.step(grads_cross, [])
+    pairs = r.live.pop("cut_cross")
+    sc, so = cut(pairs[:2], 0), cut(pairs[2:], 1)
+    r.step(lambda: bwd_self(0), [sc, so])
+    r.run(lambda: grads_self(0), [sc, so], [])
     s0 = cut(r.live.pop("cut_self0"), 1)
-    r.step(lambda: bwd_self(1), f1 + [sc, so, s0])
-    r.step(lambda: grads_self(1), f1 + [sc, so, s0])
+    r.run(lambda: bwd_self(1), [s0], [s0, sc, so])
+    r.run(lambda: grads_self(1), [sc, so, s0], [])
     s1 = cut(r.live.pop("cut_self1"), 0)
-    r.step(last, [sc, so, s0, s1])
+    r.run(last, [s1], [s1, sc, so, s0])
 
     def small():
         diag = jnp.concatenate(both("diag"), axis=0)
         bias_rows = bucket_sums(diag, buckets, rel_bias.shape[0])
         return {"small": jnp.concatenate([r["gain1"][0], r["gain2"][0], r["gain3"][0], bias_rows.reshape(-1)]).reshape(-1, 128)}
 
-    r.step(small, [sc, so, s0, s1])
+    r.live.update(small())
     total = Total(sizes, r.live.pop("small"))
-    movers = f0 + f1 + [sc, so, s0, s1, total]
+    movers = [sc, so, s0, s1, total]
+    r.live["ffn_sum"] = ffn_sum
+    r.step(encoder, movers)
+    ffn_sum = r.live.pop("ffn_sum")
     while any(m.plan for m in movers):
         r.step(None, movers)
 
@@ -865,8 +886,8 @@
         columns([sc], 0, 3),
         jnp.stack([columns([sc], 1, 3), columns([sc], 2, 3)]),
         columns([so], 0, 2).T,
-        jnp.concatenate([f0[0].keep[0], f1[0].keep[0]], axis=1),
-        jnp.concatenate([f0[1].keep[0], f1[1].keep[0]], axis=1).T,
+        ffn_sum[:, :, 0].reshape(-1, hidden),
+        ffn_sum[:, :, 1].reshape(-1, hidden).T,
     )
 
 

time: 574 us -> 459 us (0.80)
  starting transfers between devices: 127 us -> 57.2 us
  local copies, waits for them, and re-layouts: 63.8 us -> 24.6 us
  waiting for transfers between devices: 108 us -> 87.3 us
  between operations: 2.75 us -> 15.2 us
  Pallas kernels: 248 us -> 255 us
    unnamed x210 -> x92, local copies, waits for them, and re-layouts: 51.2 us -> 10.6 us
    ppermute x24 -> x12, waiting for transfers between devices: 43.9 us -> 10.1 us  [go(): self.flight = [lax.ppermute(self.sends[0], WIDE, flipped(self.wide, step))]]
    reduce_scatter x0 -> x1, waiting for transfers between devices: none -> 32.2 us  [body(): lax.psum_scatter(r.live.pop('dw'), (WIDE, NARROW), scatter_dimension=0, t...]
    ppermute x24 -> x6, starting transfers between devices: 39.2 us -> 10.1 us  [go(): lax.ppermute(g[0], NARROW, flipped(self.narrow, k))]
    ppermute x56 -> x16, starting transfers between devices: 29.4 us -> 9.64 us  [go(): lax.ppermute(p, WIDE, flipped(self.wide, self.orders[i][step]))]
    ppermute x24 -> x12, starting transfers between devices: 35.7 us -> 20.8 us  [go(): lax.ppermute(s, NARROW, flipped(self.narrow, k + 1))]
    ppermute x24 -> x12, starting transfers between devices: 18.9 us -> 9.06 us  [go(): self.flight = [lax.ppermute(self.sends[0], WIDE, flipped(self.wide, step))]]
    ppermute x5 -> x6, waiting for transfers between devices: 11.8 us -> 3.88 us  [the longest x3 3.87 us: go(): lax.ppermute(self.value, NARROW, flipped(self.narrow, k))]
  transfers between devices with their start and end apart: 133 -> 54, of which waited for: 37 -> 15; matrix products, arithmetic and copies ran while one was open for 3% -> 7% of each run, Pallas kernels for 36% -> 38%
where the time goes in v3:
time: 459 us; the launch traced here: 455 us
  Pallas kernels  255 us (56%)
  waiting for transfers between devices  87.3 us (19%)
  starting transfers between devices  57.2 us (12%)
  local copies, waits for them, and re-layouts  24.6 us (5%)
  other arithmetic  15.6 us (3%)
  between operations  15.2 us (3%)
    pallas_call x8, Pallas kernels, call(): pl.pallas_call(kernel, grid=grid, in_specs=[spec(b, i) for _, b, i in ins...  104 us
    pallas_call x4, Pallas kernels, attn_bwd(): pl.pallas_call(functools.partial(attn_bwd_kernel, causal), grid=(pairs, r...  61 us
    pallas_call x4, Pallas kernels, attn_fwd(): pl.pallas_call(functools.partial(attn_fwd_kernel, causal), grid=(pairs, r...  53.9 us
    reduce_scatter x1, waiting for transfers between devices, body(): lax.psum_scatter(r.live.pop('dw'), (WIDE, NARROW), scatter_dimension=0, t...  32.2 us
    pallas_call x3, Pallas kernels, weight_grads(): pl.pallas_call(functools.partial(grads_kernel, first_rows, lefts, groups)...  26 us
    ppermute x16, waiting for transfers between devices, go(): lax.ppermute(p, WIDE, flipped(self.wide, self.orders[i][step]))  24.1 us
    ppermute x12, starting transfers between devices, go(): lax.ppermute(s, NARROW, flipped(self.narrow, k + 1))  20.8 us
    ppermute x6, waiting for transfers between devices, go(): lax.ppermute(g[0], NARROW, flipped(self.narrow, k))  12.9 us
  transfers between devices with their start and end apart: 54, of which 15 were waited for; matrix products, arithmetic and copies ran while one was open for 7% of the time, Pallas kernels for 38%

profile of v3, /device:TPU:0, one launch (start us, length us, event | category | flops | bytes accessed | tf_op | source)
XLA Modules:
  0.0 455.1 jit_solution(12739019740967394860)
XLA Ops:
  9.6 3.1 collective-permute-start
  34.9 9.7 %collective-permute-done.6 = bf16[24,3840]{1,0:T(8,128)(2,1)S(1)} collective-permute-done((bf16[24,3840]{1,0:T(8,128)(2,1)S(1)}, bf16[24,3840]{1,0:T(8,128)(2,1)S(1)}, u32[]{:S(2)}, u32[]{:S(2)}) %collective-permute-start.6) | collective-permute-done | bytes 184352 | tf_op jit(solution)/shard_map/ppermute | solution.py:268
  46.1 7.7 %collective-permute-done.8.refs_1_ = bf16[192,1152]{1,0:T(8,128)(2,1)} collective-permute-done((bf16[192,1152]{1,0:T(8,128)(2,1)S(1)}, bf16[192,1152]{1,0:T(8,128)(2,1)}, u32[]{:S(2)}, u32[]{:S(2)}) %collective-permute-start.8) | collective-permute-done | bytes 442400 | tf_op jit(solution)/shard_map/ppermute | solution.py:272
  58.6 4.1 assemble.2.w_ref.wq_ref.wk_ref.wv_ref
  66.4 8.1 %proj_self.1 = (bf16[768,1024]{1,0:T(8,128)(2,1)}, bf16[1024,2304]{1,0:T(8,128)(2,1)}) custom-call(bf16[1024,768]{1,0:T(8,128)(2,1)} %bitcast.155, f32[3,768]{1,0:T(4,128)} %bitcast.161, bf16[768,2432]{1,0:T(8,128)(2,1)} %assemble.2.w_ref.wq_ref.wk_ref.wv_ref), custom_call_target="tpu_custom_call" | custom-call | flops 3623878656 | bytes 11609088 | tf_op jit(solution)/shard_map/proj_self/pallas_call | solution.py:483
  74.5 2.7 collective-permute-done.14
  79.8 13.1 %attn_fwd_self.2 = (bf16[1024,384]{1,0:T(8,128)(2,1)}, bf16[2,6,512,512]{3,2,1,0:T(8,128)(2,1)}) custom-call(bf16[1024,2304]{1,0:T(8,128)(2,1)} %get-tuple-element.1185.q_ref.k_ref.v_ref, bf16[1024,2304]{1,0:T(8,128)(2,1)} %get-tuple-element.1185.q_ref.k_ref.v_ref, bf16[1024,2304]{1,0:T(8,128)(2,1)} %get-tuple-element.1185.q_ref.k_ref.v_ref, ...), custom_call_target="tpu_custom_call" | custom-call | flops 6442450944 | bytes 6291456 | tf_op jit(solution)/shard_map/attn_fwd_self/pallas_call | solution.py:93
  92.9 10.3 %collective-permute-done.17.refs_5_ = bf16[192,1920]{1,0:T(8,128)(2,1)S(1)} collective-permute-done((bf16[192,1920]{1,0:T(8,128)(2,1)S(1)}, bf16[192,1920]{1,0:T(8,128)(2,1)S(1)}, u32[]{:S(2)}, u32[]{:S(2)}) %collective-permute-start.17) | collective-permute-done | bytes 737312 | tf_op jit(solution)/shard_map/ppermute | solution.py:272
  104.2 13.1 %attn_fwd_self.3 = (bf16[1024,384]{1,0:T(8,128)(2,1)}, bf16[2,6,512,512]{3,2,1,0:T(8,128)(2,1)}) custom-call(bf16[1024,2304]{1,0:T(8,128)(2,1)} %get-tuple-element.1185.q_ref.k_ref.v_ref, bf16[1024,2304]{1,0:T(8,128)(2,1)} %get-tuple-element.1185.q_ref.k_ref.v_ref, bf16[1024,2304]{1,0:T(8,128)(2,1)} %get-tuple-element.1185.q_ref.k_ref.v_ref, ...), custom_call_target="tpu_custom_call" | custom-call | flops 6442450944 | bytes 6291456 | tf_op jit(solution)/shard_map/attn_fwd_self/pallas_call | solution.py:93
  117.4 6.7 %assemble.3.wo_ref.wc_ref.wq_ref.ck_ref.cv_ref = bf16[768,3840]{1,0:T(8,128)(2,1)} custom-call(s32[1]{0:T(128)} %bitcast.12.me_ref, bf16[192,1920]{1,0:T(8,128)(2,1)} %copy-done.2, bf16[192,1920]{1,0:T(8,128)(2,1)} %copy-done.9, bf16[192,1920]{1,0:T(8,128)(2,1)} %collective-permute-done.18.refs_2_, bf16[192,1920]{1,0:T(8,128)(2,1)} %collective-permute-done.19.refs_3_, ...), custom_call_target="tpu_custom_call" | custom-call | bytes 11796480 | tf_op jit(solution)/shard_map/assemble/pallas_call | solution.py:329
  124.0 12.2 %mid.1 = (f32[1024,768]{1,0:T(8,128)}, bf16[768,1024]{1,0:T(8,128)(2,1)}, bf16[1024,768]{1,0:T(8,128)(2,1)}, bf16[1024,1536]{1,0:T(8,128)(2,1)}, bf16[768,1024]{1,0:T(8,128)(2,1)}) custom-call(bf16[1024,768]{1,0:T(8,128)(2,1)} %bitcast.156, bf16[1024,768]{1,0:T(8,128)(2,1)} %bitcast.179, f32[3,768]{1,0:T(4,128)} %bitcast.162, ...), custom_call_target="tpu_custom_call" | custom-call | flops 4831838208 | bytes 27534336 | tf_op jit(solution)/shard_map/mid/pallas_call | solution.py:483
  136.2 13.8 %attn_fwd_cross.2 = (bf16[1024,384]{1,0:T(8,128)(2,1)}, bf16[2,6,512,512]{3,2,1,0:T(8,128)(2,1)}) custom-call(bf16[1024,768]{1,0:T(8,128)(2,1)} %get-tuple-element.1046.q_ref, bf16[1024,1536]{1,0:T(8,128)(2,1)} %get-tuple-element.1047.k_ref.v_ref, bf16[1024,1536]{1,0:T(8,128)(2,1)} %get-tuple-element.1047.k_ref.v_ref, ...), custom_call_target="tpu_custom_call" | custom-call | flops 6442450944 | bytes 6291456 | tf_op jit(solution)/shard_map/attn_fwd_cross/pallas_call | solution.py:93
  150.0 13.9 %attn_fwd_cross.3 = (bf16[1024,384]{1,0:T(8,128)(2,1)}, bf16[2,6,512,512]{3,2,1,0:T(8,128)(2,1)}) custom-call(bf16[1024,768]{1,0:T(8,128)(2,1)} %get-tuple-element.1046.q_ref, bf16[1024,1536]{1,0:T(8,128)(2,1)} %get-tuple-element.1047.k_ref.v_ref, bf16[1024,1536]{1,0:T(8,128)(2,1)} %get-tuple-element.1047.k_ref.v_ref, ...), custom_call_target="tpu_custom_call" | custom-call | flops 6442450944 | bytes 6291456 | tf_op jit(solution)/shard_map/attn_fwd_cross/pallas_call | solution.py:93
  163.9 8.2 %third.1 = (f32[1024,768]{1,0:T(8,128)}, bf16[1024,768]{1,0:T(8,128)(2,1)}, bf16[768,1024]{1,0:T(8,128)(2,1)}, bf16[768,1024]{1,0:T(8,128)(2,1)}) custom-call(f32[1024,768]{1,0:T(8,128)} %get-tuple-element.1076.x2_ref, bf16[1024,768]{1,0:T(8,128)(2,1)} %bitcast.143, f32[3,768]{1,0:T(4,128)} %bitcast.163, ...), custom_call_target="tpu_custom_call" | custom-call | flops 1207959552 | bytes 20063232 | tf_op jit(solution)/shard_map/third/pallas_call | solution.py:483
  172.1 36.9 %ffn.1 = (f32[1024,768]{1,0:T(8,128)}, f32[1024,768]{1,0:T(8,128)}, bf16[768,6144]{1,0:T(8,128)(2,1)}) custom-call(bf16[1024,768]{1,0:T(8,128)(2,1)} %get-tuple-element.958.n_ref, bf16[768,1024]{1,0:T(8,128)(2,1)} %get-tuple-element.959.nt_ref, bf16[1024,768]{1,0:T(8,128)(2,1)} %bitcast.144, bf16[768,1024]{1,0:T(8,128)(2,1)} %get-tuple-element.961.gt_ref, ...), custom_call_target="tpu_custom_call" | custom-call | flops 28991029248 | bytes 40894464 | tf_op jit(solution)/shard_map/ffn/pallas_call | solution.py:483
  209.0 9.3 %top.1 = (bf16[1024,768]{1,0:T(8,128)(2,1)}, f32[1024,768]{1,0:T(8,128)}, bf16[768,1024]{1,0:T(8,128)(2,1)}, bf16[1024,768]{1,0:T(8,128)(2,1)}, f32[8,768]{1,0:T(8,128)}) custom-call(f32[1024,768]{1,0:T(8,128)} %get-tuple-element.991.y_ref, f32[1024,768]{1,0:T(8,128)} %get-tuple-element.990.dn_ref, f32[1024,768]{1,0:T(8,128)} %get-tuple-element.992.x3_ref, ...), custom_call_target="tpu_custom_call" | custom-call | flops 1207959552 | bytes 24806400 | tf_op jit(solution)/shard_map/top/pallas_call | solution.py:483
  218.3 13.7 %attn_bwd_cross.2 = (bf16[1024,384]{1,0:T(8,128)(2,1)}, bf16[1024,384]{1,0:T(8,128)(2,1)}, bf16[1024,384]{1,0:T(8,128)(2,1)}) custom-call(bf16[1024,768]{1,0:T(8,128)(2,1)} %get-tuple-element.1046.q_ref, bf16[1024,1536]{1,0:T(8,128)(2,1)} %get-tuple-element.1047.k_ref.v_ref, bf16[1024,1536]{1,0:T(8,128)(2,1)} %get-tuple-element.1047.k_ref.v_ref, ...), custom_call_target="tpu_custom_call" | custom-call | flops 6442450944 | bytes 6291456 | tf_op jit(solution)/shard_map/attn_bwd_cross/pallas_call | solution.py:183
  232.0 13.8 %attn_bwd_cross.3 = (bf16[1024,384]{1,0:T(8,128)(2,1)}, bf16[1024,384]{1,0:T(8,128)(2,1)}, bf16[1024,384]{1,0:T(8,128)(2,1)}) custom-call(bf16[1024,768]{1,0:T(8,128)(2,1)} %get-tuple-element.1046.q_ref, bf16[1024,1536]{1,0:T(8,128)(2,1)} %get-tuple-element.1047.k_ref.v_ref, bf16[1024,1536]{1,0:T(8,128)(2,1)} %get-tuple-element.1047.k_ref.v_ref, ...), custom_call_target="tpu_custom_call" | custom-call | flops 6442450944 | bytes 6291456 | tf_op jit(solution)/shard_map/attn_bwd_cross/pallas_call | solution.py:183
  245.8 10.5 %second.1 = (f32[1024,768]{1,0:T(8,128)}, bf16[768,1024]{1,0:T(8,128)(2,1)}, bf16[1024,768]{1,0:T(8,128)(2,1)}, f32[8,768]{1,0:T(8,128)}) custom-call(f32[1024,768]{1,0:T(8,128)} %get-tuple-element.1076.x2_ref, f32[1024,768]{1,0:T(8,128)} %get-tuple-element.1077.dx3_ref, f32[3,768]{1,0:T(4,128)} %bitcast.165, ...), custom_call_target="tpu_custom_call" | custom-call | flops 2415919104 | bytes 25986048 | tf_op jit(solution)/shard_map/second/pallas_call | solution.py:483
  256.3 14.1 %grads_cross.1 = (bf16[1,4,96,2304]{3,2,1,0:T(8,128)(2,1)}, bf16[1,4,96,2304]{3,2,1,0:T(8,128)(2,1)}, bf16[1,4,96,1536]{3,2,1,0:T(8,128)(2,1)}, bf16[1,4,96,1536]{3,2,1,0:T(8,128)(2,1)}) custom-call(s32[1]{0:T(128)} %bitcast.me_ref, bf16[768,1024]{1,0:T(8,128)(2,1)} %get-tuple-element.1103.refs_0_, bf16[768,1024]{1,0:T(8,128)(2,1)} %get-tuple-element.1104.refs_1_, ...), custom_call_target="tpu_custom_call" | custom-call | flops 6039797760 | bytes 15728640 | tf_op jit(solution)/shard_map/grads_cross/pallas_call | solution.py:664
  271.0 16.6 %attn_bwd_self.2 = (bf16[1024,384]{1,0:T(8,128)(2,1)}, bf16[1024,384]{1,0:T(8,128)(2,1)}, bf16[1024,384]{1,0:T(8,128)(2,1)}, f32[6,4,256]{2,1,0:T(4,128)}) custom-call(bf16[1024,2304]{1,0:T(8,128)(2,1)} %get-tuple-element.1185.q_ref.k_ref.v_ref, bf16[1024,2304]{1,0:T(8,128)(2,1)} %get-tuple-element.1185.q_ref.k_ref.v_ref, ...), custom_call_target="tpu_custom_call" | custom-call | flops 6442450944 | bytes 6291456 | tf_op jit(solution)/shard_map/attn_bwd_self/pallas_call | solution.py:183
  289.1 6.0 %grads_self.2 = (bf16[1,4,96,1152]{3,2,1,0:T(8,128)(2,1)}, bf16[1,4,96,1152]{3,2,1,0:T(8,128)(2,1)}) custom-call(s32[1]{0:T(128)} %bitcast.me_ref, bf16[768,1024]{1,0:T(8,128)(2,1)} %get-tuple-element.1215.refs_0_, bf16[1024,384]{1,0:T(8,128)(2,1)} %get-tuple-element.1244.refs_1_.refs_0_, bf16[1024,384]{1,0:T(8,128)(2,1)} %get-tuple-element.1240.refs_2_, ...), custom_call_target="tpu_custom_call" | custom-call | flops 1811939328 | bytes 4718592 | tf_op jit(solution)/shard_map/grads_self/pallas_call | solution.py:664
  297.8 16.9 %attn_bwd_self.3 = (bf16[1024,384]{1,0:T(8,128)(2,1)}, bf16[1024,384]{1,0:T(8,128)(2,1)}, bf16[1024,384]{1,0:T(8,128)(2,1)}, f32[6,4,256]{2,1,0:T(4,128)}) custom-call(bf16[1024,2304]{1,0:T(8,128)(2,1)} %get-tuple-element.1185.q_ref.k_ref.v_ref, bf16[1024,2304]{1,0:T(8,128)(2,1)} %get-tuple-element.1185.q_ref.k_ref.v_ref, ...), custom_call_target="tpu_custom_call" | custom-call | flops 6442450944 | bytes 6291456 | tf_op jit(solution)/shard_map/attn_bwd_self/pallas_call | solution.py:183
  320.5 5.9 %grads_self.3 = (bf16[1,4,96,1152]{3,2,1,0:T(8,128)(2,1)}, bf16[1,4,96,1152]{3,2,1,0:T(8,128)(2,1)}) custom-call(s32[1]{0:T(128)} %bitcast.me_ref, bf16[768,1024]{1,0:T(8,128)(2,1)} %get-tuple-element.1215.refs_0_, bf16[1024,384]{1,0:T(8,128)(2,1)} %get-tuple-element.1245.refs_1_, bf16[1024,384]{1,0:T(8,128)(2,1)} %get-tuple-element.1241.refs_2_.refs_3_, ...), custom_call_target="tpu_custom_call" | custom-call | flops 1811939328 | bytes 4718592 | tf_op jit(solution)/shard_map/grads_self/pallas_call | solution.py:664
  328.6 10.8 %last.1 = (f32[1024,768]{1,0:T(8,128)}, f32[8,768]{1,0:T(8,128)}) custom-call(bf16[1024,768]{1,0:T(8,128)(2,1)} %bitcast.157, f32[1024,768]{1,0:T(8,128)} %get-tuple-element.1251.dx2_ref, f32[3,768]{1,0:T(4,128)} %bitcast.166, bf16[768,2432]{1,0:T(8,128)(2,1)} %assemble.2.w_ref.wq_ref.wk_ref.wv_ref, bf16[768,2432]{1,0:T(8,128)(2,1)} %assemble.2.w_ref.wq_ref.wk_ref.wv_ref, ...), custom_call_target="tpu_custom_call" | custom-call | flops 3623878656 | bytes 23823360 | tf_op jit(solution)/shard_map/last/pallas_call | solution.py:483
  339.4 10.0 %collective-permute-done.27 = bf16[1,96,2304]{2,1,0:T(8,128)(2,1)} collective-permute-done((bf16[1,96,2304]{2,1,0:T(8,128)(2,1)}, bf16[1,96,2304]{2,1,0:T(8,128)(2,1)}, u32[]{:S(2)}, u32[]{:S(2)}) %collective-permute-start.27) | collective-permute-done | bytes 442400 | tf_op jit(solution)/shard_map/ppermute | solution.py:356
  356.0 4.6 %collective-permute-start.35 = (bf16[1,24,1536]{2,1,0:T(8,128)(2,1)S(1)}, bf16[1,24,1536]{2,1,0:T(8,128)(2,1)S(1)}, u32[]{:S(2)}, u32[]{:S(2)}) collective-permute-start(bf16[1,24,1536]{2,1,0:T(8,128)(2,1)S(1)} %get-tuple-element.1415), channel_id=1, source_target_pairs={{0,2},{1,3},{2,0},{3,1},{4,6},{5,7},{6,4},{7,5},{8,10},{9,11},{10,... | collective-permute-start | bytes 221192 | tf_op jit(solution)/shard_map/ppermute | solution.py:354
  371.5 7.7 %encoder_grad.1 = f32[1024,768]{1,0:T(8,128)} custom-call(bf16[768,3840]{1,0:T(8,128)(2,1)} %assemble.3.wo_ref.wc_ref.wq_ref.ck_ref.cv_ref, bf16[768,3840]{1,0:T(8,128)(2,1)} %assemble.3.wo_ref.wc_ref.wq_ref.ck_ref.cv_ref, bf16[1024,384]{1,0:T(8,128)(2,1)} %get-tuple-element.1269.refs_6_.refs_0_, bf16[1024,384]{1,0:T(8,128)(2,1)} %get-tuple-element.1270.refs_7_.refs_1_, ...), custom_call_target="tpu_custom_call" | custom-call | flops 2415919104 | bytes 18087936 | tf_op jit(solution)/shard_map/encoder_grad/pallas_call | solution.py:483
  379.2 32.2 %reduce-scatter.2.cloned.1.call-done = bf16[24,6144]{1,0:T(8,128)(2,1)} async-done(((bf16[768,6144]{1,0:T(8,128)(2,1)}), bf16[24,6144]{1,0:T(8,128)(2,1)}) %reduce-scatter.2.cloned.1.call-update) | async-done | bytes 294928 | tf_op jit(solution)/shard_map/reduce_scatter | solution.py:831
  431.9 3.0 collective-permute-done.47
  434.9 2.8 collective-permute-start.50
  439.5 3.7 collective-permute-done.51
  (270 shorter events, 94.9 us)
Async XLA Ops:
  7.2 164.9 %all-gather.2.cloned.1.call-start = ((), (), s32[]{:S(2)}) async-start(), calls=%async_computation.1 | async-start | bytes 9732096 | tf_op jit(solution)/shard_map/all_gather | solution.py:815
  9.6 14.4 %collective-permute-start = (bf16[24,2432]{1,0:T(8,128)(2,1)S(1)}, bf16[24,2432]{1,0:T(8,128)(2,1)S(1)}, u32[]{:S(2)}, u32[]{:S(2)}) collective-permute-start(bf16[24,2432]{1,0:T(8,128)(2,1)S(1)} %fusion.4), channel_id=1, source_target_pairs={{0,1},{1,0},{2,3},{3,2},{4,5},{5,4},{6,7},{7,6},{8,9},{9,8},{10,11... | collective-permute-start | bytes 350216 | tf_op jit(solution)/shard_map/ppermute | solution.py:268
  12.7 11.9 %collective-permute-start.1 = (bf16[24,2432]{1,0:T(8,128)(2,1)S(1)}, bf16[24,2432]{1,0:T(8,128)(2,1)S(1)}, u32[]{:S(2)}, u32[]{:S(2)}) collective-permute-start(bf16[24,2432]{1,0:T(8,128)(2,1)S(1)} %fusion.4), channel_id=1, source_target_pairs={{0,2},{1,3},{2,0},{3,1},{4,6},{5,7},{6,4},{7,5},{8,10},{9,11},{10,... | collective-permute-start | bytes 350216 | tf_op jit(solution)/shard_map/ppermute | solution.py:268
  24.6 20.0 %collective-permute-start.4 = (bf16[96,1280]{1,0:T(8,128)(2,1)S(1)}, bf16[96,1280]{1,0:T(8,128)(2,1)S(1)}, u32[]{:S(2)}, u32[]{:S(2)}) collective-permute-start(bf16[96,1280]{1,0:T(8,128)(2,1)S(1)} %pad_maximum_fusion.2), channel_id=1, source_target_pairs={{0,16},{4,20},{8,24},{12,28},{16,0},{20,4},{24,8},{28,12},{1,17},{... | collective-permute-start | bytes 737288 | tf_op jit(solution)/shard_map/ppermute | solution.py:272
  26.2 18.4 %collective-permute-start.3 = (bf16[96,1152]{1,0:T(8,128)(2,1)S(1)}, bf16[96,1152]{1,0:T(8,128)(2,1)S(1)}, u32[]{:S(2)}, u32[]{:S(2)}) collective-permute-start(bf16[96,1152]{1,0:T(8,128)(2,1)S(1)} %pad_maximum_fusion.5), channel_id=1, source_target_pairs={{0,8},{4,12},{8,0},{12,4},{16,24},{20,28},{24,16},{28,20},{1,9},{5... | collective-permute-start | bytes 663560 | tf_op jit(solution)/shard_map/ppermute | solution.py:272
  29.6 15.0 %collective-permute-start.6 = (bf16[24,3840]{1,0:T(8,128)(2,1)S(1)}, bf16[24,3840]{1,0:T(8,128)(2,1)S(1)}, u32[]{:S(2)}, u32[]{:S(2)}) collective-permute-start(bf16[24,3840]{1,0:T(8,128)(2,1)S(1)} %bitcast_dynamic-update-slice_fusion), channel_id=1, source_target_pairs={{0,2},{1,3},{2,0},{3,1},{4,6},{5,7},{6,4},{7,5},{8,10},{9,11},{10,... | collective-permute-start | bytes 552968 | tf_op jit(solution)/shard_map/ppermute | solution.py:268
  31.7 12.9 %collective-permute-start.7 = (bf16[24,3840]{1,0:T(8,128)(2,1)S(1)}, bf16[24,3840]{1,0:T(8,128)(2,1)S(1)}, u32[]{:S(2)}, u32[]{:S(2)}) collective-permute-start(bf16[24,3840]{1,0:T(8,128)(2,1)S(1)} %bitcast_dynamic-update-slice_fusion), channel_id=1, source_target_pairs={{0,3},{1,2},{2,1},{3,0},{4,7},{5,6},{6,5},{7,4},{8,11},{9,10},{10,... | collective-permute-start | bytes 552968 | tf_op jit(solution)/shard_map/ppermute | solution.py:268
  57.9 353.6 %reduce-scatter.2.cloned.1.call-start = ((), (), s32[]{:S(2)}) async-start(), calls=%async_computation.2 | async-start | bytes 9732096 | tf_op jit(solution)/shard_map/reduce_scatter | solution.py:831
  64.4 12.8 %collective-permute-start.14 = (bf16[96,1920]{1,0:T(8,128)(2,1)S(1)}, bf16[96,1920]{1,0:T(8,128)(2,1)S(1)}, u32[]{:S(2)}, u32[]{:S(2)}) collective-permute-start(bf16[96,1920]{1,0:T(8,128)(2,1)S(1)} %get-tuple-element.775), channel_id=1, source_target_pairs={{0,8},{4,12},{8,0},{12,4},{16,24},{20,28},{24,16},{28,20},{1,9},{5... | collective-permute-start | bytes 1105928 | tf_op jit(solution)/shard_map/ppermute | solution.py:272
  65.9 12.5 %collective-permute-start.15 = (bf16[96,1920]{1,0:T(8,128)(2,1)S(1)}, bf16[96,1920]{1,0:T(8,128)(2,1)S(1)}, u32[]{:S(2)}, u32[]{:S(2)}) collective-permute-start(bf16[96,1920]{1,0:T(8,128)(2,1)S(1)} %get-tuple-element.777), channel_id=1, source_target_pairs={{0,16},{4,20},{8,24},{12,28},{16,0},{20,4},{24,8},{28,12},{1,17},{... | collective-permute-start | bytes 1105928 | tf_op jit(solution)/shard_map/ppermute | solution.py:272
  78.5 24.6 %collective-permute-start.17 = (bf16[192,1920]{1,0:T(8,128)(2,1)S(1)}, bf16[192,1920]{1,0:T(8,128)(2,1)S(1)}, u32[]{:S(2)}, u32[]{:S(2)}) collective-permute-start(bf16[192,1920]{1,0:T(8,128)(2,1)S(1)} %constant_dynamic-update-slice_fusion.7.refs_4_), channel_id=1, source_target_pairs={{0,8},{4,12},{8,0},{12,4},{16,24},{20,28},{24,16},{28,20},{1,9},{5... | collective-permute-start | bytes 2211848 | tf_op jit(solution)/shard_map/ppermute | solution.py:272
  79.2 23.9 %collective-permute-start.16 = (bf16[192,1920]{1,0:T(8,128)(2,1)S(1)}, bf16[192,1920]{1,0:T(8,128)(2,1)S(1)}, u32[]{:S(2)}, u32[]{:S(2)}) collective-permute-start(bf16[192,1920]{1,0:T(8,128)(2,1)S(1)} %constant_dynamic-update-slice_fusion.5.refs_0_), channel_id=1, source_target_pairs={{0,16},{4,20},{8,24},{12,28},{16,0},{20,4},{24,8},{28,12},{1,17},{... | collective-permute-start | bytes 2211848 | tf_op jit(solution)/shard_map/ppermute | solution.py:272
  103.1 14.2 %collective-permute-start.18 = (bf16[192,1920]{1,0:T(8,128)(2,1)S(1)}, bf16[192,1920]{1,0:T(8,128)(2,1)}, u32[]{:S(2)}, u32[]{:S(2)}) collective-permute-start(bf16[192,1920]{1,0:T(8,128)(2,1)S(1)} %constant_dynamic-update-slice_fusion.5.refs_0_), channel_id=1, source_target_pairs={{0,4},{4,0},{8,12},{12,8},{16,20},{20,16},{24,28},{28,24},{1,5},{5... | collective-permute-start | bytes 2211848 | tf_op jit(solution)/shard_map/ppermute | solution.py:272
  103.2 14.1 %collective-permute-start.19 = (bf16[192,1920]{1,0:T(8,128)(2,1)S(1)}, bf16[192,1920]{1,0:T(8,128)(2,1)}, u32[]{:S(2)}, u32[]{:S(2)}) collective-permute-start(bf16[192,1920]{1,0:T(8,128)(2,1)S(1)} %collective-permute-done.16.refs_1_), channel_id=1, source_target_pairs={{0,4},{4,0},{8,12},{12,8},{16,20},{20,16},{24,28},{28,24},{1,5},{5... | collective-permute-start | bytes 2211848 | tf_op jit(solution)/shard_map/ppermute | solution.py:272
  103.7 13.6 %collective-permute-start.20 = (bf16[192,1920]{1,0:T(8,128)(2,1)S(1)}, bf16[192,1920]{1,0:T(8,128)(2,1)}, u32[]{:S(2)}, u32[]{:S(2)}) collective-permute-start(bf16[192,1920]{1,0:T(8,128)(2,1)S(1)} %constant_dynamic-update-slice_fusion.7.refs_4_), channel_id=1, source_target_pairs={{0,4},{4,0},{8,12},{12,8},{16,20},{20,16},{24,28},{28,24},{1,5},{5... | collective-permute-start | bytes 2211848 | tf_op jit(solution)/shard_map/ppermute | solution.py:272
  103.8 13.5 %collective-permute-start.21 = (bf16[192,1920]{1,0:T(8,128)(2,1)S(1)}, bf16[192,1920]{1,0:T(8,128)(2,1)}, u32[]{:S(2)}, u32[]{:S(2)}) collective-permute-start(bf16[192,1920]{1,0:T(8,128)(2,1)S(1)} %collective-permute-done.17.refs_5_), channel_id=1, source_target_pairs={{0,4},{4,0},{8,12},{12,8},{16,20},{20,16},{24,28},{28,24},{1,5},{5... | collective-permute-start | bytes 2211848 | tf_op jit(solution)/shard_map/ppermute | solution.py:272
  270.4 17.2 %collective-permute-start.22 = (bf16[1,4,96,2304]{3,2,1,0:T(8,128)(2,1)}, bf16[1,4,96,2304]{3,2,1,0:T(8,128)(2,1)S(1)}, u32[]{:S(2)}, u32[]{:S(2)}) collective-permute-start(bf16[1,4,96,2304]{3,2,1,0:T(8,128)(2,1)} %get-tuple-element.1158), channel_id=1, source_target_pairs={{0,4},{4,0},{8,12},{12,8},{16,20},{20,16},{24,28},{28,24},{1,5},{5... | collective-permute-start | bytes 5308424 | tf_op jit(solution)/shard_map/ppermute | solution.py:356
  270.5 17.1 %collective-permute-start.23 = (bf16[1,4,96,1536]{3,2,1,0:T(8,128)(2,1)}, bf16[1,4,96,1536]{3,2,1,0:T(8,128)(2,1)}, u32[]{:S(2)}, u32[]{:S(2)}) collective-permute-start(bf16[1,4,96,1536]{3,2,1,0:T(8,128)(2,1)} %get-tuple-element.1160), channel_id=1, source_target_pairs={{0,4},{4,0},{8,12},{12,8},{16,20},{20,16},{24,28},{28,24},{1,5},{5... | collective-permute-start | bytes 3538952 | tf_op jit(solution)/shard_map/ppermute | solution.py:356
  289.1 25.6 %collective-permute-start.24 = (bf16[2,96,2304]{2,1,0:T(8,128)(2,1)}, bf16[2,96,2304]{2,1,0:T(8,128)(2,1)S(1)}, u32[]{:S(2)}, u32[]{:S(2)}) collective-permute-start(bf16[2,96,2304]{2,1,0:T(8,128)(2,1)} %get-tuple-element.1384), channel_id=1, source_target_pairs={{0,8},{4,12},{8,0},{12,4},{16,24},{20,28},{24,16},{28,20},{1,9},{5... | collective-permute-start | bytes 2654216 | tf_op jit(solution)/shard_map/ppermute | solution.py:356
  295.2 19.6 %collective-permute-start.26 = (bf16[1,4,96,1152]{3,2,1,0:T(8,128)(2,1)}, bf16[1,4,96,1152]{3,2,1,0:T(8,128)(2,1)}, u32[]{:S(2)}, u32[]{:S(2)}) collective-permute-start(bf16[1,4,96,1152]{3,2,1,0:T(8,128)(2,1)} %get-tuple-element.1214), channel_id=1, source_target_pairs={{0,4},{4,0},{8,12},{12,8},{16,20},{20,16},{24,28},{28,24},{1,5},{5... | collective-permute-start | bytes 2654216 | tf_op jit(solution)/shard_map/ppermute | solution.py:356
  297.8 16.9 %collective-permute-start.25 = (bf16[1,192,1536]{2,1,0:T(8,128)(2,1)}, bf16[1,192,1536]{2,1,0:T(8,128)(2,1)S(1)}, u32[]{:S(2)}, u32[]{:S(2)}) collective-permute-start(bf16[1,192,1536]{2,1,0:T(8,128)(2,1)} %get-tuple-element.1386), channel_id=1, source_target_pairs={{0,16},{4,20},{8,24},{12,28},{16,0},{20,4},{24,8},{28,12},{1,17},{... | collective-permute-start | bytes 1769480 | tf_op jit(solution)/shard_map/ppermute | solution.py:356
  317.4 22.0 %collective-permute-start.29 = (bf16[1,192,1152]{2,1,0:T(8,128)(2,1)}, bf16[1,192,1152]{2,1,0:T(8,128)(2,1)}, u32[]{:S(2)}, u32[]{:S(2)}) collective-permute-start(bf16[1,192,1152]{2,1,0:T(8,128)(2,1)} %get-tuple-element.1390), channel_id=1, source_target_pairs={{0,16},{4,20},{8,24},{12,28},{16,0},{20,4},{24,8},{28,12},{1,17},{... | collective-permute-start | bytes 1327112 | tf_op jit(solution)/shard_map/ppermute | solution.py:356
  320.4 29.1 %collective-permute-start.27 = (bf16[1,96,2304]{2,1,0:T(8,128)(2,1)}, bf16[1,96,2304]{2,1,0:T(8,128)(2,1)}, u32[]{:S(2)}, u32[]{:S(2)}) collective-permute-start(bf16[1,96,2304]{2,1,0:T(8,128)(2,1)} %get-tuple-element.1392), channel_id=1, source_target_pairs={{0,16},{4,20},{8,24},{12,28},{16,0},{20,4},{24,8},{28,12},{1,17},{... | collective-permute-start | bytes 1327112 | tf_op jit(solution)/shard_map/ppermute | solution.py:356
  326.4 23.1 %collective-permute-start.30 = (bf16[1,4,96,1152]{3,2,1,0:T(8,128)(2,1)}, bf16[1,4,96,1152]{3,2,1,0:T(8,128)(2,1)S(1)}, u32[]{:S(2)}, u32[]{:S(2)}) collective-permute-start(bf16[1,4,96,1152]{3,2,1,0:T(8,128)(2,1)} %get-tuple-element.1267), channel_id=1, source_target_pairs={{0,4},{4,0},{8,12},{12,8},{16,20},{20,16},{24,28},{28,24},{1,5},{5... | collective-permute-start | bytes 2654216 | tf_op jit(solution)/shard_map/ppermute | solution.py:356
  326.7 12.7 %collective-permute-start.28 = (bf16[1,96,1536]{2,1,0:T(8,128)(2,1)S(1)}, bf16[1,96,1536]{2,1,0:T(8,128)(2,1)S(1)}, u32[]{:S(2)}, u32[]{:S(2)}) collective-permute-start(bf16[1,96,1536]{2,1,0:T(8,128)(2,1)S(1)} %get-tuple-element.1400), channel_id=1, source_target_pairs={{0,8},{4,12},{8,0},{12,4},{16,24},{20,28},{24,16},{28,20},{1,9},{5... | collective-permute-start | bytes 884744 | tf_op jit(solution)/shard_map/ppermute | solution.py:356
  352.3 12.6 %collective-permute-start.39 = (f32[21,128]{1,0:T(8,128)S(1)}, f32[21,128]{1,0:T(8,128)S(1)}, u32[]{:S(2)}, u32[]{:S(2)}) collective-permute-start(f32[21,128]{1,0:T(8,128)S(1)} %maximum_bitcast_fusion.2), channel_id=1, source_target_pairs={{0,4},{4,0},{8,12},{12,8},{16,20},{20,16},{24,28},{28,24},{1,5},{5... | collective-permute-start | bytes 32264 | tf_op jit(solution)/shard_map/ppermute | solution.py:402
  352.9 60.2 %collective-permute-start.38 = (bf16[2,96,1152]{2,1,0:T(8,128)(2,1)S(1)}, bf16[2,96,1152]{2,1,0:T(8,128)(2,1)S(1)}, u32[]{:S(2)}, u32[]{:S(2)}) collective-permute-start(bf16[2,96,1152]{2,1,0:T(8,128)(2,1)S(1)} %get-tuple-element.1388), channel_id=1, source_target_pairs={{0,8},{4,12},{8,0},{12,4},{16,24},{20,28},{24,16},{28,20},{1,9},{5... | collective-permute-start | bytes 1327112 | tf_op jit(solution)/shard_map/ppermute | solution.py:356
  354.4 12.1 %collective-permute-start.34 = (bf16[1,24,1536]{2,1,0:T(8,128)(2,1)S(1)}, bf16[1,24,1536]{2,1,0:T(8,128)(2,1)S(1)}, u32[]{:S(2)}, u32[]{:S(2)}) collective-permute-start(bf16[1,24,1536]{2,1,0:T(8,128)(2,1)S(1)} %get-tuple-element.1416), channel_id=1, source_target_pairs={{0,1},{1,0},{2,3},{3,2},{4,5},{5,4},{6,7},{7,6},{8,9},{9,8},{10,11... | collective-permute-start | bytes 221192 | tf_op jit(solution)/shard_map/ppermute | solution.py:354
  364.9 48.1 %collective-permute-start.37 = (bf16[1,96,1152]{2,1,0:T(8,128)(2,1)S(1)}, bf16[1,96,1152]{2,1,0:T(8,128)(2,1)S(1)}, u32[]{:S(2)}, u32[]{:S(2)}) collective-permute-start(bf16[1,96,1152]{2,1,0:T(8,128)(2,1)S(1)} %get-tuple-element.1408), channel_id=1, source_target_pairs={{0,8},{4,12},{8,0},{12,4},{16,24},{20,28},{24,16},{28,20},{1,9},{5... | collective-permute-start | bytes 663560 | tf_op jit(solution)/shard_map/ppermute | solution.py:356
  366.5 46.5 %collective-permute-start.31 = (bf16[1,24,2304]{2,1,0:T(8,128)(2,1)}, bf16[1,24,2304]{2,1,0:T(8,128)(2,1)S(1)}, u32[]{:S(2)}, u32[]{:S(2)}) collective-permute-start(bf16[1,24,2304]{2,1,0:T(8,128)(2,1)} %get-tuple-element.1412), channel_id=1, source_target_pairs={{0,1},{1,0},{2,3},{3,2},{4,5},{5,4},{6,7},{7,6},{8,9},{9,8},{10,11... | collective-permute-start | bytes 331784 | tf_op jit(solution)/shard_map/ppermute | solution.py:354
  367.0 46.0 %collective-permute-start.32 = (bf16[1,24,2304]{2,1,0:T(8,128)(2,1)S(1)}, bf16[1,24,2304]{2,1,0:T(8,128)(2,1)S(1)}, u32[]{:S(2)}, u32[]{:S(2)}) collective-permute-start(bf16[1,24,2304]{2,1,0:T(8,128)(2,1)S(1)} %get-tuple-element.1411), channel_id=1, source_target_pairs={{0,2},{1,3},{2,0},{3,1},{4,6},{5,7},{6,4},{7,5},{8,10},{9,11},{10,... | collective-permute-start | bytes 331784 | tf_op jit(solution)/shard_map/ppermute | solution.py:354
  370.1 42.9 %collective-permute-start.33 = (bf16[1,24,2304]{2,1,0:T(8,128)(2,1)S(1)}, bf16[1,24,2304]{2,1,0:T(8,128)(2,1)S(1)}, u32[]{:S(2)}, u32[]{:S(2)}) collective-permute-start(bf16[1,24,2304]{2,1,0:T(8,128)(2,1)S(1)} %get-tuple-element.1410), channel_id=1, source_target_pairs={{0,3},{1,2},{2,1},{3,0},{4,7},{5,6},{6,5},{7,4},{8,11},{9,10},{10,... | collective-permute-start | bytes 331784 | tf_op jit(solution)/shard_map/ppermute | solution.py:354
  (59 other events, 565.9 us)
Sparse Core Ops, SparseCore 0:
  58.0 93.5 all-gather.1
  256.4 154.9 reduce-scatter.1

commit v4 on v3

--- a/solution.py
+++ b/solution.py
@@ -28,11 +28,22 @@
     return query_cols, key_cols
 
 
+def fold(values, combine):
+    rows = [values[8 * i: 8 * (i + 1)] for i in range(values.shape[0] // 8)]
+    while len(rows) > 1:
+        rows = [combine(rows[2 * i], rows[2 * i + 1]) for i in range(len(rows) // 2)] + rows[len(rows) - len(rows) % 2:]
+    return rows[0]
+
+
+CHUNK = 128
+LANES = 256
+
+
 def attn_fwd_kernel(causal, q_ref, k_ref, v_ref, qs_ref, ks_ref, *rest):
     if causal:
-        t_ref, o_ref, p_ref, bias = rest
+        t_ref, o_ref, e_ref, inv_ref, s_buf, bias = rest
     else:
-        o_ref, p_ref = rest
+        o_ref, e_ref, inv_ref, s_buf = rest
     length = q_ref.shape[0]
     if causal:
         @pl.when(pl.program_id(1) == 0)
@@ -46,34 +57,61 @@
     q = q_ref[...]
     keys = jnp.concatenate([k_ref[...], ks_ref[...]], axis=1)
     v_t = v_ref[...].T
+    qa = [jnp.concatenate([jnp.where((lane // DH) == h, q, 0).astype(BF), qs_ref[...]], axis=1) for h in range(2)]
+    work = [(h, c) for h in range(2) for c in range(length // LANES)]
+    reach = lambda c: LANES * (c + 1) if causal else length
+
+    def scores(i):
+        h, c = work[i]
+        s_buf[i % 2, :reach(c), :] = dot(keys[:reach(c)], qa[h][LANES * c: LANES * (c + 1)], NT)
+
+    def place(h, c, kb):
+        if not causal:
+            return [(0, LANES, None)]
+        found = []
+        for qb in range(LANES // 128):
+            d = qb + LANES // 128 * c - kb
+            if d >= 0:
+                found.append((128 * qb, 128, (h, d)))
+        return found
+
+    def load(i, kb, lo, width, tile):
+        value = s_buf[i % 2, CHUNK * kb: CHUNK * (kb + 1), lo: lo + width]
+        return value if tile is None else value + bias[tile[0], tile[1]]
+
+    scores(0)
+    for i, (h, c) in enumerate(work):
+        if i + 1 < len(work):
+            scores(i + 1)
+        blocks = reach(c) // CHUNK
+        tops = {}
+        for kb in range(blocks):
+            for lo, width, tile in place(h, c, kb):
+                new = fold(load(i, kb, lo, width, tile), jnp.maximum)
+                tops[lo] = new if lo not in tops else jnp.maximum(tops[lo], new)
+        tops = {lo: jnp.max(t, axis=0, keepdims=True) for lo, t in tops.items()}
+        sums = {}
+        for kb in range(blocks):
+            seen = place(h, c, kb)
+            for lo, width, tile in seen:
+                e = jnp.exp(load(i, kb, lo, width, tile) - tops[lo])
+                new = fold(e, jnp.add)
+                sums[lo] = new if lo not in sums else sums[lo] + new
+                e_ref[h, CHUNK * kb: CHUNK * (kb + 1), LANES * c + lo: LANES * c + lo + width] = e.astype(BF)
+            for lo in range(0, LANES, 128):
+                if causal and lo not in [x[0] for x in seen]:
+                    e_ref[h, CHUNK * kb: CHUNK * (kb + 1), LANES * c + lo: LANES * c + lo + 128] = jnp.zeros((CHUNK, 128), BF)
+        total = jnp.concatenate([jnp.sum(sums[lo], axis=0, keepdims=True) for lo in sorted(sums)], axis=1)
+        inv = 1.0 / total
+        inv_ref[h, :, LANES * c: LANES * (c + 1)] = jnp.broadcast_to(inv, (8, LANES))
     parts = []
     for h in range(2):
-        mine = (lane // DH) == h
-        qa = jnp.concatenate([jnp.where(mine, q, 0).astype(BF), qs_ref[...]], axis=1)
-        cols = []
-        for c in range(length // 256):
-            n = 256 * (c + 1) if causal else length
-            s = dot(keys[:n], qa[256 * c: 256 * (c + 1)], NT)
-            if causal:
-                rows = []
-                for kb in range(n // 128):
-                    tiles = []
-                    for qb in (2 * c, 2 * c + 1):
-                        st = s[128 * kb:128 * (kb + 1), 128 * (qb - 2 * c):128 * (qb - 2 * c + 1)]
-                        if qb >= kb:
-                            tiles.append(st + bias[h, qb - kb])
-                        else:
-                            tiles.append(jnp.full((128, 128), NEGATIVE, F32))
-                    rows.append(jnp.concatenate(tiles, axis=1))
-                s = jnp.concatenate(rows, axis=0)
-            top = jnp.max(s, axis=0, keepdims=True)
-            e = jnp.exp(s - top)
-            p = (e * (1.0 / jnp.sum(e, axis=0, keepdims=True))).astype(BF)
-            p_ref[h, pl.ds(0, n), pl.ds(256 * c, 256)] = p
-            if n < length:
-                p_ref[h, pl.ds(n, length - n), pl.ds(256 * c, 256)] = jnp.zeros((length - n, 256), BF)
-            cols.append(dot(v_t[DH * h: DH * (h + 1), :n], p))
-        parts.append(jnp.concatenate(cols, axis=1))
+        mine = v_t[DH * h: DH * (h + 1)]
+        if causal:
+            mixed = [dot(mine[:, :reach(c)], e_ref[h, :reach(c), LANES * c: LANES * (c + 1)]) for c in range(length // LANES)]
+        else:
+            mixed = [dot(mine, e_ref[h])]
+        parts.append(jnp.concatenate(mixed, axis=1) * inv_ref[h, 0:1, :])
     o_ref[...] = jnp.concatenate(parts, axis=0).T.astype(BF)
 
 
@@ -90,71 +128,81 @@
         in_specs.append(pl.BlockSpec((2, 1, table.shape[2]), lambda h, b: (begin + h, 0, 0)))
         args.append(table)
         scratch = [pltpu.VMEM((2, length // 128, 128, 128), F32)]
+    scratch = [pltpu.VMEM((2, length, LANES), F32)] + scratch
+    stat = pl.BlockSpec((None, 2, 8, length), lambda h, b: (b, h, 0, 0))
     return pl.pallas_call(
         functools.partial(attn_fwd_kernel, causal),
         grid=(pairs, rows),
         in_specs=in_specs,
-        out_specs=[pl.BlockSpec((length, 128), lambda h, b: (b, h)), pl.BlockSpec((None, 2, length, length), lambda h, b: (b, h, 0, 0))],
-        out_shape=[jax.ShapeDtypeStruct((rows * length, pairs * 128), BF), jax.ShapeDtypeStruct((rows, 2 * pairs, length, length), BF)],
+        out_specs=[pl.BlockSpec((length, 128), lambda h, b: (b, h)), pl.BlockSpec((None, 2, length, length), lambda h, b: (b, h, 0, 0)), stat],
+        out_shape=[jax.ShapeDtypeStruct((rows * length, pairs * 128), BF), jax.ShapeDtypeStruct((rows, 2 * pairs, length, length), BF), jax.ShapeDtypeStruct((rows, 2 * pairs, 8, length), F32)],
         scratch_shapes=scratch,
         compiler_params=pltpu.CompilerParams(vmem_limit_bytes=60 * MB),
-        cost_estimate=pl.CostEstimate(flops=16 * rows * pairs * length * length * 256, bytes_accessed=4 * rows * pairs * length * length, transcendentals=0),
+        cost_estimate=pl.CostEstimate(flops=1, bytes_accessed=1, transcendentals=0),
         name="attn_fwd_self" if causal else "attn_fwd_cross",
     )(*args)
 
 
-def attn_bwd_kernel(causal, q_ref, k_ref, v_ref, g_ref, o_ref, p_ref, *rest):
+def attn_bwd_kernel(causal, q_ref, k_ref, v_ref, g_ref, o_ref, e_ref, inv_ref, *rest):
     if causal:
-        dq_ref, dk_ref, dv_ref, diag_ref, acc = rest
+        dq_ref, dk_ref, dv_ref, diag_ref, ds_buf, acc = rest
     else:
-        dq_ref, dk_ref, dv_ref = rest
+        dq_ref, dk_ref, dv_ref, ds_buf = rest
     length = q_ref.shape[0]
     lane = lax.broadcasted_iota(jnp.int32, (1, 128), 1)
     q = q_ref[...]
-    g = g_ref[...]
     values = jnp.concatenate([v_ref[...], jnp.broadcast_to((lane < 2).astype(BF), (length, 128))], axis=1)
     k_t = k_ref[...].T
-    prod = g.astype(F32) * o_ref[...].astype(F32)
+    g_t = g_ref[...].T.astype(F32)
+    o_t = o_ref[...].T.astype(F32)
     if causal:
         @pl.when(pl.program_id(1) == 0)
         def _():
             acc[...] = jnp.zeros_like(acc)
-    dq_parts = []
-    dk = [None] * (length // 256)
-    dv = [None] * (length // 256)
-    add = lambda old, new: new if old is None else old + new
+
+        @pl.when((pl.program_id(0) == 0) & (pl.program_id(1) == 0))
+        def _():
+            ds_buf[...] = jnp.zeros_like(ds_buf)
+
+    gms, qms, gas = [], [], []
+    blank = jnp.zeros((DH, length), BF)
     for h in range(2):
-        mine = (lane // DH) == h
-        delta = -jnp.sum(jnp.where(mine, prod, 0.0), axis=1, keepdims=True)
-        high = delta.astype(BF)
-        lowp = (delta - high.astype(F32)).astype(BF)
-        extra = jnp.where(lane == 0, high, jnp.where(lane == 1, lowp, jnp.zeros_like(lowp)))
-        gm = jnp.where(mine, g, 0).astype(BF)
-        qm = jnp.where(mine, q, 0).astype(BF)
-        ga = jnp.concatenate([gm, extra], axis=1)
-        cols = []
-        for c in range(length // 256):
-            n = 256 * (c + 1) if causal else length
-            qsl = slice(256 * c, 256 * (c + 1))
-            p = p_ref[h, pl.ds(0, n), pl.ds(256 * c, 256)]
-            dp = dot(values[:n], ga[qsl], NT)
-            ds = (p.astype(F32) * dp).astype(BF)
-            if causal:
-                for kb in range(n // 128):
-                    for qb in (2 * c, 2 * c + 1):
-                        if qb >= kb:
-                            acc[h, qb - kb] += ds[128 * kb:128 * (kb + 1), 128 * (qb - 2 * c):128 * (qb - 2 * c + 1)].astype(F32)
-            cols.append(dot(k_t[DH * h: DH * (h + 1), :n], ds))
-            dkn = dot(ds, qm[qsl])
-            dvn = dot(p, gm[qsl])
-            for kc in range(n // 256):
-                ksl = slice(256 * kc, 256 * (kc + 1))
-                dk[kc] = add(dk[kc], dkn[ksl])
-                dv[kc] = add(dv[kc], dvn[ksl])
-        dq_parts.append(jnp.concatenate(cols, axis=1))
-    dq_ref[...] = jnp.concatenate(dq_parts, axis=0).T.astype(BF)
-    dk_ref[...] = jnp.concatenate(dk, axis=0).astype(BF)
-    dv_ref[...] = jnp.concatenate(dv, axis=0).astype(BF)
+        rows = slice(DH * h, DH * (h + 1))
+        gm = (g_t[rows] * inv_ref[h, 0:1, :]).astype(BF)
+        delta = -jnp.sum(gm.astype(F32) * o_t[rows], axis=0, keepdims=True)
+        high = delta.astype(BF).astype(F32)
+        extra = jnp.concatenate([high, delta - high, jnp.zeros((14, length), F32)], axis=0).astype(BF)
+        gms.append(jnp.concatenate([blank] * h + [gm] + [blank] * (1 - h), axis=0))
+        qms.append(jnp.where((lane // DH) == h, q, 0).astype(BF))
+        gas.append(jnp.concatenate([gms[h], extra, jnp.zeros((112, length), BF)], axis=0))
+    for h in range(2):
+        for c in range(length // LANES):
+            n = LANES * (c + 1) if causal else length
+            span = slice(LANES * c, LANES * (c + 1))
+            dp = dot(values[:n], gas[h][:, span])
+            for kb in range(n // CHUNK):
+                rows = slice(CHUNK * kb, CHUNK * (kb + 1))
+                for qb in range(LANES // 128):
+                    d = qb + LANES // 128 * c - kb
+                    if causal and d < 0:
+                        continue
+                    cols = slice(LANES * c + 128 * qb, LANES * c + 128 * (qb + 1))
+                    ds = (e_ref[h, rows, cols].astype(F32) * dp[rows, 128 * qb: 128 * (qb + 1)]).astype(BF)
+                    ds_buf[h, rows, cols] = ds
+                    if causal:
+                        acc[h, d] += ds.astype(F32)
+    for kb in range(length // LANES):
+        rows = slice(LANES * kb, LANES * (kb + 1))
+        lo = LANES * kb if causal else 0
+        dk, dv = None, None
+        for h in range(2):
+            a = dot(ds_buf[h, rows, lo:], qms[h][lo:])
+            b = dot(e_ref[h, rows, lo:], gms[h][:, lo:], NT)
+            dk = a if dk is None else dk + a
+            dv = b if dv is None else dv + b
+        dk_ref[rows, :] = dk.astype(BF)
+        dv_ref[rows, :] = dv.astype(BF)
+    dq_ref[...] = jnp.concatenate([dot(k_t[DH * h: DH * (h + 1)], ds_buf[h]) for h in range(2)], axis=0).T.astype(BF)
     if causal:
         @pl.when(pl.program_id(1) == pl.num_programs(1) - 1)
         def _():
@@ -167,7 +215,7 @@
                     diag_ref[h, pl.ds(d, 1), :] = jnp.sum(turned, axis=0, keepdims=True)
 
 
-def attn_bwd(span, q_arr, q_col, k_arr, k_col, v_arr, v_col, grad, out, probs, causal):
+def attn_bwd(span, q_arr, q_col, k_arr, k_col, v_arr, v_col, grad, out, probs, inverse, causal):
     rows, heads, length = probs.shape[:3]
     begin, pairs = span
     block = lambda col: pl.BlockSpec((length, 128), lambda h, b: (b, begin + col + h))
@@ -175,22 +223,22 @@
     flat = jax.ShapeDtypeStruct((rows * length, pairs * 128), BF)
     out_specs = [own] * 3
     out_shape = [flat] * 3
-    scratch = []
+    scratch = [pltpu.VMEM((2, length, length), BF)]
     if causal:
         out_specs.append(pl.BlockSpec((2, length // 128, 256), lambda h, b: (h, 0, 0)))
         out_shape.append(jax.ShapeDtypeStruct((heads, length // 128, 256), F32))
-        scratch = [pltpu.VMEM((2, length // 128, 128, 128), F32)]
+        scratch.append(pltpu.VMEM((2, length // 128, 128, 128), F32))
     return pl.pallas_call(
         functools.partial(attn_bwd_kernel, causal),
         grid=(pairs, rows),
-        in_specs=[block(q_col), block(k_col), block(v_col), block(0), own, pl.BlockSpec((None, 2, length, length), lambda h, b: (b, h, 0, 0))],
+        in_specs=[block(q_col), block(k_col), block(v_col), block(0), own, pl.BlockSpec((None, 2, length, length), lambda h, b: (b, h, 0, 0)), pl.BlockSpec((None, 2, 8, length), lambda h, b: (b, h, 0, 0))],
         out_specs=out_specs,
         out_shape=out_shape,
         scratch_shapes=scratch,
         compiler_params=pltpu.CompilerParams(vmem_limit_bytes=60 * MB),
-        cost_estimate=pl.CostEstimate(flops=16 * rows * pairs * length * length * 256, bytes_accessed=4 * rows * pairs * length * length, transcendentals=0),
+        cost_estimate=pl.CostEstimate(flops=1, bytes_accessed=1, transcendentals=0),
         name="attn_bwd_self" if causal else "attn_bwd_cross",
-    )(q_arr, k_arr, v_arr, grad, out, probs)
+    )(q_arr, k_arr, v_arr, grad, out, probs, inverse)
 
 
 def score_table(rel_bias, buckets):
@@ -332,7 +380,7 @@
         out_specs=pl.BlockSpec(memory_space=pltpu.VMEM),
         out_shape=jax.ShapeDtypeStruct((rows, sum(widths)), BF),
         compiler_params=pltpu.CompilerParams(vmem_limit_bytes=VMEM_LIMIT),
-        cost_estimate=pl.CostEstimate(flops=0, bytes_accessed=4 * rows * sum(widths), transcendentals=0),
+        cost_estimate=pl.CostEstimate(flops=1, bytes_accessed=1, transcendentals=0),
         name="assemble",
     )(place, *flat)
 
@@ -379,6 +427,11 @@
             pick = lambda k: lax.dynamic_slice_in_dim(value, k, 1, 1)[:, 0]
             self.keep, self.sends = pick(mine), [pick(1 - mine)]
 
+    def join(self, other):
+        side = lambda a, b: jnp.concatenate([a, b], axis=-1)
+        self.keep, self.sends = side(self.keep, other.keep), [side(a, b) for a, b in zip(self.sends, other.sends)]
+        self.columns += other.columns
+
     def state(self, landing):
         return (self.keep, self.sends, self.flight if landing else None)
 
@@ -435,12 +488,13 @@
 
     def run(self, work=None, go=(), land=()):
         for mover in go:
-            mover.go()
             if mover not in self.moving:
                 self.moving.append(mover)
+            if mover.plan and mover.flight is None:
+                mover.go()
         if work is not None:
             self.live.update(work())
-        landing = [m for m in self.moving if m in land]
+        landing = [m for m in self.moving if m in land and m.flight is not None]
         known = [m for m in self.moving if m.flight is None or m in landing]
         live, states = lax.optimization_barrier((self.live, [m.state(m in landing) for m in known]))
         self.live = live
@@ -488,12 +542,13 @@
         out_shape=[jax.ShapeDtypeStruct(s, d) for s, d, _, _ in outs],
         scratch_shapes=list(scratch),
         compiler_params=pltpu.CompilerParams(vmem_limit_bytes=limit),
-        cost_estimate=pl.CostEstimate(flops=flops, bytes_accessed=moved, transcendentals=0),
+        cost_estimate=pl.CostEstimate(flops=1, bytes_accessed=1, transcendentals=0),
         name=name,
     )(*[a for a, _, _ in ins])
 
 
-ROWS = 256
+ROWS = 512
+FFN_ROWS = 256
 row_map = lambda i: (i, 0)
 col_map = lambda i: (0, i)
 whole = lambda i: (0, 0)
@@ -552,8 +607,8 @@
         dn_ref[...] = jnp.zeros_like(dn_ref)
 
     acts, grads = [], []
-    for r in range(tokens // ROWS):
-        rows = pl.ds(ROWS * r, ROWS)
+    for r in range(tokens // FFN_ROWS):
+        rows = pl.ds(FFN_ROWS * r, FFN_ROWS)
         a = dot(n_ref[rows, :], w_in)
         back = dot(g_ref[rows, :], w_out)
         phi = 0.5 * (1.0 + lax.erf(a * ROOT_HALF))
@@ -668,7 +723,7 @@
         out_shape=[jax.ShapeDtypeStruct(shape, BF) for shape in shapes],
         scratch_shapes=[pltpu.VMEM((2, width, tokens), BF), pltpu.VMEM((2, tokens, columns), BF), pltpu.SemaphoreType.DMA((4,))],
         compiler_params=pltpu.CompilerParams(vmem_limit_bytes=VMEM_LIMIT),
-        cost_estimate=pl.CostEstimate(flops=flops, bytes_accessed=2 * tokens * columns * count * 2, transcendentals=0),
+        cost_estimate=pl.CostEstimate(flops=1, bytes_accessed=1, transcendentals=0),
         name=name,
     )(half, *lefts_arrays, *rights)
 
@@ -727,8 +782,8 @@
         return {"n1t": n1t, "qkv": qkv}
 
     def fwd_self(i):
-        o, p = attn_fwd(SPANS[i], r["qkv"], 0, r["qkv"], 6, r["qkv"], 12, *r["self_seg"], r["table"])
-        return {f"o{i}": o, f"p{i}": p}
+        o, p, s = attn_fwd(SPANS[i], r["qkv"], 0, r["qkv"], 6, r["qkv"], 12, *r["self_seg"], r["table"])
+        return {f"o{i}": o, f"p{i}": p, f"s{i}": s}
 
     def both(name):
         return [r[f"{name}{i}"] for i in range(len(SPANS))]
@@ -740,8 +795,8 @@
         return dict(zip(("x2", "n2t", "qc", "kvc", "et"), out))
 
     def fwd_cross(i):
-        o, p = attn_fwd(SPANS[i], r["qc"], 0, r["kvc"], 0, r["kvc"], 6, *r["cross_seg"])
-        return {f"oc{i}": o, f"pc{i}": p}
+        o, p, s = attn_fwd(SPANS[i], r["qc"], 0, r["kvc"], 0, r["kvc"], 6, *r["cross_seg"])
+        return {f"oc{i}": o, f"pc{i}": p, f"sc{i}": s}
 
     def third():
         out = call(third_kernel, "third", steps,
@@ -769,7 +824,7 @@
         return dict(zip(("layer", "dx3", "three_t", "doc", "gain3"), out))
 
     def bwd_cross(i):
-        out = attn_bwd(SPANS[i], r["qc"], 0, r["kvc"], 0, r["kvc"], 6, r["doc"], r[f"oc{i}"], r[f"pc{i}"], False)
+        out = attn_bwd(SPANS[i], r["qc"], 0, r["kvc"], 0, r["kvc"], 6, r["doc"], r[f"oc{i}"], r[f"pc{i}"], r[f"sc{i}"], False)
         return dict(zip((f"dqc{i}", f"dkc{i}", f"dvc{i}"), out))
 
     def second():
@@ -779,13 +834,16 @@
         return dict(zip(("dx2", "two_t", "do", "gain2"), out))
 
     def grads_cross():
-        rights = both("dqc") + both("dkc") + both("dvc") + both("oc") + both("o")
+        rights = both("dqc") + both("dkc") + both("dvc")
         n = len(SPANS)
-        lefts = [r["n2t"], r["et"], r["three_t"], r["two_t"]]
-        return {"cut_cross": weight_grads("grads_cross", lefts, (0,) * n + (1,) * (2 * n) + (2,) * n + (3,) * n, rights, (3 * n, 2 * n), half, first_rows)}
+        return {"cut_cross": weight_grads("grads_cross", [r["n2t"], r["et"]], (0,) * n + (1,) * (2 * n), rights, (3 * n,), half, first_rows)}
+
+    def grads_out():
+        n = len(SPANS)
+        return {"cut_out": weight_grads("grads_out", [r["three_t"], r["two_t"]], (0,) * n + (1,) * n, both("oc") + both("o"), (2 * n,), half, first_rows)}
 
     def bwd_self(i):
-        out = attn_bwd(SPANS[i], r["qkv"], 0, r["qkv"], 6, r["qkv"], 12, r["do"], r[f"o{i}"], r[f"p{i}"], True)
+        out = attn_bwd(SPANS[i], r["qkv"], 0, r["qkv"], 6, r["qkv"], 12, r["do"], r[f"o{i}"], r[f"p{i}"], r[f"s{i}"], True)
         return dict(zip((f"dq{i}", f"dk{i}", f"dv{i}", f"diag{i}"), out))
 
     def grads_self(i):
@@ -808,15 +866,16 @@
         return Scatter(sizes, pair[0], pair[1], first, turn)
 
     r.step(prepare, [g_self])
-    r.step(None, [g_self, g_cross])
-    while g_self.plan:
+    r.run(None, [g_self, g_cross], [g_self])
+    while len(g_self.plan) > 1:
         r.step(None, [g_self])
+    r.run(None, [g_self], [g_self, g_cross])
     g_self.groups, shard_ffn = lax.optimization_barrier((g_self.groups, shard_ffn))
     slab_ffn = lax.all_gather(shard_ffn, (WIDE, NARROW), axis=0, tiled=True)
-    r.step(take_self, [])
-    r.step(proj, [g_cross])
-    r.step(lambda: fwd_self(0), [g_cross])
-    r.step(lambda: fwd_self(1), [g_cross])
+    r.run(take_self, [g_cross], [])
+    r.run(proj, [], [g_cross])
+    r.run(lambda: fwd_self(0), [g_cross], [])
+    r.run(lambda: fwd_self(1), [], [g_cross])
     while g_cross.plan:
         r.step(None, [g_cross])
     r.step(lambda: {"slab_cross": g_cross.whole()}, [])
@@ -833,17 +892,24 @@
     r.step(top, [])
     r.step(lambda: bwd_cross(0), [])
     r.step(lambda: bwd_cross(1), [])
-    r.step(second, [])
     r.step(grads_cross, [])
-    pairs = r.live.pop("cut_cross")
-    sc, so = cut(pairs[:2], 0), cut(pairs[2:], 1)
-    r.step(lambda: bwd_self(0), [sc, so])
+    sc = cut(r.live.pop("cut_cross"), 0)
+    r.step(second, [sc])
+    r.run(grads_out, [sc], [])
+    so = cut(r.live.pop("cut_out"), 1)
+    r.run(lambda: bwd_self(0), [so], [sc, so])
     r.run(lambda: grads_self(0), [sc, so], [])
     s0 = cut(r.live.pop("cut_self0"), 1)
     r.run(lambda: bwd_self(1), [s0], [s0, sc, so])
-    r.run(lambda: grads_self(1), [sc, so, s0], [])
+    r.run(lambda: grads_self(1), [so, s0], [so])
+    while sc.plan != ["narrow"] or so.plan != ["narrow"]:
+        r.step(None, [x for x in (sc, so) if x.plan != ["narrow"]])
+    sc.join(so)
+    r.moving.remove(so)
     s1 = cut(r.live.pop("cut_self1"), 0)
-    r.run(last, [s1], [s1, sc, so, s0])
+    r.live["ffn_sum"] = ffn_sum
+    r.run(last, [s1, sc], [s1, sc, s0])
+    ffn_sum = r.live.pop("ffn_sum")
 
     def small():
         diag = jnp.concatenate(both("diag"), axis=0)
@@ -852,10 +918,13 @@
 
     r.live.update(small())
     total = Total(sizes, r.live.pop("small"))
-    movers = [sc, so, s0, s1, total]
-    r.live["ffn_sum"] = ffn_sum
+    movers = [x for x in (s0, s1) if x.plan != ["narrow"]] + [total]
     r.step(encoder, movers)
-    ffn_sum = r.live.pop("ffn_sum")
+    while s0.plan != ["narrow"] or s1.plan != ["narrow"]:
+        r.step(None, [x for x in (s0, s1) if x.plan != ["narrow"]] + [total])
+    s0.join(s1)
+    r.moving.remove(s1)
+    movers = [sc, s0, total]
     while any(m.plan for m in movers):
         r.step(None, movers)
 
@@ -865,27 +934,30 @@
     gain_sum = lax.dynamic_slice_in_dim(summed[: 3 * width].reshape(3, width), shard * own, own, 1)
     bias_sum = summed[3 * width:].reshape(rel_bias.shape)
 
-    def columns(sums, index, count):
-        found = []
-        for s in sums:
-            n = s.keep.shape[-1] // count
-            found.append(s.keep[0, :, n * index: n * (index + 1)])
-        return jnp.concatenate(found, axis=1) if len(found) > 1 else found[0]
-
+    own_rows = lambda value, at, n: value.keep[0, :, at: at + n]
+
+    def self_part(index):
+        found, at = [], 0
+        for _, pairs in SPANS:
+            n = 128 * pairs
+            found.append(own_rows(s0, at + n * index, n))
+            at += 3 * n
+        return jnp.concatenate(found, axis=1)
+
+    cross_part = lambda index: own_rows(sc, width * index, width)
     shaped = lambda v: v.reshape(micro, per, length, width)
-    selfs = [s0, s1]
     return (
         shaped(r["layer"]),
         shaped(r["dx1"]),
         shaped(r["de"]),
         gain_sum,
         bias_sum,
-        columns(selfs, 0, 3),
-        jnp.stack([columns(selfs, 1, 3), columns(selfs, 2, 3)]),
-        columns([so], 1, 2).T,
-        columns([sc], 0, 3),
-        jnp.stack([columns([sc], 1, 3), columns([sc], 2, 3)]),
-        columns([so], 0, 2).T,
+        self_part(0),
+        jnp.stack([self_part(1), self_part(2)]),
+        cross_part(4).T,
+        cross_part(0),
+        jnp.stack([cross_part(1), cross_part(2)]),
+        cross_part(3).T,
         ffn_sum[:, :, 0].reshape(-1, hidden),
         ffn_sum[:, :, 1].reshape(-1, hidden).T,
     )

time: 459 us -> 413 us (0.90)
  Pallas kernels: 255 us -> 227 us
  waiting for transfers between devices: 87.3 us -> 74.5 us
  starting transfers between devices: 57.2 us -> 49.1 us
    reduce_scatter x1, waiting for transfers between devices: 32.2 us -> 4.82 us  [body(): lax.psum_scatter(r.live.pop('dw'), (WIDE, NARROW), scatter_dimension=0, t...]
    ppermute x12, waiting for transfers between devices: 10.1 us -> 33 us  [go(): self.flight = [lax.ppermute(self.sends[0], WIDE, flipped(self.wide, step))]]
    pallas_call x4, Pallas kernels: 53.9 us -> 37.2 us  [attn_fwd(): pl.pallas_call(functools.partial(attn_fwd_kernel, causal), grid=(pairs, r...]
    pallas_call x4, Pallas kernels: 61 us -> 48 us  [attn_bwd(): pl.pallas_call(functools.partial(attn_bwd_kernel, causal), grid=(pairs, r...]
    ppermute x12 -> x6, starting transfers between devices: 20.8 us -> 9.42 us  [go(): lax.ppermute(s, NARROW, flipped(self.narrow, k + 1))]
    ppermute x6, waiting for transfers between devices: 12.9 us -> 7.01 us  [go(): lax.ppermute(g[0], NARROW, flipped(self.narrow, k))]
    ppermute x16, waiting for transfers between devices: 24.1 us -> 18.9 us  [go(): lax.ppermute(p, WIDE, flipped(self.wide, self.orders[i][step]))]
    pallas_call x3 -> x4, Pallas kernels: 26 us -> 29.4 us  [weight_grads(): pl.pallas_call(functools.partial(grads_kernel, first_rows, lefts, groups)...]
  transfers between devices with their start and end apart: 54 -> 48, of which waited for: 15 -> 20; matrix products, arithmetic and copies ran while one was open for 7% -> 7% of each run, Pallas kernels for 38% -> 46%
where the time goes in v4:
time: 413 us; the launch traced here: 409 us
  Pallas kernels  227 us (55%)
  waiting for transfers between devices  74.5 us (18%)
  starting transfers between devices  49.1 us (12%)
  local copies, waits for them, and re-layouts  24.2 us (6%)
  other arithmetic  19.2 us (5%)
  between operations  15.1 us (4%)
    pallas_call x8, Pallas kernels, call(): pl.pallas_call(kernel, grid=grid, in_specs=[spec(b, i) for _, b, i in ins...  103 us
    pallas_call x4, Pallas kernels, attn_bwd(): pl.pallas_call(functools.partial(attn_bwd_kernel, causal), grid=(pairs, r...  48 us
    pallas_call x4, Pallas kernels, attn_fwd(): pl.pallas_call(functools.partial(attn_fwd_kernel, causal), grid=(pairs, r...  37.2 us
    ppermute x12, waiting for transfers between devices, go(): self.flight = [lax.ppermute(self.sends[0], WIDE, flipped(self.wide, step))]  33 us
    pallas_call x4, Pallas kernels, weight_grads(): pl.pallas_call(functools.partial(grads_kernel, first_rows, lefts, groups)...  29.4 us
    ppermute x16, waiting for transfers between devices, go(): lax.ppermute(p, WIDE, flipped(self.wide, self.orders[i][step]))  18.9 us
    ppermute x16, starting transfers between devices, go(): lax.ppermute(p, WIDE, flipped(self.wide, self.orders[i][step]))  11.4 us
    ppermute x12, starting transfers between devices, go(): self.flight = [lax.ppermute(self.sends[0], WIDE, flipped(self.wide, step))]  10.8 us
  transfers between devices with their start and end apart: 48, of which 20 were waited for; matrix products, arithmetic and copies ran while one was open for 7% of the time, Pallas kernels for 46%

profile of v4, /device:TPU:0, one launch (start us, length us, event | category | flops | bytes accessed | tf_op | source)
XLA Modules:
  0.0 409.2 jit_solution(8144307269177221924)
XLA Ops:
  27.8 4.4 %collective-permute-done.3 = bf16[96,1152]{1,0:T(8,128)(2,1)S(1)} collective-permute-done((bf16[96,1152]{1,0:T(8,128)(2,1)S(1)}, bf16[96,1152]{1,0:T(8,128)(2,1)S(1)}, u32[]{:S(2)}, u32[]{:S(2)}) %collective-permute-start.3) | collective-permute-done | bytes 221216 | tf_op jit(solution)/shard_map/ppermute | solution.py:320
  39.0 4.4 %collective-permute-done.5.refs_1_ = bf16[192,1152]{1,0:T(8,128)(2,1)S(1)} collective-permute-done((bf16[192,1152]{1,0:T(8,128)(2,1)S(1)}, bf16[192,1152]{1,0:T(8,128)(2,1)S(1)}, u32[]{:S(2)}, u32[]{:S(2)}) %collective-permute-start.5) | collective-permute-done | bytes 442400 | tf_op jit(solution)/shard_map/ppermute | solution.py:320
  44.1 6.5 %collective-permute-done.12 = bf16[24,3840]{1,0:T(8,128)(2,1)S(1)} collective-permute-done((bf16[24,3840]{1,0:T(8,128)(2,1)S(1)}, bf16[24,3840]{1,0:T(8,128)(2,1)S(1)}, u32[]{:S(2)}, u32[]{:S(2)}) %collective-permute-start.12) | collective-permute-done | bytes 184352 | tf_op jit(solution)/shard_map/ppermute | solution.py:316
  55.8 4.1 %assemble.2.w_ref.wq_ref.wk_ref.wv_ref = bf16[768,2432]{1,0:T(8,128)(2,1)} custom-call(s32[1]{0:T(128)} %bitcast.12.me_ref, bf16[192,1152]{1,0:T(8,128)(2,1)} %copy-done.5, bf16[192,1152]{1,0:T(8,128)(2,1)} %copy-done.16, bf16[192,1152]{1,0:T(8,128)(2,1)} %collective-permute-done.7.refs_2_, bf16[192,1152]{1,0:T(8,128)(2,1)} %collective-permute-done.8.refs_3_, ...), custom_call_target="tpu_custom_call" | custom-call | flops 1 | bytes 1 | tf_op jit(solution)/shard_map/assemble/pallas_call | solution.py:377
  61.6 8.1 %proj_self.1 = (bf16[768,1024]{1,0:T(8,128)(2,1)}, bf16[1024,2304]{1,0:T(8,128)(2,1)}) custom-call(bf16[1024,768]{1,0:T(8,128)(2,1)} %bitcast.145, f32[3,768]{1,0:T(4,128)} %bitcast.162, bf16[768,2432]{1,0:T(8,128)(2,1)} %assemble.2.w_ref.wq_ref.wk_ref.wv_ref), custom_call_target="tpu_custom_call" | custom-call | flops 1 | bytes 1 | tf_op jit(solution)/shard_map/proj_self/pallas_call | solution.py:537
  72.5 9.3 %attn_fwd_self.2 = (bf16[1024,384]{1,0:T(8,128)(2,1)}, bf16[2,6,512,512]{3,2,1,0:T(8,128)(2,1)}, f32[2,6,8,512]{3,2,1,0:T(8,128)}) custom-call(bf16[1024,2304]{1,0:T(8,128)(2,1)} %get-tuple-element.1358.q_ref.k_ref.v_ref, bf16[1024,2304]{1,0:T(8,128)(2,1)} %get-tuple-element.1358.q_ref.k_ref.v_ref, bf16[1024,2304]{1,0:T(8,128)(2,1)} %get-tuple-element.1358.q_ref.k_ref.v_ref, ...), custom_call_target="tpu_custom_call" | custom-call | flops 1 | bytes 1 | tf_op jit(solution)/shard_map/attn_fwd_self/pallas_call | solution.py:133
  81.9 9.4 %attn_fwd_self.3 = (bf16[1024,384]{1,0:T(8,128)(2,1)}, bf16[2,6,512,512]{3,2,1,0:T(8,128)(2,1)}, f32[2,6,8,512]{3,2,1,0:T(8,128)}) custom-call(bf16[1024,2304]{1,0:T(8,128)(2,1)} %get-tuple-element.1358.q_ref.k_ref.v_ref, bf16[1024,2304]{1,0:T(8,128)(2,1)} %get-tuple-element.1358.q_ref.k_ref.v_ref, bf16[1024,2304]{1,0:T(8,128)(2,1)} %get-tuple-element.1358.q_ref.k_ref.v_ref, ...), custom_call_target="tpu_custom_call" | custom-call | flops 1 | bytes 1 | tf_op jit(solution)/shard_map/attn_fwd_self/pallas_call | solution.py:133
  91.3 4.4 %collective-permute-done.17.refs_5_ = bf16[192,1920]{1,0:T(8,128)(2,1)S(1)} collective-permute-done((bf16[192,1920]{1,0:T(8,128)(2,1)S(1)}, bf16[192,1920]{1,0:T(8,128)(2,1)S(1)}, u32[]{:S(2)}, u32[]{:S(2)}) %collective-permute-start.17) | collective-permute-done | bytes 737312 | tf_op jit(solution)/shard_map/ppermute | solution.py:320
  102.1 5.7 %assemble.3.wo_ref.wc_ref.wq_ref.ck_ref.cv_ref = bf16[768,3840]{1,0:T(8,128)(2,1)} custom-call(s32[1]{0:T(128)} %bitcast.12.me_ref, bf16[192,1920]{1,0:T(8,128)(2,1)} %copy-done.2, bf16[192,1920]{1,0:T(8,128)(2,1)} %copy-done.9, bf16[192,1920]{1,0:T(8,128)(2,1)} %copy-done.10, bf16[192,1920]{1,0:T(8,128)(2,1)} %copy-done.11, bf16[192,1920]{1,0:T(8,128)(2,1)} %copy-done.1, ...), custom_call_target="tpu_custom_call" | custom-call | flops 1 | bytes 1 | tf_op jit(solution)/shard_map/assemble/pallas_call | solution.py:377
  107.8 13.3 %mid.1 = (f32[1024,768]{1,0:T(8,128)}, bf16[768,1024]{1,0:T(8,128)(2,1)}, bf16[1024,768]{1,0:T(8,128)(2,1)}, bf16[1024,1536]{1,0:T(8,128)(2,1)}, bf16[768,1024]{1,0:T(8,128)(2,1)}) custom-call(bf16[1024,768]{1,0:T(8,128)(2,1)} %bitcast.146, bf16[1024,768]{1,0:T(8,128)(2,1)} %bitcast.156, f32[3,768]{1,0:T(4,128)} %bitcast.163, ...), custom_call_target="tpu_custom_call" | custom-call | flops 1 | bytes 1 | tf_op jit(solution)/shard_map/mid/pallas_call | solution.py:537
  121.1 9.2 %attn_fwd_cross.2 = (bf16[1024,384]{1,0:T(8,128)(2,1)}, bf16[2,6,512,512]{3,2,1,0:T(8,128)(2,1)}, f32[2,6,8,512]{3,2,1,0:T(8,128)}) custom-call(bf16[1024,768]{1,0:T(8,128)(2,1)} %get-tuple-element.1186.q_ref, bf16[1024,1536]{1,0:T(8,128)(2,1)} %get-tuple-element.1187.k_ref.v_ref, bf16[1024,1536]{1,0:T(8,128)(2,1)} %get-tuple-element.1187.k_ref.v_ref, ...), custom_call_target="tpu_custom_call" | custom-call | flops 1 | bytes 1 | tf_op jit(solution)/shard_map/attn_fwd_cross/pallas_call | solution.py:133
  130.3 9.2 %attn_fwd_cross.3 = (bf16[1024,384]{1,0:T(8,128)(2,1)}, bf16[2,6,512,512]{3,2,1,0:T(8,128)(2,1)}, f32[2,6,8,512]{3,2,1,0:T(8,128)}) custom-call(bf16[1024,768]{1,0:T(8,128)(2,1)} %get-tuple-element.1186.q_ref, bf16[1024,1536]{1,0:T(8,128)(2,1)} %get-tuple-element.1187.k_ref.v_ref, bf16[1024,1536]{1,0:T(8,128)(2,1)} %get-tuple-element.1187.k_ref.v_ref, ...), custom_call_target="tpu_custom_call" | custom-call | flops 1 | bytes 1 | tf_op jit(solution)/shard_map/attn_fwd_cross/pallas_call | solution.py:133
  139.5 6.9 %third.1 = (f32[1024,768]{1,0:T(8,128)}, bf16[1024,768]{1,0:T(8,128)(2,1)}, bf16[768,1024]{1,0:T(8,128)(2,1)}, bf16[768,1024]{1,0:T(8,128)(2,1)}) custom-call(f32[1024,768]{1,0:T(8,128)} %get-tuple-element.1248.x2_ref, bf16[1024,768]{1,0:T(8,128)(2,1)} %bitcast.142, f32[3,768]{1,0:T(4,128)} %bitcast.164, ...), custom_call_target="tpu_custom_call" | custom-call | flops 1 | bytes 1 | tf_op jit(solution)/shard_map/third/pallas_call | solution.py:537
  146.4 37.1 %ffn.1 = (f32[1024,768]{1,0:T(8,128)}, f32[1024,768]{1,0:T(8,128)}, bf16[768,6144]{1,0:T(8,128)(2,1)}) custom-call(bf16[1024,768]{1,0:T(8,128)(2,1)} %get-tuple-element.1076.n_ref, bf16[768,1024]{1,0:T(8,128)(2,1)} %get-tuple-element.1077.nt_ref, bf16[1024,768]{1,0:T(8,128)(2,1)} %bitcast.143, bf16[768,1024]{1,0:T(8,128)(2,1)} %get-tuple-element.1079.gt_ref, ...), custom_call_target="tpu_custom_call" | custom-call | flops 1 | bytes 1 | tf_op jit(solution)/shard_map/ffn/pallas_call | solution.py:537
  183.6 8.3 %top.1 = (bf16[1024,768]{1,0:T(8,128)(2,1)}, f32[1024,768]{1,0:T(8,128)}, bf16[768,1024]{1,0:T(8,128)(2,1)}, bf16[1024,768]{1,0:T(8,128)(2,1)}, f32[8,768]{1,0:T(8,128)}) custom-call(f32[1024,768]{1,0:T(8,128)} %get-tuple-element.1115.y_ref, f32[1024,768]{1,0:T(8,128)} %get-tuple-element.1114.dn_ref, f32[1024,768]{1,0:T(8,128)} %get-tuple-element.1116.x3_ref, ...), custom_call_target="tpu_custom_call" | custom-call | flops 1 | bytes 1 | tf_op jit(solution)/shard_map/top/pallas_call | solution.py:537
  191.9 10.7 %attn_bwd_cross.2 = (bf16[1024,384]{1,0:T(8,128)(2,1)}, bf16[1024,384]{1,0:T(8,128)(2,1)}, bf16[1024,384]{1,0:T(8,128)(2,1)}) custom-call(bf16[1024,768]{1,0:T(8,128)(2,1)} %get-tuple-element.1186.q_ref, bf16[1024,1536]{1,0:T(8,128)(2,1)} %get-tuple-element.1187.k_ref.v_ref, bf16[1024,1536]{1,0:T(8,128)(2,1)} %get-tuple-element.1187.k_ref.v_ref, ...), custom_call_target="tpu_custom_call" | custom-call | flops 1 | bytes 1 | tf_op jit(solution)/shard_map/attn_bwd_cross/pallas_call | solution.py:231
  202.6 10.9 %attn_bwd_cross.3 = (bf16[1024,384]{1,0:T(8,128)(2,1)}, bf16[1024,384]{1,0:T(8,128)(2,1)}, bf16[1024,384]{1,0:T(8,128)(2,1)}) custom-call(bf16[1024,768]{1,0:T(8,128)(2,1)} %get-tuple-element.1186.q_ref, bf16[1024,1536]{1,0:T(8,128)(2,1)} %get-tuple-element.1187.k_ref.v_ref, bf16[1024,1536]{1,0:T(8,128)(2,1)} %get-tuple-element.1187.k_ref.v_ref, ...), custom_call_target="tpu_custom_call" | custom-call | flops 1 | bytes 1 | tf_op jit(solution)/shard_map/attn_bwd_cross/pallas_call | solution.py:231
  213.5 10.0 %grads_cross.1 = (bf16[1,4,96,2304]{3,2,1,0:T(8,128)(2,1)}, bf16[1,4,96,2304]{3,2,1,0:T(8,128)(2,1)}) custom-call(s32[1]{0:T(128)} %bitcast.me_ref, bf16[768,1024]{1,0:T(8,128)(2,1)} %get-tuple-element.1217.refs_0_, bf16[768,1024]{1,0:T(8,128)(2,1)} %get-tuple-element.1218.refs_1_, bf16[1024,384]{1,0:T(8,128)(2,1)} %get-tuple-element.1252.refs_2_.refs_0_, ...), custom_call_target="tpu_custom_call" | custom-call | flops 1 | bytes 1 | tf_op jit(solution)/shard_map/grads_cross/pallas_call | solution.py:719
  224.0 10.2 %second.1 = (f32[1024,768]{1,0:T(8,128)}, bf16[768,1024]{1,0:T(8,128)(2,1)}, bf16[1024,768]{1,0:T(8,128)(2,1)}, f32[8,768]{1,0:T(8,128)}) custom-call(f32[1024,768]{1,0:T(8,128)} %get-tuple-element.1248.x2_ref, f32[1024,768]{1,0:T(8,128)} %get-tuple-element.1249.dx3_ref, f32[3,768]{1,0:T(4,128)} %bitcast.166, ...), custom_call_target="tpu_custom_call" | custom-call | flops 1 | bytes 1 | tf_op jit(solution)/shard_map/second/pallas_call | solution.py:537
  234.2 7.8 %grads_out.1 = (bf16[1,4,96,1536]{3,2,1,0:T(8,128)(2,1)}, bf16[1,4,96,1536]{3,2,1,0:T(8,128)(2,1)}) custom-call(s32[1]{0:T(128)} %bitcast.me_ref, bf16[768,1024]{1,0:T(8,128)(2,1)} %get-tuple-element.1277.refs_0_, bf16[768,1024]{1,0:T(8,128)(2,1)} %get-tuple-element.1278.refs_1_, bf16[1024,384]{1,0:T(8,128)(2,1)} %get-tuple-element.1279.refs_0_.o_ref.refs_2_, ...), custom_call_target="tpu_custom_call" | custom-call | flops 1 | bytes 1 | tf_op jit(solution)/shard_map/grads_out/pallas_call | solution.py:719
  245.5 13.3 %attn_bwd_self.2 = (bf16[1024,384]{1,0:T(8,128)(2,1)}, bf16[1024,384]{1,0:T(8,128)(2,1)}, bf16[1024,384]{1,0:T(8,128)(2,1)}, f32[6,4,256]{2,1,0:T(4,128)}) custom-call(bf16[1024,2304]{1,0:T(8,128)(2,1)} %get-tuple-element.1358.q_ref.k_ref.v_ref, bf16[1024,2304]{1,0:T(8,128)(2,1)} %get-tuple-element.1358.q_ref.k_ref.v_ref, ...), custom_call_target="tpu_custom_call" | custom-call | flops 1 | bytes 1 | tf_op jit(solution)/shard_map/attn_bwd_self/pallas_call | solution.py:231
  258.8 12.3 %collective-permute-done.23 = bf16[2,96,2304]{2,1,0:T(8,128)(2,1)S(1)} collective-permute-done((bf16[2,96,2304]{2,1,0:T(8,128)(2,1)}, bf16[2,96,2304]{2,1,0:T(8,128)(2,1)S(1)}, u32[]{:S(2)}, u32[]{:S(2)}) %collective-permute-start.23) | collective-permute-done | bytes 884768 | tf_op jit(solution)/shard_map/ppermute | solution.py:404
  274.8 5.8 %grads_self.2 = (bf16[1,4,96,1152]{3,2,1,0:T(8,128)(2,1)}, bf16[1,4,96,1152]{3,2,1,0:T(8,128)(2,1)}) custom-call(s32[1]{0:T(128)} %bitcast.me_ref, bf16[768,1024]{1,0:T(8,128)(2,1)} %get-tuple-element.1389.refs_0_, bf16[1024,384]{1,0:T(8,128)(2,1)} %get-tuple-element.1422.refs_1_.refs_0_, bf16[1024,384]{1,0:T(8,128)(2,1)} %get-tuple-element.1418.refs_2_, ...), custom_call_target="tpu_custom_call" | custom-call | flops 1 | bytes 1 | tf_op jit(solution)/shard_map/grads_self/pallas_call | solution.py:719
  281.9 13.1 %attn_bwd_self.3 = (bf16[1024,384]{1,0:T(8,128)(2,1)}, bf16[1024,384]{1,0:T(8,128)(2,1)}, bf16[1024,384]{1,0:T(8,128)(2,1)}, f32[6,4,256]{2,1,0:T(4,128)}) custom-call(bf16[1024,2304]{1,0:T(8,128)(2,1)} %get-tuple-element.1358.q_ref.k_ref.v_ref, bf16[1024,2304]{1,0:T(8,128)(2,1)} %get-tuple-element.1358.q_ref.k_ref.v_ref, ...), custom_call_target="tpu_custom_call" | custom-call | flops 1 | bytes 1 | tf_op jit(solution)/shard_map/attn_bwd_self/pallas_call | solution.py:231
  295.0 11.3 %collective-permute-done.25 = bf16[1,96,2304]{2,1,0:T(8,128)(2,1)S(1)} collective-permute-done((bf16[1,96,2304]{2,1,0:T(8,128)(2,1)S(1)}, bf16[1,96,2304]{2,1,0:T(8,128)(2,1)S(1)}, u32[]{:S(2)}, u32[]{:S(2)}) %collective-permute-start.25) | collective-permute-done | bytes 442400 | tf_op jit(solution)/shard_map/ppermute | solution.py:404
  311.4 5.9 %grads_self.3 = (bf16[1,4,96,1152]{3,2,1,0:T(8,128)(2,1)}, bf16[1,4,96,1152]{3,2,1,0:T(8,128)(2,1)}) custom-call(s32[1]{0:T(128)} %bitcast.me_ref, bf16[768,1024]{1,0:T(8,128)(2,1)} %get-tuple-element.1389.refs_0_, bf16[1024,384]{1,0:T(8,128)(2,1)} %get-tuple-element.1423.refs_1_, bf16[1024,384]{1,0:T(8,128)(2,1)} %get-tuple-element.1419.refs_2_.refs_3_, ...), custom_call_target="tpu_custom_call" | custom-call | flops 1 | bytes 1 | tf_op jit(solution)/shard_map/grads_self/pallas_call | solution.py:719
  318.9 4.3 %collective-permute-start.31 = (bf16[1,24,3840]{2,1,0:T(8,128)(2,1)}, bf16[1,24,3840]{2,1,0:T(8,128)(2,1)S(1)}, u32[]{:S(2)}, u32[]{:S(2)}) collective-permute-start(bf16[1,24,3840]{2,1,0:T(8,128)(2,1)} %pad_maximum_fusion.9), channel_id=1, source_target_pairs={{0,3},{1,2},{2,1},{3,0},{4,7},{5,6},{6,5},{7,4},{8,11},{9,10},{10,... | collective-permute-start | bytes 552968 | tf_op jit(solution)/shard_map/ppermute | solution.py:402
  325.1 11.8 %last.1 = (f32[1024,768]{1,0:T(8,128)}, f32[8,768]{1,0:T(8,128)}) custom-call(bf16[1024,768]{1,0:T(8,128)(2,1)} %bitcast.147, f32[1024,768]{1,0:T(8,128)} %get-tuple-element.1429.dx2_ref, f32[3,768]{1,0:T(4,128)} %bitcast.167, bf16[768,2432]{1,0:T(8,128)(2,1)} %assemble.2.w_ref.wq_ref.wk_ref.wv_ref, bf16[768,2432]{1,0:T(8,128)(2,1)} %assemble.2.w_ref.wq_ref.wk_ref.wv_ref, ...), custom_call_target="tpu_custom_call" | custom-call | flops 1 | bytes 1 | tf_op jit(solution)/shard_map/last/pallas_call | solution.py:537
  336.9 4.8 %reduce-scatter.2.cloned.1.call-done = bf16[24,6144]{1,0:T(8,128)(2,1)} async-done(((bf16[768,6144]{1,0:T(8,128)(2,1)}), bf16[24,6144]{1,0:T(8,128)(2,1)}) %reduce-scatter.2.cloned.1.call-update) | async-done | bytes 294928 | tf_op jit(solution)/shard_map/reduce_scatter | solution.py:890
  355.8 7.0 %encoder_grad.1 = f32[1024,768]{1,0:T(8,128)} custom-call(bf16[768,3840]{1,0:T(8,128)(2,1)} %assemble.3.wo_ref.wc_ref.wq_ref.ck_ref.cv_ref, bf16[768,3840]{1,0:T(8,128)(2,1)} %assemble.3.wo_ref.wc_ref.wq_ref.ck_ref.cv_ref, bf16[1024,384]{1,0:T(8,128)(2,1)} %get-tuple-element.1450.refs_4_.refs_0_, bf16[1024,384]{1,0:T(8,128)(2,1)} %get-tuple-element.1451.refs_5_.refs_1_, ...), custom_call_target="tpu_custom_call" | custom-call | flops 1 | bytes 1 | tf_op jit(solution)/shard_map/encoder_grad/pallas_call | solution.py:537
  364.6 3.7 collective-permute-done.34
  372.7 5.0 %collective-permute-done.37 = bf16[1,96,1152]{2,1,0:T(8,128)(2,1)S(1)} collective-permute-done((bf16[1,96,1152]{2,1,0:T(8,128)(2,1)S(1)}, bf16[1,96,1152]{2,1,0:T(8,128)(2,1)S(1)}, u32[]{:S(2)}, u32[]{:S(2)}) %collective-permute-start.37) | collective-permute-done | bytes 221216 | tf_op jit(solution)/shard_map/ppermute | solution.py:404
  (241 shorter events, 105.7 us)
Async XLA Ops:
  7.2 139.2 %all-gather.2.cloned.1.call-start = ((), (), s32[]{:S(2)}) async-start(), calls=%async_computation.1 | async-start | bytes 9732096 | tf_op jit(solution)/shard_map/all_gather | solution.py:874
  9.6 14.5 %collective-permute-start = (bf16[24,2432]{1,0:T(8,128)(2,1)S(1)}, bf16[24,2432]{1,0:T(8,128)(2,1)S(1)}, u32[]{:S(2)}, u32[]{:S(2)}) collective-permute-start(bf16[24,2432]{1,0:T(8,128)(2,1)S(1)} %fusion.4), channel_id=1, source_target_pairs={{0,1},{1,0},{2,3},{3,2},{4,5},{5,4},{6,7},{7,6},{8,9},{9,8},{10,11... | collective-permute-start | bytes 350216 | tf_op jit(solution)/shard_map/ppermute | solution.py:316
  12.7 11.9 %collective-permute-start.1 = (bf16[24,2432]{1,0:T(8,128)(2,1)S(1)}, bf16[24,2432]{1,0:T(8,128)(2,1)S(1)}, u32[]{:S(2)}, u32[]{:S(2)}) collective-permute-start(bf16[24,2432]{1,0:T(8,128)(2,1)S(1)} %fusion.4), channel_id=1, source_target_pairs={{0,2},{1,3},{2,0},{3,1},{4,6},{5,7},{6,4},{7,5},{8,10},{9,11},{10,... | collective-permute-start | bytes 350216 | tf_op jit(solution)/shard_map/ppermute | solution.py:316
  15.3 9.3 %collective-permute-start.2 = (bf16[24,2432]{1,0:T(8,128)(2,1)S(1)}, bf16[24,2432]{1,0:T(8,128)(2,1)S(1)}, u32[]{:S(2)}, u32[]{:S(2)}) collective-permute-start(bf16[24,2432]{1,0:T(8,128)(2,1)S(1)} %fusion.4), channel_id=1, source_target_pairs={{0,3},{1,2},{2,1},{3,0},{4,7},{5,6},{6,5},{7,4},{8,11},{9,10},{10,... | collective-permute-start | bytes 350216 | tf_op jit(solution)/shard_map/ppermute | solution.py:316
  32.3 11.2 %collective-permute-start.6 = (bf16[192,1280]{1,0:T(8,128)(2,1)S(1)}, bf16[192,1280]{1,0:T(8,128)(2,1)S(1)}, u32[]{:S(2)}, u32[]{:S(2)}) collective-permute-start(bf16[192,1280]{1,0:T(8,128)(2,1)S(1)} %constant_dynamic-update-slice_fusion.3.refs_4_), channel_id=1, source_target_pairs={{0,8},{4,12},{8,0},{12,4},{16,24},{20,28},{24,16},{28,20},{1,9},{5... | collective-permute-start | bytes 1474568 | tf_op jit(solution)/shard_map/ppermute | solution.py:320
  33.9 9.5 %collective-permute-start.5 = (bf16[192,1152]{1,0:T(8,128)(2,1)S(1)}, bf16[192,1152]{1,0:T(8,128)(2,1)S(1)}, u32[]{:S(2)}, u32[]{:S(2)}) collective-permute-start(bf16[192,1152]{1,0:T(8,128)(2,1)S(1)} %constant_dynamic-update-slice_fusion.1.refs_0_), channel_id=1, source_target_pairs={{0,16},{4,20},{8,24},{12,28},{16,0},{20,4},{24,8},{28,12},{1,17},{... | collective-permute-start | bytes 1327112 | tf_op jit(solution)/shard_map/ppermute | solution.py:320
  34.6 9.4 %collective-permute-start.11 = (bf16[24,3840]{1,0:T(8,128)(2,1)S(1)}, bf16[24,3840]{1,0:T(8,128)(2,1)S(1)}, u32[]{:S(2)}, u32[]{:S(2)}) collective-permute-start(bf16[24,3840]{1,0:T(8,128)(2,1)S(1)} %bitcast_dynamic-update-slice_fusion), channel_id=1, source_target_pairs={{0,1},{1,0},{2,3},{3,2},{4,5},{5,4},{6,7},{7,6},{8,9},{9,8},{10,11... | collective-permute-start | bytes 552968 | tf_op jit(solution)/shard_map/ppermute | solution.py:316
  36.3 14.3 %collective-permute-start.12 = (bf16[24,3840]{1,0:T(8,128)(2,1)S(1)}, bf16[24,3840]{1,0:T(8,128)(2,1)S(1)}, u32[]{:S(2)}, u32[]{:S(2)}) collective-permute-start(bf16[24,3840]{1,0:T(8,128)(2,1)S(1)} %bitcast_dynamic-update-slice_fusion), channel_id=1, source_target_pairs={{0,2},{1,3},{2,0},{3,1},{4,6},{5,7},{6,4},{7,5},{8,10},{9,11},{10,... | collective-permute-start | bytes 552968 | tf_op jit(solution)/shard_map/ppermute | solution.py:316
  38.8 12.7 %collective-permute-start.13 = (bf16[24,3840]{1,0:T(8,128)(2,1)S(1)}, bf16[24,3840]{1,0:T(8,128)(2,1)}, u32[]{:S(2)}, u32[]{:S(2)}) collective-permute-start(bf16[24,3840]{1,0:T(8,128)(2,1)S(1)} %bitcast_dynamic-update-slice_fusion), channel_id=1, source_target_pairs={{0,3},{1,2},{2,1},{3,0},{4,7},{5,6},{6,5},{7,4},{8,11},{9,10},{10,... | collective-permute-start | bytes 552968 | tf_op jit(solution)/shard_map/ppermute | solution.py:316
  43.5 9.1 %collective-permute-start.10 = (bf16[192,1280]{1,0:T(8,128)(2,1)S(1)}, bf16[192,1280]{1,0:T(8,128)(2,1)S(1)}, u32[]{:S(2)}, u32[]{:S(2)}) collective-permute-start(bf16[192,1280]{1,0:T(8,128)(2,1)S(1)} %collective-permute-done.6.refs_5_), channel_id=1, source_target_pairs={{0,4},{4,0},{8,12},{12,8},{16,20},{20,16},{24,28},{28,24},{1,5},{5... | collective-permute-start | bytes 1474568 | tf_op jit(solution)/shard_map/ppermute | solution.py:320
  43.6 9.0 %collective-permute-start.9 = (bf16[192,1280]{1,0:T(8,128)(2,1)S(1)}, bf16[192,1280]{1,0:T(8,128)(2,1)S(1)}, u32[]{:S(2)}, u32[]{:S(2)}) collective-permute-start(bf16[192,1280]{1,0:T(8,128)(2,1)S(1)} %constant_dynamic-update-slice_fusion.3.refs_4_), channel_id=1, source_target_pairs={{0,4},{4,0},{8,12},{12,8},{16,20},{20,16},{24,28},{28,24},{1,5},{5... | collective-permute-start | bytes 1474568 | tf_op jit(solution)/shard_map/ppermute | solution.py:320
  52.6 289.1 %reduce-scatter.2.cloned.1.call-start = ((), (), s32[]{:S(2)}) async-start(), calls=%async_computation.2 | async-start | bytes 9732096 | tf_op jit(solution)/shard_map/reduce_scatter | solution.py:890
  54.2 15.6 %collective-permute-start.14 = (bf16[96,1920]{1,0:T(8,128)(2,1)S(1)}, bf16[96,1920]{1,0:T(8,128)(2,1)S(1)}, u32[]{:S(2)}, u32[]{:S(2)}) collective-permute-start(bf16[96,1920]{1,0:T(8,128)(2,1)S(1)} %get-tuple-element.872), channel_id=1, source_target_pairs={{0,8},{4,12},{8,0},{12,4},{16,24},{20,28},{24,16},{28,20},{1,9},{5... | collective-permute-start | bytes 1105928 | tf_op jit(solution)/shard_map/ppermute | solution.py:320
  54.8 15.0 %collective-permute-start.15 = (bf16[96,1920]{1,0:T(8,128)(2,1)S(1)}, bf16[96,1920]{1,0:T(8,128)(2,1)S(1)}, u32[]{:S(2)}, u32[]{:S(2)}) collective-permute-start(bf16[96,1920]{1,0:T(8,128)(2,1)S(1)} %get-tuple-element.874), channel_id=1, source_target_pairs={{0,16},{4,20},{8,24},{12,28},{16,0},{20,4},{24,8},{28,12},{1,17},{... | collective-permute-start | bytes 1105928 | tf_op jit(solution)/shard_map/ppermute | solution.py:320
  69.8 25.9 %collective-permute-start.17 = (bf16[192,1920]{1,0:T(8,128)(2,1)S(1)}, bf16[192,1920]{1,0:T(8,128)(2,1)S(1)}, u32[]{:S(2)}, u32[]{:S(2)}) collective-permute-start(bf16[192,1920]{1,0:T(8,128)(2,1)S(1)} %constant_dynamic-update-slice_fusion.7.refs_4_), channel_id=1, source_target_pairs={{0,8},{4,12},{8,0},{12,4},{16,24},{20,28},{24,16},{28,20},{1,9},{5... | collective-permute-start | bytes 2211848 | tf_op jit(solution)/shard_map/ppermute | solution.py:320
  71.5 24.3 %collective-permute-start.16 = (bf16[192,1920]{1,0:T(8,128)(2,1)S(1)}, bf16[192,1920]{1,0:T(8,128)(2,1)S(1)}, u32[]{:S(2)}, u32[]{:S(2)}) collective-permute-start(bf16[192,1920]{1,0:T(8,128)(2,1)S(1)} %constant_dynamic-update-slice_fusion.5.refs_0_), channel_id=1, source_target_pairs={{0,16},{4,20},{8,24},{12,28},{16,0},{20,4},{24,8},{28,12},{1,17},{... | collective-permute-start | bytes 2211848 | tf_op jit(solution)/shard_map/ppermute | solution.py:320
  223.5 10.7 %collective-permute-start.22 = (bf16[1,4,96,2304]{3,2,1,0:T(8,128)(2,1)}, bf16[1,4,96,2304]{3,2,1,0:T(8,128)(2,1)S(1)}, u32[]{:S(2)}, u32[]{:S(2)}) collective-permute-start(bf16[1,4,96,2304]{3,2,1,0:T(8,128)(2,1)} %get-tuple-element.1276), channel_id=1, source_target_pairs={{0,4},{4,0},{8,12},{12,8},{16,20},{20,16},{24,28},{28,24},{1,5},{5... | collective-permute-start | bytes 5308424 | tf_op jit(solution)/shard_map/ppermute | solution.py:404
  242.0 29.1 %collective-permute-start.24 = (bf16[1,4,96,1536]{3,2,1,0:T(8,128)(2,1)}, bf16[1,4,96,1536]{3,2,1,0:T(8,128)(2,1)}, u32[]{:S(2)}, u32[]{:S(2)}) collective-permute-start(bf16[1,4,96,1536]{3,2,1,0:T(8,128)(2,1)} %get-tuple-element.1332), channel_id=1, source_target_pairs={{0,4},{4,0},{8,12},{12,8},{16,20},{20,16},{24,28},{28,24},{1,5},{5... | collective-permute-start | bytes 3538952 | tf_op jit(solution)/shard_map/ppermute | solution.py:404
  243.8 27.3 %collective-permute-start.23 = (bf16[2,96,2304]{2,1,0:T(8,128)(2,1)}, bf16[2,96,2304]{2,1,0:T(8,128)(2,1)S(1)}, u32[]{:S(2)}, u32[]{:S(2)}) collective-permute-start(bf16[2,96,2304]{2,1,0:T(8,128)(2,1)} %get-tuple-element.1552), channel_id=1, source_target_pairs={{0,8},{4,12},{8,0},{12,4},{16,24},{20,28},{24,16},{28,20},{1,9},{5... | collective-permute-start | bytes 2654216 | tf_op jit(solution)/shard_map/ppermute | solution.py:404
  273.6 32.7 %collective-permute-start.26 = (bf16[1,192,1536]{2,1,0:T(8,128)(2,1)}, bf16[1,192,1536]{2,1,0:T(8,128)(2,1)S(1)}, u32[]{:S(2)}, u32[]{:S(2)}) collective-permute-start(bf16[1,192,1536]{2,1,0:T(8,128)(2,1)} %get-tuple-element.1554), channel_id=1, source_target_pairs={{0,16},{4,20},{8,24},{12,28},{16,0},{20,4},{24,8},{28,12},{1,17},{... | collective-permute-start | bytes 1769480 | tf_op jit(solution)/shard_map/ppermute | solution.py:404
  280.7 25.6 %collective-permute-start.27 = (bf16[1,4,96,1152]{3,2,1,0:T(8,128)(2,1)}, bf16[1,4,96,1152]{3,2,1,0:T(8,128)(2,1)}, u32[]{:S(2)}, u32[]{:S(2)}) collective-permute-start(bf16[1,4,96,1152]{3,2,1,0:T(8,128)(2,1)} %get-tuple-element.1388), channel_id=1, source_target_pairs={{0,4},{4,0},{8,12},{12,8},{16,20},{20,16},{24,28},{28,24},{1,5},{5... | collective-permute-start | bytes 2654216 | tf_op jit(solution)/shard_map/ppermute | solution.py:404
  281.0 25.2 %collective-permute-start.25 = (bf16[1,96,2304]{2,1,0:T(8,128)(2,1)S(1)}, bf16[1,96,2304]{2,1,0:T(8,128)(2,1)S(1)}, u32[]{:S(2)}, u32[]{:S(2)}) collective-permute-start(bf16[1,96,2304]{2,1,0:T(8,128)(2,1)S(1)} %get-tuple-element.1560), channel_id=1, source_target_pairs={{0,16},{4,20},{8,24},{12,28},{16,0},{20,4},{24,8},{28,12},{1,17},{... | collective-permute-start | bytes 1327112 | tf_op jit(solution)/shard_map/ppermute | solution.py:404
  308.5 34.8 %collective-permute-start.32 = (bf16[1,192,1152]{2,1,0:T(8,128)(2,1)}, bf16[1,192,1152]{2,1,0:T(8,128)(2,1)}, u32[]{:S(2)}, u32[]{:S(2)}) collective-permute-start(bf16[1,192,1152]{2,1,0:T(8,128)(2,1)} %get-tuple-element.1558), channel_id=1, source_target_pairs={{0,16},{4,20},{8,24},{12,28},{16,0},{20,4},{24,8},{28,12},{1,17},{... | collective-permute-start | bytes 1327112 | tf_op jit(solution)/shard_map/ppermute | solution.py:404
  318.9 24.4 %collective-permute-start.31 = (bf16[1,24,3840]{2,1,0:T(8,128)(2,1)}, bf16[1,24,3840]{2,1,0:T(8,128)(2,1)S(1)}, u32[]{:S(2)}, u32[]{:S(2)}) collective-permute-start(bf16[1,24,3840]{2,1,0:T(8,128)(2,1)} %pad_maximum_fusion.9), channel_id=1, source_target_pairs={{0,3},{1,2},{2,1},{3,0},{4,7},{5,6},{6,5},{7,4},{8,11},{9,10},{10,... | collective-permute-start | bytes 552968 | tf_op jit(solution)/shard_map/ppermute | solution.py:402
  323.8 19.5 %collective-permute-start.30 = (bf16[1,24,3840]{2,1,0:T(8,128)(2,1)}, bf16[1,24,3840]{2,1,0:T(8,128)(2,1)S(1)}, u32[]{:S(2)}, u32[]{:S(2)}) collective-permute-start(bf16[1,24,3840]{2,1,0:T(8,128)(2,1)} %pad_maximum_fusion.8), channel_id=1, source_target_pairs={{0,2},{1,3},{2,0},{3,1},{4,6},{5,7},{6,4},{7,5},{8,10},{9,11},{10,... | collective-permute-start | bytes 552968 | tf_op jit(solution)/shard_map/ppermute | solution.py:402
  323.8 19.5 %collective-permute-start.33 = (bf16[1,4,96,1152]{3,2,1,0:T(8,128)(2,1)}, bf16[1,4,96,1152]{3,2,1,0:T(8,128)(2,1)S(1)}, u32[]{:S(2)}, u32[]{:S(2)}) collective-permute-start(bf16[1,4,96,1152]{3,2,1,0:T(8,128)(2,1)} %get-tuple-element.1448), channel_id=1, source_target_pairs={{0,4},{4,0},{8,12},{12,8},{16,20},{20,16},{24,28},{28,24},{1,5},{5... | collective-permute-start | bytes 2654216 | tf_op jit(solution)/shard_map/ppermute | solution.py:404
  324.5 18.8 %collective-permute-start.29 = (bf16[1,24,3840]{2,1,0:T(8,128)(2,1)}, bf16[1,24,3840]{2,1,0:T(8,128)(2,1)S(1)}, u32[]{:S(2)}, u32[]{:S(2)}) collective-permute-start(bf16[1,24,3840]{2,1,0:T(8,128)(2,1)} %pad_maximum_fusion.7), channel_id=1, source_target_pairs={{0,1},{1,0},{2,3},{3,2},{4,5},{5,4},{6,7},{7,6},{8,9},{9,8},{10,11... | collective-permute-start | bytes 552968 | tf_op jit(solution)/shard_map/ppermute | solution.py:402
  350.2 14.4 %collective-permute-start.36 = (f32[21,128]{1,0:T(8,128)S(1)}, f32[21,128]{1,0:T(8,128)}, u32[]{:S(2)}, u32[]{:S(2)}) collective-permute-start(f32[21,128]{1,0:T(8,128)S(1)} %maximum_bitcast_fusion.2), channel_id=1, source_target_pairs={{0,4},{4,0},{8,12},{12,8},{16,20},{20,16},{24,28},{28,24},{1,5},{5... | collective-permute-start | bytes 32264 | tf_op jit(solution)/shard_map/ppermute | solution.py:455
  350.6 17.7 %collective-permute-start.35 = (bf16[2,96,1152]{2,1,0:T(8,128)(2,1)S(1)}, bf16[2,96,1152]{2,1,0:T(8,128)(2,1)S(1)}, u32[]{:S(2)}, u32[]{:S(2)}) collective-permute-start(bf16[2,96,1152]{2,1,0:T(8,128)(2,1)S(1)} %get-tuple-element.1556), channel_id=1, source_target_pairs={{0,8},{4,12},{8,0},{12,4},{16,24},{20,28},{24,16},{28,20},{1,9},{5... | collective-permute-start | bytes 1327112 | tf_op jit(solution)/shard_map/ppermute | solution.py:404
  353.9 14.4 %collective-permute-start.34 = (bf16[1,96,1152]{2,1,0:T(8,128)(2,1)S(1)}, bf16[1,96,1152]{2,1,0:T(8,128)(2,1)S(1)}, u32[]{:S(2)}, u32[]{:S(2)}) collective-permute-start(bf16[1,96,1152]{2,1,0:T(8,128)(2,1)S(1)} %get-tuple-element.1576), channel_id=1, source_target_pairs={{0,8},{4,12},{8,0},{12,4},{16,24},{20,28},{24,16},{28,20},{1,9},{5... | collective-permute-start | bytes 663560 | tf_op jit(solution)/shard_map/ppermute | solution.py:404
  381.0 8.8 %collective-permute-start.40 = (bf16[1,24,2304]{2,1,0:T(8,128)(2,1)S(1)}, bf16[1,24,2304]{2,1,0:T(8,128)(2,1)S(1)}, u32[]{:S(2)}, u32[]{:S(2)}) collective-permute-start(bf16[1,24,2304]{2,1,0:T(8,128)(2,1)S(1)} %pad_maximum_fusion.14), channel_id=1, source_target_pairs={{0,2},{1,3},{2,0},{3,1},{4,6},{5,7},{6,4},{7,5},{8,10},{9,11},{10,... | collective-permute-start | bytes 331784 | tf_op jit(solution)/shard_map/ppermute | solution.py:402
  381.4 8.4 %collective-permute-start.39 = (bf16[1,24,2304]{2,1,0:T(8,128)(2,1)S(1)}, bf16[1,24,2304]{2,1,0:T(8,128)(2,1)S(1)}, u32[]{:S(2)}, u32[]{:S(2)}) collective-permute-start(bf16[1,24,2304]{2,1,0:T(8,128)(2,1)S(1)} %pad_maximum_fusion.13), channel_id=1, source_target_pairs={{0,1},{1,0},{2,3},{3,2},{4,5},{5,4},{6,7},{7,6},{8,9},{9,8},{10,11... | collective-permute-start | bytes 331784 | tf_op jit(solution)/shard_map/ppermute | solution.py:402
  (42 other events, 394.3 us)
Sparse Core Ops, SparseCore 0:
  52.8 88.3 all-gather.1
  183.7 157.9 reduce-scatter.1

commit v5 on v4

--- a/solution.py
+++ b/solution.py
@@ -386,20 +386,23 @@
 
 
 class Scatter:
-    def __init__(self, sizes, keep, send, first, turn):
+    def __init__(self, sizes, keep, send, first, turn, direct=False):
         self.wide, self.narrow = sizes
+        self.first = first
         self.keep, self.sends = keep, [send]
         self.columns, self.lead = keep.shape[-1], keep.shape[0]
         self.left = [b for b in bits_of(self.wide) if b != first]
         high, low = [b for b in self.left if b > first], [b for b in self.left if b < first]
         turn = turn % max(len(high), 1)
-        self.plan = [first] + high[turn:] + high[:turn] + low[::-1] + ["narrow"]
+        self.plan = [first] + (["high"] if direct else high[turn:] + high[:turn]) + low[::-1] + ["narrow"]
         self.flight = None
 
     def go(self):
         step = self.plan[0]
         if step == "narrow":
             self.flight = [lax.ppermute(s, NARROW, flipped(self.narrow, k + 1)) for k, s in enumerate(self.sends)]
+        elif step == "high":
+            self.flight = [lax.ppermute(s, WIDE, flipped(self.wide, 2 * self.first * (k + 1))) for k, s in enumerate(self.sends)]
         else:
             self.flight = [lax.ppermute(self.sends[0], WIDE, flipped(self.wide, step))]
 
@@ -419,6 +422,13 @@
             at = lax.axis_index(NARROW)
             pick = lambda k: lax.dynamic_slice_in_dim(value, at ^ k, 1, 1)[:, 0]
             self.keep, self.sends = pick(0), [pick(k) for k in range(1, self.narrow)]
+        elif step == "high":
+            count = self.wide // (2 * self.first)
+            self.left = [b for b in self.left if b < self.first]
+            value = value.reshape(self.lead, count, -1, self.columns)
+            at = lax.axis_index(WIDE) // (2 * self.first)
+            pick = lambda k: lax.dynamic_slice_in_dim(value, at ^ k, 1, 1)[:, 0]
+            self.keep, self.sends = pick(0), [pick(k) for k in range(1, count)]
         else:
             parts = self.lead << sum(b > step for b in self.left)
             self.left.remove(step)
@@ -862,8 +872,8 @@
                    [wide_f32()], 2 * unit)
         return {"de": out[0]}
 
-    def cut(pair, turn):
-        return Scatter(sizes, pair[0], pair[1], first, turn)
+    def cut(pair, turn, direct=False):
+        return Scatter(sizes, pair[0], pair[1], first, turn, direct)
 
     r.step(prepare, [g_self])
     r.run(None, [g_self, g_cross], [g_self])
@@ -897,19 +907,13 @@
     r.step(second, [sc])
     r.run(grads_out, [sc], [])
     so = cut(r.live.pop("cut_out"), 1)
-    r.run(lambda: bwd_self(0), [so], [sc, so])
-    r.run(lambda: grads_self(0), [sc, so], [])
-    s0 = cut(r.live.pop("cut_self0"), 1)
-    r.run(lambda: bwd_self(1), [s0], [s0, sc, so])
-    r.run(lambda: grads_self(1), [so, s0], [so])
-    while sc.plan != ["narrow"] or so.plan != ["narrow"]:
-        r.step(None, [x for x in (sc, so) if x.plan != ["narrow"]])
-    sc.join(so)
-    r.moving.remove(so)
-    s1 = cut(r.live.pop("cut_self1"), 0)
-    r.live["ffn_sum"] = ffn_sum
-    r.run(last, [s1, sc], [s1, sc, s0])
-    ffn_sum = r.live.pop("ffn_sum")
+    r.run(lambda: bwd_self(0), [so], [so])
+    r.run(lambda: grads_self(0), [so], [sc])
+    s0 = cut(r.live.pop("cut_self0"), 1, True)
+    r.run(lambda: bwd_self(1), [sc, s0], [s0, sc, so])
+    r.run(lambda: grads_self(1), [sc, so], [sc])
+    s1 = cut(r.live.pop("cut_self1"), 0, True)
+    r.run(last, [s0, s1], [s0, s1, so])
 
     def small():
         diag = jnp.concatenate(both("diag"), axis=0)
@@ -918,15 +922,19 @@
 
     r.live.update(small())
     total = Total(sizes, r.live.pop("small"))
-    movers = [x for x in (s0, s1) if x.plan != ["narrow"]] + [total]
-    r.step(encoder, movers)
-    while s0.plan != ["narrow"] or s1.plan != ["narrow"]:
-        r.step(None, [x for x in (s0, s1) if x.plan != ["narrow"]] + [total])
-    s0.join(s1)
-    r.moving.remove(s1)
-    movers = [sc, s0, total]
-    while any(m.plan for m in movers):
-        r.step(None, movers)
+    r.live["ffn_sum"] = ffn_sum
+    r.step(encoder, [s1, total])
+    ffn_sum = r.live.pop("ffn_sum")
+    ends = [so, s0, s1]
+    while any(s.plan != ["narrow"] for s in ends):
+        r.step(None, [s for s in ends if s.plan != ["narrow"]])
+    for other in (s0, s1):
+        so.join(other)
+        r.moving.remove(other)
+    r.run(None, [so, total], [total])
+    r.run(None, [total], [so, total])
+    while any(s.plan for s in (sc, so, total)):
+        r.step(None, [sc, so, total])
 
     summed = total.value.reshape(-1)
     shard = me * narrow + lax.axis_index(NARROW)
@@ -937,10 +945,10 @@
     own_rows = lambda value, at, n: value.keep[0, :, at: at + n]
 
     def self_part(index):
-        found, at = [], 0
+        found, at = [], 2 * width
         for _, pairs in SPANS:
             n = 128 * pairs
-            found.append(own_rows(s0, at + n * index, n))
+            found.append(own_rows(so, at + n * index, n))
             at += 3 * n
         return jnp.concatenate(found, axis=1)
 
@@ -954,10 +962,10 @@
         bias_sum,
         self_part(0),
         jnp.stack([self_part(1), self_part(2)]),
-        cross_part(4).T,
+        own_rows(so, width, width).T,
         cross_part(0),
         jnp.stack([cross_part(1), cross_part(2)]),
-        cross_part(3).T,
+        own_rows(so, 0, width).T,
         ffn_sum[:, :, 0].reshape(-1, hidden),
         ffn_sum[:, :, 1].reshape(-1, hidden).T,
     )

time: 413 us -> 395 us (0.956)
  waiting for transfers between devices: 74.5 us -> 58.7 us
  other arithmetic: 19.2 us -> 13.9 us
    ppermute x12 -> x8, waiting for transfers between devices: 33 us -> 9.82 us  [go(): self.flight = [lax.ppermute(self.sends[0], WIDE, flipped(self.wide, step))]]
    ppermute x6, waiting for transfers between devices: 6.36 us -> 14.2 us  [go(): lax.ppermute(s, NARROW, flipped(self.narrow, k + 1))]
    ppermute x0 -> x6, starting transfers between devices: none -> 6.98 us  [go(): lax.ppermute(s, WIDE, flipped(self.wide, 2 * self.first * (k + 1)))]
    ppermute x0 -> x6, waiting for transfers between devices: none -> 5.68 us  [go(): lax.ppermute(s, WIDE, flipped(self.wide, 2 * self.first * (k + 1)))]
    reduce_scatter x1, waiting for transfers between devices: 4.82 us -> 0.01 us  [body(): lax.psum_scatter(r.live.pop('dw'), (WIDE, NARROW), scatter_dimension=0, t...]
    ppermute x12 -> x8, starting transfers between devices: 10.8 us -> 7.12 us  [go(): self.flight = [lax.ppermute(self.sends[0], WIDE, flipped(self.wide, step))]]
    unnamed x70 -> x62, local copies, waits for them, and re-layouts: 10.3 us -> 9.5 us
  transfers between devices with their start and end apart: 48 -> 50, of which waited for: 20 -> 17; matrix products, arithmetic and copies ran while one was open for 7% -> 7% of each run, Pallas kernels for 46% -> 49%
where the time goes in v5:
time: 395 us; the launch traced here: 391 us
  Pallas kernels  227 us (57%)
  waiting for transfers between devices  58.7 us (15%)
  starting transfers between devices  53.2 us (13%)
  local copies, waits for them, and re-layouts  22.6 us (6%)
  between operations  15.1 us (4%)
  other arithmetic  13.9 us (4%)
    pallas_call x8, Pallas kernels, call(): pl.pallas_call(kernel, grid=grid, in_specs=[spec(b, i) for _, b, i in ins...  103 us
    pallas_call x4, Pallas kernels, attn_bwd(): pl.pallas_call(functools.partial(attn_bwd_kernel, causal), grid=(pairs, r...  48 us
    pallas_call x4, Pallas kernels, attn_fwd(): pl.pallas_call(functools.partial(attn_fwd_kernel, causal), grid=(pairs, r...  37.3 us
    pallas_call x4, Pallas kernels, weight_grads(): pl.pallas_call(functools.partial(grads_kernel, first_rows, lefts, groups)...  29.3 us
    ppermute x16, waiting for transfers between devices, go(): lax.ppermute(p, WIDE, flipped(self.wide, self.orders[i][step]))  18.8 us
    ppermute x6, waiting for transfers between devices, go(): lax.ppermute(s, NARROW, flipped(self.narrow, k + 1))  14.2 us
    ppermute x16, starting transfers between devices, go(): lax.ppermute(p, WIDE, flipped(self.wide, self.orders[i][step]))  11.4 us
    ppermute x6, starting transfers between devices, go(): lax.ppermute(s, NARROW, flipped(self.narrow, k + 1))  10.7 us
  transfers between devices with their start and end apart: 50, of which 17 were waited for; matrix products, arithmetic and copies ran while one was open for 7% of the time, Pallas kernels for 49%

profile of v5, /device:TPU:0, one launch (start us, length us, event | category | flops | bytes accessed | tf_op | source)
XLA Modules:
  0.0 390.5 jit_solution(17585459540308110541)
XLA Ops:
  9.6 3.1 collective-permute-start
  27.8 4.4 %collective-permute-done.3 = bf16[96,1152]{1,0:T(8,128)(2,1)S(1)} collective-permute-done((bf16[96,1152]{1,0:T(8,128)(2,1)S(1)}, bf16[96,1152]{1,0:T(8,128)(2,1)S(1)}, u32[]{:S(2)}, u32[]{:S(2)}) %collective-permute-start.3) | collective-permute-done | bytes 221216 | tf_op jit(solution)/shard_map/ppermute | solution.py:320
  39.0 4.4 %collective-permute-done.5.refs_1_ = bf16[192,1152]{1,0:T(8,128)(2,1)S(1)} collective-permute-done((bf16[192,1152]{1,0:T(8,128)(2,1)S(1)}, bf16[192,1152]{1,0:T(8,128)(2,1)S(1)}, u32[]{:S(2)}, u32[]{:S(2)}) %collective-permute-start.5) | collective-permute-done | bytes 442400 | tf_op jit(solution)/shard_map/ppermute | solution.py:320
  44.1 6.5 %collective-permute-done.12 = bf16[24,3840]{1,0:T(8,128)(2,1)S(1)} collective-permute-done((bf16[24,3840]{1,0:T(8,128)(2,1)S(1)}, bf16[24,3840]{1,0:T(8,128)(2,1)S(1)}, u32[]{:S(2)}, u32[]{:S(2)}) %collective-permute-start.12) | collective-permute-done | bytes 184352 | tf_op jit(solution)/shard_map/ppermute | solution.py:316
  55.8 4.1 %assemble.2.w_ref.wq_ref.wk_ref.wv_ref = bf16[768,2432]{1,0:T(8,128)(2,1)} custom-call(s32[1]{0:T(128)} %bitcast.12.me_ref, bf16[192,1152]{1,0:T(8,128)(2,1)} %copy-done.5, bf16[192,1152]{1,0:T(8,128)(2,1)} %copy-done.16, bf16[192,1152]{1,0:T(8,128)(2,1)} %collective-permute-done.7.refs_2_, bf16[192,1152]{1,0:T(8,128)(2,1)} %collective-permute-done.8.refs_3_, ...), custom_call_target="tpu_custom_call" | custom-call | flops 1 | bytes 1 | tf_op jit(solution)/shard_map/assemble/pallas_call | solution.py:377
  61.6 8.1 %proj_self.1 = (bf16[768,1024]{1,0:T(8,128)(2,1)}, bf16[1024,2304]{1,0:T(8,128)(2,1)}) custom-call(bf16[1024,768]{1,0:T(8,128)(2,1)} %bitcast.146, f32[3,768]{1,0:T(4,128)} %bitcast.160, bf16[768,2432]{1,0:T(8,128)(2,1)} %assemble.2.w_ref.wq_ref.wk_ref.wv_ref), custom_call_target="tpu_custom_call" | custom-call | flops 1 | bytes 1 | tf_op jit(solution)/shard_map/proj_self/pallas_call | solution.py:547
  72.5 9.4 %attn_fwd_self.2 = (bf16[1024,384]{1,0:T(8,128)(2,1)}, bf16[2,6,512,512]{3,2,1,0:T(8,128)(2,1)}, f32[2,6,8,512]{3,2,1,0:T(8,128)}) custom-call(bf16[1024,2304]{1,0:T(8,128)(2,1)} %get-tuple-element.1363.q_ref.k_ref.v_ref, bf16[1024,2304]{1,0:T(8,128)(2,1)} %get-tuple-element.1363.q_ref.k_ref.v_ref, bf16[1024,2304]{1,0:T(8,128)(2,1)} %get-tuple-element.1363.q_ref.k_ref.v_ref, ...), custom_call_target="tpu_custom_call" | custom-call | flops 1 | bytes 1 | tf_op jit(solution)/shard_map/attn_fwd_self/pallas_call | solution.py:133
  81.9 9.5 %attn_fwd_self.3 = (bf16[1024,384]{1,0:T(8,128)(2,1)}, bf16[2,6,512,512]{3,2,1,0:T(8,128)(2,1)}, f32[2,6,8,512]{3,2,1,0:T(8,128)}) custom-call(bf16[1024,2304]{1,0:T(8,128)(2,1)} %get-tuple-element.1363.q_ref.k_ref.v_ref, bf16[1024,2304]{1,0:T(8,128)(2,1)} %get-tuple-element.1363.q_ref.k_ref.v_ref, bf16[1024,2304]{1,0:T(8,128)(2,1)} %get-tuple-element.1363.q_ref.k_ref.v_ref, ...), custom_call_target="tpu_custom_call" | custom-call | flops 1 | bytes 1 | tf_op jit(solution)/shard_map/attn_fwd_self/pallas_call | solution.py:133
  91.4 4.3 %collective-permute-done.17.refs_5_ = bf16[192,1920]{1,0:T(8,128)(2,1)S(1)} collective-permute-done((bf16[192,1920]{1,0:T(8,128)(2,1)S(1)}, bf16[192,1920]{1,0:T(8,128)(2,1)S(1)}, u32[]{:S(2)}, u32[]{:S(2)}) %collective-permute-start.17) | collective-permute-done | bytes 737312 | tf_op jit(solution)/shard_map/ppermute | solution.py:320
  102.1 5.6 %assemble.3.wo_ref.wc_ref.wq_ref.ck_ref.cv_ref = bf16[768,3840]{1,0:T(8,128)(2,1)} custom-call(s32[1]{0:T(128)} %bitcast.12.me_ref, bf16[192,1920]{1,0:T(8,128)(2,1)} %copy-done.2, bf16[192,1920]{1,0:T(8,128)(2,1)} %copy-done.9, bf16[192,1920]{1,0:T(8,128)(2,1)} %copy-done.10, bf16[192,1920]{1,0:T(8,128)(2,1)} %copy-done.11, bf16[192,1920]{1,0:T(8,128)(2,1)} %copy-done.1, ...), custom_call_target="tpu_custom_call" | custom-call | flops 1 | bytes 1 | tf_op jit(solution)/shard_map/assemble/pallas_call | solution.py:377
  107.7 13.4 %mid.1 = (f32[1024,768]{1,0:T(8,128)}, bf16[768,1024]{1,0:T(8,128)(2,1)}, bf16[1024,768]{1,0:T(8,128)(2,1)}, bf16[1024,1536]{1,0:T(8,128)(2,1)}, bf16[768,1024]{1,0:T(8,128)(2,1)}) custom-call(bf16[1024,768]{1,0:T(8,128)(2,1)} %bitcast.147, bf16[1024,768]{1,0:T(8,128)(2,1)} %bitcast.154, f32[3,768]{1,0:T(4,128)} %bitcast.161, ...), custom_call_target="tpu_custom_call" | custom-call | flops 1 | bytes 1 | tf_op jit(solution)/shard_map/mid/pallas_call | solution.py:547
  121.1 9.1 %attn_fwd_cross.2 = (bf16[1024,384]{1,0:T(8,128)(2,1)}, bf16[2,6,512,512]{3,2,1,0:T(8,128)(2,1)}, f32[2,6,8,512]{3,2,1,0:T(8,128)}) custom-call(bf16[1024,768]{1,0:T(8,128)(2,1)} %get-tuple-element.1191.q_ref, bf16[1024,1536]{1,0:T(8,128)(2,1)} %get-tuple-element.1192.k_ref.v_ref, bf16[1024,1536]{1,0:T(8,128)(2,1)} %get-tuple-element.1192.k_ref.v_ref, ...), custom_call_target="tpu_custom_call" | custom-call | flops 1 | bytes 1 | tf_op jit(solution)/shard_map/attn_fwd_cross/pallas_call | solution.py:133
  130.2 9.3 %attn_fwd_cross.3 = (bf16[1024,384]{1,0:T(8,128)(2,1)}, bf16[2,6,512,512]{3,2,1,0:T(8,128)(2,1)}, f32[2,6,8,512]{3,2,1,0:T(8,128)}) custom-call(bf16[1024,768]{1,0:T(8,128)(2,1)} %get-tuple-element.1191.q_ref, bf16[1024,1536]{1,0:T(8,128)(2,1)} %get-tuple-element.1192.k_ref.v_ref, bf16[1024,1536]{1,0:T(8,128)(2,1)} %get-tuple-element.1192.k_ref.v_ref, ...), custom_call_target="tpu_custom_call" | custom-call | flops 1 | bytes 1 | tf_op jit(solution)/shard_map/attn_fwd_cross/pallas_call | solution.py:133
  139.5 6.8 %third.1 = (f32[1024,768]{1,0:T(8,128)}, bf16[1024,768]{1,0:T(8,128)(2,1)}, bf16[768,1024]{1,0:T(8,128)(2,1)}, bf16[768,1024]{1,0:T(8,128)(2,1)}) custom-call(f32[1024,768]{1,0:T(8,128)} %get-tuple-element.1253.x2_ref, bf16[1024,768]{1,0:T(8,128)(2,1)} %bitcast.143, f32[3,768]{1,0:T(4,128)} %bitcast.162, ...), custom_call_target="tpu_custom_call" | custom-call | flops 1 | bytes 1 | tf_op jit(solution)/shard_map/third/pallas_call | solution.py:547
  146.3 36.9 %ffn.1 = (f32[1024,768]{1,0:T(8,128)}, f32[1024,768]{1,0:T(8,128)}, bf16[768,6144]{1,0:T(8,128)(2,1)}) custom-call(bf16[1024,768]{1,0:T(8,128)(2,1)} %get-tuple-element.1081.n_ref, bf16[768,1024]{1,0:T(8,128)(2,1)} %get-tuple-element.1082.nt_ref, bf16[1024,768]{1,0:T(8,128)(2,1)} %bitcast.144, bf16[768,1024]{1,0:T(8,128)(2,1)} %get-tuple-element.1084.gt_ref, ...), custom_call_target="tpu_custom_call" | custom-call | flops 1 | bytes 1 | tf_op jit(solution)/shard_map/ffn/pallas_call | solution.py:547
  183.3 8.3 %top.1 = (bf16[1024,768]{1,0:T(8,128)(2,1)}, f32[1024,768]{1,0:T(8,128)}, bf16[768,1024]{1,0:T(8,128)(2,1)}, bf16[1024,768]{1,0:T(8,128)(2,1)}, f32[8,768]{1,0:T(8,128)}) custom-call(f32[1024,768]{1,0:T(8,128)} %get-tuple-element.1120.y_ref, f32[1024,768]{1,0:T(8,128)} %get-tuple-element.1119.dn_ref, f32[1024,768]{1,0:T(8,128)} %get-tuple-element.1121.x3_ref, ...), custom_call_target="tpu_custom_call" | custom-call | flops 1 | bytes 1 | tf_op jit(solution)/shard_map/top/pallas_call | solution.py:547
  191.6 10.7 %attn_bwd_cross.2 = (bf16[1024,384]{1,0:T(8,128)(2,1)}, bf16[1024,384]{1,0:T(8,128)(2,1)}, bf16[1024,384]{1,0:T(8,128)(2,1)}) custom-call(bf16[1024,768]{1,0:T(8,128)(2,1)} %get-tuple-element.1191.q_ref, bf16[1024,1536]{1,0:T(8,128)(2,1)} %get-tuple-element.1192.k_ref.v_ref, bf16[1024,1536]{1,0:T(8,128)(2,1)} %get-tuple-element.1192.k_ref.v_ref, ...), custom_call_target="tpu_custom_call" | custom-call | flops 1 | bytes 1 | tf_op jit(solution)/shard_map/attn_bwd_cross/pallas_call | solution.py:231
  202.3 11.2 %attn_bwd_cross.3 = (bf16[1024,384]{1,0:T(8,128)(2,1)}, bf16[1024,384]{1,0:T(8,128)(2,1)}, bf16[1024,384]{1,0:T(8,128)(2,1)}) custom-call(bf16[1024,768]{1,0:T(8,128)(2,1)} %get-tuple-element.1191.q_ref, bf16[1024,1536]{1,0:T(8,128)(2,1)} %get-tuple-element.1192.k_ref.v_ref, bf16[1024,1536]{1,0:T(8,128)(2,1)} %get-tuple-element.1192.k_ref.v_ref, ...), custom_call_target="tpu_custom_call" | custom-call | flops 1 | bytes 1 | tf_op jit(solution)/shard_map/attn_bwd_cross/pallas_call | solution.py:231
  213.5 9.9 %grads_cross.1 = (bf16[1,4,96,2304]{3,2,1,0:T(8,128)(2,1)}, bf16[1,4,96,2304]{3,2,1,0:T(8,128)(2,1)}) custom-call(s32[1]{0:T(128)} %bitcast.me_ref, bf16[768,1024]{1,0:T(8,128)(2,1)} %get-tuple-element.1222.refs_0_, bf16[768,1024]{1,0:T(8,128)(2,1)} %get-tuple-element.1223.refs_1_, bf16[1024,384]{1,0:T(8,128)(2,1)} %get-tuple-element.1257.refs_2_.refs_0_, ...), custom_call_target="tpu_custom_call" | custom-call | flops 1 | bytes 1 | tf_op jit(solution)/shard_map/grads_cross/pallas_call | solution.py:729
  223.9 10.2 %second.1 = (f32[1024,768]{1,0:T(8,128)}, bf16[768,1024]{1,0:T(8,128)(2,1)}, bf16[1024,768]{1,0:T(8,128)(2,1)}, f32[8,768]{1,0:T(8,128)}) custom-call(f32[1024,768]{1,0:T(8,128)} %get-tuple-element.1253.x2_ref, f32[1024,768]{1,0:T(8,128)} %get-tuple-element.1254.dx3_ref, f32[3,768]{1,0:T(4,128)} %bitcast.164, ...), custom_call_target="tpu_custom_call" | custom-call | flops 1 | bytes 1 | tf_op jit(solution)/shard_map/second/pallas_call | solution.py:547
  234.1 7.7 %grads_out.1 = (bf16[1,4,96,1536]{3,2,1,0:T(8,128)(2,1)}, bf16[1,4,96,1536]{3,2,1,0:T(8,128)(2,1)}) custom-call(s32[1]{0:T(128)} %bitcast.me_ref, bf16[768,1024]{1,0:T(8,128)(2,1)} %get-tuple-element.1282.refs_0_, bf16[768,1024]{1,0:T(8,128)(2,1)} %get-tuple-element.1283.refs_1_, bf16[1024,384]{1,0:T(8,128)(2,1)} %get-tuple-element.1284.refs_0_.o_ref.refs_2_, ...), custom_call_target="tpu_custom_call" | custom-call | flops 1 | bytes 1 | tf_op jit(solution)/shard_map/grads_out/pallas_call | solution.py:729
  245.4 13.2 %attn_bwd_self.2 = (bf16[1024,384]{1,0:T(8,128)(2,1)}, bf16[1024,384]{1,0:T(8,128)(2,1)}, bf16[1024,384]{1,0:T(8,128)(2,1)}, f32[6,4,256]{2,1,0:T(4,128)}) custom-call(bf16[1024,2304]{1,0:T(8,128)(2,1)} %get-tuple-element.1363.q_ref.k_ref.v_ref, bf16[1024,2304]{1,0:T(8,128)(2,1)} %get-tuple-element.1363.q_ref.k_ref.v_ref, ...), custom_call_target="tpu_custom_call" | custom-call | flops 1 | bytes 1 | tf_op jit(solution)/shard_map/attn_bwd_self/pallas_call | solution.py:231
  262.6 5.8 %grads_self.2 = (bf16[1,4,96,1152]{3,2,1,0:T(8,128)(2,1)}, bf16[1,4,96,1152]{3,2,1,0:T(8,128)(2,1)}) custom-call(s32[1]{0:T(128)} %bitcast.me_ref, bf16[768,1024]{1,0:T(8,128)(2,1)} %get-tuple-element.1394.refs_0_, bf16[1024,384]{1,0:T(8,128)(2,1)} %get-tuple-element.1427.refs_1_.refs_0_, bf16[1024,384]{1,0:T(8,128)(2,1)} %get-tuple-element.1423.refs_2_, ...), custom_call_target="tpu_custom_call" | custom-call | flops 1 | bytes 1 | tf_op jit(solution)/shard_map/grads_self/pallas_call | solution.py:729
  272.8 12.9 %attn_bwd_self.3 = (bf16[1024,384]{1,0:T(8,128)(2,1)}, bf16[1024,384]{1,0:T(8,128)(2,1)}, bf16[1024,384]{1,0:T(8,128)(2,1)}, f32[6,4,256]{2,1,0:T(4,128)}) custom-call(bf16[1024,2304]{1,0:T(8,128)(2,1)} %get-tuple-element.1363.q_ref.k_ref.v_ref, bf16[1024,2304]{1,0:T(8,128)(2,1)} %get-tuple-element.1363.q_ref.k_ref.v_ref, ...), custom_call_target="tpu_custom_call" | custom-call | flops 1 | bytes 1 | tf_op jit(solution)/shard_map/attn_bwd_self/pallas_call | solution.py:231
  285.7 7.2 %collective-permute-done.25 = bf16[1,96,2304]{2,1,0:T(8,128)(2,1)S(1)} collective-permute-done((bf16[1,96,2304]{2,1,0:T(8,128)(2,1)S(1)}, bf16[1,96,2304]{2,1,0:T(8,128)(2,1)S(1)}, u32[]{:S(2)}, u32[]{:S(2)}) %collective-permute-start.25) | collective-permute-done | bytes 442400 | tf_op jit(solution)/shard_map/ppermute | solution.py:407
  299.9 5.8 %grads_self.3 = (bf16[1,4,96,1152]{3,2,1,0:T(8,128)(2,1)}, bf16[1,4,96,1152]{3,2,1,0:T(8,128)(2,1)}) custom-call(s32[1]{0:T(128)} %bitcast.me_ref, bf16[768,1024]{1,0:T(8,128)(2,1)} %get-tuple-element.1394.refs_0_, bf16[1024,384]{1,0:T(8,128)(2,1)} %get-tuple-element.1428.refs_1_, bf16[1024,384]{1,0:T(8,128)(2,1)} %get-tuple-element.1424.refs_2_.refs_3_, ...), custom_call_target="tpu_custom_call" | custom-call | flops 1 | bytes 1 | tf_op jit(solution)/shard_map/grads_self/pallas_call | solution.py:729
  305.8 5.2 %collective-permute-done.30 = bf16[1,24,2304]{2,1,0:T(8,128)(2,1)S(1)} collective-permute-done((bf16[1,24,2304]{2,1,0:T(8,128)(2,1)S(1)}, bf16[1,24,2304]{2,1,0:T(8,128)(2,1)S(1)}, u32[]{:S(2)}, u32[]{:S(2)}) %collective-permute-start.30) | collective-permute-done | bytes 110624 | tf_op jit(solution)/shard_map/ppermute | solution.py:403
  316.1 11.6 %last.1 = (f32[1024,768]{1,0:T(8,128)}, f32[8,768]{1,0:T(8,128)}) custom-call(bf16[1024,768]{1,0:T(8,128)(2,1)} %bitcast.148, f32[1024,768]{1,0:T(8,128)} %get-tuple-element.1434.dx2_ref, f32[3,768]{1,0:T(4,128)} %bitcast.165, bf16[768,2432]{1,0:T(8,128)(2,1)} %assemble.2.w_ref.wq_ref.wk_ref.wv_ref, bf16[768,2432]{1,0:T(8,128)(2,1)} %assemble.2.w_ref.wq_ref.wk_ref.wv_ref, ...), custom_call_target="tpu_custom_call" | custom-call | flops 1 | bytes 1 | tf_op jit(solution)/shard_map/last/pallas_call | solution.py:547
  327.7 4.2 %collective-permute-done.34 = bf16[1,96,1152]{2,1,0:T(8,128)(2,1)S(1)} collective-permute-done((bf16[1,96,1152]{2,1,0:T(8,128)(2,1)}, bf16[1,96,1152]{2,1,0:T(8,128)(2,1)S(1)}, u32[]{:S(2)}, u32[]{:S(2)}) %collective-permute-start.34) | collective-permute-done | bytes 221216 | tf_op jit(solution)/shard_map/ppermute | solution.py:405
  339.7 7.2 %encoder_grad.1 = f32[1024,768]{1,0:T(8,128)} custom-call(bf16[768,3840]{1,0:T(8,128)(2,1)} %assemble.3.wo_ref.wc_ref.wq_ref.ck_ref.cv_ref, bf16[768,3840]{1,0:T(8,128)(2,1)} %assemble.3.wo_ref.wc_ref.wq_ref.ck_ref.cv_ref, bf16[1024,384]{1,0:T(8,128)(2,1)} %get-tuple-element.1456.refs_4_.refs_0_, bf16[1024,384]{1,0:T(8,128)(2,1)} %get-tuple-element.1457.refs_5_.refs_1_, ...), custom_call_target="tpu_custom_call" | custom-call | flops 1 | bytes 1 | tf_op jit(solution)/shard_map/encoder_grad/pallas_call | solution.py:547
  353.0 4.5 %collective-permute-start.42 = (bf16[1,24,3840]{2,1,0:T(8,128)(2,1)S(1)}, bf16[1,24,3840]{2,1,0:T(8,128)(2,1)S(1)}, u32[]{:S(2)}, u32[]{:S(2)}) collective-permute-start(bf16[1,24,3840]{2,1,0:T(8,128)(2,1)S(1)} %pad_maximum_fusion.8), channel_id=1, source_target_pairs={{0,2},{1,3},{2,0},{3,1},{4,6},{5,7},{6,4},{7,5},{8,10},{9,11},{10,... | collective-permute-start | bytes 552968 | tf_op jit(solution)/shard_map/ppermute | solution.py:403
  362.0 9.0 %collective-permute-done.42 = bf16[1,24,3840]{2,1,0:T(8,128)(2,1)S(1)} collective-permute-done((bf16[1,24,3840]{2,1,0:T(8,128)(2,1)S(1)}, bf16[1,24,3840]{2,1,0:T(8,128)(2,1)S(1)}, u32[]{:S(2)}, u32[]{:S(2)}) %collective-permute-start.42) | collective-permute-done | bytes 184352 | tf_op jit(solution)/shard_map/ppermute | solution.py:403
  (230 shorter events, 95.5 us)
Async XLA Ops:
  7.2 139.1 %all-gather.2.cloned.1.call-start = ((), (), s32[]{:S(2)}) async-start(), calls=%async_computation.1 | async-start | bytes 9732096 | tf_op jit(solution)/shard_map/all_gather | solution.py:884
  9.6 14.4 %collective-permute-start = (bf16[24,2432]{1,0:T(8,128)(2,1)S(1)}, bf16[24,2432]{1,0:T(8,128)(2,1)S(1)}, u32[]{:S(2)}, u32[]{:S(2)}) collective-permute-start(bf16[24,2432]{1,0:T(8,128)(2,1)S(1)} %fusion.4), channel_id=1, source_target_pairs={{0,1},{1,0},{2,3},{3,2},{4,5},{5,4},{6,7},{7,6},{8,9},{9,8},{10,11... | collective-permute-start | bytes 350216 | tf_op jit(solution)/shard_map/ppermute | solution.py:316
  12.7 11.9 %collective-permute-start.1 = (bf16[24,2432]{1,0:T(8,128)(2,1)S(1)}, bf16[24,2432]{1,0:T(8,128)(2,1)S(1)}, u32[]{:S(2)}, u32[]{:S(2)}) collective-permute-start(bf16[24,2432]{1,0:T(8,128)(2,1)S(1)} %fusion.4), channel_id=1, source_target_pairs={{0,2},{1,3},{2,0},{3,1},{4,6},{5,7},{6,4},{7,5},{8,10},{9,11},{10,... | collective-permute-start | bytes 350216 | tf_op jit(solution)/shard_map/ppermute | solution.py:316
  32.3 11.2 %collective-permute-start.6 = (bf16[192,1280]{1,0:T(8,128)(2,1)S(1)}, bf16[192,1280]{1,0:T(8,128)(2,1)S(1)}, u32[]{:S(2)}, u32[]{:S(2)}) collective-permute-start(bf16[192,1280]{1,0:T(8,128)(2,1)S(1)} %constant_dynamic-update-slice_fusion.3.refs_4_), channel_id=1, source_target_pairs={{0,8},{4,12},{8,0},{12,4},{16,24},{20,28},{24,16},{28,20},{1,9},{5... | collective-permute-start | bytes 1474568 | tf_op jit(solution)/shard_map/ppermute | solution.py:320
  36.3 14.3 %collective-permute-start.12 = (bf16[24,3840]{1,0:T(8,128)(2,1)S(1)}, bf16[24,3840]{1,0:T(8,128)(2,1)S(1)}, u32[]{:S(2)}, u32[]{:S(2)}) collective-permute-start(bf16[24,3840]{1,0:T(8,128)(2,1)S(1)} %bitcast_dynamic-update-slice_fusion), channel_id=1, source_target_pairs={{0,2},{1,3},{2,0},{3,1},{4,6},{5,7},{6,4},{7,5},{8,10},{9,11},{10,... | collective-permute-start | bytes 552968 | tf_op jit(solution)/shard_map/ppermute | solution.py:316
  38.7 12.7 %collective-permute-start.13 = (bf16[24,3840]{1,0:T(8,128)(2,1)S(1)}, bf16[24,3840]{1,0:T(8,128)(2,1)}, u32[]{:S(2)}, u32[]{:S(2)}) collective-permute-start(bf16[24,3840]{1,0:T(8,128)(2,1)S(1)} %bitcast_dynamic-update-slice_fusion), channel_id=1, source_target_pairs={{0,3},{1,2},{2,1},{3,0},{4,7},{5,6},{6,5},{7,4},{8,11},{9,10},{10,... | collective-permute-start | bytes 552968 | tf_op jit(solution)/shard_map/ppermute | solution.py:316
  52.6 294.3 %reduce-scatter.2.cloned.1.call-start = ((), (), s32[]{:S(2)}) async-start(), calls=%async_computation.2 | async-start | bytes 9732096 | tf_op jit(solution)/shard_map/reduce_scatter | solution.py:900
  54.1 15.6 %collective-permute-start.14 = (bf16[96,1920]{1,0:T(8,128)(2,1)S(1)}, bf16[96,1920]{1,0:T(8,128)(2,1)S(1)}, u32[]{:S(2)}, u32[]{:S(2)}) collective-permute-start(bf16[96,1920]{1,0:T(8,128)(2,1)S(1)} %get-tuple-element.877), channel_id=1, source_target_pairs={{0,8},{4,12},{8,0},{12,4},{16,24},{20,28},{24,16},{28,20},{1,9},{5... | collective-permute-start | bytes 1105928 | tf_op jit(solution)/shard_map/ppermute | solution.py:320
  54.7 15.0 %collective-permute-start.15 = (bf16[96,1920]{1,0:T(8,128)(2,1)S(1)}, bf16[96,1920]{1,0:T(8,128)(2,1)S(1)}, u32[]{:S(2)}, u32[]{:S(2)}) collective-permute-start(bf16[96,1920]{1,0:T(8,128)(2,1)S(1)} %get-tuple-element.879), channel_id=1, source_target_pairs={{0,16},{4,20},{8,24},{12,28},{16,0},{20,4},{24,8},{28,12},{1,17},{... | collective-permute-start | bytes 1105928 | tf_op jit(solution)/shard_map/ppermute | solution.py:320
  69.8 25.9 %collective-permute-start.17 = (bf16[192,1920]{1,0:T(8,128)(2,1)S(1)}, bf16[192,1920]{1,0:T(8,128)(2,1)S(1)}, u32[]{:S(2)}, u32[]{:S(2)}) collective-permute-start(bf16[192,1920]{1,0:T(8,128)(2,1)S(1)} %constant_dynamic-update-slice_fusion.7.refs_4_), channel_id=1, source_target_pairs={{0,8},{4,12},{8,0},{12,4},{16,24},{20,28},{24,16},{28,20},{1,9},{5... | collective-permute-start | bytes 2211848 | tf_op jit(solution)/shard_map/ppermute | solution.py:320
  71.5 24.3 %collective-permute-start.16 = (bf16[192,1920]{1,0:T(8,128)(2,1)S(1)}, bf16[192,1920]{1,0:T(8,128)(2,1)S(1)}, u32[]{:S(2)}, u32[]{:S(2)}) collective-permute-start(bf16[192,1920]{1,0:T(8,128)(2,1)S(1)} %constant_dynamic-update-slice_fusion.5.refs_0_), channel_id=1, source_target_pairs={{0,16},{4,20},{8,24},{12,28},{16,0},{20,4},{24,8},{28,12},{1,17},{... | collective-permute-start | bytes 2211848 | tf_op jit(solution)/shard_map/ppermute | solution.py:320
  223.5 10.6 %collective-permute-start.22 = (bf16[1,4,96,2304]{3,2,1,0:T(8,128)(2,1)}, bf16[1,4,96,2304]{3,2,1,0:T(8,128)(2,1)S(1)}, u32[]{:S(2)}, u32[]{:S(2)}) collective-permute-start(bf16[1,4,96,2304]{3,2,1,0:T(8,128)(2,1)} %get-tuple-element.1281), channel_id=1, source_target_pairs={{0,4},{4,0},{8,12},{12,8},{16,20},{20,16},{24,28},{28,24},{1,5},{5... | collective-permute-start | bytes 5308424 | tf_op jit(solution)/shard_map/ppermute | solution.py:407
  241.9 16.7 %collective-permute-start.23 = (bf16[1,4,96,1536]{3,2,1,0:T(8,128)(2,1)}, bf16[1,4,96,1536]{3,2,1,0:T(8,128)(2,1)}, u32[]{:S(2)}, u32[]{:S(2)}) collective-permute-start(bf16[1,4,96,1536]{3,2,1,0:T(8,128)(2,1)} %get-tuple-element.1335), channel_id=1, source_target_pairs={{0,4},{4,0},{8,12},{12,8},{16,20},{20,16},{24,28},{28,24},{1,5},{5... | collective-permute-start | bytes 3538952 | tf_op jit(solution)/shard_map/ppermute | solution.py:407
  243.7 27.3 %collective-permute-start.24 = (bf16[2,96,2304]{2,1,0:T(8,128)(2,1)}, bf16[2,96,2304]{2,1,0:T(8,128)(2,1)S(1)}, u32[]{:S(2)}, u32[]{:S(2)}) collective-permute-start(bf16[2,96,2304]{2,1,0:T(8,128)(2,1)} %get-tuple-element.1562), channel_id=1, source_target_pairs={{0,8},{4,12},{8,0},{12,4},{16,24},{20,28},{24,16},{28,20},{1,9},{5... | collective-permute-start | bytes 2654216 | tf_op jit(solution)/shard_map/ppermute | solution.py:407
  261.1 31.9 %collective-permute-start.26 = (bf16[1,192,1536]{2,1,0:T(8,128)(2,1)}, bf16[1,192,1536]{2,1,0:T(8,128)(2,1)}, u32[]{:S(2)}, u32[]{:S(2)}) collective-permute-start(bf16[1,192,1536]{2,1,0:T(8,128)(2,1)} %get-tuple-element.1564), channel_id=1, source_target_pairs={{0,16},{4,20},{8,24},{12,28},{16,0},{20,4},{24,8},{28,12},{1,17},{... | collective-permute-start | bytes 1769480 | tf_op jit(solution)/shard_map/ppermute | solution.py:407
  271.0 22.0 %collective-permute-start.27 = (bf16[1,4,96,1152]{3,2,1,0:T(8,128)(2,1)}, bf16[1,4,96,1152]{3,2,1,0:T(8,128)(2,1)S(1)}, u32[]{:S(2)}, u32[]{:S(2)}) collective-permute-start(bf16[1,4,96,1152]{3,2,1,0:T(8,128)(2,1)} %get-tuple-element.1393), channel_id=1, source_target_pairs={{0,4},{4,0},{8,12},{12,8},{16,20},{20,16},{24,28},{28,24},{1,5},{5... | collective-permute-start | bytes 2654216 | tf_op jit(solution)/shard_map/ppermute | solution.py:407
  271.3 21.7 %collective-permute-start.25 = (bf16[1,96,2304]{2,1,0:T(8,128)(2,1)S(1)}, bf16[1,96,2304]{2,1,0:T(8,128)(2,1)S(1)}, u32[]{:S(2)}, u32[]{:S(2)}) collective-permute-start(bf16[1,96,2304]{2,1,0:T(8,128)(2,1)S(1)} %get-tuple-element.1574), channel_id=1, source_target_pairs={{0,16},{4,20},{8,24},{12,28},{16,0},{20,4},{24,8},{28,12},{1,17},{... | collective-permute-start | bytes 1327112 | tf_op jit(solution)/shard_map/ppermute | solution.py:407
  293.1 12.6 %collective-permute-start.28 = (bf16[1,24,2304]{2,1,0:T(8,128)(2,1)S(1)}, bf16[1,24,2304]{2,1,0:T(8,128)(2,1)S(1)}, u32[]{:S(2)}, u32[]{:S(2)}) collective-permute-start(bf16[1,24,2304]{2,1,0:T(8,128)(2,1)S(1)} %get-tuple-element.1590), channel_id=1, source_target_pairs={{0,1},{1,0},{2,3},{3,2},{4,5},{5,4},{6,7},{7,6},{8,9},{9,8},{10,11... | collective-permute-start | bytes 331784 | tf_op jit(solution)/shard_map/ppermute | solution.py:403
  293.2 12.5 %collective-permute-start.29 = (bf16[1,24,2304]{2,1,0:T(8,128)(2,1)S(1)}, bf16[1,24,2304]{2,1,0:T(8,128)(2,1)S(1)}, u32[]{:S(2)}, u32[]{:S(2)}) collective-permute-start(bf16[1,24,2304]{2,1,0:T(8,128)(2,1)S(1)} %get-tuple-element.1589), channel_id=1, source_target_pairs={{0,2},{1,3},{2,0},{3,1},{4,6},{5,7},{6,4},{7,5},{8,10},{9,11},{10,... | collective-permute-start | bytes 331784 | tf_op jit(solution)/shard_map/ppermute | solution.py:403
  295.3 15.6 %collective-permute-start.30 = (bf16[1,24,2304]{2,1,0:T(8,128)(2,1)S(1)}, bf16[1,24,2304]{2,1,0:T(8,128)(2,1)S(1)}, u32[]{:S(2)}, u32[]{:S(2)}) collective-permute-start(bf16[1,24,2304]{2,1,0:T(8,128)(2,1)S(1)} %get-tuple-element.1588), channel_id=1, source_target_pairs={{0,3},{1,2},{2,1},{3,0},{4,7},{5,6},{6,5},{7,4},{8,11},{9,10},{10,... | collective-permute-start | bytes 331784 | tf_op jit(solution)/shard_map/ppermute | solution.py:403
  310.9 21.1 %collective-permute-start.35 = (bf16[1,4,96,1152]{3,2,1,0:T(8,128)(2,1)}, bf16[1,4,96,1152]{3,2,1,0:T(8,128)(2,1)S(1)}, u32[]{:S(2)}, u32[]{:S(2)}) collective-permute-start(bf16[1,4,96,1152]{3,2,1,0:T(8,128)(2,1)} %get-tuple-element.1454), channel_id=1, source_target_pairs={{0,4},{4,0},{8,12},{12,8},{16,20},{20,16},{24,28},{28,24},{1,5},{5... | collective-permute-start | bytes 2654216 | tf_op jit(solution)/shard_map/ppermute | solution.py:407
  311.0 16.8 %collective-permute-start.31 = (bf16[1,96,1536]{2,1,0:T(8,128)(2,1)S(1)}, bf16[1,96,1536]{2,1,0:T(8,128)(2,1)S(1)}, u32[]{:S(2)}, u32[]{:S(2)}) collective-permute-start(bf16[1,96,1536]{2,1,0:T(8,128)(2,1)S(1)} %get-tuple-element.1582), channel_id=1, source_target_pairs={{0,8},{4,12},{8,0},{12,4},{16,24},{20,28},{24,16},{28,20},{1,9},{5... | collective-permute-start | bytes 884744 | tf_op jit(solution)/shard_map/ppermute | solution.py:407
  312.5 15.2 %collective-permute-start.32 = (bf16[1,96,1152]{2,1,0:T(8,128)(2,1)}, bf16[1,96,1152]{2,1,0:T(8,128)(2,1)S(1)}, u32[]{:S(2)}, u32[]{:S(2)}) collective-permute-start(bf16[1,96,1152]{2,1,0:T(8,128)(2,1)} %get-tuple-element.1450), channel_id=1, source_target_pairs={{0,8},{4,12},{8,0},{12,4},{16,24},{20,28},{24,16},{28,20},{1,9},{5... | collective-permute-start | bytes 663560 | tf_op jit(solution)/shard_map/ppermute | solution.py:405
  313.1 14.7 %collective-permute-start.33 = (bf16[1,96,1152]{2,1,0:T(8,128)(2,1)}, bf16[1,96,1152]{2,1,0:T(8,128)(2,1)S(1)}, u32[]{:S(2)}, u32[]{:S(2)}) collective-permute-start(bf16[1,96,1152]{2,1,0:T(8,128)(2,1)} %get-tuple-element.1451), channel_id=1, source_target_pairs={{0,16},{4,20},{8,24},{12,28},{16,0},{20,4},{24,8},{28,12},{1,17},{... | collective-permute-start | bytes 663560 | tf_op jit(solution)/shard_map/ppermute | solution.py:405
  313.6 18.4 %collective-permute-start.34 = (bf16[1,96,1152]{2,1,0:T(8,128)(2,1)}, bf16[1,96,1152]{2,1,0:T(8,128)(2,1)S(1)}, u32[]{:S(2)}, u32[]{:S(2)}) collective-permute-start(bf16[1,96,1152]{2,1,0:T(8,128)(2,1)} %get-tuple-element.1452), channel_id=1, source_target_pairs={{0,24},{4,28},{8,16},{12,20},{16,8},{20,12},{24,0},{28,4},{1,25},{... | collective-permute-start | bytes 663560 | tf_op jit(solution)/shard_map/ppermute | solution.py:405
  334.8 13.7 %collective-permute-start.39 = (f32[21,128]{1,0:T(8,128)S(1)}, f32[21,128]{1,0:T(8,128)S(1)}, u32[]{:S(2)}, u32[]{:S(2)}) collective-permute-start(f32[21,128]{1,0:T(8,128)S(1)} %maximum_bitcast_fusion.2), channel_id=1, source_target_pairs={{0,4},{4,0},{8,12},{12,8},{16,20},{20,16},{24,28},{28,24},{1,5},{5... | collective-permute-start | bytes 32264 | tf_op jit(solution)/shard_map/ppermute | solution.py:465
  335.9 12.6 %collective-permute-start.36 = (bf16[1,96,1152]{2,1,0:T(8,128)(2,1)}, bf16[1,96,1152]{2,1,0:T(8,128)(2,1)S(1)}, u32[]{:S(2)}, u32[]{:S(2)}) collective-permute-start(bf16[1,96,1152]{2,1,0:T(8,128)(2,1)} %get-tuple-element.1568), channel_id=1, source_target_pairs={{0,8},{4,12},{8,0},{12,4},{16,24},{20,28},{24,16},{28,20},{1,9},{5... | collective-permute-start | bytes 663560 | tf_op jit(solution)/shard_map/ppermute | solution.py:405
  337.4 12.5 %collective-permute-start.37 = (bf16[1,96,1152]{2,1,0:T(8,128)(2,1)}, bf16[1,96,1152]{2,1,0:T(8,128)(2,1)S(1)}, u32[]{:S(2)}, u32[]{:S(2)}) collective-permute-start(bf16[1,96,1152]{2,1,0:T(8,128)(2,1)} %get-tuple-element.1567), channel_id=1, source_target_pairs={{0,16},{4,20},{8,24},{12,28},{16,0},{20,4},{24,8},{28,12},{1,17},{... | collective-permute-start | bytes 663560 | tf_op jit(solution)/shard_map/ppermute | solution.py:405
  338.9 11.0 %collective-permute-start.38 = (bf16[1,96,1152]{2,1,0:T(8,128)(2,1)S(1)}, bf16[1,96,1152]{2,1,0:T(8,128)(2,1)S(1)}, u32[]{:S(2)}, u32[]{:S(2)}) collective-permute-start(bf16[1,96,1152]{2,1,0:T(8,128)(2,1)S(1)} %get-tuple-element.1566), channel_id=1, source_target_pairs={{0,24},{4,28},{8,16},{12,20},{16,8},{20,12},{24,0},{28,4},{1,25},{... | collective-permute-start | bytes 663560 | tf_op jit(solution)/shard_map/ppermute | solution.py:405
  351.3 10.7 %collective-permute-start.43 = (bf16[1,24,3840]{2,1,0:T(8,128)(2,1)S(1)}, bf16[1,24,3840]{2,1,0:T(8,128)(2,1)S(1)}, u32[]{:S(2)}, u32[]{:S(2)}) collective-permute-start(bf16[1,24,3840]{2,1,0:T(8,128)(2,1)S(1)} %pad_maximum_fusion.9), channel_id=1, source_target_pairs={{0,3},{1,2},{2,1},{3,0},{4,7},{5,6},{6,5},{7,4},{8,11},{9,10},{10,... | collective-permute-start | bytes 552968 | tf_op jit(solution)/shard_map/ppermute | solution.py:403
  353.0 18.0 %collective-permute-start.42 = (bf16[1,24,3840]{2,1,0:T(8,128)(2,1)S(1)}, bf16[1,24,3840]{2,1,0:T(8,128)(2,1)S(1)}, u32[]{:S(2)}, u32[]{:S(2)}) collective-permute-start(bf16[1,24,3840]{2,1,0:T(8,128)(2,1)S(1)} %pad_maximum_fusion.8), channel_id=1, source_target_pairs={{0,2},{1,3},{2,0},{3,1},{4,6},{5,7},{6,4},{7,5},{8,10},{9,11},{10,... | collective-permute-start | bytes 552968 | tf_op jit(solution)/shard_map/ppermute | solution.py:403
  357.5 13.5 %collective-permute-start.41 = (bf16[1,24,3840]{2,1,0:T(8,128)(2,1)S(1)}, bf16[1,24,3840]{2,1,0:T(8,128)(2,1)S(1)}, u32[]{:S(2)}, u32[]{:S(2)}) collective-permute-start(bf16[1,24,3840]{2,1,0:T(8,128)(2,1)S(1)} %pad_maximum_fusion.7), channel_id=1, source_target_pairs={{0,1},{1,0},{2,3},{3,2},{4,5},{5,4},{6,7},{7,6},{8,9},{9,8},{10,11... | collective-permute-start | bytes 552968 | tf_op jit(solution)/shard_map/ppermute | solution.py:403
  (40 other events, 394.9 us)
Sparse Core Ops, SparseCore 0:
  52.7 88.2 all-gather.1
  183.4 152.6 reduce-scatter.1

commit v6 on v5

--- a/solution.py
+++ b/solution.py
@@ -693,11 +693,10 @@
     left_refs, right_refs = refs[:n_left], refs[n_left: n_left + count]
     outs = refs[n_left + count: n_left + count + 2 * len(groups)]
     left_buf, right_buf, sems = refs[n_left + count + 2 * len(groups):]
-    width = right_buf.shape[2]
-    tile = 384 if width % 256 else 256
+    widths = [ref.shape[1] for ref in right_refs]
 
     def copies(p):
-        found = [pltpu.make_async_copy(right_refs[p], right_buf.at[p % 2], sems.at[p % 2])]
+        found = [pltpu.make_async_copy(right_refs[p], right_buf.at[p % 2, :, pl.ds(0, widths[p])], sems.at[p % 2])]
         if p == 0 or lefts[p] != lefts[p - 1]:
             found.append(pltpu.make_async_copy(left_refs[lefts[p]], left_buf.at[lefts[p] % 2], sems.at[2 + lefts[p] % 2]))
         return found
@@ -711,7 +710,9 @@
         for copy in copies(p):
             copy.wait()
         group = next(g for g in range(len(groups)) if p < sum(groups[: g + 1]))
-        base = (p - sum(groups[:group])) * width
+        base = sum(widths[sum(groups[:group]): p])
+        width = widths[p]
+        tile = 384 if width % 256 else 256
         keep_ref, send_ref = outs[2 * group], outs[2 * group + 1]
         for col in range(0, width, tile):
             result = dot(left_buf[lefts[p] % 2], right_buf[p % 2, :, col: col + tile])
@@ -722,9 +723,11 @@
 def weight_grads(name, lefts_arrays, lefts, rights, groups, half, first_rows):
     width = lefts_arrays[0].shape[0]
     tokens = rights[0].shape[0]
-    columns = rights[0].shape[1]
+    columns = max(v.shape[1] for v in rights)
     count = len(rights)
-    shapes = [(1, width // (2 * first_rows), first_rows, n * columns) for n in groups for _ in range(2)]
+    ends = [sum(groups[:g]) for g in range(len(groups) + 1)]
+    sizes = [sum(v.shape[1] for v in rights[ends[g]: ends[g + 1]]) for g in range(len(groups))]
+    shapes = [(1, width // (2 * first_rows), first_rows, n) for n in sizes for _ in range(2)]
     flops = 2 * width * tokens * columns * count
     return pl.pallas_call(
         functools.partial(grads_kernel, first_rows, lefts, groups),
@@ -739,6 +742,7 @@
 
 
 SPANS = ((0, 3), (3, 3))
+CROSS_SPANS = ((0, 6),)
 
 
 def body(sizes, inputs, encoder_out, segments, enc_segments, buckets, gains, rel_bias, self_q, self_kv, self_out, cross_q, cross_kv, cross_out, ffn_in, ffn_out, out_grad):
@@ -796,7 +800,7 @@
         return {f"o{i}": o, f"p{i}": p, f"s{i}": s}
 
     def both(name):
-        return [r[f"{name}{i}"] for i in range(len(SPANS))]
+        return [r[f"{name}{i}"] for i in range(2) if f"{name}{i}" in r.live]
 
     def mid():
         out = call(mid_kernel, "mid", steps,
@@ -805,7 +809,7 @@
         return dict(zip(("x2", "n2t", "qc", "kvc", "et"), out))
 
     def fwd_cross(i):
-        o, p, s = attn_fwd(SPANS[i], r["qc"], 0, r["kvc"], 0, r["kvc"], 6, *r["cross_seg"])
+        o, p, s = attn_fwd(CROSS_SPANS[i], r["qc"], 0, r["kvc"], 0, r["kvc"], 6, *r["cross_seg"])
         return {f"oc{i}": o, f"pc{i}": p, f"sc{i}": s}
 
     def third():
@@ -834,7 +838,7 @@
         return dict(zip(("layer", "dx3", "three_t", "doc", "gain3"), out))
 
     def bwd_cross(i):
-        out = attn_bwd(SPANS[i], r["qc"], 0, r["kvc"], 0, r["kvc"], 6, r["doc"], r[f"oc{i}"], r[f"pc{i}"], r[f"sc{i}"], False)
+        out = attn_bwd(CROSS_SPANS[i], r["qc"], 0, r["kvc"], 0, r["kvc"], 6, r["doc"], r[f"oc{i}"], r[f"pc{i}"], r[f"sc{i}"], False)
         return dict(zip((f"dqc{i}", f"dkc{i}", f"dvc{i}"), out))
 
     def second():
@@ -845,12 +849,12 @@
 
     def grads_cross():
         rights = both("dqc") + both("dkc") + both("dvc")
-        n = len(SPANS)
+        n = len(CROSS_SPANS)
         return {"cut_cross": weight_grads("grads_cross", [r["n2t"], r["et"]], (0,) * n + (1,) * (2 * n), rights, (3 * n,), half, first_rows)}
 
     def grads_out():
-        n = len(SPANS)
-        return {"cut_out": weight_grads("grads_out", [r["three_t"], r["two_t"]], (0,) * n + (1,) * n, both("oc") + both("o"), (2 * n,), half, first_rows)}
+        lefts = (0,) * len(CROSS_SPANS) + (1,) * len(SPANS)
+        return {"cut_out": weight_grads("grads_out", [r["three_t"], r["two_t"]], lefts, both("oc") + both("o"), (len(lefts),), half, first_rows)}
 
     def bwd_self(i):
         out = attn_bwd(SPANS[i], r["qkv"], 0, r["qkv"], 6, r["qkv"], 12, r["do"], r[f"o{i}"], r[f"p{i}"], r[f"s{i}"], True)
@@ -891,7 +895,6 @@
     r.step(lambda: {"slab_cross": g_cross.whole()}, [])
     r.step(mid, [])
     r.step(lambda: fwd_cross(0), [])
-    r.step(lambda: fwd_cross(1), [])
     r.step(third, [])
     r.moving = []
     r.live["slab_ffn"] = slab_ffn
@@ -901,7 +904,6 @@
     ffn_sum = ffn_sum.reshape(-1, tiles, 2, tile)
     r.step(top, [])
     r.step(lambda: bwd_cross(0), [])
-    r.step(lambda: bwd_cross(1), [])
     r.step(grads_cross, [])
     sc = cut(r.live.pop("cut_cross"), 0)
     r.step(second, [sc])

time: 395 us -> 389 us (0.985)
  Pallas kernels: 227 us -> 219 us
    ppermute x6, waiting for transfers between devices: 14.2 us -> 8.09 us  [go(): lax.ppermute(s, NARROW, flipped(self.narrow, k + 1))]
    ppermute x6, starting transfers between devices: 10.7 us -> 15.1 us  [go(): lax.ppermute(s, NARROW, flipped(self.narrow, k + 1))]
    pallas_call x4 -> x3, Pallas kernels: 48 us -> 45.7 us  [attn_bwd(): pl.pallas_call(functools.partial(attn_bwd_kernel, causal), grid=(pairs, r...]
    pallas_call x4 -> x3, Pallas kernels: 37.3 us -> 35.4 us  [attn_fwd(): pl.pallas_call(functools.partial(attn_fwd_kernel, causal), grid=(pairs, r...]
  transfers between devices with their start and end apart: 50 -> 50, of which waited for: 17 -> 17; matrix products, arithmetic and copies ran while one was open for 7% -> 7% of each run, Pallas kernels for 49% -> 47%
where the time goes in v6:
time: 389 us; the launch traced here: 385 us
  Pallas kernels  219 us (56%)
  waiting for transfers between devices  58.4 us (15%)
  starting transfers between devices  55 us (14%)
  local copies, waits for them, and re-layouts  22.7 us (6%)
  between operations  15.3 us (4%)
  other arithmetic  14.1 us (4%)
    pallas_call x8, Pallas kernels, call(): pl.pallas_call(kernel, grid=grid, in_specs=[spec(b, i) for _, b, i in ins...  101 us
    pallas_call x3, Pallas kernels, attn_bwd(): pl.pallas_call(functools.partial(attn_bwd_kernel, causal), grid=(pairs, r...  45.7 us
    pallas_call x3, Pallas kernels, attn_fwd(): pl.pallas_call(functools.partial(attn_fwd_kernel, causal), grid=(pairs, r...  35.4 us
    pallas_call x4, Pallas kernels, weight_grads(): pl.pallas_call(functools.partial(grads_kernel, first_rows, lefts, groups)...  27.3 us
    ppermute x16, waiting for transfers between devices, go(): lax.ppermute(p, WIDE, flipped(self.wide, self.orders[i][step]))  19.1 us
    ppermute x6, starting transfers between devices, go(): lax.ppermute(s, NARROW, flipped(self.narrow, k + 1))  15.1 us
    ppermute x8, waiting for transfers between devices, go(): self.flight = [lax.ppermute(self.sends[0], WIDE, flipped(self.wide, step))]  12.6 us
    ppermute x16, starting transfers between devices, go(): lax.ppermute(p, WIDE, flipped(self.wide, self.orders[i][step]))  11.4 us
  transfers between devices with their start and end apart: 50, of which 17 were waited for; matrix products, arithmetic and copies ran while one was open for 7% of the time, Pallas kernels for 47%

profile of v6, /device:TPU:0, one launch (start us, length us, event | category | flops | bytes accessed | tf_op | source)
XLA Modules:
  0.0 384.9 jit_solution(10110385701048449929)
XLA Ops:
  27.8 4.4 %collective-permute-done.3 = bf16[96,1152]{1,0:T(8,128)(2,1)S(1)} collective-permute-done((bf16[96,1152]{1,0:T(8,128)(2,1)S(1)}, bf16[96,1152]{1,0:T(8,128)(2,1)S(1)}, u32[]{:S(2)}, u32[]{:S(2)}) %collective-permute-start.3) | collective-permute-done | bytes 221216 | tf_op jit(solution)/shard_map/ppermute | solution.py:320
  39.0 4.4 %collective-permute-done.5.refs_1_ = bf16[192,1152]{1,0:T(8,128)(2,1)S(1)} collective-permute-done((bf16[192,1152]{1,0:T(8,128)(2,1)S(1)}, bf16[192,1152]{1,0:T(8,128)(2,1)S(1)}, u32[]{:S(2)}, u32[]{:S(2)}) %collective-permute-start.5) | collective-permute-done | bytes 442400 | tf_op jit(solution)/shard_map/ppermute | solution.py:320
  44.1 6.5 %collective-permute-done.12 = bf16[24,3840]{1,0:T(8,128)(2,1)S(1)} collective-permute-done((bf16[24,3840]{1,0:T(8,128)(2,1)S(1)}, bf16[24,3840]{1,0:T(8,128)(2,1)S(1)}, u32[]{:S(2)}, u32[]{:S(2)}) %collective-permute-start.12) | collective-permute-done | bytes 184352 | tf_op jit(solution)/shard_map/ppermute | solution.py:316
  56.0 4.1 %assemble.2.w_ref.wq_ref.wk_ref.wv_ref = bf16[768,2432]{1,0:T(8,128)(2,1)} custom-call(s32[1]{0:T(128)} %bitcast.12.me_ref, bf16[192,1152]{1,0:T(8,128)(2,1)} %copy-done.5, bf16[192,1152]{1,0:T(8,128)(2,1)} %copy-done.16, bf16[192,1152]{1,0:T(8,128)(2,1)} %collective-permute-done.7.refs_2_, bf16[192,1152]{1,0:T(8,128)(2,1)} %collective-permute-done.8.refs_3_, ...), custom_call_target="tpu_custom_call" | custom-call | flops 1 | bytes 1 | tf_op jit(solution)/shard_map/assemble/pallas_call | solution.py:377
  61.9 8.1 %proj_self.1 = (bf16[768,1024]{1,0:T(8,128)(2,1)}, bf16[1024,2304]{1,0:T(8,128)(2,1)}) custom-call(bf16[1024,768]{1,0:T(8,128)(2,1)} %bitcast.146, f32[3,768]{1,0:T(4,128)} %bitcast.160, bf16[768,2432]{1,0:T(8,128)(2,1)} %assemble.2.w_ref.wq_ref.wk_ref.wv_ref), custom_call_target="tpu_custom_call" | custom-call | flops 1 | bytes 1 | tf_op jit(solution)/shard_map/proj_self/pallas_call | solution.py:547
  72.8 9.3 %attn_fwd_self.2 = (bf16[1024,384]{1,0:T(8,128)(2,1)}, bf16[2,6,512,512]{3,2,1,0:T(8,128)(2,1)}, f32[2,6,8,512]{3,2,1,0:T(8,128)}) custom-call(bf16[1024,2304]{1,0:T(8,128)(2,1)} %get-tuple-element.1151.q_ref.k_ref.v_ref, bf16[1024,2304]{1,0:T(8,128)(2,1)} %get-tuple-element.1151.q_ref.k_ref.v_ref, bf16[1024,2304]{1,0:T(8,128)(2,1)} %get-tuple-element.1151.q_ref.k_ref.v_ref, ...), custom_call_target="tpu_custom_call" | custom-call | flops 1 | bytes 1 | tf_op jit(solution)/shard_map/attn_fwd_self/pallas_call | solution.py:133
  82.1 9.4 %attn_fwd_self.3 = (bf16[1024,384]{1,0:T(8,128)(2,1)}, bf16[2,6,512,512]{3,2,1,0:T(8,128)(2,1)}, f32[2,6,8,512]{3,2,1,0:T(8,128)}) custom-call(bf16[1024,2304]{1,0:T(8,128)(2,1)} %get-tuple-element.1151.q_ref.k_ref.v_ref, bf16[1024,2304]{1,0:T(8,128)(2,1)} %get-tuple-element.1151.q_ref.k_ref.v_ref, bf16[1024,2304]{1,0:T(8,128)(2,1)} %get-tuple-element.1151.q_ref.k_ref.v_ref, ...), custom_call_target="tpu_custom_call" | custom-call | flops 1 | bytes 1 | tf_op jit(solution)/shard_map/attn_fwd_self/pallas_call | solution.py:133
  91.5 4.7 %collective-permute-done.17.refs_5_ = bf16[192,1920]{1,0:T(8,128)(2,1)S(1)} collective-permute-done((bf16[192,1920]{1,0:T(8,128)(2,1)S(1)}, bf16[192,1920]{1,0:T(8,128)(2,1)S(1)}, u32[]{:S(2)}, u32[]{:S(2)}) %collective-permute-start.17) | collective-permute-done | bytes 737312 | tf_op jit(solution)/shard_map/ppermute | solution.py:320
  102.5 5.6 %assemble.3.wo_ref.wc_ref.wq_ref.ck_ref.cv_ref = bf16[768,3840]{1,0:T(8,128)(2,1)} custom-call(s32[1]{0:T(128)} %bitcast.12.me_ref, bf16[192,1920]{1,0:T(8,128)(2,1)} %copy-done.2, bf16[192,1920]{1,0:T(8,128)(2,1)} %copy-done.9, bf16[192,1920]{1,0:T(8,128)(2,1)} %copy-done.10, bf16[192,1920]{1,0:T(8,128)(2,1)} %copy-done.11, bf16[192,1920]{1,0:T(8,128)(2,1)} %copy-done.1, ...), custom_call_target="tpu_custom_call" | custom-call | flops 1 | bytes 1 | tf_op jit(solution)/shard_map/assemble/pallas_call | solution.py:377
  108.2 13.1 %mid.1 = (f32[1024,768]{1,0:T(8,128)}, bf16[768,1024]{1,0:T(8,128)(2,1)}, bf16[1024,768]{1,0:T(8,128)(2,1)}, bf16[1024,1536]{1,0:T(8,128)(2,1)}, bf16[768,1024]{1,0:T(8,128)(2,1)}) custom-call(bf16[1024,768]{1,0:T(8,128)(2,1)} %bitcast.147, bf16[1024,768]{1,0:T(8,128)(2,1)} %bitcast.154, f32[3,768]{1,0:T(4,128)} %bitcast.161, ...), custom_call_target="tpu_custom_call" | custom-call | flops 1 | bytes 1 | tf_op jit(solution)/shard_map/mid/pallas_call | solution.py:547
  121.3 16.7 %attn_fwd_cross.1 = (bf16[1024,768]{1,0:T(8,128)(2,1)}, bf16[2,12,512,512]{3,2,1,0:T(8,128)(2,1)}, f32[2,12,8,512]{3,2,1,0:T(8,128)}) custom-call(bf16[1024,768]{1,0:T(8,128)(2,1)} %get-tuple-element.997.q_ref, bf16[1024,1536]{1,0:T(8,128)(2,1)} %get-tuple-element.998.k_ref.v_ref, bf16[1024,1536]{1,0:T(8,128)(2,1)} %get-tuple-element.998.k_ref.v_ref, ...), custom_call_target="tpu_custom_call" | custom-call | flops 1 | bytes 1 | tf_op jit(solution)/shard_map/attn_fwd_cross/pallas_call | solution.py:133
  137.9 6.8 %third.1 = (f32[1024,768]{1,0:T(8,128)}, bf16[1024,768]{1,0:T(8,128)(2,1)}, bf16[768,1024]{1,0:T(8,128)(2,1)}, bf16[768,1024]{1,0:T(8,128)(2,1)}) custom-call(f32[1024,768]{1,0:T(8,128)} %get-tuple-element.1051.x2_ref, bf16[1024,768]{1,0:T(8,128)(2,1)} %bitcast.143, f32[3,768]{1,0:T(4,128)} %bitcast.162, ...), custom_call_target="tpu_custom_call" | custom-call | flops 1 | bytes 1 | tf_op jit(solution)/shard_map/third/pallas_call | solution.py:547
  144.8 36.7 %ffn.1 = (f32[1024,768]{1,0:T(8,128)}, f32[1024,768]{1,0:T(8,128)}, bf16[768,6144]{1,0:T(8,128)(2,1)}) custom-call(bf16[1024,768]{1,0:T(8,128)(2,1)} %get-tuple-element.935.n_ref, bf16[768,1024]{1,0:T(8,128)(2,1)} %get-tuple-element.936.nt_ref, bf16[1024,768]{1,0:T(8,128)(2,1)} %bitcast.144, bf16[768,1024]{1,0:T(8,128)(2,1)} %get-tuple-element.938.gt_ref, ...), custom_call_target="tpu_custom_call" | custom-call | flops 1 | bytes 1 | tf_op jit(solution)/shard_map/ffn/pallas_call | solution.py:547
  181.5 8.3 %top.1 = (bf16[1024,768]{1,0:T(8,128)(2,1)}, f32[1024,768]{1,0:T(8,128)}, bf16[768,1024]{1,0:T(8,128)(2,1)}, bf16[1024,768]{1,0:T(8,128)(2,1)}, f32[8,768]{1,0:T(8,128)}) custom-call(f32[1024,768]{1,0:T(8,128)} %get-tuple-element.969.y_ref, f32[1024,768]{1,0:T(8,128)} %get-tuple-element.968.dn_ref, f32[1024,768]{1,0:T(8,128)} %get-tuple-element.970.x3_ref, ...), custom_call_target="tpu_custom_call" | custom-call | flops 1 | bytes 1 | tf_op jit(solution)/shard_map/top/pallas_call | solution.py:547
  189.8 19.5 %attn_bwd_cross.1 = (bf16[1024,768]{1,0:T(8,128)(2,1)}, bf16[1024,768]{1,0:T(8,128)(2,1)}, bf16[1024,768]{1,0:T(8,128)(2,1)}) custom-call(bf16[1024,768]{1,0:T(8,128)(2,1)} %get-tuple-element.997.q_ref, bf16[1024,1536]{1,0:T(8,128)(2,1)} %get-tuple-element.998.k_ref.v_ref, bf16[1024,1536]{1,0:T(8,128)(2,1)} %get-tuple-element.998.k_ref.v_ref, ...), custom_call_target="tpu_custom_call" | custom-call | flops 1 | bytes 1 | tf_op jit(solution)/shard_map/attn_bwd_cross/pallas_call | solution.py:231
  209.3 8.8 %grads_cross.1 = (bf16[1,4,96,2304]{3,2,1,0:T(8,128)(2,1)}, bf16[1,4,96,2304]{3,2,1,0:T(8,128)(2,1)}) custom-call(s32[1]{0:T(128)} %bitcast.me_ref, bf16[768,1024]{1,0:T(8,128)(2,1)} %get-tuple-element.1025.refs_0_, bf16[768,1024]{1,0:T(8,128)(2,1)} %get-tuple-element.1026.refs_1_, bf16[1024,768]{1,0:T(8,128)(2,1)} %get-tuple-element.1055.refs_2_.refs_0_, ...), custom_call_target="tpu_custom_call" | custom-call | flops 1 | bytes 1 | tf_op jit(solution)/shard_map/grads_cross/pallas_call | solution.py:732
  218.3 10.3 %second.1 = (f32[1024,768]{1,0:T(8,128)}, bf16[768,1024]{1,0:T(8,128)(2,1)}, bf16[1024,768]{1,0:T(8,128)(2,1)}, f32[8,768]{1,0:T(8,128)}) custom-call(f32[1024,768]{1,0:T(8,128)} %get-tuple-element.1051.x2_ref, f32[1024,768]{1,0:T(8,128)} %get-tuple-element.1052.dx3_ref, f32[3,768]{1,0:T(4,128)} %bitcast.164, ...), custom_call_target="tpu_custom_call" | custom-call | flops 1 | bytes 1 | tf_op jit(solution)/shard_map/second/pallas_call | solution.py:547
  228.6 6.8 %grads_out.1 = (bf16[1,4,96,1536]{3,2,1,0:T(8,128)(2,1)}, bf16[1,4,96,1536]{3,2,1,0:T(8,128)(2,1)}) custom-call(s32[1]{0:T(128)} %bitcast.me_ref, bf16[768,1024]{1,0:T(8,128)(2,1)} %get-tuple-element.1077.refs_0_, bf16[768,1024]{1,0:T(8,128)(2,1)} %get-tuple-element.1078.refs_1_, bf16[1024,768]{1,0:T(8,128)(2,1)} %get-tuple-element.1079.refs_0_.o_ref.refs_2_, ...), custom_call_target="tpu_custom_call" | custom-call | flops 1 | bytes 1 | tf_op jit(solution)/shard_map/grads_out/pallas_call | solution.py:732
  239.3 13.1 %attn_bwd_self.2 = (bf16[1024,384]{1,0:T(8,128)(2,1)}, bf16[1024,384]{1,0:T(8,128)(2,1)}, bf16[1024,384]{1,0:T(8,128)(2,1)}, f32[6,4,256]{2,1,0:T(4,128)}) custom-call(bf16[1024,2304]{1,0:T(8,128)(2,1)} %get-tuple-element.1151.q_ref.k_ref.v_ref, bf16[1024,2304]{1,0:T(8,128)(2,1)} %get-tuple-element.1151.q_ref.k_ref.v_ref, ...), custom_call_target="tpu_custom_call" | custom-call | flops 1 | bytes 1 | tf_op jit(solution)/shard_map/attn_bwd_self/pallas_call | solution.py:231
  255.9 5.8 %grads_self.2 = (bf16[1,4,96,1152]{3,2,1,0:T(8,128)(2,1)}, bf16[1,4,96,1152]{3,2,1,0:T(8,128)(2,1)}) custom-call(s32[1]{0:T(128)} %bitcast.me_ref, bf16[768,1024]{1,0:T(8,128)(2,1)} %get-tuple-element.1180.refs_0_, bf16[1024,384]{1,0:T(8,128)(2,1)} %get-tuple-element.1210.refs_1_.refs_0_, bf16[1024,384]{1,0:T(8,128)(2,1)} %get-tuple-element.1207.refs_2_, ...), custom_call_target="tpu_custom_call" | custom-call | flops 1 | bytes 1 | tf_op jit(solution)/shard_map/grads_self/pallas_call | solution.py:732
  261.8 6.9 %collective-permute-done.24 = bf16[2,96,2304]{2,1,0:T(8,128)(2,1)S(1)} collective-permute-done((bf16[2,96,2304]{2,1,0:T(8,128)(2,1)}, bf16[2,96,2304]{2,1,0:T(8,128)(2,1)S(1)}, u32[]{:S(2)}, u32[]{:S(2)}) %collective-permute-start.24) | collective-permute-done | bytes 884768 | tf_op jit(solution)/shard_map/ppermute | solution.py:407
  269.1 13.2 %attn_bwd_self.3 = (bf16[1024,384]{1,0:T(8,128)(2,1)}, bf16[1024,384]{1,0:T(8,128)(2,1)}, bf16[1024,384]{1,0:T(8,128)(2,1)}, f32[6,4,256]{2,1,0:T(4,128)}) custom-call(bf16[1024,2304]{1,0:T(8,128)(2,1)} %get-tuple-element.1151.q_ref.k_ref.v_ref, bf16[1024,2304]{1,0:T(8,128)(2,1)} %get-tuple-element.1151.q_ref.k_ref.v_ref, ...), custom_call_target="tpu_custom_call" | custom-call | flops 1 | bytes 1 | tf_op jit(solution)/shard_map/attn_bwd_self/pallas_call | solution.py:231
  282.3 5.7 %collective-permute-done.25 = bf16[1,96,2304]{2,1,0:T(8,128)(2,1)S(1)} collective-permute-done((bf16[1,96,2304]{2,1,0:T(8,128)(2,1)S(1)}, bf16[1,96,2304]{2,1,0:T(8,128)(2,1)S(1)}, u32[]{:S(2)}, u32[]{:S(2)}) %collective-permute-start.25) | collective-permute-done | bytes 442400 | tf_op jit(solution)/shard_map/ppermute | solution.py:407
  295.1 5.9 %grads_self.3 = (bf16[1,4,96,1152]{3,2,1,0:T(8,128)(2,1)}, bf16[1,4,96,1152]{3,2,1,0:T(8,128)(2,1)}) custom-call(s32[1]{0:T(128)} %bitcast.me_ref, bf16[768,1024]{1,0:T(8,128)(2,1)} %get-tuple-element.1180.refs_0_, bf16[1024,384]{1,0:T(8,128)(2,1)} %get-tuple-element.1211.refs_1_, bf16[1024,384]{1,0:T(8,128)(2,1)} %get-tuple-element.1208.refs_2_.refs_3_, ...), custom_call_target="tpu_custom_call" | custom-call | flops 1 | bytes 1 | tf_op jit(solution)/shard_map/grads_self/pallas_call | solution.py:732
  307.1 11.6 %last.1 = (f32[1024,768]{1,0:T(8,128)}, f32[8,768]{1,0:T(8,128)}) custom-call(bf16[1024,768]{1,0:T(8,128)(2,1)} %bitcast.148, f32[1024,768]{1,0:T(8,128)} %get-tuple-element.1216.dx2_ref, f32[3,768]{1,0:T(4,128)} %bitcast.165, bf16[768,2432]{1,0:T(8,128)(2,1)} %assemble.2.w_ref.wq_ref.wk_ref.wv_ref, bf16[768,2432]{1,0:T(8,128)(2,1)} %assemble.2.w_ref.wq_ref.wk_ref.wv_ref, ...), custom_call_target="tpu_custom_call" | custom-call | flops 1 | bytes 1 | tf_op jit(solution)/shard_map/last/pallas_call | solution.py:547
  318.8 4.9 %collective-permute-done.34 = bf16[1,96,1152]{2,1,0:T(8,128)(2,1)S(1)} collective-permute-done((bf16[1,96,1152]{2,1,0:T(8,128)(2,1)}, bf16[1,96,1152]{2,1,0:T(8,128)(2,1)S(1)}, u32[]{:S(2)}, u32[]{:S(2)}) %collective-permute-start.34) | collective-permute-done | bytes 221216 | tf_op jit(solution)/shard_map/ppermute | solution.py:405
  331.4 6.1 %encoder_grad.1 = f32[1024,768]{1,0:T(8,128)} custom-call(bf16[768,3840]{1,0:T(8,128)(2,1)} %assemble.3.wo_ref.wc_ref.wq_ref.ck_ref.cv_ref, bf16[768,3840]{1,0:T(8,128)(2,1)} %assemble.3.wo_ref.wc_ref.wq_ref.ck_ref.cv_ref, bf16[1024,768]{1,0:T(8,128)(2,1)} %get-tuple-element.1238.refs_3_.refs_0_, bf16[1024,768]{1,0:T(8,128)(2,1)} %get-tuple-element.1239.refs_4_.refs_1_), custom_call_target="tpu_custom_call" | custom-call | flops 1 | bytes 1 | tf_op jit(solution)/shard_map/encoder_grad/pallas_call | solution.py:547
  342.3 4.3 %collective-permute-start.43 = (bf16[1,24,3840]{2,1,0:T(8,128)(2,1)S(1)}, bf16[1,24,3840]{2,1,0:T(8,128)(2,1)S(1)}, u32[]{:S(2)}, u32[]{:S(2)}) collective-permute-start(bf16[1,24,3840]{2,1,0:T(8,128)(2,1)S(1)} %pad_maximum_fusion.9), channel_id=1, source_target_pairs={{0,3},{1,2},{2,1},{3,0},{4,7},{5,6},{6,5},{7,4},{8,11},{9,10},{10,... | collective-permute-start | bytes 552968 | tf_op jit(solution)/shard_map/ppermute | solution.py:403
  346.6 5.7 %collective-permute-start.42 = (bf16[1,24,3840]{2,1,0:T(8,128)(2,1)S(1)}, bf16[1,24,3840]{2,1,0:T(8,128)(2,1)S(1)}, u32[]{:S(2)}, u32[]{:S(2)}) collective-permute-start(bf16[1,24,3840]{2,1,0:T(8,128)(2,1)S(1)} %pad_maximum_fusion.8), channel_id=1, source_target_pairs={{0,2},{1,3},{2,0},{3,1},{4,6},{5,7},{6,4},{7,5},{8,10},{9,11},{10,... | collective-permute-start | bytes 552968 | tf_op jit(solution)/shard_map/ppermute | solution.py:403
  358.2 5.9 %collective-permute-done.42 = bf16[1,24,3840]{2,1,0:T(8,128)(2,1)S(1)} collective-permute-done((bf16[1,24,3840]{2,1,0:T(8,128)(2,1)S(1)}, bf16[1,24,3840]{2,1,0:T(8,128)(2,1)S(1)}, u32[]{:S(2)}, u32[]{:S(2)}) %collective-permute-start.42) | collective-permute-done | bytes 184352 | tf_op jit(solution)/shard_map/ppermute | solution.py:403
  364.1 3.2 collective-permute-start.46
  369.0 3.8 collective-permute-done.47
  (228 shorter events, 89.7 us)
Async XLA Ops:
  7.2 137.6 %all-gather.2.cloned.1.call-start = ((), (), s32[]{:S(2)}) async-start(), calls=%async_computation.1 | async-start | bytes 9732096 | tf_op jit(solution)/shard_map/all_gather | solution.py:888
  9.6 14.4 %collective-permute-start = (bf16[24,2432]{1,0:T(8,128)(2,1)S(1)}, bf16[24,2432]{1,0:T(8,128)(2,1)S(1)}, u32[]{:S(2)}, u32[]{:S(2)}) collective-permute-start(bf16[24,2432]{1,0:T(8,128)(2,1)S(1)} %fusion.4), channel_id=1, source_target_pairs={{0,1},{1,0},{2,3},{3,2},{4,5},{5,4},{6,7},{7,6},{8,9},{9,8},{10,11... | collective-permute-start | bytes 350216 | tf_op jit(solution)/shard_map/ppermute | solution.py:316
  12.7 11.9 %collective-permute-start.1 = (bf16[24,2432]{1,0:T(8,128)(2,1)S(1)}, bf16[24,2432]{1,0:T(8,128)(2,1)S(1)}, u32[]{:S(2)}, u32[]{:S(2)}) collective-permute-start(bf16[24,2432]{1,0:T(8,128)(2,1)S(1)} %fusion.4), channel_id=1, source_target_pairs={{0,2},{1,3},{2,0},{3,1},{4,6},{5,7},{6,4},{7,5},{8,10},{9,11},{10,... | collective-permute-start | bytes 350216 | tf_op jit(solution)/shard_map/ppermute | solution.py:316
  32.3 11.1 %collective-permute-start.6 = (bf16[192,1280]{1,0:T(8,128)(2,1)S(1)}, bf16[192,1280]{1,0:T(8,128)(2,1)S(1)}, u32[]{:S(2)}, u32[]{:S(2)}) collective-permute-start(bf16[192,1280]{1,0:T(8,128)(2,1)S(1)} %constant_dynamic-update-slice_fusion.3.refs_4_), channel_id=1, source_target_pairs={{0,8},{4,12},{8,0},{12,4},{16,24},{20,28},{24,16},{28,20},{1,9},{5... | collective-permute-start | bytes 1474568 | tf_op jit(solution)/shard_map/ppermute | solution.py:320
  36.3 14.3 %collective-permute-start.12 = (bf16[24,3840]{1,0:T(8,128)(2,1)S(1)}, bf16[24,3840]{1,0:T(8,128)(2,1)S(1)}, u32[]{:S(2)}, u32[]{:S(2)}) collective-permute-start(bf16[24,3840]{1,0:T(8,128)(2,1)S(1)} %bitcast_dynamic-update-slice_fusion), channel_id=1, source_target_pairs={{0,2},{1,3},{2,0},{3,1},{4,6},{5,7},{6,4},{7,5},{8,10},{9,11},{10,... | collective-permute-start | bytes 552968 | tf_op jit(solution)/shard_map/ppermute | solution.py:316
  38.7 12.7 %collective-permute-start.13 = (bf16[24,3840]{1,0:T(8,128)(2,1)S(1)}, bf16[24,3840]{1,0:T(8,128)(2,1)}, u32[]{:S(2)}, u32[]{:S(2)}) collective-permute-start(bf16[24,3840]{1,0:T(8,128)(2,1)S(1)} %bitcast_dynamic-update-slice_fusion), channel_id=1, source_target_pairs={{0,3},{1,2},{2,1},{3,0},{4,7},{5,6},{6,5},{7,4},{8,11},{9,10},{10,... | collective-permute-start | bytes 552968 | tf_op jit(solution)/shard_map/ppermute | solution.py:316
  52.6 284.9 %reduce-scatter.2.cloned.1.call-start = ((), (), s32[]{:S(2)}) async-start(), calls=%async_computation.2 | async-start | bytes 9732096 | tf_op jit(solution)/shard_map/reduce_scatter | solution.py:903
  54.4 15.6 %collective-permute-start.14 = (bf16[96,1920]{1,0:T(8,128)(2,1)S(1)}, bf16[96,1920]{1,0:T(8,128)(2,1)S(1)}, u32[]{:S(2)}, u32[]{:S(2)}) collective-permute-start(bf16[96,1920]{1,0:T(8,128)(2,1)S(1)} %get-tuple-element.767), channel_id=1, source_target_pairs={{0,8},{4,12},{8,0},{12,4},{16,24},{20,28},{24,16},{28,20},{1,9},{5... | collective-permute-start | bytes 1105928 | tf_op jit(solution)/shard_map/ppermute | solution.py:320
  55.0 15.0 %collective-permute-start.15 = (bf16[96,1920]{1,0:T(8,128)(2,1)S(1)}, bf16[96,1920]{1,0:T(8,128)(2,1)S(1)}, u32[]{:S(2)}, u32[]{:S(2)}) collective-permute-start(bf16[96,1920]{1,0:T(8,128)(2,1)S(1)} %get-tuple-element.769), channel_id=1, source_target_pairs={{0,16},{4,20},{8,24},{12,28},{16,0},{20,4},{24,8},{28,12},{1,17},{... | collective-permute-start | bytes 1105928 | tf_op jit(solution)/shard_map/ppermute | solution.py:320
  70.1 26.1 %collective-permute-start.17 = (bf16[192,1920]{1,0:T(8,128)(2,1)S(1)}, bf16[192,1920]{1,0:T(8,128)(2,1)S(1)}, u32[]{:S(2)}, u32[]{:S(2)}) collective-permute-start(bf16[192,1920]{1,0:T(8,128)(2,1)S(1)} %constant_dynamic-update-slice_fusion.7.refs_4_), channel_id=1, source_target_pairs={{0,8},{4,12},{8,0},{12,4},{16,24},{20,28},{24,16},{28,20},{1,9},{5... | collective-permute-start | bytes 2211848 | tf_op jit(solution)/shard_map/ppermute | solution.py:320
  71.7 24.5 %collective-permute-start.16 = (bf16[192,1920]{1,0:T(8,128)(2,1)S(1)}, bf16[192,1920]{1,0:T(8,128)(2,1)S(1)}, u32[]{:S(2)}, u32[]{:S(2)}) collective-permute-start(bf16[192,1920]{1,0:T(8,128)(2,1)S(1)} %constant_dynamic-update-slice_fusion.5.refs_0_), channel_id=1, source_target_pairs={{0,16},{4,20},{8,24},{12,28},{16,0},{20,4},{24,8},{28,12},{1,17},{... | collective-permute-start | bytes 2211848 | tf_op jit(solution)/shard_map/ppermute | solution.py:320
  235.4 16.9 %collective-permute-start.23 = (bf16[1,4,96,1536]{3,2,1,0:T(8,128)(2,1)}, bf16[1,4,96,1536]{3,2,1,0:T(8,128)(2,1)}, u32[]{:S(2)}, u32[]{:S(2)}) collective-permute-start(bf16[1,4,96,1536]{3,2,1,0:T(8,128)(2,1)} %get-tuple-element.1125), channel_id=1, source_target_pairs={{0,4},{4,0},{8,12},{12,8},{16,20},{20,16},{24,28},{28,24},{1,5},{5... | collective-permute-start | bytes 3538952 | tf_op jit(solution)/shard_map/ppermute | solution.py:407
  237.4 31.3 %collective-permute-start.24 = (bf16[2,96,2304]{2,1,0:T(8,128)(2,1)}, bf16[2,96,2304]{2,1,0:T(8,128)(2,1)S(1)}, u32[]{:S(2)}, u32[]{:S(2)}) collective-permute-start(bf16[2,96,2304]{2,1,0:T(8,128)(2,1)} %get-tuple-element.1342), channel_id=1, source_target_pairs={{0,8},{4,12},{8,0},{12,4},{16,24},{20,28},{24,16},{28,20},{1,9},{5... | collective-permute-start | bytes 2654216 | tf_op jit(solution)/shard_map/ppermute | solution.py:407
  254.9 33.1 %collective-permute-start.26 = (bf16[1,192,1536]{2,1,0:T(8,128)(2,1)}, bf16[1,192,1536]{2,1,0:T(8,128)(2,1)}, u32[]{:S(2)}, u32[]{:S(2)}) collective-permute-start(bf16[1,192,1536]{2,1,0:T(8,128)(2,1)} %get-tuple-element.1344), channel_id=1, source_target_pairs={{0,16},{4,20},{8,24},{12,28},{16,0},{20,4},{24,8},{28,12},{1,17},{... | collective-permute-start | bytes 1769480 | tf_op jit(solution)/shard_map/ppermute | solution.py:407
  268.7 19.3 %collective-permute-start.27 = (bf16[1,4,96,1152]{3,2,1,0:T(8,128)(2,1)}, bf16[1,4,96,1152]{3,2,1,0:T(8,128)(2,1)S(1)}, u32[]{:S(2)}, u32[]{:S(2)}) collective-permute-start(bf16[1,4,96,1152]{3,2,1,0:T(8,128)(2,1)} %get-tuple-element.1179), channel_id=1, source_target_pairs={{0,4},{4,0},{8,12},{12,8},{16,20},{20,16},{24,28},{28,24},{1,5},{5... | collective-permute-start | bytes 2654216 | tf_op jit(solution)/shard_map/ppermute | solution.py:407
  268.9 19.0 %collective-permute-start.25 = (bf16[1,96,2304]{2,1,0:T(8,128)(2,1)S(1)}, bf16[1,96,2304]{2,1,0:T(8,128)(2,1)S(1)}, u32[]{:S(2)}, u32[]{:S(2)}) collective-permute-start(bf16[1,96,2304]{2,1,0:T(8,128)(2,1)S(1)} %get-tuple-element.1354), channel_id=1, source_target_pairs={{0,16},{4,20},{8,24},{12,28},{16,0},{20,4},{24,8},{28,12},{1,17},{... | collective-permute-start | bytes 1327112 | tf_op jit(solution)/shard_map/ppermute | solution.py:407
  288.1 12.8 %collective-permute-start.28 = (bf16[1,24,2304]{2,1,0:T(8,128)(2,1)S(1)}, bf16[1,24,2304]{2,1,0:T(8,128)(2,1)S(1)}, u32[]{:S(2)}, u32[]{:S(2)}) collective-permute-start(bf16[1,24,2304]{2,1,0:T(8,128)(2,1)S(1)} %get-tuple-element.1370), channel_id=1, source_target_pairs={{0,1},{1,0},{2,3},{3,2},{4,5},{5,4},{6,7},{7,6},{8,9},{9,8},{10,11... | collective-permute-start | bytes 331784 | tf_op jit(solution)/shard_map/ppermute | solution.py:403
  288.2 14.9 %collective-permute-start.29 = (bf16[1,24,2304]{2,1,0:T(8,128)(2,1)S(1)}, bf16[1,24,2304]{2,1,0:T(8,128)(2,1)S(1)}, u32[]{:S(2)}, u32[]{:S(2)}) collective-permute-start(bf16[1,24,2304]{2,1,0:T(8,128)(2,1)S(1)} %get-tuple-element.1369), channel_id=1, source_target_pairs={{0,2},{1,3},{2,0},{3,1},{4,6},{5,7},{6,4},{7,5},{8,10},{9,11},{10,... | collective-permute-start | bytes 331784 | tf_op jit(solution)/shard_map/ppermute | solution.py:403
  291.4 11.7 %collective-permute-start.30 = (bf16[1,24,2304]{2,1,0:T(8,128)(2,1)S(1)}, bf16[1,24,2304]{2,1,0:T(8,128)(2,1)S(1)}, u32[]{:S(2)}, u32[]{:S(2)}) collective-permute-start(bf16[1,24,2304]{2,1,0:T(8,128)(2,1)S(1)} %get-tuple-element.1368), channel_id=1, source_target_pairs={{0,3},{1,2},{2,1},{3,0},{4,7},{5,6},{6,5},{7,4},{8,11},{9,10},{10,... | collective-permute-start | bytes 331784 | tf_op jit(solution)/shard_map/ppermute | solution.py:403
  303.1 20.6 %collective-permute-start.35 = (bf16[1,4,96,1152]{3,2,1,0:T(8,128)(2,1)}, bf16[1,4,96,1152]{3,2,1,0:T(8,128)(2,1)S(1)}, u32[]{:S(2)}, u32[]{:S(2)}) collective-permute-start(bf16[1,4,96,1152]{3,2,1,0:T(8,128)(2,1)} %get-tuple-element.1236), channel_id=1, source_target_pairs={{0,4},{4,0},{8,12},{12,8},{16,20},{20,16},{24,28},{28,24},{1,5},{5... | collective-permute-start | bytes 2654216 | tf_op jit(solution)/shard_map/ppermute | solution.py:407
  303.1 15.6 %collective-permute-start.31 = (bf16[1,96,1536]{2,1,0:T(8,128)(2,1)S(1)}, bf16[1,96,1536]{2,1,0:T(8,128)(2,1)S(1)}, u32[]{:S(2)}, u32[]{:S(2)}) collective-permute-start(bf16[1,96,1536]{2,1,0:T(8,128)(2,1)S(1)} %get-tuple-element.1362), channel_id=1, source_target_pairs={{0,8},{4,12},{8,0},{12,4},{16,24},{20,28},{24,16},{28,20},{1,9},{5... | collective-permute-start | bytes 884744 | tf_op jit(solution)/shard_map/ppermute | solution.py:407
  303.5 15.2 %collective-permute-start.32 = (bf16[1,96,1152]{2,1,0:T(8,128)(2,1)}, bf16[1,96,1152]{2,1,0:T(8,128)(2,1)S(1)}, u32[]{:S(2)}, u32[]{:S(2)}) collective-permute-start(bf16[1,96,1152]{2,1,0:T(8,128)(2,1)} %get-tuple-element.1232), channel_id=1, source_target_pairs={{0,8},{4,12},{8,0},{12,4},{16,24},{20,28},{24,16},{28,20},{1,9},{5... | collective-permute-start | bytes 663560 | tf_op jit(solution)/shard_map/ppermute | solution.py:405
  305.2 13.6 %collective-permute-start.33 = (bf16[1,96,1152]{2,1,0:T(8,128)(2,1)}, bf16[1,96,1152]{2,1,0:T(8,128)(2,1)S(1)}, u32[]{:S(2)}, u32[]{:S(2)}) collective-permute-start(bf16[1,96,1152]{2,1,0:T(8,128)(2,1)} %get-tuple-element.1233), channel_id=1, source_target_pairs={{0,16},{4,20},{8,24},{12,28},{16,0},{20,4},{24,8},{28,12},{1,17},{... | collective-permute-start | bytes 663560 | tf_op jit(solution)/shard_map/ppermute | solution.py:405
  306.2 17.4 %collective-permute-start.34 = (bf16[1,96,1152]{2,1,0:T(8,128)(2,1)}, bf16[1,96,1152]{2,1,0:T(8,128)(2,1)S(1)}, u32[]{:S(2)}, u32[]{:S(2)}) collective-permute-start(bf16[1,96,1152]{2,1,0:T(8,128)(2,1)} %get-tuple-element.1234), channel_id=1, source_target_pairs={{0,24},{4,28},{8,16},{12,20},{16,8},{20,12},{24,0},{28,4},{1,25},{... | collective-permute-start | bytes 663560 | tf_op jit(solution)/shard_map/ppermute | solution.py:405
  326.4 12.6 %collective-permute-start.39 = (f32[21,128]{1,0:T(8,128)S(1)}, f32[21,128]{1,0:T(8,128)S(1)}, u32[]{:S(2)}, u32[]{:S(2)}) collective-permute-start(f32[21,128]{1,0:T(8,128)S(1)} %maximum_bitcast_fusion.2), channel_id=1, source_target_pairs={{0,4},{4,0},{8,12},{12,8},{16,20},{20,16},{24,28},{28,24},{1,5},{5... | collective-permute-start | bytes 32264 | tf_op jit(solution)/shard_map/ppermute | solution.py:465
  327.6 11.5 %collective-permute-start.36 = (bf16[1,96,1152]{2,1,0:T(8,128)(2,1)}, bf16[1,96,1152]{2,1,0:T(8,128)(2,1)S(1)}, u32[]{:S(2)}, u32[]{:S(2)}) collective-permute-start(bf16[1,96,1152]{2,1,0:T(8,128)(2,1)} %get-tuple-element.1348), channel_id=1, source_target_pairs={{0,8},{4,12},{8,0},{12,4},{16,24},{20,28},{24,16},{28,20},{1,9},{5... | collective-permute-start | bytes 663560 | tf_op jit(solution)/shard_map/ppermute | solution.py:405
  329.0 12.5 %collective-permute-start.37 = (bf16[1,96,1152]{2,1,0:T(8,128)(2,1)}, bf16[1,96,1152]{2,1,0:T(8,128)(2,1)S(1)}, u32[]{:S(2)}, u32[]{:S(2)}) collective-permute-start(bf16[1,96,1152]{2,1,0:T(8,128)(2,1)} %get-tuple-element.1347), channel_id=1, source_target_pairs={{0,16},{4,20},{8,24},{12,28},{16,0},{20,4},{24,8},{28,12},{1,17},{... | collective-permute-start | bytes 663560 | tf_op jit(solution)/shard_map/ppermute | solution.py:405
  329.4 12.1 %collective-permute-start.38 = (bf16[1,96,1152]{2,1,0:T(8,128)(2,1)S(1)}, bf16[1,96,1152]{2,1,0:T(8,128)(2,1)S(1)}, u32[]{:S(2)}, u32[]{:S(2)}) collective-permute-start(bf16[1,96,1152]{2,1,0:T(8,128)(2,1)S(1)} %get-tuple-element.1346), channel_id=1, source_target_pairs={{0,24},{4,28},{8,16},{12,20},{16,8},{20,12},{24,0},{28,4},{1,25},{... | collective-permute-start | bytes 663560 | tf_op jit(solution)/shard_map/ppermute | solution.py:405
  341.5 11.5 %collective-permute-start.40 = (f32[21,128]{1,0:T(8,128)S(1)}, f32[21,128]{1,0:T(8,128)S(1)}, u32[]{:S(2)}, u32[]{:S(2)}) collective-permute-start(f32[21,128]{1,0:T(8,128)S(1)} %add.198), channel_id=1, source_target_pairs={{0,8},{4,12},{8,0},{12,4},{16,24},{20,28},{24,16},{28,20},{1,9},{5... | collective-permute-start | bytes 32264 | tf_op jit(solution)/shard_map/ppermute | solution.py:465
  342.3 15.9 %collective-permute-start.43 = (bf16[1,24,3840]{2,1,0:T(8,128)(2,1)S(1)}, bf16[1,24,3840]{2,1,0:T(8,128)(2,1)S(1)}, u32[]{:S(2)}, u32[]{:S(2)}) collective-permute-start(bf16[1,24,3840]{2,1,0:T(8,128)(2,1)S(1)} %pad_maximum_fusion.9), channel_id=1, source_target_pairs={{0,3},{1,2},{2,1},{3,0},{4,7},{5,6},{6,5},{7,4},{8,11},{9,10},{10,... | collective-permute-start | bytes 552968 | tf_op jit(solution)/shard_map/ppermute | solution.py:403
  346.6 17.5 %collective-permute-start.42 = (bf16[1,24,3840]{2,1,0:T(8,128)(2,1)S(1)}, bf16[1,24,3840]{2,1,0:T(8,128)(2,1)S(1)}, u32[]{:S(2)}, u32[]{:S(2)}) collective-permute-start(bf16[1,24,3840]{2,1,0:T(8,128)(2,1)S(1)} %pad_maximum_fusion.8), channel_id=1, source_target_pairs={{0,2},{1,3},{2,0},{3,1},{4,6},{5,7},{6,4},{7,5},{8,10},{9,11},{10,... | collective-permute-start | bytes 552968 | tf_op jit(solution)/shard_map/ppermute | solution.py:403
  352.3 11.8 %collective-permute-start.41 = (bf16[1,24,3840]{2,1,0:T(8,128)(2,1)S(1)}, bf16[1,24,3840]{2,1,0:T(8,128)(2,1)S(1)}, u32[]{:S(2)}, u32[]{:S(2)}) collective-permute-start(bf16[1,24,3840]{2,1,0:T(8,128)(2,1)S(1)} %pad_maximum_fusion.7), channel_id=1, source_target_pairs={{0,1},{1,0},{2,3},{3,2},{4,5},{5,4},{6,7},{7,6},{8,9},{9,8},{10,11... | collective-permute-start | bytes 552968 | tf_op jit(solution)/shard_map/ppermute | solution.py:403
  (40 other events, 401.9 us)
Sparse Core Ops, SparseCore 0:
  52.7 88.3 all-gather.1
  181.6 152.4 reduce-scatter.1

commit v7 on v6

--- a/solution.py
+++ b/solution.py
@@ -455,29 +455,15 @@
     def __init__(self, sizes, value):
         self.value = value
         self.flight = None
-        self.narrow = sizes[1]
-        self.plan = [(sizes[0], bit) for bit in bits_of(sizes[0])] + ["narrow"]
+        self.plan = [(name, size, bit) for name, size in ((NARROW, sizes[1]), (WIDE, sizes[0])) for bit in bits_of(size)]
 
     def go(self):
-        if self.plan[0] == "narrow":
-            self.flight = [lax.ppermute(self.value, NARROW, flipped(self.narrow, k)) for k in range(1, self.narrow)]
-        else:
-            self.flight = [lax.ppermute(self.value, WIDE, flipped(*self.plan[0]))]
+        name, size, bit = self.plan[0]
+        self.flight = lax.ppermute(self.value, name, flipped(size, bit))
 
     def land(self):
-        if self.plan.pop(0) == "narrow":
-            at = lax.axis_index(NARROW)
-            parts = [self.value] + self.flight
-            total = None
-            for j in range(self.narrow):
-                term = parts[0]
-                for k in range(1, self.narrow):
-                    term = jnp.where((at ^ k) == j, parts[k], term)
-                total = term if total is None else total + term
-            self.value = total
-        else:
-            self.value = self.value + self.flight[0]
-        self.flight = None
+        self.plan.pop(0)
+        self.value, self.flight = self.value + self.flight, None
 
     def state(self, landing):
         return (self.value, self.flight if landing else None)
@@ -934,6 +920,8 @@
         so.join(other)
         r.moving.remove(other)
     r.run(None, [so, total], [total])
+    while len(total.plan) > 1:
+        r.run(None, [total], [total])
     r.run(None, [total], [so, total])
     while any(s.plan for s in (sc, so, total)):
         r.step(None, [sc, so, total])

time: 389 us -> 385 us (0.990)
    ppermute x6, starting transfers between devices: 15.1 us -> 9.03 us  [go(): lax.ppermute(s, NARROW, flipped(self.narrow, k + 1))]
    ppermute x6 -> x5, starting transfers between devices: 6.89 us -> 11.4 us  [go(): self.flight = lax.ppermute(self.value, name, flipped(size, bit))]
  transfers between devices with their start and end apart: 50 -> 49, of which waited for: 17 -> 16; matrix products, arithmetic and copies ran while one was open for 7% -> 7% of each run, Pallas kernels for 47% -> 48%
where the time goes in v7:
time: 385 us; the launch traced here: 381 us
  Pallas kernels  219 us (57%)
  waiting for transfers between devices  56.2 us (15%)
  starting transfers between devices  53.4 us (14%)
  local copies, waits for them, and re-layouts  22.7 us (6%)
  between operations  15.3 us (4%)
  other arithmetic  14.1 us (4%)
    pallas_call x8, Pallas kernels, call(): pl.pallas_call(kernel, grid=grid, in_specs=[spec(b, i) for _, b, i in ins...  101 us
    pallas_call x3, Pallas kernels, attn_bwd(): pl.pallas_call(functools.partial(attn_bwd_kernel, causal), grid=(pairs, r...  45.6 us
    pallas_call x3, Pallas kernels, attn_fwd(): pl.pallas_call(functools.partial(attn_fwd_kernel, causal), grid=(pairs, r...  35.4 us
    pallas_call x4, Pallas kernels, weight_grads(): pl.pallas_call(functools.partial(grads_kernel, first_rows, lefts, groups)...  27.3 us
    ppermute x16, waiting for transfers between devices, go(): lax.ppermute(p, WIDE, flipped(self.wide, self.orders[i][step]))  19.1 us
    ppermute x8, waiting for transfers between devices, go(): self.flight = [lax.ppermute(self.sends[0], WIDE, flipped(self.wide, step))]  12.6 us
    ppermute x5, starting transfers between devices, go(): self.flight = lax.ppermute(self.value, name, flipped(size, bit))  11.4 us
    ppermute x16, starting transfers between devices, go(): lax.ppermute(p, WIDE, flipped(self.wide, self.orders[i][step]))  11.3 us
  transfers between devices with their start and end apart: 49, of which 16 were waited for; matrix products, arithmetic and copies ran while one was open for 7% of the time, Pallas kernels for 48%

profile of v7, /device:TPU:0, one launch (start us, length us, event | category | flops | bytes accessed | tf_op | source)
XLA Modules:
  0.0 381.0 jit_solution(15369341320118505759)
XLA Ops:
  27.8 4.4 %collective-permute-done.3 = bf16[96,1152]{1,0:T(8,128)(2,1)S(1)} collective-permute-done((bf16[96,1152]{1,0:T(8,128)(2,1)S(1)}, bf16[96,1152]{1,0:T(8,128)(2,1)S(1)}, u32[]{:S(2)}, u32[]{:S(2)}) %collective-permute-start.3) | collective-permute-done | bytes 221216 | tf_op jit(solution)/shard_map/ppermute | solution.py:320
  39.0 4.4 %collective-permute-done.5.refs_1_ = bf16[192,1152]{1,0:T(8,128)(2,1)S(1)} collective-permute-done((bf16[192,1152]{1,0:T(8,128)(2,1)S(1)}, bf16[192,1152]{1,0:T(8,128)(2,1)S(1)}, u32[]{:S(2)}, u32[]{:S(2)}) %collective-permute-start.5) | collective-permute-done | bytes 442400 | tf_op jit(solution)/shard_map/ppermute | solution.py:320
  44.1 6.5 %collective-permute-done.12 = bf16[24,3840]{1,0:T(8,128)(2,1)S(1)} collective-permute-done((bf16[24,3840]{1,0:T(8,128)(2,1)S(1)}, bf16[24,3840]{1,0:T(8,128)(2,1)S(1)}, u32[]{:S(2)}, u32[]{:S(2)}) %collective-permute-start.12) | collective-permute-done | bytes 184352 | tf_op jit(solution)/shard_map/ppermute | solution.py:316
  56.0 4.1 %assemble.2.w_ref.wq_ref.wk_ref.wv_ref = bf16[768,2432]{1,0:T(8,128)(2,1)} custom-call(s32[1]{0:T(128)} %bitcast.12.me_ref, bf16[192,1152]{1,0:T(8,128)(2,1)} %copy-done.5, bf16[192,1152]{1,0:T(8,128)(2,1)} %copy-done.16, bf16[192,1152]{1,0:T(8,128)(2,1)} %collective-permute-done.7.refs_2_, bf16[192,1152]{1,0:T(8,128)(2,1)} %collective-permute-done.8.refs_3_, ...), custom_call_target="tpu_custom_call" | custom-call | flops 1 | bytes 1 | tf_op jit(solution)/shard_map/assemble/pallas_call | solution.py:377
  61.9 8.1 %proj_self.1 = (bf16[768,1024]{1,0:T(8,128)(2,1)}, bf16[1024,2304]{1,0:T(8,128)(2,1)}) custom-call(bf16[1024,768]{1,0:T(8,128)(2,1)} %bitcast.146, f32[3,768]{1,0:T(4,128)} %bitcast.160, bf16[768,2432]{1,0:T(8,128)(2,1)} %assemble.2.w_ref.wq_ref.wk_ref.wv_ref), custom_call_target="tpu_custom_call" | custom-call | flops 1 | bytes 1 | tf_op jit(solution)/shard_map/proj_self/pallas_call | solution.py:533
  72.7 9.3 %attn_fwd_self.2 = (bf16[1024,384]{1,0:T(8,128)(2,1)}, bf16[2,6,512,512]{3,2,1,0:T(8,128)(2,1)}, f32[2,6,8,512]{3,2,1,0:T(8,128)}) custom-call(bf16[1024,2304]{1,0:T(8,128)(2,1)} %get-tuple-element.1174.q_ref.k_ref.v_ref, bf16[1024,2304]{1,0:T(8,128)(2,1)} %get-tuple-element.1174.q_ref.k_ref.v_ref, bf16[1024,2304]{1,0:T(8,128)(2,1)} %get-tuple-element.1174.q_ref.k_ref.v_ref, ...), custom_call_target="tpu_custom_call" | custom-call | flops 1 | bytes 1 | tf_op jit(solution)/shard_map/attn_fwd_self/pallas_call | solution.py:133
  82.1 9.4 %attn_fwd_self.3 = (bf16[1024,384]{1,0:T(8,128)(2,1)}, bf16[2,6,512,512]{3,2,1,0:T(8,128)(2,1)}, f32[2,6,8,512]{3,2,1,0:T(8,128)}) custom-call(bf16[1024,2304]{1,0:T(8,128)(2,1)} %get-tuple-element.1174.q_ref.k_ref.v_ref, bf16[1024,2304]{1,0:T(8,128)(2,1)} %get-tuple-element.1174.q_ref.k_ref.v_ref, bf16[1024,2304]{1,0:T(8,128)(2,1)} %get-tuple-element.1174.q_ref.k_ref.v_ref, ...), custom_call_target="tpu_custom_call" | custom-call | flops 1 | bytes 1 | tf_op jit(solution)/shard_map/attn_fwd_self/pallas_call | solution.py:133
  91.5 4.7 %collective-permute-done.17.refs_5_ = bf16[192,1920]{1,0:T(8,128)(2,1)S(1)} collective-permute-done((bf16[192,1920]{1,0:T(8,128)(2,1)S(1)}, bf16[192,1920]{1,0:T(8,128)(2,1)S(1)}, u32[]{:S(2)}, u32[]{:S(2)}) %collective-permute-start.17) | collective-permute-done | bytes 737312 | tf_op jit(solution)/shard_map/ppermute | solution.py:320
  102.5 5.6 %assemble.3.wo_ref.wc_ref.wq_ref.ck_ref.cv_ref = bf16[768,3840]{1,0:T(8,128)(2,1)} custom-call(s32[1]{0:T(128)} %bitcast.12.me_ref, bf16[192,1920]{1,0:T(8,128)(2,1)} %copy-done.2, bf16[192,1920]{1,0:T(8,128)(2,1)} %copy-done.9, bf16[192,1920]{1,0:T(8,128)(2,1)} %copy-done.10, bf16[192,1920]{1,0:T(8,128)(2,1)} %copy-done.11, bf16[192,1920]{1,0:T(8,128)(2,1)} %copy-done.1, ...), custom_call_target="tpu_custom_call" | custom-call | flops 1 | bytes 1 | tf_op jit(solution)/shard_map/assemble/pallas_call | solution.py:377
  108.1 13.1 %mid.1 = (f32[1024,768]{1,0:T(8,128)}, bf16[768,1024]{1,0:T(8,128)(2,1)}, bf16[1024,768]{1,0:T(8,128)(2,1)}, bf16[1024,1536]{1,0:T(8,128)(2,1)}, bf16[768,1024]{1,0:T(8,128)(2,1)}) custom-call(bf16[1024,768]{1,0:T(8,128)(2,1)} %bitcast.147, bf16[1024,768]{1,0:T(8,128)(2,1)} %bitcast.154, f32[3,768]{1,0:T(4,128)} %bitcast.161, ...), custom_call_target="tpu_custom_call" | custom-call | flops 1 | bytes 1 | tf_op jit(solution)/shard_map/mid/pallas_call | solution.py:533
  121.2 16.6 %attn_fwd_cross.1 = (bf16[1024,768]{1,0:T(8,128)(2,1)}, bf16[2,12,512,512]{3,2,1,0:T(8,128)(2,1)}, f32[2,12,8,512]{3,2,1,0:T(8,128)}) custom-call(bf16[1024,768]{1,0:T(8,128)(2,1)} %get-tuple-element.1020.q_ref, bf16[1024,1536]{1,0:T(8,128)(2,1)} %get-tuple-element.1021.k_ref.v_ref, bf16[1024,1536]{1,0:T(8,128)(2,1)} %get-tuple-element.1021.k_ref.v_ref, ...), custom_call_target="tpu_custom_call" | custom-call | flops 1 | bytes 1 | tf_op jit(solution)/shard_map/attn_fwd_cross/pallas_call | solution.py:133
  137.9 6.8 %third.1 = (f32[1024,768]{1,0:T(8,128)}, bf16[1024,768]{1,0:T(8,128)(2,1)}, bf16[768,1024]{1,0:T(8,128)(2,1)}, bf16[768,1024]{1,0:T(8,128)(2,1)}) custom-call(f32[1024,768]{1,0:T(8,128)} %get-tuple-element.1074.x2_ref, bf16[1024,768]{1,0:T(8,128)(2,1)} %bitcast.143, f32[3,768]{1,0:T(4,128)} %bitcast.162, ...), custom_call_target="tpu_custom_call" | custom-call | flops 1 | bytes 1 | tf_op jit(solution)/shard_map/third/pallas_call | solution.py:533
  144.7 36.8 %ffn.1 = (f32[1024,768]{1,0:T(8,128)}, f32[1024,768]{1,0:T(8,128)}, bf16[768,6144]{1,0:T(8,128)(2,1)}) custom-call(bf16[1024,768]{1,0:T(8,128)(2,1)} %get-tuple-element.948.n_ref, bf16[768,1024]{1,0:T(8,128)(2,1)} %get-tuple-element.949.nt_ref, bf16[1024,768]{1,0:T(8,128)(2,1)} %bitcast.144, bf16[768,1024]{1,0:T(8,128)(2,1)} %get-tuple-element.951.gt_ref, ...), custom_call_target="tpu_custom_call" | custom-call | flops 1 | bytes 1 | tf_op jit(solution)/shard_map/ffn/pallas_call | solution.py:533
  181.5 8.3 %top.1 = (bf16[1024,768]{1,0:T(8,128)(2,1)}, f32[1024,768]{1,0:T(8,128)}, bf16[768,1024]{1,0:T(8,128)(2,1)}, bf16[1024,768]{1,0:T(8,128)(2,1)}, f32[8,768]{1,0:T(8,128)}) custom-call(f32[1024,768]{1,0:T(8,128)} %get-tuple-element.984.y_ref, f32[1024,768]{1,0:T(8,128)} %get-tuple-element.983.dn_ref, f32[1024,768]{1,0:T(8,128)} %get-tuple-element.985.x3_ref, ...), custom_call_target="tpu_custom_call" | custom-call | flops 1 | bytes 1 | tf_op jit(solution)/shard_map/top/pallas_call | solution.py:533
  189.8 19.4 %attn_bwd_cross.1 = (bf16[1024,768]{1,0:T(8,128)(2,1)}, bf16[1024,768]{1,0:T(8,128)(2,1)}, bf16[1024,768]{1,0:T(8,128)(2,1)}) custom-call(bf16[1024,768]{1,0:T(8,128)(2,1)} %get-tuple-element.1020.q_ref, bf16[1024,1536]{1,0:T(8,128)(2,1)} %get-tuple-element.1021.k_ref.v_ref, bf16[1024,1536]{1,0:T(8,128)(2,1)} %get-tuple-element.1021.k_ref.v_ref, ...), custom_call_target="tpu_custom_call" | custom-call | flops 1 | bytes 1 | tf_op jit(solution)/shard_map/attn_bwd_cross/pallas_call | solution.py:231
  209.3 8.8 %grads_cross.1 = (bf16[1,4,96,2304]{3,2,1,0:T(8,128)(2,1)}, bf16[1,4,96,2304]{3,2,1,0:T(8,128)(2,1)}) custom-call(s32[1]{0:T(128)} %bitcast.me_ref, bf16[768,1024]{1,0:T(8,128)(2,1)} %get-tuple-element.1048.refs_0_, bf16[768,1024]{1,0:T(8,128)(2,1)} %get-tuple-element.1049.refs_1_, bf16[1024,768]{1,0:T(8,128)(2,1)} %get-tuple-element.1078.refs_2_.refs_0_, ...), custom_call_target="tpu_custom_call" | custom-call | flops 1 | bytes 1 | tf_op jit(solution)/shard_map/grads_cross/pallas_call | solution.py:718
  218.2 10.3 %second.1 = (f32[1024,768]{1,0:T(8,128)}, bf16[768,1024]{1,0:T(8,128)(2,1)}, bf16[1024,768]{1,0:T(8,128)(2,1)}, f32[8,768]{1,0:T(8,128)}) custom-call(f32[1024,768]{1,0:T(8,128)} %get-tuple-element.1074.x2_ref, f32[1024,768]{1,0:T(8,128)} %get-tuple-element.1075.dx3_ref, f32[3,768]{1,0:T(4,128)} %bitcast.164, ...), custom_call_target="tpu_custom_call" | custom-call | flops 1 | bytes 1 | tf_op jit(solution)/shard_map/second/pallas_call | solution.py:533
  228.6 6.8 %grads_out.1 = (bf16[1,4,96,1536]{3,2,1,0:T(8,128)(2,1)}, bf16[1,4,96,1536]{3,2,1,0:T(8,128)(2,1)}) custom-call(s32[1]{0:T(128)} %bitcast.me_ref, bf16[768,1024]{1,0:T(8,128)(2,1)} %get-tuple-element.1100.refs_0_, bf16[768,1024]{1,0:T(8,128)(2,1)} %get-tuple-element.1101.refs_1_, bf16[1024,768]{1,0:T(8,128)(2,1)} %get-tuple-element.1102.refs_0_.o_ref.refs_2_, ...), custom_call_target="tpu_custom_call" | custom-call | flops 1 | bytes 1 | tf_op jit(solution)/shard_map/grads_out/pallas_call | solution.py:718
  239.2 13.0 %attn_bwd_self.2 = (bf16[1024,384]{1,0:T(8,128)(2,1)}, bf16[1024,384]{1,0:T(8,128)(2,1)}, bf16[1024,384]{1,0:T(8,128)(2,1)}, f32[6,4,256]{2,1,0:T(4,128)}) custom-call(bf16[1024,2304]{1,0:T(8,128)(2,1)} %get-tuple-element.1174.q_ref.k_ref.v_ref, bf16[1024,2304]{1,0:T(8,128)(2,1)} %get-tuple-element.1174.q_ref.k_ref.v_ref, ...), custom_call_target="tpu_custom_call" | custom-call | flops 1 | bytes 1 | tf_op jit(solution)/shard_map/attn_bwd_self/pallas_call | solution.py:231
  255.9 5.8 %grads_self.2 = (bf16[1,4,96,1152]{3,2,1,0:T(8,128)(2,1)}, bf16[1,4,96,1152]{3,2,1,0:T(8,128)(2,1)}) custom-call(s32[1]{0:T(128)} %bitcast.me_ref, bf16[768,1024]{1,0:T(8,128)(2,1)} %get-tuple-element.1203.refs_0_, bf16[1024,384]{1,0:T(8,128)(2,1)} %get-tuple-element.1233.refs_1_.refs_0_, bf16[1024,384]{1,0:T(8,128)(2,1)} %get-tuple-element.1230.refs_2_, ...), custom_call_target="tpu_custom_call" | custom-call | flops 1 | bytes 1 | tf_op jit(solution)/shard_map/grads_self/pallas_call | solution.py:718
  261.7 6.9 %collective-permute-done.24 = bf16[2,96,2304]{2,1,0:T(8,128)(2,1)S(1)} collective-permute-done((bf16[2,96,2304]{2,1,0:T(8,128)(2,1)}, bf16[2,96,2304]{2,1,0:T(8,128)(2,1)S(1)}, u32[]{:S(2)}, u32[]{:S(2)}) %collective-permute-start.24) | collective-permute-done | bytes 884768 | tf_op jit(solution)/shard_map/ppermute | solution.py:407
  269.1 13.2 %attn_bwd_self.3 = (bf16[1024,384]{1,0:T(8,128)(2,1)}, bf16[1024,384]{1,0:T(8,128)(2,1)}, bf16[1024,384]{1,0:T(8,128)(2,1)}, f32[6,4,256]{2,1,0:T(4,128)}) custom-call(bf16[1024,2304]{1,0:T(8,128)(2,1)} %get-tuple-element.1174.q_ref.k_ref.v_ref, bf16[1024,2304]{1,0:T(8,128)(2,1)} %get-tuple-element.1174.q_ref.k_ref.v_ref, ...), custom_call_target="tpu_custom_call" | custom-call | flops 1 | bytes 1 | tf_op jit(solution)/shard_map/attn_bwd_self/pallas_call | solution.py:231
  282.2 5.7 %collective-permute-done.25 = bf16[1,96,2304]{2,1,0:T(8,128)(2,1)S(1)} collective-permute-done((bf16[1,96,2304]{2,1,0:T(8,128)(2,1)S(1)}, bf16[1,96,2304]{2,1,0:T(8,128)(2,1)S(1)}, u32[]{:S(2)}, u32[]{:S(2)}) %collective-permute-start.25) | collective-permute-done | bytes 442400 | tf_op jit(solution)/shard_map/ppermute | solution.py:407
  288.1 3.1 collective-permute-start.29
  295.0 5.8 %grads_self.3 = (bf16[1,4,96,1152]{3,2,1,0:T(8,128)(2,1)}, bf16[1,4,96,1152]{3,2,1,0:T(8,128)(2,1)}) custom-call(s32[1]{0:T(128)} %bitcast.me_ref, bf16[768,1024]{1,0:T(8,128)(2,1)} %get-tuple-element.1203.refs_0_, bf16[1024,384]{1,0:T(8,128)(2,1)} %get-tuple-element.1234.refs_1_, bf16[1024,384]{1,0:T(8,128)(2,1)} %get-tuple-element.1231.refs_2_.refs_3_, ...), custom_call_target="tpu_custom_call" | custom-call | flops 1 | bytes 1 | tf_op jit(solution)/shard_map/grads_self/pallas_call | solution.py:718
  307.0 11.6 %last.1 = (f32[1024,768]{1,0:T(8,128)}, f32[8,768]{1,0:T(8,128)}) custom-call(bf16[1024,768]{1,0:T(8,128)(2,1)} %bitcast.148, f32[1024,768]{1,0:T(8,128)} %get-tuple-element.1239.dx2_ref, f32[3,768]{1,0:T(4,128)} %bitcast.165, bf16[768,2432]{1,0:T(8,128)(2,1)} %assemble.2.w_ref.wq_ref.wk_ref.wv_ref, bf16[768,2432]{1,0:T(8,128)(2,1)} %assemble.2.w_ref.wq_ref.wk_ref.wv_ref, ...), custom_call_target="tpu_custom_call" | custom-call | flops 1 | bytes 1 | tf_op jit(solution)/shard_map/last/pallas_call | solution.py:533
  318.7 5.0 %collective-permute-done.34 = bf16[1,96,1152]{2,1,0:T(8,128)(2,1)S(1)} collective-permute-done((bf16[1,96,1152]{2,1,0:T(8,128)(2,1)}, bf16[1,96,1152]{2,1,0:T(8,128)(2,1)S(1)}, u32[]{:S(2)}, u32[]{:S(2)}) %collective-permute-start.34) | collective-permute-done | bytes 221216 | tf_op jit(solution)/shard_map/ppermute | solution.py:405
  326.4 6.9 %collective-permute-start.39 = (f32[21,128]{1,0:T(8,128)S(1)}, f32[21,128]{1,0:T(8,128)S(1)}, u32[]{:S(2)}, u32[]{:S(2)}) collective-permute-start(f32[21,128]{1,0:T(8,128)S(1)} %maximum_bitcast_fusion.2), channel_id=1, source_target_pairs={{0,1},{1,0},{2,3},{3,2},{4,5},{5,4},{6,7},{7,6},{8,9},{9,8},{10,11... | collective-permute-start | bytes 32264 | tf_op jit(solution)/shard_map/ppermute | solution.py:462
  338.1 6.1 %encoder_grad.1 = f32[1024,768]{1,0:T(8,128)} custom-call(bf16[768,3840]{1,0:T(8,128)(2,1)} %assemble.3.wo_ref.wc_ref.wq_ref.ck_ref.cv_ref, bf16[768,3840]{1,0:T(8,128)(2,1)} %assemble.3.wo_ref.wc_ref.wq_ref.ck_ref.cv_ref, bf16[1024,768]{1,0:T(8,128)(2,1)} %get-tuple-element.1261.refs_3_.refs_0_, bf16[1024,768]{1,0:T(8,128)(2,1)} %get-tuple-element.1262.refs_4_.refs_1_), custom_call_target="tpu_custom_call" | custom-call | flops 1 | bytes 1 | tf_op jit(solution)/shard_map/encoder_grad/pallas_call | solution.py:533
  347.5 3.1 collective-permute-start.40
  356.1 3.1 collective-permute-done.42
  363.3 5.5 %collective-permute-done.44 = bf16[1,24,3840]{2,1,0:T(8,128)(2,1)S(1)} collective-permute-done((bf16[1,24,3840]{2,1,0:T(8,128)(2,1)S(1)}, bf16[1,24,3840]{2,1,0:T(8,128)(2,1)S(1)}, u32[]{:S(2)}, u32[]{:S(2)}) %collective-permute-start.44) | collective-permute-done | bytes 184352 | tf_op jit(solution)/shard_map/ppermute | solution.py:403
  (227 shorter events, 87.2 us)
Async XLA Ops:
  7.2 137.5 %all-gather.2.cloned.1.call-start = ((), (), s32[]{:S(2)}) async-start(), calls=%async_computation.1 | async-start | bytes 9732096 | tf_op jit(solution)/shard_map/all_gather | solution.py:874
  9.6 14.4 %collective-permute-start = (bf16[24,2432]{1,0:T(8,128)(2,1)S(1)}, bf16[24,2432]{1,0:T(8,128)(2,1)S(1)}, u32[]{:S(2)}, u32[]{:S(2)}) collective-permute-start(bf16[24,2432]{1,0:T(8,128)(2,1)S(1)} %fusion.4), channel_id=1, source_target_pairs={{0,1},{1,0},{2,3},{3,2},{4,5},{5,4},{6,7},{7,6},{8,9},{9,8},{10,11... | collective-permute-start | bytes 350216 | tf_op jit(solution)/shard_map/ppermute | solution.py:316
  12.7 11.9 %collective-permute-start.1 = (bf16[24,2432]{1,0:T(8,128)(2,1)S(1)}, bf16[24,2432]{1,0:T(8,128)(2,1)S(1)}, u32[]{:S(2)}, u32[]{:S(2)}) collective-permute-start(bf16[24,2432]{1,0:T(8,128)(2,1)S(1)} %fusion.4), channel_id=1, source_target_pairs={{0,2},{1,3},{2,0},{3,1},{4,6},{5,7},{6,4},{7,5},{8,10},{9,11},{10,... | collective-permute-start | bytes 350216 | tf_op jit(solution)/shard_map/ppermute | solution.py:316
  32.3 11.1 %collective-permute-start.6 = (bf16[192,1280]{1,0:T(8,128)(2,1)S(1)}, bf16[192,1280]{1,0:T(8,128)(2,1)S(1)}, u32[]{:S(2)}, u32[]{:S(2)}) collective-permute-start(bf16[192,1280]{1,0:T(8,128)(2,1)S(1)} %constant_dynamic-update-slice_fusion.3.refs_4_), channel_id=1, source_target_pairs={{0,8},{4,12},{8,0},{12,4},{16,24},{20,28},{24,16},{28,20},{1,9},{5... | collective-permute-start | bytes 1474568 | tf_op jit(solution)/shard_map/ppermute | solution.py:320
  36.3 14.3 %collective-permute-start.12 = (bf16[24,3840]{1,0:T(8,128)(2,1)S(1)}, bf16[24,3840]{1,0:T(8,128)(2,1)S(1)}, u32[]{:S(2)}, u32[]{:S(2)}) collective-permute-start(bf16[24,3840]{1,0:T(8,128)(2,1)S(1)} %bitcast_dynamic-update-slice_fusion), channel_id=1, source_target_pairs={{0,2},{1,3},{2,0},{3,1},{4,6},{5,7},{6,4},{7,5},{8,10},{9,11},{10,... | collective-permute-start | bytes 552968 | tf_op jit(solution)/shard_map/ppermute | solution.py:316
  38.7 12.7 %collective-permute-start.13 = (bf16[24,3840]{1,0:T(8,128)(2,1)S(1)}, bf16[24,3840]{1,0:T(8,128)(2,1)}, u32[]{:S(2)}, u32[]{:S(2)}) collective-permute-start(bf16[24,3840]{1,0:T(8,128)(2,1)S(1)} %bitcast_dynamic-update-slice_fusion), channel_id=1, source_target_pairs={{0,3},{1,2},{2,1},{3,0},{4,7},{5,6},{6,5},{7,4},{8,11},{9,10},{10,... | collective-permute-start | bytes 552968 | tf_op jit(solution)/shard_map/ppermute | solution.py:316
  52.6 291.7 %reduce-scatter.2.cloned.1.call-start = ((), (), s32[]{:S(2)}) async-start(), calls=%async_computation.2 | async-start | bytes 9732096 | tf_op jit(solution)/shard_map/reduce_scatter | solution.py:889
  54.4 15.6 %collective-permute-start.14 = (bf16[96,1920]{1,0:T(8,128)(2,1)S(1)}, bf16[96,1920]{1,0:T(8,128)(2,1)S(1)}, u32[]{:S(2)}, u32[]{:S(2)}) collective-permute-start(bf16[96,1920]{1,0:T(8,128)(2,1)S(1)} %get-tuple-element.780), channel_id=1, source_target_pairs={{0,8},{4,12},{8,0},{12,4},{16,24},{20,28},{24,16},{28,20},{1,9},{5... | collective-permute-start | bytes 1105928 | tf_op jit(solution)/shard_map/ppermute | solution.py:320
  55.0 15.0 %collective-permute-start.15 = (bf16[96,1920]{1,0:T(8,128)(2,1)S(1)}, bf16[96,1920]{1,0:T(8,128)(2,1)S(1)}, u32[]{:S(2)}, u32[]{:S(2)}) collective-permute-start(bf16[96,1920]{1,0:T(8,128)(2,1)S(1)} %get-tuple-element.782), channel_id=1, source_target_pairs={{0,16},{4,20},{8,24},{12,28},{16,0},{20,4},{24,8},{28,12},{1,17},{... | collective-permute-start | bytes 1105928 | tf_op jit(solution)/shard_map/ppermute | solution.py:320
  70.1 26.1 %collective-permute-start.17 = (bf16[192,1920]{1,0:T(8,128)(2,1)S(1)}, bf16[192,1920]{1,0:T(8,128)(2,1)S(1)}, u32[]{:S(2)}, u32[]{:S(2)}) collective-permute-start(bf16[192,1920]{1,0:T(8,128)(2,1)S(1)} %constant_dynamic-update-slice_fusion.7.refs_4_), channel_id=1, source_target_pairs={{0,8},{4,12},{8,0},{12,4},{16,24},{20,28},{24,16},{28,20},{1,9},{5... | collective-permute-start | bytes 2211848 | tf_op jit(solution)/shard_map/ppermute | solution.py:320
  71.7 24.5 %collective-permute-start.16 = (bf16[192,1920]{1,0:T(8,128)(2,1)S(1)}, bf16[192,1920]{1,0:T(8,128)(2,1)S(1)}, u32[]{:S(2)}, u32[]{:S(2)}) collective-permute-start(bf16[192,1920]{1,0:T(8,128)(2,1)S(1)} %constant_dynamic-update-slice_fusion.5.refs_0_), channel_id=1, source_target_pairs={{0,16},{4,20},{8,24},{12,28},{16,0},{20,4},{24,8},{28,12},{1,17},{... | collective-permute-start | bytes 2211848 | tf_op jit(solution)/shard_map/ppermute | solution.py:320
  218.1 10.5 %collective-permute-start.22 = (bf16[1,4,96,2304]{3,2,1,0:T(8,128)(2,1)}, bf16[1,4,96,2304]{3,2,1,0:T(8,128)(2,1)S(1)}, u32[]{:S(2)}, u32[]{:S(2)}) collective-permute-start(bf16[1,4,96,2304]{3,2,1,0:T(8,128)(2,1)} %get-tuple-element.1099), channel_id=1, source_target_pairs={{0,4},{4,0},{8,12},{12,8},{16,20},{20,16},{24,28},{28,24},{1,5},{5... | collective-permute-start | bytes 5308424 | tf_op jit(solution)/shard_map/ppermute | solution.py:407
  235.4 16.9 %collective-permute-start.23 = (bf16[1,4,96,1536]{3,2,1,0:T(8,128)(2,1)}, bf16[1,4,96,1536]{3,2,1,0:T(8,128)(2,1)}, u32[]{:S(2)}, u32[]{:S(2)}) collective-permute-start(bf16[1,4,96,1536]{3,2,1,0:T(8,128)(2,1)} %get-tuple-element.1148), channel_id=1, source_target_pairs={{0,4},{4,0},{8,12},{12,8},{16,20},{20,16},{24,28},{28,24},{1,5},{5... | collective-permute-start | bytes 3538952 | tf_op jit(solution)/shard_map/ppermute | solution.py:407
  237.3 31.3 %collective-permute-start.24 = (bf16[2,96,2304]{2,1,0:T(8,128)(2,1)}, bf16[2,96,2304]{2,1,0:T(8,128)(2,1)S(1)}, u32[]{:S(2)}, u32[]{:S(2)}) collective-permute-start(bf16[2,96,2304]{2,1,0:T(8,128)(2,1)} %get-tuple-element.1368), channel_id=1, source_target_pairs={{0,8},{4,12},{8,0},{12,4},{16,24},{20,28},{24,16},{28,20},{1,9},{5... | collective-permute-start | bytes 2654216 | tf_op jit(solution)/shard_map/ppermute | solution.py:407
  254.8 33.1 %collective-permute-start.26 = (bf16[1,192,1536]{2,1,0:T(8,128)(2,1)}, bf16[1,192,1536]{2,1,0:T(8,128)(2,1)}, u32[]{:S(2)}, u32[]{:S(2)}) collective-permute-start(bf16[1,192,1536]{2,1,0:T(8,128)(2,1)} %get-tuple-element.1370), channel_id=1, source_target_pairs={{0,16},{4,20},{8,24},{12,28},{16,0},{20,4},{24,8},{28,12},{1,17},{... | collective-permute-start | bytes 1769480 | tf_op jit(solution)/shard_map/ppermute | solution.py:407
  268.6 19.2 %collective-permute-start.27 = (bf16[1,4,96,1152]{3,2,1,0:T(8,128)(2,1)}, bf16[1,4,96,1152]{3,2,1,0:T(8,128)(2,1)S(1)}, u32[]{:S(2)}, u32[]{:S(2)}) collective-permute-start(bf16[1,4,96,1152]{3,2,1,0:T(8,128)(2,1)} %get-tuple-element.1202), channel_id=1, source_target_pairs={{0,4},{4,0},{8,12},{12,8},{16,20},{20,16},{24,28},{28,24},{1,5},{5... | collective-permute-start | bytes 2654216 | tf_op jit(solution)/shard_map/ppermute | solution.py:407
  268.9 19.0 %collective-permute-start.25 = (bf16[1,96,2304]{2,1,0:T(8,128)(2,1)S(1)}, bf16[1,96,2304]{2,1,0:T(8,128)(2,1)S(1)}, u32[]{:S(2)}, u32[]{:S(2)}) collective-permute-start(bf16[1,96,2304]{2,1,0:T(8,128)(2,1)S(1)} %get-tuple-element.1380), channel_id=1, source_target_pairs={{0,16},{4,20},{8,24},{12,28},{16,0},{20,4},{24,8},{28,12},{1,17},{... | collective-permute-start | bytes 1327112 | tf_op jit(solution)/shard_map/ppermute | solution.py:407
  288.1 12.8 %collective-permute-start.28 = (bf16[1,24,2304]{2,1,0:T(8,128)(2,1)S(1)}, bf16[1,24,2304]{2,1,0:T(8,128)(2,1)S(1)}, u32[]{:S(2)}, u32[]{:S(2)}) collective-permute-start(bf16[1,24,2304]{2,1,0:T(8,128)(2,1)S(1)} %get-tuple-element.1396), channel_id=1, source_target_pairs={{0,1},{1,0},{2,3},{3,2},{4,5},{5,4},{6,7},{7,6},{8,9},{9,8},{10,11... | collective-permute-start | bytes 331784 | tf_op jit(solution)/shard_map/ppermute | solution.py:403
  288.1 14.8 %collective-permute-start.29 = (bf16[1,24,2304]{2,1,0:T(8,128)(2,1)S(1)}, bf16[1,24,2304]{2,1,0:T(8,128)(2,1)S(1)}, u32[]{:S(2)}, u32[]{:S(2)}) collective-permute-start(bf16[1,24,2304]{2,1,0:T(8,128)(2,1)S(1)} %get-tuple-element.1395), channel_id=1, source_target_pairs={{0,2},{1,3},{2,0},{3,1},{4,6},{5,7},{6,4},{7,5},{8,10},{9,11},{10,... | collective-permute-start | bytes 331784 | tf_op jit(solution)/shard_map/ppermute | solution.py:403
  291.3 11.7 %collective-permute-start.30 = (bf16[1,24,2304]{2,1,0:T(8,128)(2,1)S(1)}, bf16[1,24,2304]{2,1,0:T(8,128)(2,1)S(1)}, u32[]{:S(2)}, u32[]{:S(2)}) collective-permute-start(bf16[1,24,2304]{2,1,0:T(8,128)(2,1)S(1)} %get-tuple-element.1394), channel_id=1, source_target_pairs={{0,3},{1,2},{2,1},{3,0},{4,7},{5,6},{6,5},{7,4},{8,11},{9,10},{10,... | collective-permute-start | bytes 331784 | tf_op jit(solution)/shard_map/ppermute | solution.py:403
  302.9 20.7 %collective-permute-start.35 = (bf16[1,4,96,1152]{3,2,1,0:T(8,128)(2,1)}, bf16[1,4,96,1152]{3,2,1,0:T(8,128)(2,1)S(1)}, u32[]{:S(2)}, u32[]{:S(2)}) collective-permute-start(bf16[1,4,96,1152]{3,2,1,0:T(8,128)(2,1)} %get-tuple-element.1259), channel_id=1, source_target_pairs={{0,4},{4,0},{8,12},{12,8},{16,20},{20,16},{24,28},{28,24},{1,5},{5... | collective-permute-start | bytes 2654216 | tf_op jit(solution)/shard_map/ppermute | solution.py:407
  303.0 15.6 %collective-permute-start.31 = (bf16[1,96,1536]{2,1,0:T(8,128)(2,1)S(1)}, bf16[1,96,1536]{2,1,0:T(8,128)(2,1)S(1)}, u32[]{:S(2)}, u32[]{:S(2)}) collective-permute-start(bf16[1,96,1536]{2,1,0:T(8,128)(2,1)S(1)} %get-tuple-element.1388), channel_id=1, source_target_pairs={{0,8},{4,12},{8,0},{12,4},{16,24},{20,28},{24,16},{28,20},{1,9},{5... | collective-permute-start | bytes 884744 | tf_op jit(solution)/shard_map/ppermute | solution.py:407
  303.4 15.2 %collective-permute-start.32 = (bf16[1,96,1152]{2,1,0:T(8,128)(2,1)}, bf16[1,96,1152]{2,1,0:T(8,128)(2,1)S(1)}, u32[]{:S(2)}, u32[]{:S(2)}) collective-permute-start(bf16[1,96,1152]{2,1,0:T(8,128)(2,1)} %get-tuple-element.1255), channel_id=1, source_target_pairs={{0,8},{4,12},{8,0},{12,4},{16,24},{20,28},{24,16},{28,20},{1,9},{5... | collective-permute-start | bytes 663560 | tf_op jit(solution)/shard_map/ppermute | solution.py:405
  305.1 13.6 %collective-permute-start.33 = (bf16[1,96,1152]{2,1,0:T(8,128)(2,1)}, bf16[1,96,1152]{2,1,0:T(8,128)(2,1)S(1)}, u32[]{:S(2)}, u32[]{:S(2)}) collective-permute-start(bf16[1,96,1152]{2,1,0:T(8,128)(2,1)} %get-tuple-element.1256), channel_id=1, source_target_pairs={{0,16},{4,20},{8,24},{12,28},{16,0},{20,4},{24,8},{28,12},{1,17},{... | collective-permute-start | bytes 663560 | tf_op jit(solution)/shard_map/ppermute | solution.py:405
  306.2 17.5 %collective-permute-start.34 = (bf16[1,96,1152]{2,1,0:T(8,128)(2,1)}, bf16[1,96,1152]{2,1,0:T(8,128)(2,1)S(1)}, u32[]{:S(2)}, u32[]{:S(2)}) collective-permute-start(bf16[1,96,1152]{2,1,0:T(8,128)(2,1)} %get-tuple-element.1257), channel_id=1, source_target_pairs={{0,24},{4,28},{8,16},{12,20},{16,8},{20,12},{24,0},{28,4},{1,25},{... | collective-permute-start | bytes 663560 | tf_op jit(solution)/shard_map/ppermute | solution.py:405
  326.4 19.4 %collective-permute-start.39 = (f32[21,128]{1,0:T(8,128)S(1)}, f32[21,128]{1,0:T(8,128)S(1)}, u32[]{:S(2)}, u32[]{:S(2)}) collective-permute-start(f32[21,128]{1,0:T(8,128)S(1)} %maximum_bitcast_fusion.2), channel_id=1, source_target_pairs={{0,1},{1,0},{2,3},{3,2},{4,5},{5,4},{6,7},{7,6},{8,9},{9,8},{10,11... | collective-permute-start | bytes 32264 | tf_op jit(solution)/shard_map/ppermute | solution.py:462
  334.4 11.5 %collective-permute-start.36 = (bf16[1,96,1152]{2,1,0:T(8,128)(2,1)}, bf16[1,96,1152]{2,1,0:T(8,128)(2,1)S(1)}, u32[]{:S(2)}, u32[]{:S(2)}) collective-permute-start(bf16[1,96,1152]{2,1,0:T(8,128)(2,1)} %get-tuple-element.1374), channel_id=1, source_target_pairs={{0,8},{4,12},{8,0},{12,4},{16,24},{20,28},{24,16},{28,20},{1,9},{5... | collective-permute-start | bytes 663560 | tf_op jit(solution)/shard_map/ppermute | solution.py:405
  334.6 11.2 %collective-permute-start.37 = (bf16[1,96,1152]{2,1,0:T(8,128)(2,1)}, bf16[1,96,1152]{2,1,0:T(8,128)(2,1)S(1)}, u32[]{:S(2)}, u32[]{:S(2)}) collective-permute-start(bf16[1,96,1152]{2,1,0:T(8,128)(2,1)} %get-tuple-element.1373), channel_id=1, source_target_pairs={{0,16},{4,20},{8,24},{12,28},{16,0},{20,4},{24,8},{28,12},{1,17},{... | collective-permute-start | bytes 663560 | tf_op jit(solution)/shard_map/ppermute | solution.py:405
  336.5 11.0 %collective-permute-start.38 = (bf16[1,96,1152]{2,1,0:T(8,128)(2,1)S(1)}, bf16[1,96,1152]{2,1,0:T(8,128)(2,1)S(1)}, u32[]{:S(2)}, u32[]{:S(2)}) collective-permute-start(bf16[1,96,1152]{2,1,0:T(8,128)(2,1)S(1)} %get-tuple-element.1372), channel_id=1, source_target_pairs={{0,24},{4,28},{8,16},{12,20},{16,8},{20,12},{24,0},{28,4},{1,25},{... | collective-permute-start | bytes 663560 | tf_op jit(solution)/shard_map/ppermute | solution.py:405
  350.8 12.5 %collective-permute-start.45 = (bf16[1,24,3840]{2,1,0:T(8,128)(2,1)S(1)}, bf16[1,24,3840]{2,1,0:T(8,128)(2,1)S(1)}, u32[]{:S(2)}, u32[]{:S(2)}) collective-permute-start(bf16[1,24,3840]{2,1,0:T(8,128)(2,1)S(1)} %pad_maximum_fusion.9), channel_id=1, source_target_pairs={{0,3},{1,2},{2,1},{3,0},{4,7},{5,6},{6,5},{7,4},{8,11},{9,10},{10,... | collective-permute-start | bytes 552968 | tf_op jit(solution)/shard_map/ppermute | solution.py:403
  352.1 16.8 %collective-permute-start.44 = (bf16[1,24,3840]{2,1,0:T(8,128)(2,1)S(1)}, bf16[1,24,3840]{2,1,0:T(8,128)(2,1)S(1)}, u32[]{:S(2)}, u32[]{:S(2)}) collective-permute-start(bf16[1,24,3840]{2,1,0:T(8,128)(2,1)S(1)} %pad_maximum_fusion.8), channel_id=1, source_target_pairs={{0,2},{1,3},{2,0},{3,1},{4,6},{5,7},{6,4},{7,5},{8,10},{9,11},{10,... | collective-permute-start | bytes 552968 | tf_op jit(solution)/shard_map/ppermute | solution.py:403
  354.2 14.7 %collective-permute-start.43 = (bf16[1,24,3840]{2,1,0:T(8,128)(2,1)S(1)}, bf16[1,24,3840]{2,1,0:T(8,128)(2,1)S(1)}, u32[]{:S(2)}, u32[]{:S(2)}) collective-permute-start(bf16[1,24,3840]{2,1,0:T(8,128)(2,1)S(1)} %pad_maximum_fusion.7), channel_id=1, source_target_pairs={{0,1},{1,0},{2,3},{3,2},{4,5},{5,4},{6,7},{7,6},{8,9},{9,8},{10,11... | collective-permute-start | bytes 552968 | tf_op jit(solution)/shard_map/ppermute | solution.py:403
  (39 other events, 394.2 us)
Sparse Core Ops, SparseCore 0:
  52.7 88.3 all-gather.1
  181.6 152.3 reduce-scatter.1
